TPU v7x, 32 devices: a whole 2x2x4 slice. The times are simulated.
32 devices in a mesh: dp: 4 (over y, core), ctx: 8 (over z, x).
Axes of the slice: x: 2, y: 2, z: 4, core: 2. Of those that a mesh axis runs over, the one named last changes fastest.
Arguments:
- inputs: bfloat16 [8, 1024, 2048], P('dp', 'ctx'), may hold values from -6 to 6
- norm_gain: bfloat16 [2048], P(('dp', 'ctx')), may hold values from 0.25 to 1.75
- norm_bias: bfloat16 [2048], P(('dp', 'ctx')), may hold values from -3 to 3
- joined_weight: bfloat16 [2048, 6144], P(('dp', 'ctx')), may hold values from -0.125 to 0.125
- gate_weight: bfloat16 [2048, 5632], P(('dp', 'ctx')), may hold values from -0.125 to 0.125
- up_weight: bfloat16 [2048, 5632], P(('dp', 'ctx')), may hold values from -0.125 to 0.125
- out_weight: bfloat16 [2048, 2048], P(('dp', 'ctx')), may hold values from -3 to 3
- down_weight: bfloat16 [2048, 5632], P(('dp', 'ctx')), may hold values from -0.078125 to 0.078125
- cotangent: bfloat16 [8, 1024, 2048], P('dp', 'ctx'), may hold values from -6 to 6
- lengths: int32 [8], P('dp'), may hold values from 128 to 1024, as said below
Outputs:
- output: bfloat16 [8, 1024, 2048], P('dp', 'ctx')
- input_grad: bfloat16 [8, 1024, 2048], P('dp', 'ctx')
- gain_grad: float32 [2048], P(('dp', 'ctx'))
- bias_grad: float32 [2048], P(('dp', 'ctx'))
- joined_grad: float32 [2048, 6144], P(('dp', 'ctx'))
- gate_grad: float32 [2048, 5632], P(('dp', 'ctx'))
- up_grad: float32 [2048, 5632], P(('dp', 'ctx'))
- out_grad: float32 [2048, 2048], P(('dp', 'ctx'))
- down_grad: float32 [2048, 5632], P(('dp', 'ctx'))
Inputs may be any that keep to these rules, and one draw needn't show every extreme that they name: `lengths`: of the 2 sequences on each index of dp, one drawn from the seed has all 1024 tokens; each other one has from 128 to 512 real tokens.
All inputs are finite; a program needn't handle non-finite values.
Results may differ from a plain program's by a relative error of at most 0.011.
Values may be sent and summed in bfloat16 or wider, within the bound.
No kernel may reach another device: no remote copies, remote signals or barrier semaphores. Data moves between devices by JAX's collectives and lax.ppermute only.
A program may use at most 640 MiB of HBM per device.

v0:
```python
import jax
import jax.numpy as jnp
from jax import lax
from jax.sharding import PartitionSpec as P

H = 32
HD = 64
ROT = 16
FF = 5632


EPSILON = 1e-05
THETA = 10000.0
NEGATIVE = -1e30
HIGHEST = lax.Precision.HIGHEST
CONTRACT_LAST = (((1,), (1,)), ((), ()))
CONTRACT_FIRST = (((0,), (0,)), ((), ()))


def rotary_tables(positions):
    halfway = ROT // 2
    frequency = THETA ** (-(2.0 * jnp.arange(halfway, dtype=jnp.float32)) / ROT)
    angles = positions.astype(jnp.float32)[:, None] * frequency[None, :]
    return (jnp.cos(angles)[:, None, :], jnp.sin(angles)[:, None, :])


def rotate(tensor, cosine_table, sine_table):
    halfway = ROT // 2
    first = tensor[..., :halfway]
    second = tensor[..., halfway:ROT]
    return jnp.concatenate(
        [
            first * cosine_table - second * sine_table,
            second * cosine_table + first * sine_table,
            tensor[..., ROT:],
        ],
        axis=-1,
    )


def unrotate(gradient, cosine_table, sine_table):
    halfway = ROT // 2
    first = gradient[..., :halfway]
    second = gradient[..., halfway:ROT]
    return jnp.concatenate(
        [
            first * cosine_table + second * sine_table,
            second * cosine_table - first * sine_table,
            gradient[..., ROT:],
        ],
        axis=-1,
    )


def allowed_mask(query_pos, key_pos, alive_rows):
    return (key_pos[None, None, :] <= query_pos[None, :, None]) & alive_rows[:, :, None]


def matmul_last(left, right):
    return lax.dot_general(left, right, CONTRACT_LAST, preferred_element_type=jnp.float32)


def on_device(
    inputs,
    norm_gain,
    norm_bias,
    joined_weight,
    gate_weight,
    up_weight,
    out_weight,
    down_weight,
    cotangent,
    lengths,
):
    groups, seq_rows, features = inputs.shape
    tokens = groups * seq_rows
    flat_in = inputs.reshape(tokens, features).astype(jnp.float32)
    center = flat_in - jnp.mean(flat_in, axis=-1, keepdims=True)
    variance = jnp.mean(center * center, axis=-1, keepdims=True)
    inverse = lax.rsqrt(variance + EPSILON)
    standard = center * inverse
    local_pos = lax.axis_index("ctx") * seq_rows + jnp.arange(seq_rows, dtype=jnp.int32)
    cosine_table, sine_table = rotary_tables(jnp.tile(local_pos, groups))
    query_live = local_pos[None, :] < lengths[:, None]
    piece_joined = lax.all_gather(joined_weight, ("dp", "ctx"), axis=0, tiled=True)
    piece_gate = lax.all_gather(gate_weight, ("dp", "ctx"), axis=0, tiled=True)
    piece_up = lax.all_gather(up_weight, ("dp", "ctx"), axis=0, tiled=True)
    piece_gain = lax.all_gather(norm_gain, ("dp", "ctx"), axis=0, tiled=True)
    piece_bias = lax.all_gather(norm_bias, ("dp", "ctx"), axis=0, tiled=True)
    amount = piece_joined.shape[0]
    columns = standard
    block_cols = (columns * piece_gain.astype(jnp.float32) + piece_bias.astype(jnp.float32)).astype(
        jnp.bfloat16
    )
    joined_sum = jnp.dot(block_cols, piece_joined, preferred_element_type=jnp.float32)
    gate_sum = jnp.dot(block_cols, piece_gate, preferred_element_type=jnp.float32)
    up_sum = jnp.dot(block_cols, piece_up, preferred_element_type=jnp.float32)
    queries = joined_sum[:, :features].reshape(tokens, H, HD)
    keys = joined_sum[:, features : 2 * features].reshape(tokens, H, HD)
    values = joined_sum[:, 2 * features :]
    queries_rot = (
        rotate(queries, cosine_table, sine_table)
        .astype(jnp.bfloat16)
        .reshape(groups, seq_rows, H, HD)
    )
    keys_rot = (
        rotate(keys, cosine_table, sine_table)
        .astype(jnp.bfloat16)
        .reshape(groups, seq_rows, features)
    )
    values_low = values.astype(jnp.bfloat16).reshape(groups, seq_rows, features)
    sigmoid_gate = jax.nn.sigmoid(gate_sum)
    silu_gate = gate_sum * sigmoid_gate
    hidden = (silu_gate * up_sum).astype(jnp.bfloat16)
    start_attend = (
        jnp.full((groups, H, seq_rows), NEGATIVE, jnp.float32),
        jnp.zeros((groups, H, seq_rows), jnp.float32),
        jnp.zeros((groups, H, seq_rows, HD), jnp.float32),
    )
    piece_keys = lax.all_gather(keys_rot, "ctx", axis=1, tiled=True)
    piece_values = lax.all_gather(values_low, "ctx", axis=1, tiled=True)
    amount = piece_keys.shape[1]
    allowed = allowed_mask(local_pos, jnp.arange(amount, dtype=jnp.int32), query_live)

    def compute(running):
        row_max, row_sum, weighted = running
        keys_split = piece_keys.reshape(groups, amount, H, HD)
        values_split = piece_values.reshape(groups, amount, H, HD).astype(jnp.float32)
        scores = (
            jnp.einsum(
                "gqhd,gkhd->ghqk", queries_rot, keys_split, preferred_element_type=jnp.float32
            )
            * 0.125
        )
        masked = jnp.where(allowed[:, None], scores, NEGATIVE)
        new_max = jnp.maximum(row_max, jnp.max(masked, axis=-1))
        exponent = jnp.where(allowed[:, None], jnp.exp(masked - new_max[..., None]), 0.0)
        row_sum = jnp.sum(exponent, axis=-1)
        weighted = jnp.einsum("ghqk,gkhd->ghqd", exponent, values_split, precision=HIGHEST)
        return (new_max, row_sum, weighted)

    row_max, row_sum, weighted = lax.cond(
        jnp.any(allowed), compute, lambda running: running, start_attend
    )
    live_heads = query_live[:, None, :]
    safe_sum = jnp.where(live_heads, row_sum, 1.0)
    attended = jnp.where(live_heads[..., None], weighted / safe_sum[..., None], 0.0)
    log_total = jnp.where(live_heads, row_max + jnp.log(safe_sum), 0.0)
    attended_rows = attended.transpose(0, 2, 1, 3)
    attn_rows = attended_rows.reshape(tokens, features).astype(jnp.bfloat16)
    cot_rows = cotangent.reshape(tokens, features)
    piece_out = lax.all_gather(out_weight, ("dp", "ctx"), axis=0, tiled=True)
    piece_down = lax.all_gather(down_weight, ("dp", "ctx"), axis=0, tiled=True)
    columns = matmul_last(attn_rows, piece_out) + matmul_last(hidden, piece_down)
    output = (flat_in + columns).astype(jnp.bfloat16).reshape(groups, seq_rows, features)
    piece_out = lax.all_gather(out_weight, ("dp", "ctx"), axis=0, tiled=True)
    piece_down = lax.all_gather(down_weight, ("dp", "ctx"), axis=0, tiled=True)
    d_attn = jnp.dot(cot_rows, piece_out, preferred_element_type=jnp.float32)
    d_hidden = jnp.dot(cot_rows, piece_down, preferred_element_type=jnp.float32)
    out_operands = jnp.concatenate([attn_rows, hidden], axis=1)
    attended_grad = jnp.where(
        query_live[:, :, None], d_attn.astype(jnp.bfloat16).reshape(groups, seq_rows, features), 0
    )
    grad_split = attended_grad.reshape(groups, seq_rows, H, HD)
    row_delta = jnp.sum(grad_split.astype(jnp.float32) * attended_rows, axis=-1).transpose(0, 2, 1)
    grad_piece_keys = lax.all_gather(keys_rot, "ctx", axis=1, tiled=True)
    grad_piece_values = lax.all_gather(values_low, "ctx", axis=1, tiled=True)
    grad_amount = grad_piece_keys.shape[1]
    grad_allowed = allowed_mask(local_pos, jnp.arange(grad_amount, dtype=jnp.int32), query_live)

    def compute(query_grads):
        keys_split = grad_piece_keys.reshape(groups, grad_amount, H, HD)
        values_split = grad_piece_values.reshape(groups, grad_amount, H, HD)
        scores = (
            jnp.einsum(
                "gqhd,gkhd->ghqk", queries_rot, keys_split, preferred_element_type=jnp.float32
            )
            * 0.125
        )
        probs = jnp.where(grad_allowed[:, None], jnp.exp(scores - log_total[..., None]), 0.0)
        prob_grads = jnp.einsum(
            "gqhd,gkhd->ghqk", grad_split, values_split, preferred_element_type=jnp.float32
        )
        score_grads = (probs * (prob_grads - row_delta[..., None])).astype(jnp.bfloat16)
        return jnp.einsum(
            "ghqk,gkhd->ghqd", score_grads, keys_split, preferred_element_type=jnp.float32
        )

    query_grads = lax.cond(
        jnp.any(grad_allowed),
        compute,
        lambda query_grads: query_grads,
        jnp.zeros((groups, H, seq_rows, HD), jnp.float32),
    )
    all_log, all_delta = (
        lax.all_gather(log_total, "ctx", axis=2, tiled=True),
        lax.all_gather(row_delta, "ctx", axis=2, tiled=True),
    )
    keys_own = keys_rot.reshape(groups, seq_rows, H, HD)
    values_own = values_low.reshape(groups, seq_rows, H, HD)
    query_send = queries_rot.reshape(groups, seq_rows, features)

    def grad_keys(totals, pieces):
        piece_queries, piece_grads = pieces
        amount = piece_queries.shape[1]
        remote_pos = jnp.arange(amount, dtype=jnp.int32)
        remote_live = remote_pos[None, :] < lengths[:, None]
        allowed = allowed_mask(remote_pos, local_pos, remote_live)

        def compute(running):
            queries_split = piece_queries.reshape(groups, amount, H, HD)
            grads_split = piece_grads.reshape(groups, amount, H, HD)
            scores = (
                jnp.einsum(
                    "gqhd,gkhd->ghqk", queries_split, keys_own, preferred_element_type=jnp.float32
                )
                * 0.125
            )
            probs = jnp.where(allowed[:, None], jnp.exp(scores - all_log[..., None]), 0.0)
            prob_grads = jnp.einsum(
                "gqhd,gkhd->ghqk", grads_split, values_own, preferred_element_type=jnp.float32
            )
            score_grads = (probs * (prob_grads - all_delta[..., None])).astype(jnp.bfloat16)
            key_grads = jnp.einsum(
                "ghqk,gqhd->ghkd", score_grads, queries_split, preferred_element_type=jnp.float32
            )
            value_grads = jnp.einsum(
                "ghqk,gqhd->ghkd", probs, grads_split.astype(jnp.float32), precision=HIGHEST
            )
            return (key_grads, value_grads)

        return lax.cond(jnp.any(allowed), compute, lambda running: running, totals)

    start_keys = (
        jnp.zeros((groups, H, seq_rows, HD), jnp.float32),
        jnp.zeros((groups, H, seq_rows, HD), jnp.float32),
    )
    key_grads, value_grads = grad_keys(
        start_keys,
        (
            lax.all_gather(query_send, "ctx", axis=1, tiled=True),
            lax.all_gather(attended_grad, "ctx", axis=1, tiled=True),
        ),
    )

    def to_rows(tensor):
        return tensor.transpose(0, 2, 1, 3).reshape(tokens, H, HD)

    query_plain = unrotate(to_rows(query_grads) * 0.125, cosine_table, sine_table).reshape(
        tokens, features
    )
    key_plain = unrotate(to_rows(key_grads) * 0.125, cosine_table, sine_table).reshape(
        tokens, features
    )
    value_plain = to_rows(value_grads).reshape(tokens, features)
    joined_grads = jnp.concatenate([query_plain, key_plain, value_plain], axis=1).astype(
        jnp.bfloat16
    )
    gate_grads = (
        d_hidden * up_sum * sigmoid_gate * (1.0 + gate_sum * (1.0 - sigmoid_gate))
    ).astype(jnp.bfloat16)
    up_grads = (d_hidden * silu_gate).astype(jnp.bfloat16)
    grads_rows = jnp.concatenate([joined_grads, gate_grads, up_grads], axis=1)

    def grad_normed(pieces):
        piece_joined, piece_gate, piece_up, piece_gain = pieces
        amount = piece_joined.shape[0]
        normed_grads = (
            matmul_last(joined_grads, piece_joined)
            + matmul_last(gate_grads, piece_gate)
            + matmul_last(up_grads, piece_up)
        )
        standard_grad = normed_grads * piece_gain.astype(jnp.float32)
        gain_term = jnp.sum(normed_grads * standard, axis=0)
        bias_term = jnp.sum(normed_grads, axis=0)
        return (standard_grad, gain_term, bias_term)

    standard_grad, gain_term, bias_term = grad_normed(
        (
            lax.all_gather(joined_weight, ("dp", "ctx"), axis=0, tiled=True),
            lax.all_gather(gate_weight, ("dp", "ctx"), axis=0, tiled=True),
            lax.all_gather(up_weight, ("dp", "ctx"), axis=0, tiled=True),
            lax.all_gather(norm_gain, ("dp", "ctx"), axis=0, tiled=True),
        )
    )
    centered_grad = (
        standard_grad
        - jnp.mean(standard_grad, axis=-1, keepdims=True)
        - standard * jnp.mean(standard_grad * standard, axis=-1, keepdims=True)
    )
    input_grad = (cot_rows.astype(jnp.float32) + inverse * centered_grad).astype(jnp.bfloat16)
    input_grad = input_grad.reshape(groups, seq_rows, features)
    out_term = lax.dot_general(
        cot_rows, out_operands, CONTRACT_FIRST, preferred_element_type=jnp.float32
    )
    products = lax.dot_general(
        block_cols, grads_rows, CONTRACT_FIRST, preferred_element_type=jnp.float32
    )
    norm_cols = jnp.pad(jnp.stack([gain_term, bias_term], axis=1), ((0, 0), (0, 126)))
    in_term = jnp.concatenate([products, norm_cols], axis=1)
    out_sums, in_sums = (
        lax.psum_scatter(out_term, ("dp", "ctx"), scatter_dimension=0, tiled=True),
        lax.psum_scatter(in_term, ("dp", "ctx"), scatter_dimension=0, tiled=True),
    )
    out_grad = out_sums[:, :features]
    down_grad = out_sums[:, features:]
    joined_grad = in_sums[:, : 3 * features]
    gate_grad = in_sums[:, 3 * features : 3 * features + FF]
    up_grad = in_sums[:, 3 * features + FF : 3 * features + 2 * FF]
    gain_grad = in_sums[:, 3 * features + 2 * FF]
    bias_grad = in_sums[:, 3 * features + 2 * FF + 1]
    return (
        output,
        input_grad,
        gain_grad,
        bias_grad,
        joined_grad,
        gate_grad,
        up_grad,
        out_grad,
        down_grad,
    )


def solution(mesh):
    in_specs = (
        P("dp", "ctx", None),
        P(("dp", "ctx")),
        P(("dp", "ctx")),
        P(("dp", "ctx"), None),
        P(("dp", "ctx"), None),
        P(("dp", "ctx"), None),
        P(("dp", "ctx"), None),
        P(("dp", "ctx"), None),
        P("dp", "ctx", None),
        P("dp"),
    )
    out_specs = (
        P("dp", "ctx", None),
        P("dp", "ctx", None),
        P(("dp", "ctx")),
        P(("dp", "ctx")),
        P(("dp", "ctx"), None),
        P(("dp", "ctx"), None),
        P(("dp", "ctx"), None),
        P(("dp", "ctx"), None),
        P(("dp", "ctx"), None),
    )
    return jax.shard_map(
        on_device, mesh=mesh, in_specs=in_specs, out_specs=out_specs, check_vma=False
    )
```

profile of v0, /device:TPU:0, one launch (start us, length us, event | category | flops | bytes accessed | tf_op | source)
XLA Modules:
  0.0 4847.6 jit_solution(4989319874931158845)
XLA Ops:
  11.7 43.6 all-reduce.3
  60.8 109.1 %all-gather.10.cloned.1.call-done = bf16[2048,6144]{1,0:T(8,128)(2,1)} async-done(((bf16[64,6144]{1,0:T(8,128)(2,1)}), bf16[2048,6144]{1,0:T(8,128)(2,1)}) %all-gather.10.cloned.1.call-update) | async-done | bytes 25165840 | tf_op jit(solution)/shard_map/all_gather | solution.py:85
  206.3 42.2 all-gather.16.cloned.1.call-done
  268.8 125.8 %all-gather.18.cloned.1.call-done = bf16[2048,5632]{1,0:T(8,128)(2,1)} async-done(((bf16[64,5632]{1,0:T(8,128)(2,1)}), bf16[2048,5632]{1,0:T(8,128)(2,1)}) %all-gather.18.cloned.1.call-update) | async-done | bytes 23068688 | tf_op jit(solution)/shard_map/all_gather | solution.py:86
  407.8 132.4 %all-gather.20.cloned.1.call-done = bf16[2048,5632]{1,0:T(8,128)(2,1)} async-done(((bf16[64,5632]{1,0:T(8,128)(2,1)}), bf16[2048,5632]{1,0:T(8,128)(2,1)}) %all-gather.20.cloned.1.call-update) | async-done | bytes 23068688 | tf_op jit(solution)/shard_map/all_gather | solution.py:87
  540.2 18.7 multiply_convert_fusion.6
  561.2 105.1 %all-gather.14.cloned.1.call-done = bf16[2,1024,2048]{1,2,0:T(8,128)(2,1)} async-done(((bf16[2,128,2048]{1,2,0:T(8,128)(2,1)}), bf16[2,1024,2048]{1,2,0:T(8,128)(2,1)}) %all-gather.14.cloned.1.call-update) | async-done | bytes 8388624 | tf_op jit(solution)/shard_map/all_gather | solution.py:121
  666.3 186.2 %all-gather.12.cloned.1.call-done = bf16[2,1024,2048]{1,0,2:T(2,128)(2,1)} async-done(((bf16[2,128,2048]{1,0,2:T(2,128)(2,1)}), bf16[2,1024,2048]{1,0,2:T(2,128)(2,1)}) %all-gather.12.cloned.1.call-update) | async-done | bytes 8388624 | tf_op jit(solution)/shard_map/all_gather | solution.py:120
  852.5 77.7 %conditional.3 = (f32[2,32,128]{2,1,0:T(8,128)}, f32[2,32,128]{2,1,0:T(8,128)S(1)}, f32[2,32,128,64]{2,0,3,1:T(2,128)S(1)}) conditional(s32[]{:T(128)} %convert_element_type.96, () %tuple.30, (pred[2,128,1024]{2,1,0:T(8,128)(4,1)S(1)}, bf16[2,1024,2048]{1,0,2:T(2,128)(2,1)}, bf16[2,128,32,64]{1,3,2,0:T(8,128)(2,1)}, ...), branch_computations={%region_3.0_spmd, %region_4.7_spmd} | conditional | flops 7616847872 | bytes 142540832 | solution.py:142
  861.8 17.0 fusion
  879.4 33.1 fusion.1
  912.5 15.6 fusion.2
  937.3 23.8 convolution_bitcast_fusion
  961.1 61.5 %copy.86 = f32[2048,7680]{1,0:T(8,128)} copy(f32[2048,7680]{0,1:T(8,128)} %convolution_bitcast_fusion) | data formatting | bytes 125829120
  1040.5 20.8 all_gather.59
  1061.3 40.0 all_gather.57
  1101.3 31.8 all-gather.26.cloned.1.call-done
  1133.1 186.4 %all-gather.24.cloned.1.call-done = bf16[2,1024,2048]{1,0,2:T(2,128)(2,1)} async-done(((bf16[2,128,2048]{1,0,2:T(2,128)(2,1)}), bf16[2,1024,2048]{1,0,2:T(2,128)(2,1)}) %all-gather.24.cloned.1.call-update) | async-done | bytes 8388624 | tf_op jit(solution)/shard_map/all_gather | solution.py:241
  1319.6 100.1 %conditional.5 = (f32[2,32,128,64]{2,3,1,0:T(8,128)}, f32[2,32,128,64]{2,3,1,0:T(8,128)}) conditional(s32[]{:T(128)} %convert_element_type.111, () %tuple.34, (pred[2,1024,128]{2,1,0:T(8,128)(4,1)S(1)}, bf16[2,1024,2048]{1,0,2:T(2,128)(2,1)}, bf16[2,128,32,64]{1,0,3,2:T(2,128)(2,1)S(1)}, f32[2,32,1024]{2,1,0:T(8,128)S(1)}, ...), branch_computations={%region_11.12_spmd, %region_12.13_spmd} | conditional | flops 9739173888 | bytes 161218576 | solution.py:232
  1333.1 24.8 fusion.30
  1357.9 35.8 fusion.23
  1393.7 25.5 fusion.19
  1422.8 52.2 %conditional.4 = (f32[2,32,128,64]{2,3,1,0:T(8,128)S(1)}) conditional(s32[]{:T(128)} %convert_element_type.96, () %tuple.32, (pred[2,128,1024]{2,1,0:T(8,128)(4,1)S(1)}, bf16[2,1024,2048]{1,0,2:T(2,128)(2,1)}, bf16[2,128,32,64]{1,3,2,0:T(8,128)(2,1)}, f32[2,32,128]{2,1,0:T(8,128)S(1)}, bf16[2,1024,2048]{1,2,0:T(8,128)(2,1)}, ...), branch_computations={%region_8.9_spmd, %region_9.10_spmd} | conditional | flops 3271557120 | bytes 113639432 | solution.py:189
  1432.2 20.4 fusion.59
  1452.6 22.3 fusion.11
  1508.5 21.4 fusion.40
  1529.8 14.2 convolution_add_fusion.1
  1544.1 14.4 multiply_reduce_fusion
  1558.9 52.5 %fusion.63 = f32[2048,17408]{1,0:T(8,128)} fusion(bf16[256,2048]{1,0:T(8,128)(2,1)S(1)} %copy-done.11, bf16[256,17408]{1,0:T(8,128)(2,1)} %get-tuple-element.153), kind=kOutput, calls=%fused_computation.143 | convolution fusion | flops 18253611008 | bytes 152567808 | tf_op jit(solution)/shard_map/dot_general | solution.py:296
  1611.4 95.9 %select_maximum_fusion = f32[2048,17536]{1,0:T(8,128)} fusion(f32[2048,2]{1,0:T(8,128)S(1)} %copy.80, f32[2048,17408]{1,0:T(8,128)} %fusion.63), kind=kLoop, calls=%fused_computation.38 | loop fusion | flops 107741184 | bytes 286277632 | tf_op jit(solution)/shard_map/concatenate | solution.py:300
  1733.4 106.4 %reduce-scatter.7.cloned.1.call-done = f32[64,7680]{1,0:T(8,128)} async-done(((f32[2048,7680]{1,0:T(8,128)}), f32[64,7680]{1,0:T(8,128)}) %reduce-scatter.7.cloned.1.call-update) | async-done | bytes 1966096
  1844.2 2988.8 %reduce-scatter.5.cloned.1.call-done = f32[64,17536]{1,0:T(8,128)} async-done(((f32[2048,17536]{1,0:T(8,128)}), f32[64,17536]{1,0:T(8,128)}) %reduce-scatter.5.cloned.1.call-update) | async-done | bytes 4489232 | tf_op jit(solution)/shard_map/reduce_scatter | solution.py:303
  (204 shorter events, 214.6 us)
Async XLA Ops:
  7.2 162.7 %all-gather.10.cloned.1.call-start = ((), (), s32[]{:S(2)}) async-start(), calls=%async_computation.2 | async-start | bytes 25952256 | tf_op jit(solution)/shard_map/all_gather | solution.py:85
  7.9 240.6 %all-gather.16.cloned.1.call-start = ((), (), s32[]{:S(2)}) async-start(), calls=%async_computation.5 | async-start | bytes 8650752 | tf_op jit(solution)/shard_map/all_gather | solution.py:152
  8.7 386.0 %all-gather.18.cloned.1.call-start = ((), (), s32[]{:S(2)}) async-start(), calls=%async_computation.6 | async-start | bytes 23789568 | tf_op jit(solution)/shard_map/all_gather | solution.py:86
  9.4 530.8 %all-gather.20.cloned.1.call-start = ((), (), s32[]{:S(2)}) async-start(), calls=%async_computation.7 | async-start | bytes 23789568 | tf_op jit(solution)/shard_map/all_gather | solution.py:87
  10.0 656.3 %all-gather.14.cloned.1.call-start = ((), (), s32[]{:S(2)}) async-start(), calls=%async_computation.4 | async-start | bytes 9437184 | tf_op jit(solution)/shard_map/all_gather | solution.py:121
  60.8 479.4 %copy-start.10 = (bf16[256,2048]{1,0:T(8,128)(2,1)}, bf16[256,2048]{1,0:T(8,128)(2,1)S(1)}, u32[]{:S(2)}) copy-start(bf16[256,2048]{1,0:T(8,128)(2,1)S(1)} %add_convert_fusion.1) | copy-start | bytes 3145732
  185.7 666.8 %all-gather.12.cloned.1.call-start = ((), (), s32[]{:S(2)}) async-start(), calls=%async_computation.3 | async-start | bytes 9437184 | tf_op jit(solution)/shard_map/all_gather | solution.py:120
  185.9 12.3 copy-start.25
  185.9 12.3 copy-start.27
  199.7 55.8 %copy-start.16 = (bf16[256,32,8]{0,2,1:T(8,128)(2,1)}, bf16[256,32,8]{0,2,1:T(8,128)(2,1)S(1)}, u32[]{:S(2)}) copy-start(bf16[256,32,8]{0,2,1:T(8,128)(2,1)S(1)} %get-tuple-element.183) | copy-start | bytes 393220
  199.7 55.8 %copy-start.18 = (bf16[256,32,8]{0,2,1:T(8,128)(2,1)}, bf16[256,32,8]{0,2,1:T(8,128)(2,1)S(1)}, u32[]{:S(2)}) copy-start(bf16[256,32,8]{0,2,1:T(8,128)(2,1)S(1)} %get-tuple-element.182) | copy-start | bytes 393220
  204.7 820.5 %all-gather.22.cloned.1.call-start = ((), (), s32[]{:S(2)}) async-start(), calls=%async_computation.8 | async-start | bytes 23789568 | tf_op jit(solution)/shard_map/all_gather | solution.py:153
  205.5 927.7 %all-gather.26.cloned.1.call-start = ((), (), s32[]{:S(2)}) async-start(), calls=%async_computation.10 | async-start | bytes 9437184 | tf_op jit(solution)/shard_map/all_gather | solution.py:242
  205.5 57.1 %copy-start.35 = (s32[128]{0:T(128)}, s32[128]{0:T(128)S(1)}, u32[]{:S(2)}) copy-start(s32[128]{0:T(128)S(1)} %iota_add_fusion) | copy-start | bytes 1540
  260.2 1059.4 %all-gather.24.cloned.1.call-start = ((), (), s32[]{:S(2)}) async-start(), calls=%async_computation.9 | async-start | bytes 9437184 | tf_op jit(solution)/shard_map/all_gather | solution.py:241
  262.4 1577.4 %reduce-scatter.7.cloned.1.call-start = ((), (), s32[]{:S(2)}) async-start(), calls=%async_computation.12 | async-start | bytes 64880640
  263.8 588.7 %copy-start.8 = (pred[2,128,1024]{2,1,0:T(8,128)(4,1)}, pred[2,128,1024]{2,1,0:T(8,128)(4,1)S(1)}, u32[]{:S(2)}) copy-start(pred[2,128,1024]{2,1,0:T(8,128)(4,1)S(1)} %get-tuple-element.176) | copy-start | bytes 786436
  540.2 18.7 copy-start.21
  1022.6 3810.5 %reduce-scatter.5.cloned.1.call-start = ((), (), s32[]{:S(2)}) async-start(), calls=%async_computation.11 | async-start | bytes 148144128 | tf_op jit(solution)/shard_map/reduce_scatter | solution.py:303
  1025.1 13.6 copy-start.19
  1025.2 13.6 copy-start.17
  1025.2 13.7 copy-start.5
  1025.2 294.4 %copy-start.3 = (bf16[256,2048]{1,0:T(8,128)(2,1)S(1)}, bf16[256,2048]{1,0:T(8,128)(2,1)}, u32[]{:S(2)}) copy-start(bf16[256,2048]{1,0:T(8,128)(2,1)} %copy-done.2) | copy-start | bytes 3145732
  1488.5 16.6 slice-start
  1488.5 16.6 slice-start.2
  1494.4 10.7 slice-start.1
  1494.4 10.7 slice-start.3
  1529.8 14.2 copy-start
  1529.8 14.2 copy-start.23
  1529.8 14.3 copy-start.30
  1529.8 14.3 copy-start.33
  1544.1 14.8 copy-start.11
  (23 other events, 47.9 us)
Sparse Core Ops, SparseCore 0:
  11.0 158.8 all-gather.9
  172.9 75.5 all-gather.15
  251.4 143.1 all-gather.17
  397.4 142.7 all-gather.19
  542.7 123.5 all-gather.13
  668.7 183.7 all-gather.11
  855.4 144.5 all-gather.21
  1002.6 130.4 all-gather.25
  1135.7 183.7 all-gather.23
  1325.8 513.9 reduce-scatter.6
  1842.3 2990.7 reduce-scatter.4
where the time goes:
time: 4860 us; the launch traced here: 4850 us
  waiting for transfers between devices  4020 us (83%)
  matrix products  390 us (8%)
  local copies, waits for them, and re-layouts  160 us (3%)
  other arithmetic  158 us (3%)
  blocking collectives  104 us (2%)
    reduce_scatter x1, waiting for transfers between devices, on_device(): lax.psum_scatter(in_term, ('dp', 'ctx'), scatter_dimension=0, tiled=True)  2990 us
    all_gather x1, waiting for transfers between devices, on_device(): lax.all_gather(query_send, 'ctx', axis=1, tiled=True)  186 us
    all_gather x1, waiting for transfers between devices, on_device(): piece_keys = lax.all_gather(keys_rot, 'ctx', axis=1, tiled=True)  186 us
    all_gather x1, waiting for transfers between devices, on_device(): piece_up = lax.all_gather(up_weight, ('dp', 'ctx'), axis=0, tiled=True)  132 us
    all_gather x1, waiting for transfers between devices, on_device(): piece_gate = lax.all_gather(gate_weight, ('dp', 'ctx'), axis=0, tiled=True)  126 us
    unnamed x12, waiting for transfers between devices  110 us
    all_gather x1, waiting for transfers between devices, on_device(): lax.all_gather(joined_weight, ('dp', 'ctx'), axis=0, tiled=True)  109 us
    all_gather x1, waiting for transfers between devices, on_device(): piece_values = lax.all_gather(values_low, 'ctx', axis=1, tiled=True)  105 us
  transfers between devices with their start and end apart: 11, of which 10 were waited for; matrix products, arithmetic and copies ran while one was open for 14% of the time, Pallas kernels for 0%

commit v1 on v0

v1 whole, which is shorter than its diff:
```python
import functools

import jax
import jax.numpy as jnp
from jax import lax
from jax.experimental import pallas as pl
from jax.experimental.pallas import tpu as pltpu
from jax.sharding import PartitionSpec as P

HD = 64
ROT = 16
EPSILON = 1e-05
THETA = 10000.0
NEGATIVE = -1e30
BF = jnp.bfloat16
F32 = jnp.float32
LAST = (((1,), (1,)), ((), ()))
FIRST = (((0,), (0,)), ((), ()))


def dot(left, right):
    return jnp.dot(left, right, preferred_element_type=F32)


def dot_last(left, right):
    return lax.dot_general(left, right, LAST, preferred_element_type=F32)


def dot_first(left, right):
    return lax.dot_general(left, right, FIRST, preferred_element_type=F32)


def rotary_tables(length, width):
    half = ROT // 2
    lane = jnp.arange(width, dtype=jnp.int32) % HD
    frequency = THETA ** (-(2.0 * (lane % half).astype(F32)) / ROT)
    angles = jnp.arange(length, dtype=jnp.int32).astype(F32)[:, None] * frequency[None, :]
    cosine = jnp.where(lane[None, :] < ROT, jnp.cos(angles), 1.0)
    sine = jnp.sin(angles)
    sine = jnp.where(lane[None, :] < half, -sine, jnp.where(lane[None, :] < ROT, sine, 0.0))
    return cosine, sine


def partner(x):
    half = ROT // 2
    lane = lax.broadcasted_iota(jnp.int32, x.shape, 1) % HD
    down = jnp.concatenate([x[:, half:], x[:, :half]], axis=1)
    up = jnp.concatenate([x[:, -half:], x[:, :-half]], axis=1)
    return jnp.where(lane < half, down, up)


def attend_forward(length_ref, joined_ref, cos_ref, sin_ref, rot_ref, attn_ref, lse_ref, total):
    parts, _, rows, triple = joined_ref.shape
    width = triple // 3
    length = parts * rows
    seq = pl.program_id(0)
    head = pl.program_id(1)
    alive_count = length_ref[seq]
    block = min(256, length)
    lane = lax.broadcasted_iota(jnp.int32, (1, width), 1)
    mine = (lane // HD) == head

    @pl.when(head == 0)
    def _():
        def rotated(start, scale):
            x = joined_ref[:, 0, :, start : start + width].reshape(length, width)
            x = x * cos_ref[...] + partner(x) * sin_ref[...]
            return (x.astype(BF) * scale).reshape(parts, rows, width)

        rot_ref[:, 0, :, :width] = rotated(0, 0.125)
        rot_ref[:, 0, :, width : 2 * width] = rotated(width, 1.0)
        rot_ref[:, 0, :, 2 * width :] = joined_ref[:, 0, :, 2 * width :].astype(BF)
        total[...] = jnp.zeros_like(total)
        lse_ref[...] = jnp.zeros_like(lse_ref)

    per = block // rows if block >= rows else 1
    block = per * rows
    for step in range(length // block):
        begin, end = step * per, (step + 1) * per
        stop = end * rows

        @pl.when(begin * rows < alive_count)
        def _(begin=begin, end=end, stop=stop):
            q = rot_ref[begin:end, 0, :, :width].reshape(block, width)
            q = jnp.where(mine, q, jnp.zeros_like(q))
            k = rot_ref[:end, 0, :, width : 2 * width].reshape(stop, width)
            v = rot_ref[:end, 0, :, 2 * width :].reshape(stop, width)
            scores = dot_last(q, k)
            q_pos = begin * rows + lax.broadcasted_iota(jnp.int32, (block, 1), 0)
            k_pos = lax.broadcasted_iota(jnp.int32, (block, stop), 1)
            scores = jnp.where(k_pos <= q_pos, scores, NEGATIVE)
            top = jnp.max(scores, axis=1, keepdims=True)
            expo = jnp.exp(scores - top)
            weight = jnp.sum(expo, axis=1, keepdims=True)
            out = dot(expo.astype(BF), v) / weight
            alive = q_pos < alive_count
            here = slice(begin * rows, stop)
            total[here, :] += jnp.where(mine & alive, out, 0.0)
            lse = jnp.where(alive, top + jnp.log(weight), 0.0)
            spot = lax.broadcasted_iota(jnp.int32, (1, lse_ref.shape[3]), 1) == head
            held = lse_ref[begin:end, 0].reshape(block, lse_ref.shape[3])
            lse_ref[begin:end, 0] = jnp.where(spot, lse, held).reshape(per, rows, -1)

    @pl.when(head == pl.num_programs(1) - 1)
    def _():
        attn_ref[:, 0] = total[...].astype(BF).reshape(parts, rows, width)


def attend_backward(
    length_ref, rot_ref, attn_ref, grad_ref, lse_ref, cos_ref, sin_ref, out_ref, dq, dk, dv
):
    parts, _, rows, triple = rot_ref.shape
    width = triple // 3
    length = parts * rows
    seq = pl.program_id(0)
    head = pl.program_id(1)
    alive_count = length_ref[seq]
    per = max(1, min(256, length) // rows)
    block = per * rows
    lane = lax.broadcasted_iota(jnp.int32, (1, width), 1)
    mine = (lane // HD) == head

    @pl.when(head == 0)
    def _():
        dq[...] = jnp.zeros_like(dq)
        dk[...] = jnp.zeros_like(dk)
        dv[...] = jnp.zeros_like(dv)

    for step in range(length // block):
        begin, end = step * per, (step + 1) * per
        stop = end * rows

        @pl.when(begin * rows < alive_count)
        def _(begin=begin, end=end, stop=stop):
            q_pos = begin * rows + lax.broadcasted_iota(jnp.int32, (block, 1), 0)
            alive = q_pos < alive_count
            q = rot_ref[begin:end, 0, :, :width].reshape(block, width)
            q = jnp.where(mine, q, jnp.zeros_like(q))
            k = rot_ref[:end, 0, :, width : 2 * width].reshape(stop, width)
            v = rot_ref[:end, 0, :, 2 * width :].reshape(stop, width)
            g = grad_ref[begin:end, 0].reshape(block, width)
            g = jnp.where(mine & alive, g, jnp.zeros_like(g))
            o = attn_ref[begin:end, 0].reshape(block, width)
            delta = jnp.sum(g.astype(F32) * o.astype(F32), axis=1, keepdims=True)
            held = lse_ref[begin:end, 0].reshape(block, lse_ref.shape[3])
            spot = lax.broadcasted_iota(jnp.int32, (1, lse_ref.shape[3]), 1) == head
            lse = jnp.sum(jnp.where(spot, held, 0.0), axis=1, keepdims=True)
            scores = dot_last(q, k)
            k_pos = lax.broadcasted_iota(jnp.int32, (block, stop), 1)
            probs = jnp.where((k_pos <= q_pos) & alive, jnp.exp(scores - lse), 0.0)
            d_probs = dot_last(g, v)
            d_scores = (probs * (d_probs - delta)).astype(BF)
            here = slice(begin * rows, stop)
            dq[here, :] += jnp.where(mine, dot(d_scores, k), 0.0)
            dk[:stop, :] += dot_first(d_scores, q)
            dv[:stop, :] += dot_first(probs.astype(BF), g)

    @pl.when(head == pl.num_programs(1) - 1)
    def _():
        def unrotated(x):
            return (x * cos_ref[...] - partner(x) * sin_ref[...]).astype(BF)

        shape = (parts, rows, width)
        out_ref[:, 0, :, :width] = unrotated(dq[...] * 0.125).reshape(shape)
        out_ref[:, 0, :, width : 2 * width] = unrotated(dk[...]).reshape(shape)
        out_ref[:, 0, :, 2 * width :] = dv[...].astype(BF).reshape(shape)


def attention_calls(parts, groups, rows, width, heads):
    length = parts * rows
    smem = pl.BlockSpec(memory_space=pltpu.SMEM)

    def spec(last):
        return pl.BlockSpec((parts, 1, rows, last), lambda s, h: (0, s, 0, 0))

    table = pl.BlockSpec((length, width), lambda s, h: (0, 0))

    def shape(last, dtype):
        return jax.ShapeDtypeStruct((parts, groups, rows, last), dtype)

    pairs = groups * heads * length * length // 2
    params = pltpu.CompilerParams(vmem_limit_bytes=48 * 1024 * 1024)
    forward = pl.pallas_call(
        attend_forward,
        grid=(groups, heads),
        in_specs=[smem, spec(3 * width), table, table],
        out_specs=[spec(3 * width), spec(width), spec(heads)],
        out_shape=[shape(3 * width, BF), shape(width, BF), shape(heads, F32)],
        scratch_shapes=[pltpu.VMEM((length, width), F32)],
        compiler_params=params,
        cost_estimate=pl.CostEstimate(
            flops=pairs * 1024, bytes_accessed=16 * length * width, transcendentals=pairs
        ),
        name="attend_forward",
    )
    backward = pl.pallas_call(
        attend_backward,
        grid=(groups, heads),
        in_specs=[smem, spec(3 * width), spec(width), spec(width), spec(heads), table, table],
        out_specs=spec(3 * width),
        out_shape=shape(3 * width, BF),
        scratch_shapes=[pltpu.VMEM((length, width), F32)] * 3,
        compiler_params=params,
        cost_estimate=pl.CostEstimate(
            flops=pairs * 2560, bytes_accessed=16 * length * width, transcendentals=pairs
        ),
        name="attend_backward",
    )
    return forward, backward


def on_device(
    n_ctx,
    n_dp,
    inputs,
    norm_gain,
    norm_bias,
    joined_weight,
    gate_weight,
    up_weight,
    out_weight,
    down_weight,
    cotangent,
    lengths,
):
    groups, rows, features = inputs.shape
    tokens = groups * rows
    own = norm_gain.shape[0]
    hidden_units = gate_weight.shape[1]
    width = features // n_ctx
    units = hidden_units // n_ctx
    heads = width // HD
    length = n_ctx * rows
    both = ("dp", "ctx")

    def split_columns(weight, last):
        return weight.reshape(own, -1, n_ctx, last).transpose(2, 1, 0, 3)

    narrow = jnp.concatenate(
        [split_columns(joined_weight, width), split_columns(out_weight, width)], axis=1
    )
    wide = jnp.concatenate(
        [split_columns(w, units) for w in (gate_weight, up_weight, down_weight)], axis=1
    )
    narrow = lax.all_to_all(narrow, "ctx", split_axis=0, concat_axis=0, tiled=True)
    wide = lax.all_to_all(wide, "ctx", split_axis=0, concat_axis=0, tiled=True)
    joined_part = narrow[:, :3].transpose(0, 2, 1, 3).reshape(n_ctx * own, 3 * width)

    def gather_rows(part):
        return lax.all_gather(part.reshape(n_ctx * own, -1), "dp", axis=0, tiled=True)

    w_joined = gather_rows(joined_part)
    w_gate, w_up = gather_rows(wide[:, 0]), gather_rows(wide[:, 1])
    w_out, w_down = gather_rows(narrow[:, 3]), gather_rows(wide[:, 2])

    scales = jnp.concatenate([norm_gain, norm_bias]).reshape(1, 2 * own)
    scales = lax.all_gather(scales, both, axis=0, tiled=True).astype(F32)
    gain = scales[:, :own].reshape(1, features)
    bias = scales[:, own:].reshape(1, features)
    flat_in = inputs.reshape(tokens, features).astype(F32)
    center = flat_in - jnp.mean(flat_in, axis=-1, keepdims=True)
    variance = jnp.mean(center * center, axis=-1, keepdims=True)
    inverse = lax.rsqrt(variance + EPSILON)
    standard = center * inverse
    normed_own = (standard * gain + bias).astype(BF)
    cot_own = cotangent.reshape(tokens, features)

    def gather_tokens(part):
        return lax.all_gather(part, "ctx", axis=0, tiled=True)

    def scatter_tokens(total):
        return lax.psum_scatter(total, "ctx", scatter_dimension=0, tiled=True)

    normed = gather_tokens(normed_own)
    cot = gather_tokens(cot_own)
    all_tokens = n_ctx * tokens

    forward, backward = attention_calls(n_ctx, groups, rows, width, heads)
    cosine, sine = rotary_tables(length, width)
    blocks = (n_ctx, groups, rows)
    joined = dot(normed, w_joined)
    rotated, attn, lse = forward(lengths, joined.reshape(*blocks, 3 * width), cosine, sine)
    attn_rows = attn.reshape(all_tokens, width)
    gate = dot(normed, w_gate)
    up = dot(normed, w_up)
    sigmoid = jax.nn.sigmoid(gate)
    silu = gate * sigmoid
    hidden = (silu * up).astype(BF)
    partial = (dot_last(attn_rows, w_out) + dot_last(hidden, w_down)).astype(BF)
    output = (flat_in + scatter_tokens(partial).astype(F32)).astype(BF)

    d_attn = dot(cot, w_out).astype(BF)
    d_hidden = dot(cot, w_down)
    d_gate = (d_hidden * up * sigmoid * (1.0 + gate * (1.0 - sigmoid))).astype(BF)
    d_up = (d_hidden * silu).astype(BF)
    d_joined = backward(
        lengths, rotated, attn, d_attn.reshape(*blocks, width), lse, cosine, sine
    ).reshape(all_tokens, 3 * width)

    normed_partial = (
        dot_last(d_gate, w_gate) + dot_last(d_up, w_up) + dot_last(d_joined, w_joined)
    ).astype(BF)
    d_normed = scatter_tokens(normed_partial).astype(F32)
    standard_grad = d_normed * gain
    centered = (
        standard_grad
        - jnp.mean(standard_grad, axis=-1, keepdims=True)
        - standard * jnp.mean(standard_grad * standard, axis=-1, keepdims=True)
    )
    input_grad = (cot_own.astype(F32) + inverse * centered).astype(BF)

    def reduce_rows(left, right):
        total = dot_first(left, right).astype(BF)
        total = lax.psum_scatter(total, "dp", scatter_dimension=0, tiled=True)
        return total.reshape(n_ctx, own, -1)

    g_down = reduce_rows(cot, hidden)
    g_gate = reduce_rows(normed, d_gate)
    g_up = reduce_rows(normed, d_up)
    g_out = reduce_rows(cot, attn_rows)
    g_joined = reduce_rows(normed, d_joined)
    g_wide = jnp.stack([g_gate, g_up, g_down], axis=1)
    g_narrow = jnp.concatenate(
        [
            g_joined.reshape(n_ctx, own, 3, width).transpose(0, 2, 1, 3),
            g_out.reshape(n_ctx, 1, own, width),
        ],
        axis=1,
    )
    g_wide = lax.all_to_all(g_wide, "ctx", split_axis=0, concat_axis=0, tiled=True)
    g_narrow = lax.all_to_all(g_narrow, "ctx", split_axis=0, concat_axis=0, tiled=True)

    def own_rows(pieces):
        return pieces.transpose(2, 1, 0, 3).reshape(own, -1).astype(F32)

    norm_sums = jnp.stack([jnp.sum(d_normed * standard, axis=0), jnp.sum(d_normed, axis=0)])
    norm_sums = norm_sums.reshape(2, n_ctx * n_dp, own).transpose(1, 0, 2).reshape(-1, 2 * own)
    norm_sums = lax.psum_scatter(norm_sums, both, scatter_dimension=0, tiled=True)
    return (
        output.reshape(inputs.shape),
        input_grad.reshape(inputs.shape),
        norm_sums[0, :own],
        norm_sums[0, own:],
        own_rows(g_narrow[:, :3]),
        own_rows(g_wide[:, :1]),
        own_rows(g_wide[:, 1:2]),
        own_rows(g_narrow[:, 3:]),
        own_rows(g_wide[:, 2:]),
    )


def solution(mesh):
    rows = P(("dp", "ctx"), None)
    vector = P(("dp", "ctx"))
    tokens = P("dp", "ctx", None)
    return jax.shard_map(
        functools.partial(on_device, mesh.shape["ctx"], mesh.shape["dp"]),
        mesh=mesh,
        in_specs=(tokens, vector, vector, rows, rows, rows, rows, rows, tokens, P("dp")),
        out_specs=(tokens, tokens, vector, vector, rows, rows, rows, rows, rows),
        check_vma=False,
    )
```

time: 4860 us -> 1040 us (0.21)
  waiting for transfers between devices: 4020 us -> 470 us
  matrix products: 390 us -> 176 us
  blocking collectives: 104 us -> 253 us
  other arithmetic: 158 us -> 18 us
  local copies, waits for them, and re-layouts: 160 us -> 45 us
    reduce_scatter x1 -> x7, waiting for transfers between devices: 2990 us -> 216 us  [the longest x2 175 us: scatter_tokens(): return lax.psum_scatter(total, 'ctx', scatter_dimension=0, tiled=True)]
    all_gather x9 -> x7, waiting for transfers between devices: 919 us -> 148 us  [the longest x2 128 us: gather_tokens(): return lax.all_gather(part, 'ctx', axis=0, tiled=True)]
    dot_general x19 -> x15, matrix products: 390 us -> 176 us  [the longest x5 67.8 us: dot_last(): return lax.dot_general(left, right, LAST, preferred_element_type=F32)]
    all_to_all x0 -> x2, blocking collectives: none -> 145 us  [the longest x1 112 us: on_device(): wide = lax.all_to_all(wide, 'ctx', split_axis=0, concat_axis=0, tiled=True)]
    unnamed x12 -> x14, waiting for transfers between devices: 110 us -> 2.06 us
    all_to_all x0 -> x2, waiting for transfers between devices: none -> 104 us  [the longest x1 104 us: on_device(): lax.all_to_all(g_wide, 'ctx', split_axis=0, concat_axis=0, tiled=True)]
    concatenate x6 -> x3, other arithmetic: 105 us -> 2.44 us  [the longest x1 2.05 us: on_device(): jnp.concatenate([g_joined.reshape(n_ctx, own, 3, width).transpose(0, 2, 1...]
    unnamed x100 -> x53, local copies, waits for them, and re-layouts: 80.5 us -> 12.3 us
  transfers between devices with their start and end apart: 11 -> 16, of which waited for: 10 -> 7; matrix products, arithmetic and copies ran while one was open for 14% -> 22% of each run, Pallas kernels for 0% -> 5%
where the time goes in v1:
time: 1040 us; the launch traced here: 1030 us
  waiting for transfers between devices  470 us (45%)
  blocking collectives  253 us (24%)
  matrix products  176 us (17%)
  Pallas kernels  46.9 us (5%)
  local copies, waits for them, and re-layouts  45 us (4%)
  other arithmetic  18 us (2%)
  between operations  14.6 us (1%)
    reduce_scatter x2, waiting for transfers between devices, scatter_tokens(): return lax.psum_scatter(total, 'ctx', scatter_dimension=0, tiled=True)  175 us
    all_gather x2, waiting for transfers between devices, gather_tokens(): return lax.all_gather(part, 'ctx', axis=0, tiled=True)  128 us
    all_to_all x1, blocking collectives, on_device(): wide = lax.all_to_all(wide, 'ctx', split_axis=0, concat_axis=0, tiled=True)  112 us
    all_to_all x1, waiting for transfers between devices, on_device(): lax.all_to_all(g_wide, 'ctx', split_axis=0, concat_axis=0, tiled=True)  104 us
    dot_general x5, matrix products, dot_last(): return lax.dot_general(left, right, LAST, preferred_element_type=F32)  67.8 us
    all_gather x1, blocking collectives, on_device(): scales = lax.all_gather(scales, both, axis=0, tiled=True).astype(F32)  66 us
    dot_general x5, matrix products, dot(): return jnp.dot(left, right, preferred_element_type=F32)  56.8 us
    dot_general x5, matrix products, dot_first(): return lax.dot_general(left, right, FIRST, preferred_element_type=F32)  51.1 us
  transfers between devices with their start and end apart: 16, of which 7 were waited for; matrix products, arithmetic and copies ran while one was open for 22% of the time, Pallas kernels for 5%

profile of v1, /device:TPU:0, one launch (start us, length us, event | category | flops | bytes accessed | tf_op | source)
XLA Modules:
  0.0 1032.7 jit_solution(11161250951171965256)
XLA Ops:
  10.0 32.8 %all_to_all.20 = bf16[8,4,64,256]{3,1,2,0:T(4,128)(2,1)S(1)} all-to-all(bf16[8,4,64,256]{3,1,2,0:T(4,128)(2,1)S(1)} %copy.70), channel_id=1, replica_groups=mesh['dp'=4,'ctx'=8] {'ctx'}, dimensions={0} | all-to-all | bytes 2097152 | tf_op jit(solution)/shard_map/all_to_all | solution.py:245
  46.2 66.0 %all-gather.1 = bf16[32,1,128]{2,1,0:T(2,128)(2,1)S(1)} all-gather(bf16[1,1,128]{2,1,0:T(2,128)(2,1)S(1)} %maximum_bitcast_fusion.1), channel_id=2, replica_groups=mesh['dp'=4,'ctx'=8] {'dp','ctx'}, dimensions={0}, use_global_device_ids=true | all-gather | bytes 8448 | tf_op jit(solution)/shard_map/all_gather | solution.py:257
  118.1 111.7 %all_to_all.21 = bf16[8,3,64,704]{3,2,1,0:T(8,128)(2,1)S(1)} all-to-all(bf16[8,3,64,704]{3,2,1,0:T(8,128)(2,1)S(1)} %copy.72), channel_id=1, replica_groups=mesh['dp'=4,'ctx'=8] {'ctx'}, dimensions={0} | all-to-all | bytes 4325376 | tf_op jit(solution)/shard_map/all_to_all | solution.py:246
  232.8 3.8 fusion.27
  236.8 6.1 fusion.9
  244.4 20.5 %all-gather.12.cloned.1.call-done = bf16[2048,768]{1,0:T(8,128)(2,1)} async-done(((bf16[512,768]{1,0:T(8,128)(2,1)}), bf16[2048,768]{1,0:T(8,128)(2,1)}) %all-gather.12.cloned.1.call-update) | async-done | bytes 3145744 | tf_op jit(solution)/shard_map/all_gather | solution.py:250
  264.9 127.5 %all-gather.10.cloned.1.call-done = bf16[2048,2048]{1,0:T(8,128)(2,1)} async-done(((bf16[256,2048]{1,0:T(8,128)(2,1)}), bf16[2048,2048]{1,0:T(8,128)(2,1)}) %all-gather.10.cloned.1.call-update) | async-done | bytes 8388624 | tf_op jit(solution)/shard_map/all_gather | solution.py:269
  392.4 11.7 %fusion.39 = f32[2048,768]{1,0:T(8,128)} fusion(bf16[2048,2048]{1,0:T(8,128)(2,1)} %all-gather.10.cloned.1.call-done, bf16[2048,768]{1,0:T(8,128)(2,1)} %all-gather.12.cloned.1.call-done), kind=kOutput, calls=%fused_computation.85 | convolution fusion | flops 6442450944 | bytes 17825792 | tf_op jit(solution)/shard_map/dot_general | solution.py:22
  404.1 22.6 %attend_forward.1 = (bf16[8,2,128,768]{3,2,1,0:T(8,128)(2,1)}, bf16[8,2,128,256]{3,2,1,0:T(8,128)(2,1)S(1)}, f32[8,2,128,4]{3,2,1,0:T(8,128)S(1)}) custom-call(s32[2]{0:T(128)S(1)} %copy-done.1, f32[8,2,128,768]{3,2,1,0:T(8,128)} %bitcast.177, f32[1024,256]{1,0:T(8,128)S(1)} %get-tuple-element.33.cos_ref, f32[1024,256]{1,0:T(8,128)S(1)} %get-tuple-element.32.sin_ref), custom_call_target="tpu_custom_call" | custom-call | flops 4294967296 | bytes 4194304 | tf_op jit(solution)/shard_map/attend_forward/pallas_call | solution.py:282
  427.6 7.2 fusion.10
  437.4 24.3 %attend_backward.1 = bf16[8,2,128,768]{3,2,1,0:T(8,128)(2,1)} custom-call(s32[2]{0:T(128)S(1)} %copy-done.1, bf16[8,2,128,768]{3,2,1,0:T(8,128)(2,1)} %get-tuple-element.13.rot_ref, bf16[8,2,128,256]{3,2,1,0:T(8,128)(2,1)S(1)} %get-tuple-element.12.attn_ref, bf16[8,2,128,256]{3,2,1,0:T(8,128)(2,1)S(1)} %bitcast.150, f32[8,2,128,4]{3,2,1,0:T(8,128)S(1)} %copy-done.3, ...), custom_call_target="tpu_custom_call" | custom-call | flops 10737418240 | bytes 4194304 | tf_op jit(solution)/shard_map/attend_backward/pallas_call | solution.py:296
  461.7 11.7 %convolution_convert_fusion = bf16[2048,768]{1,0:T(8,128)(2,1)} fusion(bf16[2048,2048]{1,0:T(8,128)(2,1)} %all-gather.10.cloned.1.call-done, bf16[2048,768]{1,0:T(8,128)(2,1)} %bitcast.178), kind=kOutput, calls=%fused_computation.11 | convolution fusion | flops 6444023808 | bytes 14680064 | tf_op jit(solution)/shard_map/dot_general | solution.py:30
  473.5 11.4 %fusion.41 = f32[2048,704]{0,1:T(8,128)} fusion(bf16[2048,2048]{1,0:T(8,128)(2,1)} %all-gather.10.cloned.1.call-done, bf16[2048,704]{1,0:T(8,128)(2,1)} %all-gather.18.cloned.1.call-done), kind=kOutput, calls=%fused_computation.87 | convolution fusion | flops 5905580032 | bytes 17039360 | tf_op jit(solution)/shard_map/dot_general | solution.py:22
  485.0 11.2 %fusion.40 = f32[2048,704]{0,1:T(8,128)} fusion(bf16[2048,2048]{1,0:T(8,128)(2,1)} %all-gather.10.cloned.1.call-done, bf16[2048,704]{1,0:T(8,128)(2,1)} %all-gather.16.cloned.1.call-done), kind=kOutput, calls=%fused_computation.86 | convolution fusion | flops 5905580032 | bytes 17039360 | tf_op jit(solution)/shard_map/dot_general | solution.py:22
  496.2 16.3 %fusion.3 = (bf16[2048,704]{0,1:T(8,128)(2,1)S(1)}, bf16[2048,704]{0,1:T(8,128)(2,1)}, bf16[2048,704]{0,1:T(8,128)(2,1)}) fusion(f32[2048,704]{0,1:T(8,128)} %fusion.40, f32[2048,704]{0,1:T(8,128)} %fusion.41, bf16[2048,704]{1,0:T(8,128)(2,1)} %all-gather.20.cloned.1.call-done, bf16[2048,2048]{1,0:T(8,128)(2,1)} %all-gather.22.cloned.1.call-done), kind=kOutput, calls=%fused_computation.7 | convolution fusion | flops 5927206912 | bytes 31457280 | tf_op jit(solution)/shard_map/dot_general | solution.py:22
  514.1 11.0 %convolution_convert_fusion.1 = bf16[2048,704]{0,1:T(8,128)(2,1)} fusion(bf16[2048,704]{0,1:T(8,128)(2,1)S(1)} %get-tuple-element.19, bf16[2048,2048]{1,0:T(8,128)(2,1)} %all-gather.10.cloned.1.call-done), kind=kOutput, calls=%fused_computation.12 | convolution fusion | flops 5907021824 | bytes 14155776 | tf_op jit(solution)/shard_map/dot_general | solution.py:30
  525.2 10.6 %convolution_convert_fusion.2 = bf16[2048,704]{0,1:T(8,128)(2,1)} fusion(bf16[2048,704]{0,1:T(8,128)(2,1)} %get-tuple-element.20, bf16[2048,2048]{1,0:T(8,128)(2,1)} %all-gather.10.cloned.1.call-done), kind=kOutput, calls=%fused_computation.13 | convolution fusion | flops 5907021824 | bytes 14155776 | tf_op jit(solution)/shard_map/dot_general | solution.py:30
  535.8 10.6 %fusion.5 = bf16[2048,704]{0,1:T(8,128)(2,1)} fusion(bf16[2048,704]{0,1:T(8,128)(2,1)} %get-tuple-element.21, bf16[2048,2048]{1,0:T(8,128)(2,1)} %all-gather.22.cloned.1.call-done), kind=kOutput, calls=%fused_computation.18 | convolution fusion | flops 5907021824 | bytes 14155776 | tf_op jit(solution)/shard_map/dot_general | solution.py:30
  546.5 13.4 %fusion.43 = f32[2048,2048]{1,0:T(8,128)} fusion(bf16[2048,704]{0,1:T(8,128)(2,1)} %get-tuple-element.20, bf16[2048,704]{1,0:T(8,128)(2,1)} %all-gather.16.cloned.1.call-done), kind=kOutput, calls=%fused_computation.89 | convolution fusion | flops 5905580032 | bytes 22544384 | tf_op jit(solution)/shard_map/dot_general | solution.py:26
  559.9 10.5 %fusion.44 = f32[2048,2048]{1,0:T(8,128)} fusion(bf16[2048,704]{0,1:T(8,128)(2,1)S(1)} %copy-done.22, bf16[2048,704]{1,0:T(8,128)(2,1)S(1)} %copy-done.18), kind=kOutput, calls=%fused_computation.90 | convolution fusion | flops 5905580032 | bytes 22544384 | tf_op jit(solution)/shard_map/dot_general | solution.py:26
  570.4 19.2 %add_convert_fusion = bf16[2048,2048]{1,0:T(8,128)(2,1)} fusion(f32[2048,2048]{1,0:T(8,128)} %fusion.43, f32[2048,2048]{1,0:T(8,128)} %fusion.44, bf16[2048,768]{1,0:T(8,128)(2,1)} %bitcast.179, bf16[2048,768]{1,0:T(8,128)(2,1)} %all-gather.12.cloned.1.call-done), kind=kOutput, calls=%fused_computation | convolution fusion | flops 6455033856 | bytes 48234496 | tf_op jit(solution)/shard_map/dot_general | solution.py:26
  589.6 13.3 %fusion.42 = f32[2048,2048]{1,0:T(8,128)} fusion(bf16[2048,704]{0,1:T(8,128)(2,1)} %get-tuple-element.21, bf16[2048,704]{1,0:T(8,128)(2,1)} %all-gather.20.cloned.1.call-done), kind=kOutput, calls=%fused_computation.88 | convolution fusion | flops 5905580032 | bytes 22544384 | tf_op jit(solution)/shard_map/dot_general | solution.py:26
  603.0 11.4 %add_convert_fusion.1 = bf16[2048,2048]{1,0:T(8,128)(2,1)} fusion(f32[2048,2048]{1,0:T(8,128)} %fusion.42, bf16[2048,256]{1,0:T(8,128)(2,1)S(1)} %bitcast.149, bf16[2048,256]{1,0:T(8,128)(2,1)S(1)} %copy-done.8), kind=kOutput, calls=%fused_computation.1 | convolution fusion | flops 2155872256 | bytes 27262976 | tf_op jit(solution)/shard_map/dot_general | solution.py:26
  620.6 3.6 all-to-all-start.2
  630.3 37.4 %reduce-scatter.20.cloned.1.call-done = bf16[512,704]{0,1:T(8,128)(2,1)} async-done(((bf16[2048,704]{0,1:T(8,128)(2,1)}), bf16[512,704]{0,1:T(8,128)(2,1)}) %reduce-scatter.20.cloned.1.call-update) | async-done | bytes 720912 | tf_op jit(solution)/shard_map/reduce_scatter | solution.py:314
  671.1 5.8 all-to-all-start.3
  681.5 103.8 %all-to-all-done.3 = bf16[8,3,64,704]{3,2,1,0:T(8,128)(2,1)S(1)} async-done(((bf16[8,3,64,704]{3,2,1,0:T(8,128)(2,1)}), bf16[8,3,64,704]{3,2,1,0:T(8,128)(2,1)S(1)}, u32[]{:S(2)}, u32[]{:S(2)}) %all-to-all-start.3) | async-done | bytes 2162720 | tf_op jit(solution)/shard_map/all_to_all | solution.py:330
  790.0 3.7 copy.82
  801.5 68.0 %reduce-scatter.10.cloned.1.call-done = bf16[256,2048]{1,0:T(8,128)(2,1)} async-done(((bf16[2048,2048]{1,0:T(8,128)(2,1)}), bf16[256,2048]{1,0:T(8,128)(2,1)}) %reduce-scatter.10.cloned.1.call-update) | async-done | bytes 1048592 | tf_op jit(solution)/shard_map/reduce_scatter | solution.py:272
  872.1 42.1 %all-reduce = f32[32,128]{1,0:T(8,128)S(1)} all-reduce(f32[32,128]{1,0:T(8,128)S(1)} %reshape.181), channel_id=5, replica_groups=mesh['dp'=4,'ctx'=8] {'dp','ctx'}, use_global_device_ids=true, to_apply=%region_8.9.clone | all-reduce | flops 4096 | bytes 32768
  914.7 107.2 %reduce-scatter.8.cloned.1.call-done = bf16[256,2048]{1,0:T(8,128)(2,1)} async-done(((bf16[2048,2048]{1,0:T(8,128)(2,1)}), bf16[256,2048]{1,0:T(8,128)(2,1)}) %reduce-scatter.8.cloned.1.call-update) | async-done | bytes 1048592 | tf_op jit(solution)/shard_map/reduce_scatter | solution.py:272
  1021.9 4.0 fusion.14
  (141 shorter events, 57.8 us)
Async XLA Ops:
  7.2 229.5 %all-gather.14.cloned.1.call-start = ((), (), s32[]{:S(2)}) async-start(), calls=%async_computation.13 | async-start | bytes 1310720 | tf_op jit(solution)/shard_map/all_gather | solution.py:250
  42.9 3.3 copy-start.20
  42.9 69.6 %copy-start.4 = (bf16[2,128,2048]{2,1,0:T(8,128)(2,1)S(1)}, bf16[2,128,2048]{2,1,0:T(8,128)(2,1)}, u32[]{:S(2)}) copy-start(bf16[2,128,2048]{2,1,0:T(8,128)(2,1)} %param.10) | copy-start | bytes 3145732
  44.2 192.5 %all-gather.22.cloned.1.call-start = ((), (), s32[]{:S(2)}) async-start(), calls=%async_computation.18 | async-start | bytes 9437184 | tf_op jit(solution)/shard_map/all_gather | solution.py:269
  45.0 219.9 %all-gather.12.cloned.1.call-start = ((), (), s32[]{:S(2)}) async-start(), calls=%async_computation.12 | async-start | bytes 3932160 | tf_op jit(solution)/shard_map/all_gather | solution.py:250
  46.1 69.1 %copy-start.9 = (bf16[64,5632]{1,0:T(8,128)(2,1)S(1)}, bf16[64,5632]{1,0:T(8,128)(2,1)}, u32[]{:S(2)}) copy-start(bf16[64,5632]{1,0:T(8,128)(2,1)} %param.14) | copy-start | bytes 2162692
  46.1 346.3 %all-gather.10.cloned.1.call-start = ((), (), s32[]{:S(2)}) async-start(), calls=%async_computation.11 | async-start | bytes 9437184 | tf_op jit(solution)/shard_map/all_gather | solution.py:269
  112.4 3.5 copy-start.12
  112.4 3.5 copy-start.10
  113.1 3.5 copy-start.11
  115.1 358.4 %all-gather.18.cloned.1.call-start = ((), (), s32[]{:S(2)}) async-start(), calls=%async_computation.15 | async-start | bytes 3932160 | tf_op jit(solution)/shard_map/all_gather | solution.py:250
  231.3 253.7 %all-gather.16.cloned.1.call-start = ((), (), s32[]{:S(2)}) async-start(), calls=%async_computation.14 | async-start | bytes 3932160 | tf_op jit(solution)/shard_map/all_gather | solution.py:250
  231.8 264.4 %all-gather.20.cloned.1.call-start = ((), (), s32[]{:S(2)}) async-start(), calls=%async_computation.16 | async-start | bytes 3932160 | tf_op jit(solution)/shard_map/all_gather | solution.py:250
  232.6 381.9 %reduce-scatter.14.cloned.1.call-start = ((), (), s32[]{:S(2)}) async-start(), calls=%async_computation.21 | async-start | bytes 1310720 | tf_op jit(solution)/shard_map/reduce_scatter | solution.py:314
  244.4 159.7 %copy-start.1 = (s32[2]{0:T(128)S(1)}, s32[2]{0:T(128)}, u32[]{:S(2)}) copy-start(s32[2]{0:T(128)} %length_ref.3) | copy-start | bytes 28
  434.9 181.1 %reduce-scatter.12.cloned.1.call-start = ((), (), s32[]{:S(2)}) async-start(), calls=%async_computation.20 | async-start | bytes 3932160 | tf_op jit(solution)/shard_map/reduce_scatter | solution.py:314
  473.4 150.8 %reduce-scatter.18.cloned.1.call-start = ((), (), s32[]{:S(2)}) async-start(), calls=%async_computation.23 | async-start | bytes 3604480 | tf_op jit(solution)/shard_map/reduce_scatter | solution.py:314
  525.1 103.8 %reduce-scatter.16.cloned.1.call-start = ((), (), s32[]{:S(2)}) async-start(), calls=%async_computation.22 | async-start | bytes 3604480 | tf_op jit(solution)/shard_map/reduce_scatter | solution.py:314
  535.8 131.9 %reduce-scatter.20.cloned.1.call-start = ((), (), s32[]{:S(2)}) async-start(), calls=%async_computation.24 | async-start | bytes 3604480 | tf_op jit(solution)/shard_map/reduce_scatter | solution.py:314
  546.4 323.0 %reduce-scatter.10.cloned.1.call-start = ((), (), s32[]{:S(2)}) async-start(), calls=%async_computation.19 | async-start | bytes 9437184 | tf_op jit(solution)/shard_map/reduce_scatter | solution.py:272
  546.5 13.4 %copy-start.18 = (bf16[2048,704]{1,0:T(8,128)(2,1)S(1)}, bf16[2048,704]{1,0:T(8,128)(2,1)}, u32[]{:S(2)}) copy-start(bf16[2048,704]{1,0:T(8,128)(2,1)} %all-gather.18.cloned.1.call-done) | copy-start | bytes 8650756
  546.5 13.4 %copy-start.22 = (bf16[2048,704]{0,1:T(8,128)(2,1)S(1)}, bf16[2048,704]{0,1:T(8,128)(2,1)}, u32[]{:S(2)}) copy-start(bf16[2048,704]{0,1:T(8,128)(2,1)} %copy-done.21) | copy-start | bytes 8650756
  589.6 13.4 %copy-start.8 = (bf16[2048,256]{1,0:T(8,128)(2,1)S(1)}, bf16[2048,256]{1,0:T(8,128)(2,1)}, u32[]{:S(2)}) copy-start(bf16[2048,256]{1,0:T(8,128)(2,1)} %all-gather.14.cloned.1.call-done) | copy-start | bytes 3145732
  589.6 432.4 %reduce-scatter.8.cloned.1.call-start = ((), (), s32[]{:S(2)}) async-start(), calls=%async_computation.17 | async-start | bytes 9437184 | tf_op jit(solution)/shard_map/reduce_scatter | solution.py:272
  620.6 50.5 %all-to-all-start.2 = ((bf16[8,4,64,256]{3,1,2,0:T(4,128)(2,1)}), bf16[8,4,64,256]{3,1,2,0:T(4,128)(2,1)S(1)}, u32[]{:S(2)}, u32[]{:S(2)}) async-start(bf16[8,4,64,256]{3,1,2,0:T(4,128)(2,1)} %pad_maximum_fusion.3), calls=%async_computation.6 | async-start | bytes 2097152 | tf_op jit(solution)/shard_map/all_to_all | solution.py:331
  671.1 114.2 %all-to-all-start.3 = ((bf16[8,3,64,704]{3,2,1,0:T(8,128)(2,1)}), bf16[8,3,64,704]{3,2,1,0:T(8,128)(2,1)S(1)}, u32[]{:S(2)}, u32[]{:S(2)}) async-start(bf16[8,3,64,704]{3,2,1,0:T(8,128)(2,1)} %copy.80), calls=%async_computation.10 | async-start | bytes 4718592 | tf_op jit(solution)/shard_map/all_to_all | solution.py:330
  790.0 6.5 copy-start.6
  796.5 73.0 %copy-start.5 = (bf16[2,128,2048]{2,1,0:T(8,128)(2,1)S(1)}, bf16[2,128,2048]{2,1,0:T(8,128)(2,1)}, u32[]{:S(2)}) copy-start(bf16[2,128,2048]{2,1,0:T(8,128)(2,1)} %param.10) | copy-start | bytes 3145732
  796.5 73.0 %copy-start.13 = (f32[2048]{0:T(1024)S(1)}, f32[2048]{0:T(1024)}, u32[]{:S(2)}) copy-start(f32[2048]{0:T(1024)} %copy-done.12) | copy-start | bytes 24580
  796.5 73.0 %copy-start.15 = (f32[256]{0:T(256)S(1)}, f32[256]{0:T(256)}, u32[]{:S(2)}) copy-start(f32[256]{0:T(256)} %copy-done.14) | copy-start | bytes 3076
  796.5 73.0 %copy-start.17 = (f32[256]{0:T(256)S(1)}, f32[256]{0:T(256)}, u32[]{:S(2)}) copy-start(f32[256]{0:T(256)} %copy-done.16) | copy-start | bytes 3076
  798.6 223.3 %copy-start.7 = (bf16[2,128,2048]{2,1,0:T(8,128)(2,1)S(1)}, bf16[2,128,2048]{2,1,0:T(8,128)(2,1)}, u32[]{:S(2)}) copy-start(bf16[2,128,2048]{2,1,0:T(8,128)(2,1)} %param.18) | copy-start | bytes 3145732
  (7 other events, 9.4 us)
Sparse Core Ops, SparseCore 0:
  44.3 15.7 all-gather.13
  62.3 172.8 all-gather.21
  237.3 27.5 all-gather.11
  267.5 124.9 all-gather.9
  394.4 26.7 all-gather.17
  423.1 28.5 all-gather.15
  453.8 28.5 all-gather.19
  485.5 24.8 reduce-scatter.13
  513.1 37.9 reduce-scatter.11
  553.5 36.3 reduce-scatter.17
  592.6 36.3 reduce-scatter.15
  631.3 36.3 reduce-scatter.19
  671.8 197.6 reduce-scatter.9
  873.0 148.9 reduce-scatter.7

commit v2 on v1

v2 whole, which is shorter than its diff:
```python
import functools

import jax
import jax.numpy as jnp
from jax import lax
from jax.experimental import pallas as pl
from jax.experimental.pallas import tpu as pltpu
from jax.sharding import PartitionSpec as P

HD = 64
ROT = 16
EPSILON = 1e-05
THETA = 10000.0
NEGATIVE = -1e30
BF = jnp.bfloat16
F32 = jnp.float32
LAST = (((1,), (1,)), ((), ()))
FIRST = (((0,), (0,)), ((), ()))


def dot(left, right):
    return jnp.dot(left, right, preferred_element_type=F32)


def dot_last(left, right):
    return lax.dot_general(left, right, LAST, preferred_element_type=F32)


def dot_first(left, right):
    return lax.dot_general(left, right, FIRST, preferred_element_type=F32)


def rotary_tables(length, width):
    half = ROT // 2
    lane = jnp.arange(width, dtype=jnp.int32) % HD
    frequency = THETA ** (-(2.0 * (lane % half).astype(F32)) / ROT)
    angles = jnp.arange(length, dtype=jnp.int32).astype(F32)[:, None] * frequency[None, :]
    cosine = jnp.where(lane[None, :] < ROT, jnp.cos(angles), 1.0)
    sine = jnp.sin(angles)
    sine = jnp.where(lane[None, :] < half, -sine, jnp.where(lane[None, :] < ROT, sine, 0.0))
    return cosine, sine


def partner(x):
    half = ROT // 2
    lane = lax.broadcasted_iota(jnp.int32, x.shape, 1) % HD
    down = jnp.concatenate([x[:, half:], x[:, :half]], axis=1)
    up = jnp.concatenate([x[:, -half:], x[:, :-half]], axis=1)
    return jnp.where(lane < half, down, up)


def attend_forward(length_ref, slot_ref, joined_ref, cos_ref, sin_ref, rot_ref, attn_ref, lse_ref, total):
    parts, _, rows, triple = joined_ref.shape
    width = triple // 3
    length = parts * rows
    seq = pl.program_id(0)
    head = pl.program_id(1)
    alive_count = length_ref[seq]
    block = min(256, length)
    lane = lax.broadcasted_iota(jnp.int32, (1, width), 1)
    mine = (lane // HD) == head

    @pl.when(head == 0)
    def _():
        for part in range(parts):
            slot = slot_ref[part]
            here = slice(part * rows, (part + 1) * rows)

            def rotated(start):
                x = joined_ref[slot, 0, :, start : start + width]
                return (x * cos_ref[here, :] + partner(x) * sin_ref[here, :]).astype(BF)

            rot_ref[part, 0, :, :width] = rotated(0) * 0.125
            rot_ref[part, 0, :, width : 2 * width] = rotated(width)
            rot_ref[part, 0, :, 2 * width :] = joined_ref[slot, 0, :, 2 * width :].astype(BF)
        total[...] = jnp.zeros_like(total)
        lse_ref[...] = jnp.zeros_like(lse_ref)

    per = block // rows if block >= rows else 1
    block = per * rows
    for step in range(length // block):
        begin, end = step * per, (step + 1) * per
        stop = end * rows

        @pl.when(begin * rows < alive_count)
        def _(begin=begin, end=end, stop=stop):
            q = rot_ref[begin:end, 0, :, :width].reshape(block, width)
            q = jnp.where(mine, q, jnp.zeros_like(q))
            k = rot_ref[:end, 0, :, width : 2 * width].reshape(stop, width)
            v = rot_ref[:end, 0, :, 2 * width :].reshape(stop, width)
            scores = dot_last(q, k)
            q_pos = begin * rows + lax.broadcasted_iota(jnp.int32, (block, 1), 0)
            k_pos = lax.broadcasted_iota(jnp.int32, (block, stop), 1)
            scores = jnp.where(k_pos <= q_pos, scores, NEGATIVE)
            top = jnp.max(scores, axis=1, keepdims=True)
            expo = jnp.exp(scores - top)
            weight = jnp.sum(expo, axis=1, keepdims=True)
            out = dot(expo.astype(BF), v) / weight
            alive = q_pos < alive_count
            here = slice(begin * rows, stop)
            total[here, :] += jnp.where(mine & alive, out, 0.0)
            lse = jnp.where(alive, top + jnp.log(weight), 0.0)
            spot = lax.broadcasted_iota(jnp.int32, (1, lse_ref.shape[3]), 1) == head
            held = lse_ref[begin:end, 0].reshape(block, lse_ref.shape[3])
            lse_ref[begin:end, 0] = jnp.where(spot, lse, held).reshape(per, rows, -1)

    @pl.when(head == pl.num_programs(1) - 1)
    def _():
        for part in range(parts):
            attn_ref[slot_ref[part], 0] = total[part * rows : (part + 1) * rows, :].astype(BF)


def attend_backward(
    length_ref, slot_ref, rot_ref, attn_ref, grad_ref, lse_ref, cos_ref, sin_ref, out_ref, dq, dk, dv
):
    parts, _, rows, triple = rot_ref.shape
    width = triple // 3
    length = parts * rows
    seq = pl.program_id(0)
    head = pl.program_id(1)
    alive_count = length_ref[seq]
    per = max(1, min(256, length) // rows)
    block = per * rows
    lane = lax.broadcasted_iota(jnp.int32, (1, width), 1)
    mine = (lane // HD) == head

    @pl.when(head == 0)
    def _():
        dq[...] = jnp.zeros_like(dq)
        dk[...] = jnp.zeros_like(dk)
        dv[...] = jnp.zeros_like(dv)

    for step in range(length // block):
        begin, end = step * per, (step + 1) * per
        stop = end * rows

        @pl.when(begin * rows < alive_count)
        def _(begin=begin, end=end, stop=stop):
            q_pos = begin * rows + lax.broadcasted_iota(jnp.int32, (block, 1), 0)
            alive = q_pos < alive_count
            q = rot_ref[begin:end, 0, :, :width].reshape(block, width)
            q = jnp.where(mine, q, jnp.zeros_like(q))
            k = rot_ref[:end, 0, :, width : 2 * width].reshape(stop, width)
            v = rot_ref[:end, 0, :, 2 * width :].reshape(stop, width)
            slots = [slot_ref[part] for part in range(begin, end)]
            g = jnp.concatenate([grad_ref[slot, 0] for slot in slots], axis=0)
            g = jnp.where(mine & alive, g, jnp.zeros_like(g))
            o = jnp.concatenate([attn_ref[slot, 0] for slot in slots], axis=0)
            delta = jnp.sum(g.astype(F32) * o.astype(F32), axis=1, keepdims=True)
            held = lse_ref[begin:end, 0].reshape(block, lse_ref.shape[3])
            spot = lax.broadcasted_iota(jnp.int32, (1, lse_ref.shape[3]), 1) == head
            lse = jnp.sum(jnp.where(spot, held, 0.0), axis=1, keepdims=True)
            scores = dot_last(q, k)
            k_pos = lax.broadcasted_iota(jnp.int32, (block, stop), 1)
            probs = jnp.where((k_pos <= q_pos) & alive, jnp.exp(scores - lse), 0.0)
            d_probs = dot_last(g, v)
            d_scores = (probs * (d_probs - delta)).astype(BF)
            here = slice(begin * rows, stop)
            dq[here, :] += jnp.where(mine, dot(d_scores, k), 0.0)
            dk[:stop, :] += dot_first(d_scores, q)
            dv[:stop, :] += dot_first(probs.astype(BF), g)

    @pl.when(head == pl.num_programs(1) - 1)
    def _():
        for part in range(parts):
            slot = slot_ref[part]
            here = slice(part * rows, (part + 1) * rows)

            def unrotated(x):
                return (x * cos_ref[here, :] - partner(x) * sin_ref[here, :]).astype(BF)

            out_ref[slot, 0, :, :width] = unrotated(dq[here, :] * 0.125)
            out_ref[slot, 0, :, width : 2 * width] = unrotated(dk[here, :])
            out_ref[slot, 0, :, 2 * width :] = dv[here, :].astype(BF)


def attention_calls(parts, groups, rows, width, heads):
    length = parts * rows
    smem = pl.BlockSpec(memory_space=pltpu.SMEM)

    def spec(last):
        return pl.BlockSpec((parts, 1, rows, last), lambda s, h: (0, s, 0, 0))

    table = pl.BlockSpec((length, width), lambda s, h: (0, 0))

    def shape(last, dtype):
        return jax.ShapeDtypeStruct((parts, groups, rows, last), dtype)

    pairs = groups * heads * length * length // 2
    params = pltpu.CompilerParams(vmem_limit_bytes=48 * 1024 * 1024)
    forward = pl.pallas_call(
        attend_forward,
        grid=(groups, heads),
        in_specs=[smem, smem, spec(3 * width), table, table],
        out_specs=[spec(3 * width), spec(width), spec(heads)],
        out_shape=[shape(3 * width, BF), shape(width, BF), shape(heads, F32)],
        scratch_shapes=[pltpu.VMEM((length, width), F32)],
        compiler_params=params,
        cost_estimate=pl.CostEstimate(
            flops=pairs * 1024, bytes_accessed=16 * length * width, transcendentals=pairs
        ),
        name="attend_forward",
    )
    backward = pl.pallas_call(
        attend_backward,
        grid=(groups, heads),
        in_specs=[smem, smem, spec(3 * width), spec(width), spec(width), spec(heads), table, table],
        out_specs=spec(3 * width),
        out_shape=shape(3 * width, BF),
        scratch_shapes=[pltpu.VMEM((length, width), F32)] * 3,
        compiler_params=params,
        cost_estimate=pl.CostEstimate(
            flops=pairs * 2560, bytes_accessed=16 * length * width, transcendentals=pairs
        ),
        name="attend_backward",
    )
    return forward, backward


def pack_kernel(specs, n, own, *refs):
    sources, out_ref = refs[:-1], refs[-1]
    offset = 0
    for source, (repeat, width) in zip(sources, specs):
        for part in range(repeat):
            for dest in range(n):
                start = (part * n + dest) * width
                out_ref[dest, :, offset : offset + width] = source[:, start : start + width]
            offset += width


def unpack_kernel(specs, n, own, in_ref, *outs):
    offset = 0
    for out, (repeat, width) in zip(outs, specs):
        span = repeat * width
        for source in range(n):
            out[source * own : (source + 1) * own, :] = in_ref[source, :, offset : offset + span]
        offset += span


def pack_rows_kernel(specs, n, own, me_ref, *refs):
    sources, outs = refs[: len(specs)], refs[len(specs) :]
    for step, out in enumerate(outs):
        row = pl.multiple_of((me_ref[0] ^ step) * own, own)
        offset = 0
        for source, (repeat, width) in zip(sources, specs):
            span = repeat * width
            out[:, offset : offset + span] = source[pl.ds(row, own), :]
            offset += span


def unpack_rows_kernel(specs, n, own, me_ref, *refs):
    pieces, outs, held = refs[:n], refs[n:-1], refs[-1]
    for step, piece in enumerate(pieces):
        held[me_ref[0] ^ step] = piece[...]
    offset = 0
    for out, (repeat, width) in zip(outs, specs):
        for part in range(repeat):
            for source in range(n):
                start = (part * n + source) * width
                block = held[source, :, offset : offset + width]
                out[:, start : start + width] = block.astype(F32)
            offset += width


def total_width(specs):
    return sum(repeat * width for repeat, width in specs)


def in_vmem(kernel, name, out_shape, scratch=(), scalars=0):
    def call(*operands):
        places = [pltpu.SMEM] * scalars + [pltpu.VMEM] * (len(operands) - scalars)
        outs = jax.tree.map(lambda _: pl.BlockSpec(memory_space=pltpu.VMEM), out_shape)
        moved = sum(o.size * o.dtype.itemsize for o in operands)
        return pl.pallas_call(
            kernel,
            in_specs=[pl.BlockSpec(memory_space=place) for place in places],
            out_specs=outs,
            out_shape=out_shape,
            scratch_shapes=list(scratch),
            compiler_params=pltpu.CompilerParams(vmem_limit_bytes=48 * 1024 * 1024),
            cost_estimate=pl.CostEstimate(flops=0, bytes_accessed=3 * moved, transcendentals=0),
            name=name,
        )(*operands)

    return call


def pack_columns(specs, n, own, weights):
    shape = jax.ShapeDtypeStruct((n, own, total_width(specs)), BF)
    return in_vmem(functools.partial(pack_kernel, specs, n, own), "pack_columns", shape)(*weights)


def unpack_columns(specs, n, own, packed):
    shapes = [jax.ShapeDtypeStruct((n * own, repeat * width), BF) for repeat, width in specs]
    return in_vmem(functools.partial(unpack_kernel, specs, n, own), "unpack_columns", shapes)(
        packed
    )


def pack_rows(specs, n, own, me, gradients):
    shapes = [jax.ShapeDtypeStruct((own, total_width(specs)), BF)] * n
    kernel = functools.partial(pack_rows_kernel, specs, n, own)
    return in_vmem(kernel, "pack_rows", shapes, scalars=1)(me.reshape(1), *gradients)


def unpack_rows(specs, n, own, me, pieces):
    shapes = [jax.ShapeDtypeStruct((own, repeat * n * width), F32) for repeat, width in specs]
    kernel = functools.partial(unpack_rows_kernel, specs, n, own)
    held = pltpu.VMEM((n, own, total_width(specs)), BF)
    return in_vmem(kernel, "unpack_rows", shapes, scratch=[held], scalars=1)(
        me.reshape(1), *pieces
    )


class Layer:
    def __init__(self, n_ctx, slots, inputs, norm_gain, cotangent, lengths):
        self.groups, self.rows, self.features = inputs.shape
        self.tokens = self.groups * self.rows
        self.n_ctx, self.slots, self.lengths = n_ctx, slots, lengths
        self.own = norm_gain.shape[0]
        self.width = self.features // n_ctx
        self.flat = inputs.reshape(self.tokens, self.features).astype(F32)
        self.cot = cotangent.reshape(self.tokens, self.features)
        self.forward, self.backward = attention_calls(
            n_ctx, self.groups, self.rows, self.width, self.width // HD
        )
        self.tables = rotary_tables(n_ctx * self.rows, self.width)
        self.blocks = (n_ctx, self.groups, self.rows)

    def norm(self, scales):
        self.gain = scales[:, : self.own].astype(F32).reshape(1, self.features)
        bias = scales[:, self.own :].astype(F32).reshape(1, self.features)
        center = self.flat - jnp.mean(self.flat, axis=-1, keepdims=True)
        variance = jnp.mean(center * center, axis=-1, keepdims=True)
        self.inverse = lax.rsqrt(variance + EPSILON)
        self.standard = center * self.inverse
        return (self.standard * self.gain + bias).astype(BF)

    def attend(self, joined):
        joined = joined.reshape(*self.blocks, 3 * self.width)
        rotated, attn, lse = self.forward(self.lengths, self.slots, joined, *self.tables)
        return rotated, attn.reshape(-1, self.width), lse

    def attend_back(self, rotated, attn, d_attn, lse):
        shape = (*self.blocks, self.width)
        return self.backward(
            self.lengths,
            self.slots,
            rotated,
            attn.reshape(shape),
            d_attn.reshape(shape),
            lse,
            *self.tables,
        ).reshape(-1, 3 * self.width)

    def hide(self, gate, up):
        return (gate * jax.nn.sigmoid(gate) * up).astype(BF)

    def hide_back(self, d_hidden, gate, up):
        sigmoid = jax.nn.sigmoid(gate)
        d_gate = d_hidden * up * sigmoid * (1.0 + gate * (1.0 - sigmoid))
        return d_gate.astype(BF), (d_hidden * (gate * sigmoid)).astype(BF)

    def finish_output(self, branches):
        return (self.flat + branches.astype(F32)).astype(BF)

    def norm_back(self, d_normed):
        d_normed = d_normed.astype(F32)
        grad = d_normed * self.gain
        centered = (
            grad
            - jnp.mean(grad, axis=-1, keepdims=True)
            - self.standard * jnp.mean(grad * self.standard, axis=-1, keepdims=True)
        )
        sums = [jnp.sum(d_normed * self.standard, axis=0), jnp.sum(d_normed, axis=0)]
        sums = jnp.concatenate([v.reshape(-1, self.own) for v in sums], axis=1)
        return (self.cot.astype(F32) + self.inverse * centered).astype(BF), sums


def on_any_mesh(layer, specs, weights, scales):
    n, own = layer.n_ctx, layer.own
    both = ("dp", "ctx")
    me = jnp.zeros((), jnp.int32)

    def swap(pieces):
        return lax.all_to_all(pieces, "ctx", split_axis=0, concat_axis=0, tiled=True)

    parts = unpack_columns(specs, n, own, swap(pack_columns(specs, n, own, weights)))
    w_joined, w_out, w_gate, w_up, w_down = (
        lax.all_gather(part, "dp", axis=0, tiled=True) for part in parts
    )
    normed = layer.norm(lax.all_gather(scales, both, axis=0, tiled=True))
    normed, cot = (lax.all_gather(v, "ctx", axis=0, tiled=True) for v in (normed, layer.cot))
    rotated, attn, lse = layer.attend(dot(normed, w_joined))
    gate, up = dot(normed, w_gate), dot(normed, w_up)
    hidden = layer.hide(gate, up)
    branches = (dot_last(attn, w_out) + dot_last(hidden, w_down)).astype(BF)
    branches = lax.psum_scatter(branches, "ctx", scatter_dimension=0, tiled=True)
    d_gate, d_up = layer.hide_back(dot(cot, w_down), gate, up)
    d_joined = layer.attend_back(rotated, attn, dot(cot, w_out).astype(BF), lse)
    d_normed = dot_last(d_gate, w_gate) + dot_last(d_up, w_up) + dot_last(d_joined, w_joined)
    d_normed = lax.psum_scatter(d_normed.astype(BF), "ctx", scatter_dimension=0, tiled=True)
    pairs = [(normed, d_joined), (cot, attn), (normed, d_gate), (normed, d_up), (cot, hidden)]
    sums = [
        lax.psum_scatter(dot_first(*pair).astype(BF), "dp", scatter_dimension=0, tiled=True)
        for pair in pairs
    ]
    pieces = swap(jnp.stack(pack_rows(specs, n, own, me, sums)))
    grads = unpack_rows(specs, n, own, me, [pieces[i] for i in range(n)])
    input_grad, norm_sums = layer.norm_back(d_normed)
    norm_sums = lax.psum_scatter(norm_sums, both, scatter_dimension=0, tiled=True)
    return layer.finish_output(branches), input_grad, norm_sums, grads


def swaps(bit, n):
    return [(i, i ^ bit) for i in range(n)]


class State:
    def __init__(self, **arrays):
        self.held = arrays

    def __getitem__(self, name):
        return self.held[name]

    def drop(self, *names):
        for name in names:
            del self.held[name]

    def tick(self, before=(), sends=(), work=()):
        for action in before:
            self.held.update(action(self.held))
        view = dict(self.held)
        for name, source, axis, pairs in sends:
            view[name] = lax.ppermute(self.held[source], axis, pairs)
        for action in work:
            view.update(action(view))
        self.held = lax.optimization_barrier(view)


def on_grid(layer, specs, weights, scales):
    n, own, features = layer.n_ctx, layer.own, layer.features
    ctx, dp = lax.axis_index("ctx"), lax.axis_index("dp")
    z = ctx // 2
    inner = (z == 1) | (z == 2)
    quarter = features // 4
    side, pair = ("ctx", swaps(1, n)), ("ctx", swaps(2, n))
    middle = ("ctx", [(2, 4), (3, 5), (4, 2), (5, 3)])
    outward = ("ctx", [(2, 0), (3, 1), (4, 6), (5, 7)])
    inward = ("ctx", [(b, a) for a, b in outward[1]])
    core, across = ("dp", swaps(1, 4)), ("dp", swaps(2, 4))

    def blocks_of(v, first, steps):
        blocks = [
            lax.dynamic_slice_in_dim(v, (first ^ step) * quarter, quarter, 1) for step in steps
        ]
        return jnp.concatenate(blocks, axis=1)

    def reorder(v):
        return blocks_of(v, dp, (0, 2, 1, 3))

    def unorder(v):
        return blocks_of(v, (dp % 2) * 2 + dp // 2, (0, 2, 1, 3))

    def all_scales(s):
        held = s["scales"]
        for axis, bit, size in [("ctx", b, n) for b in (1, 2, 4)] + [("dp", b, 4) for b in (1, 2)]:
            mine = lax.axis_index(axis) // bit % 2
            got = lax.ppermute(held, axis, swaps(bit, size))
            first, second = jnp.where(mine == 0, held, got), jnp.where(mine == 0, got, held)
            held = jnp.concatenate([first, second], axis=0)
        return {"n0": reorder(layer.norm(held))}

    def weights_in(s):
        packed = pack_columns(specs, n, own, weights)
        packed = lax.all_to_all(packed, "ctx", split_axis=0, concat_axis=0, tiled=True)
        names = ("joined0", "out0", "gate0", "up0", "down0")
        return dict(zip(names, unpack_columns(specs, n, own, packed)))

    def joint(name, keys):
        return lambda s: {name: jnp.concatenate([s[key] for key in keys], axis=0)}

    def whole(name):
        return joint("w_" + name, [name + i for i in "0213"])

    def gathered(letter):
        return joint(letter, [letter + i for i in ("0", "0x", "1", "1x", "2", "2x", "3", "3x")])

    def select(name):
        return lambda s: {name: jnp.where(inner, s[name + "i"], s[name + "o"])}

    def plus(name, *parts):
        return lambda s: {name: sum(s[part].astype(F32) for part in parts).astype(BF)}

    def project(s):
        return {"joined": dot(s["n"], s["w_joined"])}

    def attend(s):
        rotated, attn, lse = layer.attend(s["joined"])
        return {"rotated": rotated, "attn": attn, "lse": lse}

    def gate(s):
        return {"gate": dot(s["n"], s["w_gate"])}

    def up(s):
        up = dot(s["n"], s["w_up"])
        return {"up": up, "hidden": layer.hide(s["gate"], up)}

    def two_slots(name, total, place):
        rows = total.shape[0] // 2
        return {f"{name}{place}k": total[:rows], f"{name}{place}a": total[rows:]}

    def rows_of(array, place):
        rows = array.shape[0] // 4
        return array[place * rows : (place + 1) * rows]

    def output_part(place):
        def work(s):
            total = dot_last(rows_of(s["attn"], place), s["w_out"])
            total += dot_last(rows_of(s["hidden"], place), s["w_down"])
            return two_slots("o", total.astype(BF), place)

        return work

    def normed_part(place):
        def work(s):
            total = dot_last(rows_of(s["d_gate"], place), s["w_gate"])
            total += dot_last(rows_of(s["d_up"], place), s["w_up"])
            total += dot_last(rows_of(s["d_joined"], place), s["w_joined"])
            return two_slots("d", total.astype(BF), place)

        return work

    def attn_back(s):
        return {"d_attn": dot(s["c"], s["w_out"]).astype(BF)}

    def hidden_back(s):
        d_gate, d_up = layer.hide_back(dot(s["c"], s["w_down"]), s["gate"], s["up"])
        return {"d_gate": d_gate, "d_up": d_up}

    def attend_back(s):
        d_joined = layer.attend_back(s["rotated"], s["attn"], s["d_attn"], s["lse"])
        return {"d_joined": d_joined}

    factors = {
        "joined": ("n", "d_joined"),
        "out": ("c", "attn"),
        "gate": ("n", "d_gate"),
        "up": ("n", "d_up"),
        "down": ("c", "hidden"),
    }

    def product(s, name, begin, end):
        left, right = factors[name]
        return dot_first(s[left][:, begin * quarter : end * quarter], s[right])

    def grad_a(name):
        return lambda s: {name + "A": product(s, name, 2, 4).astype(BF)}

    def grad_b(name):
        def work(s):
            total = product(s, name, 1, 2) + s[name + "Ar"][quarter:].astype(F32)
            return {name + "B": total.astype(BF)}

        return work

    def grad_c(name):
        def work(s):
            total = product(s, name, 0, 1) + s[name + "Ar"][:quarter].astype(F32)
            return {name + "C": (total + s[name + "Br"].astype(F32)).astype(BF)}

        return work

    def send_a(name):
        return (name + "Ar", name + "A", *core)

    def send_b(name):
        return (name + "Br", name + "B", *across)

    def swap_rows(names, chosen):
        def work(s):
            pieces = pack_rows(chosen, n, own, ctx, [s[name + "C"] for name in names])
            pieces = [
                lax.ppermute(piece, "ctx", swaps(step, n)) if step else piece
                for step, piece in enumerate(pieces)
            ]
            grads = unpack_rows(chosen, n, own, ctx, pieces)
            return {"g_" + name: grad for name, grad in zip(names, grads)}

        return work

    def norm_back(s):
        input_grad, sums = layer.norm_back(unorder(s["d"]))
        for axis, bit, size in [("dp", b, 4) for b in (2, 1)] + [("ctx", b, n) for b in (4, 2, 1)]:
            mine = lax.axis_index(axis) // bit % 2
            halves = sums.reshape(2, -1, sums.shape[1])
            first, second = halves[0], halves[1]
            give = jnp.where(mine == 0, second, first)
            keep = jnp.where(mine == 0, first, second)
            sums = keep + lax.ppermute(give, axis, swaps(bit, size))
        return {"input_grad": input_grad, "norm_sums": sums}

    def to(name, source, way):
        return (name, source, *way)

    def y(name):
        return (name + "2", name + "0", *across)

    def near(name):
        return (name + "1", name + "0", *core)

    def far(name):
        return (name + "3", name + "2", *core)

    st = State(scales=scales, c0=reorder(layer.cot))
    tick = st.tick
    tick(
        sends=[to("c0x", "c0", side), to("c1", "c0", pair), to("c2i", "c0", middle)],
        work=[all_scales, weights_in],
    )
    tick(
        sends=[
            to("n0x", "n0", side),
            to("n1", "n0", pair),
            to("n2i", "n0", middle),
            y("joined"),
            y("out"),
        ]
    )
    tick(
        sends=[
            to("n1x", "n1", side),
            to("n3i", "n1", middle),
            to("n2o", "n2i", outward),
            y("gate"),
            near("joined"),
        ]
    )
    tick(
        [select("n2")],
        [
            to("n2x", "n2", side),
            to("n3o", "n3i", outward),
            to("c3i", "c1", middle),
            y("up"),
            far("joined"),
        ],
    )
    tick(
        [select("n3")],
        [
            to("n3x", "n3", side),
            to("c2o", "c2i", outward),
            y("down"),
            near("out"),
            far("out"),
        ],
        [whole("joined")],
    )
    tick(
        (),
        [to("c1x", "c1", side), to("c3o", "c3i", outward), near("gate"), far("gate"), near("up")],
        [gathered("n"), project],
    )
    tick(
        [select("c2")],
        [to("c2x", "c2", side), far("up"), near("down"), far("down")],
        [attend, whole("gate"), gate],
    )
    tick(
        [select("c3")],
        [to("c3x", "c3", side)],
        [whole("up"), up, whole("out"), whole("down"), output_part(3)],
    )
    tick(
        (),
        [to("o3x", "o3a", side)],
        [output_part(2), gathered("c"), attn_back, output_part(1)],
    )
    tick(
        [plus("o3", "o3k", "o3x")],
        [to("o2x", "o2a", side), to("o3i", "o3", inward)],
        [hidden_back, output_part(0)],
    )
    tick(
        [plus("o2", "o2k", "o2x"), plus("o3", "o3", "o3i")],
        [to("o1x", "o1a", side), to("o2i", "o2", inward), to("o3m", "o3", middle)],
        [attend_back],
    )
    tick(
        [plus("o2", "o2", "o2i")],
        [to("o0x", "o0a", side), to("o2m", "o2", middle)],
        [normed_part(3), normed_part(2), grad_a("down")],
    )
    tick(
        [plus("o1", "o1k", "o1x", "o3m")],
        [to("o1p", "o1", pair), to("d3x", "d3a", side), send_a("down")],
        [normed_part(1), grad_b("down"), grad_a("gate")],
    )
    tick(
        [plus("o", "o0k", "o0x", "o2m", "o1p"), plus("d3", "d3k", "d3x")],
        [to("d2x", "d2a", side), to("d3i", "d3", inward), send_b("down"), send_a("gate")],
        [normed_part(0), grad_b("gate"), grad_a("up")],
    )
    tick(
        [plus("d2", "d2k", "d2x"), plus("d3", "d3", "d3i")],
        [
            to("d1x", "d1a", side),
            to("d2i", "d2", inward),
            to("d3m", "d3", middle),
            send_b("gate"),
            send_a("up"),
        ],
        [grad_c("down"), grad_b("up"), grad_a("joined")],
    )
    tick(
        [plus("d2", "d2", "d2i")],
        [to("d0x", "d0a", side), to("d2m", "d2", middle), send_b("up"), send_a("joined")],
        [grad_c("gate"), grad_b("joined"), grad_a("out")],
    )
    tick(
        [plus("d1", "d1k", "d1x", "d3m")],
        [to("d1p", "d1", pair), send_b("joined"), send_a("out")],
        [grad_c("up"), grad_b("out")],
    )
    wide, narrow = ("gate", "up", "down"), ("joined", "out")
    tick(
        [plus("d", "d0k", "d0x", "d2m", "d1p")],
        [send_b("out")],
        [swap_rows(wide, specs[2:]), grad_c("joined"), norm_back],
    )
    tick((), (), [grad_c("out"), swap_rows(narrow, specs[:2])])
    grads = [st["g_" + name] for name in narrow + wide]
    return layer.finish_output(unorder(st["o"])), st["input_grad"], st["norm_sums"], grads


def on_device(
    n_ctx,
    n_dp,
    inputs,
    norm_gain,
    norm_bias,
    joined_weight,
    gate_weight,
    up_weight,
    out_weight,
    down_weight,
    cotangent,
    lengths,
):
    grid = (n_ctx, n_dp) == (8, 4)
    if grid:
        ctx = lax.axis_index("ctx")
        z, x = ctx // 2, ctx % 2
        high = z >= 2
        order = [z, z ^ 1, jnp.where(high, 1, 2), jnp.where(high, 0, 3)]
        natural = [2 * o + (x ^ r) for o in order for r in range(2)]
        slots = jnp.zeros((n_ctx,), jnp.int32)
        for slot, part in enumerate(natural):
            slots = jnp.where(jnp.arange(n_ctx) == part, slot, slots)
    else:
        slots = jnp.arange(n_ctx, dtype=jnp.int32)
    layer = Layer(n_ctx, slots, inputs, norm_gain, cotangent, lengths)
    units = gate_weight.shape[1] // n_ctx
    specs = [(3, layer.width), (1, layer.width)] + [(1, units)] * 3
    weights = (joined_weight, out_weight, gate_weight, up_weight, down_weight)
    scales = jnp.concatenate([norm_gain, norm_bias]).reshape(1, 2 * layer.own)
    run = on_grid if grid else on_any_mesh
    output, input_grad, norm_sums, grads = run(layer, specs, weights, scales)
    joined_grad, out_grad, gate_grad, up_grad, down_grad = grads
    return (
        output.reshape(inputs.shape),
        input_grad.reshape(inputs.shape),
        norm_sums[0, : layer.own],
        norm_sums[0, layer.own :],
        joined_grad,
        gate_grad,
        up_grad,
        out_grad,
        down_grad,
    )


def solution(mesh):
    rows = P(("dp", "ctx"), None)
    vector = P(("dp", "ctx"))
    tokens = P("dp", "ctx", None)
    return jax.shard_map(
        functools.partial(on_device, mesh.shape["ctx"], mesh.shape["dp"]),
        mesh=mesh,
        in_specs=(tokens, vector, vector, rows, rows, rows, rows, rows, tokens, P("dp")),
        out_specs=(tokens, tokens, vector, vector, rows, rows, rows, rows, rows),
        check_vma=False,
    )
```

time: 1040 us -> 778 us (0.75)
  blocking collectives: 253 us -> 0 us
  waiting for transfers between devices: 470 us -> 240 us
  starting transfers between devices: 10.1 us -> 136 us
  local copies, waits for them, and re-layouts: 45 us -> 102 us
  other arithmetic: 18 us -> 66.4 us
  between operations: 14.6 us -> 2.51 us
    ppermute x0 -> x85, waiting for transfers between devices: none -> 240 us  [the longest x61 124 us: tick(): view[name] = lax.ppermute(self.held[source], axis, pairs)]
    reduce_scatter x7 -> x0, waiting for transfers between devices: 216 us -> none  [the longest x2 175 us: scatter_tokens(): return lax.psum_scatter(total, 'ctx', scatter_dimension=0, tiled=True)]
    all_gather x7 -> x0, waiting for transfers between devices: 148 us -> none  [the longest x2 128 us: gather_tokens(): return lax.all_gather(part, 'ctx', axis=0, tiled=True)]
    all_to_all x2 -> x0, blocking collectives: 145 us -> none  [the longest x1 112 us: on_device(): wide = lax.all_to_all(wide, 'ctx', split_axis=0, concat_axis=0, tiled=True)]
    ppermute x0 -> x85, starting transfers between devices: none -> 129 us  [the longest x61 81.9 us: tick(): view[name] = lax.ppermute(self.held[source], axis, pairs)]
    all_to_all x2 -> x1, waiting for transfers between devices: 104 us -> 0.01 us  [weights_in(): lax.all_to_all(packed, 'ctx', split_axis=0, concat_axis=0, tiled=True)]
    all_gather x1 -> x0, blocking collectives: 66 us -> none  [on_device(): scales = lax.all_gather(scales, both, axis=0, tiled=True).astype(F32)]
    unnamed x1 -> x0, blocking collectives: 42.1 us -> none
  transfers between devices with their start and end apart: 16 -> 86, of which waited for: 7 -> 30; matrix products, arithmetic and copies ran while one was open for 22% -> 36% of each run, Pallas kernels for 5% -> 7%
where the time goes in v2:
time: 778 us; the launch traced here: 769 us
  waiting for transfers between devices  240 us (31%)
  matrix products  166 us (21%)
  starting transfers between devices  136 us (17%)
  local copies, waits for them, and re-layouts  102 us (13%)
  other arithmetic  66.4 us (9%)
  Pallas kernels  55.2 us (7%)
    ppermute x61, waiting for transfers between devices, tick(): view[name] = lax.ppermute(self.held[source], axis, pairs)  124 us
    ppermute x61, starting transfers between devices, tick(): view[name] = lax.ppermute(self.held[source], axis, pairs)  81.9 us
    dot_general x15, matrix products, dot_first(): return lax.dot_general(left, right, FIRST, preferred_element_type=F32)  69.7 us
    ppermute x5, waiting for transfers between devices, all_scales(): got = lax.ppermute(held, axis, swaps(bit, size))  68 us
    dot_general x5, matrix products, dot(): return jnp.dot(left, right, preferred_element_type=F32)  56.9 us
    unnamed x195, local copies, waits for them, and re-layouts  47.1 us
    dot_general x20, matrix products, dot_last(): return lax.dot_general(left, right, LAST, preferred_element_type=F32)  39.4 us
    optimization_barrier x21, local copies, waits for them, and re-layouts, tick(): self.held = lax.optimization_barrier(view)  39.2 us
  transfers between devices with their start and end apart: 86, of which 30 were waited for; matrix products, arithmetic and copies ran while one was open for 36% of the time, Pallas kernels for 7%

profile of v2, /device:TPU:0, one launch (start us, length us, event | category | flops | bytes accessed | tf_op | source)
XLA Modules:
  0.0 768.8 jit_solution(10191073003807823110)
XLA Ops:
  8.3 7.4 all-to-all-start
  18.0 24.2 %collective-permute-done.3 = bf16[1,128]{1,0:T(2,128)(2,1)S(1)} collective-permute-done((bf16[1,128]{1,0:T(2,128)(2,1)S(1)}, bf16[1,128]{1,0:T(2,128)(2,1)S(1)}, u32[]{:S(2)}, u32[]{:S(2)}) %collective-permute-start.3) | collective-permute-done | bytes 288 | tf_op jit(solution)/shard_map/ppermute | solution.py:469
  44.1 25.5 %collective-permute-done.4 = bf16[2,128]{1,0:T(2,128)(2,1)S(1)} collective-permute-done((bf16[2,128]{1,0:T(2,128)(2,1)S(1)}, bf16[2,128]{1,0:T(2,128)(2,1)S(1)}, u32[]{:S(2)}, u32[]{:S(2)}) %collective-permute-start.4) | collective-permute-done | bytes 544 | tf_op jit(solution)/shard_map/ppermute | solution.py:469
  73.2 16.1 %collective-permute-done.5 = bf16[4,128]{1,0:T(4,128)(2,1)S(1)} collective-permute-done((bf16[4,128]{1,0:T(4,128)(2,1)S(1)}, bf16[4,128]{1,0:T(4,128)(2,1)S(1)}, u32[]{:S(2)}, u32[]{:S(2)}) %collective-permute-start.5) | collective-permute-done | bytes 1056 | tf_op jit(solution)/shard_map/ppermute | solution.py:469
  103.6 17.1 %collective-permute-done = bf16[256,2048]{1,0:T(8,128)(2,1)} collective-permute-done((bf16[256,2048]{1,0:T(8,128)(2,1)}, bf16[256,2048]{1,0:T(8,128)(2,1)}, u32[]{:S(2)}, u32[]{:S(2)}) %collective-permute-start) | collective-permute-done | bytes 1048608 | tf_op jit(solution)/shard_map/ppermute | solution.py:435
  129.8 20.0 %collective-permute-done.12 = bf16[512,256]{1,0:T(8,128)(2,1)S(1)} collective-permute-done((bf16[512,256]{1,0:T(8,128)(2,1)}, bf16[512,256]{1,0:T(8,128)(2,1)S(1)}, u32[]{:S(2)}, u32[]{:S(2)}) %collective-permute-start.12) | collective-permute-done | bytes 262176 | tf_op jit(solution)/shard_map/ppermute | solution.py:435
  157.0 17.3 %collective-permute-done.13 = bf16[512,704]{0,1:T(8,128)(2,1)} collective-permute-done((bf16[512,704]{0,1:T(8,128)(2,1)}, bf16[512,704]{0,1:T(8,128)(2,1)}, u32[]{:S(2)}, u32[]{:S(2)}) %collective-permute-start.13) | collective-permute-done | bytes 720928 | tf_op jit(solution)/shard_map/ppermute | solution.py:435
  183.1 17.3 %collective-permute-done.22 = bf16[512,704]{0,1:T(8,128)(2,1)} collective-permute-done((bf16[512,704]{0,1:T(8,128)(2,1)}, bf16[512,704]{0,1:T(8,128)(2,1)}, u32[]{:S(2)}, u32[]{:S(2)}) %collective-permute-start.22) | collective-permute-done | bytes 720928 | tf_op jit(solution)/shard_map/ppermute | solution.py:435
  203.5 5.7 collective-permute-done.21
  216.9 4.9 fusion.82
  225.6 6.4 collective-permute-done.24
  260.9 10.9 %fusion.149 = f32[2048,768]{1,0:T(8,128)} fusion(bf16[2048,2048]{1,0:T(8,128)(2,1)} %constant_dynamic-update-slice_fusion, bf16[2048,768]{1,0:T(8,128)(2,1)S(1)} %copy-done.15), kind=kOutput, calls=%fused_computation.254 | convolution fusion | flops 6442450944 | bytes 17825792 | tf_op jit(solution)/shard_map/dot_general | solution.py:22
  283.2 12.0 %fusion.140 = f32[2048,704]{0,1:T(8,128)} fusion(bf16[2048,2048]{1,0:T(8,128)(2,1)} %constant_dynamic-update-slice_fusion, bf16[512,704]{1,0:T(8,128)(2,1)} %copy.36, bf16[512,704]{1,0:T(8,128)(2,1)} %copy.35, bf16[512,704]{1,0:T(8,128)(2,1)} %copy.34, bf16[512,704]{1,0:T(8,128)(2,1)S(1)} %get-tuple-element.525), kind=kOutput, calls=%fused_computation.245 | convolution fusion | flops 5917114368 | bytes 17039360 | tf_op jit(solution)/shard_map/dot_general | solution.py:22
  297.3 21.8 %attend_forward.1 = (bf16[8,2,128,768]{3,2,1,0:T(8,128)(2,1)}, bf16[8,2,128,256]{3,2,1,0:T(8,128)(2,1)S(1)}, f32[8,2,128,4]{3,2,1,0:T(8,128)S(1)}) custom-call(s32[2]{0:T(128)S(1)} %copy-done.11, s32[8]{0:T(128)S(1)} %compare_select_fusion.8.slot_ref, f32[8,2,128,768]{3,2,1,0:T(8,128)} %bitcast.110, f32[1024,256]{1,0:T(8,128)S(1)} %copy-done, ...), custom_call_target="tpu_custom_call" | custom-call | flops 4294967296 | bytes 4194304 | tf_op jit(solution)/shard_map/attend_forward/pallas_call | solution.py:341
  341.4 14.4 %multiply_convert_fusion.2 = (bf16[2048,704]{0,1:T(8,128)(2,1)}, f32[2048,704]{0,1:T(8,128)}) fusion(f32[2048,704]{0,1:T(8,128)} %fusion.140, bf16[2048,2048]{1,0:T(8,128)(2,1)} %constant_dynamic-update-slice_fusion, bf16[512,704]{1,0:T(8,128)(2,1)S(1)} %copy.39, bf16[512,704]{1,0:T(8,128)(2,1)S(1)} %copy-done.38, bf16[512,704]{1,0:T(8,128)(2,1)} %copy.37, ...), kind=kOutput, calls=%fused_computation.3 | convolution fusion | flops 5925765120 | bytes 25690112 | tf_op jit(solution)/shard_map/dot_general | solution.py:22
  387.2 9.7 %collective-permute-done.38 = bf16[256,2048]{1,0:T(8,128)(2,1)S(1)} collective-permute-done((bf16[256,2048]{1,0:T(8,128)(2,1)S(1)}, bf16[256,2048]{1,0:T(8,128)(2,1)S(1)}, u32[]{:S(2)}, u32[]{:S(2)}) %collective-permute-start.38) | collective-permute-done | bytes 1048608 | tf_op jit(solution)/shard_map/ppermute | solution.py:435
  397.7 6.3 collective-permute-start.40
  404.0 15.9 %multiply_convert_fusion = (bf16[2048,704]{0,1:T(8,128)(2,1)}, bf16[2048,704]{0,1:T(8,128)(2,1)}) fusion(f32[2048,704]{0,1:T(8,128)} %fusion.140, f32[2048,704]{0,1:T(8,128)} %get-tuple-element.592, bf16[2048,2048]{1,0:T(8,128)(2,1)} %copy-done.65, bf16[2048,704]{1,0:T(8,128)(2,1)} %copy-done.49), kind=kOutput, calls=%fused_computation | convolution fusion | flops 5924323328 | bytes 28573696 | tf_op jit(solution)/shard_map/dot_general | solution.py:22
  438.1 23.7 %attend_backward.1 = bf16[8,2,128,768]{3,2,1,0:T(8,128)(2,1)} custom-call(s32[2]{0:T(128)S(1)} %copy-done.11, s32[8]{0:T(128)S(1)} %compare_select_fusion.8.slot_ref, bf16[8,2,128,768]{3,2,1,0:T(8,128)(2,1)} %get-tuple-element.612.rot_ref, bf16[8,2,128,256]{3,2,1,0:T(8,128)(2,1)S(1)} %copy-done.3, bf16[8,2,128,256]{3,2,1,0:T(8,128)(2,1)S(1)} %bitcast.88, ...), custom_call_target="tpu_custom_call" | custom-call | flops 10737418240 | bytes 4194304 | tf_op jit(solution)/shard_map/attend_backward/pallas_call | solution.py:346
  481.5 6.8 fusion.43
  488.4 9.1 %collective-permute-done.44 = bf16[256,2048]{1,0:T(8,128)(2,1)S(1)} collective-permute-done((bf16[256,2048]{1,0:T(8,128)(2,1)S(1)}, bf16[256,2048]{1,0:T(8,128)(2,1)S(1)}, u32[]{:S(2)}, u32[]{:S(2)}) %collective-permute-start.44) | collective-permute-done | bytes 1048608 | tf_op jit(solution)/shard_map/ppermute | solution.py:435
  508.9 7.3 fusion.46
  534.6 11.0 %collective-permute-start.51 = (bf16[512,704]{0,1:T(8,128)(2,1)}, bf16[512,704]{0,1:T(8,128)(2,1)S(1)}, u32[]{:S(2)}, u32[]{:S(2)}) collective-permute-start(bf16[512,704]{0,1:T(8,128)(2,1)} %add_convert_fusion.29), channel_id=1, source_target_pairs={{0,16},{8,24},{16,0},{24,8},{1,17},{9,25},{17,1},{25,9},{2,18},{10... | collective-permute-start | bytes 2162696 | tf_op jit(solution)/shard_map/ppermute | solution.py:435
  555.1 7.4 fusion.49
  578.5 4.7 fusion.40
  593.8 5.3 add_convert_fusion.27
  628.4 7.6 collective-permute-start.62
  676.6 4.8 add_convert_fusion.22.refs_0_
  681.5 8.9 %collective-permute-done.74 = f32[4,128]{1,0:T(4,128)S(1)} collective-permute-done((f32[4,128]{1,0:T(4,128)S(1)}, f32[4,128]{1,0:T(4,128)S(1)}, u32[]{:S(2)}, u32[]{:S(2)}) %collective-permute-start.74) | collective-permute-done | bytes 2080 | tf_op jit(solution)/shard_map/ppermute | solution.py:600
  707.9 18.4 %collective-permute-done.69.refs_5_ = bf16[64,2112]{1,0:T(8,128)(2,1)S(1)} collective-permute-done((bf16[64,2112]{1,0:T(8,128)(2,1)S(1)}, bf16[64,2112]{1,0:T(8,128)(2,1)S(1)}, u32[]{:S(2)}, u32[]{:S(2)}) %collective-permute-start.69) | collective-permute-done | bytes 270368 | tf_op jit(solution)/shard_map/ppermute | solution.py:584
  731.8 11.2 %collective-permute-start.79 = (bf16[64,1024]{1,0:T(8,128)(2,1)S(1)}, bf16[64,1024]{1,0:T(8,128)(2,1)S(1)}, u32[]{:S(2)}, u32[]{:S(2)}) collective-permute-start(bf16[64,1024]{1,0:T(8,128)(2,1)S(1)} %get-tuple-element.785), channel_id=1, source_target_pairs={{0,2},{1,3},{2,0},{3,1},{4,6},{5,7},{6,4},{7,5},{8,10},{9,11},{10,... | collective-permute-start | bytes 393224 | tf_op jit(solution)/shard_map/ppermute | solution.py:584
  752.8 9.3 %collective-permute-done.81.refs_4_ = bf16[64,1024]{1,0:T(8,128)(2,1)S(1)} collective-permute-done((bf16[64,1024]{1,0:T(8,128)(2,1)S(1)}, bf16[64,1024]{1,0:T(8,128)(2,1)S(1)}, u32[]{:S(2)}, u32[]{:S(2)}) %collective-permute-start.81) | collective-permute-done | bytes 131104 | tf_op jit(solution)/shard_map/ppermute | solution.py:584
  (487 shorter events, 377.7 us)
Async XLA Ops:
  8.3 92.3 %all-to-all-start = ((bf16[8,64,3136]{2,1,0:T(8,128)(2,1)}), bf16[8,64,3136]{2,1,0:T(8,128)(2,1)}, u32[]{:S(2)}, u32[]{:S(2)}) async-start(bf16[8,64,3136]{2,1,0:T(8,128)(2,1)} %pack_columns.1), calls=%async_computation | async-start | bytes 6553600 | tf_op jit(solution)/shard_map/all_to_all | solution.py:476
  15.7 26.5 %collective-permute-start.3 = (bf16[1,128]{1,0:T(2,128)(2,1)S(1)}, bf16[1,128]{1,0:T(2,128)(2,1)S(1)}, u32[]{:S(2)}, u32[]{:S(2)}) collective-permute-start(bf16[1,128]{1,0:T(2,128)(2,1)S(1)} %maximum_bitcast_fusion), channel_id=1, source_target_pairs={{0,1},{1,0},{2,3},{3,2},{4,5},{5,4},{6,7},{7,6},{8,9},{9,8},{10,11... | collective-permute-start | bytes 776 | tf_op jit(solution)/shard_map/ppermute | solution.py:469
  42.3 27.4 %collective-permute-start.4 = (bf16[2,128]{1,0:T(2,128)(2,1)S(1)}, bf16[2,128]{1,0:T(2,128)(2,1)S(1)}, u32[]{:S(2)}, u32[]{:S(2)}) collective-permute-start(bf16[2,128]{1,0:T(2,128)(2,1)S(1)} %pad_maximum_fusion.13), channel_id=1, source_target_pairs={{0,2},{1,3},{2,0},{3,1},{4,6},{5,7},{6,4},{7,5},{8,10},{9,11},{10,... | collective-permute-start | bytes 1544 | tf_op jit(solution)/shard_map/ppermute | solution.py:469
  121.9 27.9 %collective-permute-start.9 = (bf16[256,2048]{1,0:T(8,128)(2,1)S(1)}, bf16[256,2048]{1,0:T(8,128)(2,1)S(1)}, u32[]{:S(2)}, u32[]{:S(2)}) collective-permute-start(bf16[256,2048]{1,0:T(8,128)(2,1)S(1)} %copy-done.30), channel_id=1, source_target_pairs={{0,1},{1,0},{2,3},{3,2},{4,5},{5,4},{6,7},{7,6},{8,9},{9,8},{10,11... | collective-permute-start | bytes 3145736 | tf_op jit(solution)/shard_map/ppermute | solution.py:435
  122.5 27.3 %collective-permute-start.10 = (bf16[256,2048]{1,0:T(8,128)(2,1)S(1)}, bf16[256,2048]{1,0:T(8,128)(2,1)}, u32[]{:S(2)}, u32[]{:S(2)}) collective-permute-start(bf16[256,2048]{1,0:T(8,128)(2,1)S(1)} %copy-done.30), channel_id=1, source_target_pairs={{0,2},{1,3},{2,0},{3,1},{4,6},{5,7},{6,4},{7,5},{8,10},{9,11},{10,... | collective-permute-start | bytes 3145736 | tf_op jit(solution)/shard_map/ppermute | solution.py:435
  179.1 30.1 %collective-permute-start.21 = (bf16[256,2048]{1,0:T(8,128)(2,1)}, bf16[256,2048]{1,0:T(8,128)(2,1)}, u32[]{:S(2)}, u32[]{:S(2)}) collective-permute-start(bf16[256,2048]{1,0:T(8,128)(2,1)} %collective-permute-done.17), channel_id=1, source_target_pairs={{2,0},{3,1},{4,6},{5,7},{10,8},{11,9},{12,14},{13,15},{18,16},{19,... | collective-permute-start | bytes 3145736 | tf_op jit(solution)/shard_map/ppermute | solution.py:435
  236.4 35.4 %collective-permute-start.28 = (bf16[256,2048]{1,0:T(8,128)(2,1)}, bf16[256,2048]{1,0:T(8,128)(2,1)}, u32[]{:S(2)}, u32[]{:S(2)}) collective-permute-start(bf16[256,2048]{1,0:T(8,128)(2,1)} %collective-permute-done.1), channel_id=1, source_target_pairs={{0,1},{1,0},{2,3},{3,2},{4,5},{5,4},{6,7},{7,6},{8,9},{9,8},{10,11... | collective-permute-start | bytes 3145736 | tf_op jit(solution)/shard_map/ppermute | solution.py:435
  238.1 33.8 %collective-permute-start.29 = (bf16[256,2048]{1,0:T(8,128)(2,1)}, bf16[256,2048]{1,0:T(8,128)(2,1)}, u32[]{:S(2)}, u32[]{:S(2)}) collective-permute-start(bf16[256,2048]{1,0:T(8,128)(2,1)} %collective-permute-done.18), channel_id=1, source_target_pairs={{2,0},{3,1},{4,6},{5,7},{10,8},{11,9},{12,14},{13,15},{18,16},{19,... | collective-permute-start | bytes 3145736 | tf_op jit(solution)/shard_map/ppermute | solution.py:435
  240.5 31.3 %collective-permute-start.30 = (bf16[512,704]{0,1:T(8,128)(2,1)}, bf16[512,704]{0,1:T(8,128)(2,1)}, u32[]{:S(2)}, u32[]{:S(2)}) collective-permute-start(bf16[512,704]{0,1:T(8,128)(2,1)} %copy.31), channel_id=1, source_target_pairs={{0,8},{8,0},{16,24},{24,16},{1,9},{9,1},{17,25},{25,17},{2,10},{10... | collective-permute-start | bytes 2162696 | tf_op jit(solution)/shard_map/ppermute | solution.py:435
  240.5 31.3 %collective-permute-start.31 = (bf16[512,704]{0,1:T(8,128)(2,1)}, bf16[512,704]{0,1:T(8,128)(2,1)}, u32[]{:S(2)}, u32[]{:S(2)}) collective-permute-start(bf16[512,704]{0,1:T(8,128)(2,1)} %collective-permute-done.13), channel_id=1, source_target_pairs={{0,8},{8,0},{16,24},{24,16},{1,9},{9,1},{17,25},{25,17},{2,10},{10... | collective-permute-start | bytes 2162696 | tf_op jit(solution)/shard_map/ppermute | solution.py:435
  244.5 27.4 %collective-permute-start.32 = (bf16[512,704]{0,1:T(8,128)(2,1)}, bf16[512,704]{0,1:T(8,128)(2,1)}, u32[]{:S(2)}, u32[]{:S(2)}) collective-permute-start(bf16[512,704]{0,1:T(8,128)(2,1)} %copy.32), channel_id=1, source_target_pairs={{0,8},{8,0},{16,24},{24,16},{1,9},{9,1},{17,25},{25,17},{2,10},{10... | collective-permute-start | bytes 2162696 | tf_op jit(solution)/shard_map/ppermute | solution.py:435
  274.2 46.9 %collective-permute-start.33 = (bf16[256,2048]{1,0:T(8,128)(2,1)}, bf16[256,2048]{1,0:T(8,128)(2,1)}, u32[]{:S(2)}, u32[]{:S(2)}) collective-permute-start(bf16[256,2048]{1,0:T(8,128)(2,1)} %broadcast_select_fusion.1), channel_id=1, source_target_pairs={{0,1},{1,0},{2,3},{3,2},{4,5},{5,4},{6,7},{7,6},{8,9},{9,8},{10,11... | collective-permute-start | bytes 3145736 | tf_op jit(solution)/shard_map/ppermute | solution.py:435
  275.7 45.4 %collective-permute-start.34 = (bf16[512,704]{0,1:T(8,128)(2,1)}, bf16[512,704]{0,1:T(8,128)(2,1)}, u32[]{:S(2)}, u32[]{:S(2)}) collective-permute-start(bf16[512,704]{0,1:T(8,128)(2,1)} %copy.33), channel_id=1, source_target_pairs={{0,8},{8,0},{16,24},{24,16},{1,9},{9,1},{17,25},{25,17},{2,10},{10... | collective-permute-start | bytes 2162696 | tf_op jit(solution)/shard_map/ppermute | solution.py:435
  275.9 45.2 %collective-permute-start.35 = (bf16[512,704]{0,1:T(8,128)(2,1)}, bf16[512,704]{0,1:T(8,128)(2,1)}, u32[]{:S(2)}, u32[]{:S(2)}) collective-permute-start(bf16[512,704]{0,1:T(8,128)(2,1)} %collective-permute-done.24), channel_id=1, source_target_pairs={{0,8},{8,0},{16,24},{24,16},{1,9},{9,1},{17,25},{25,17},{2,10},{10... | collective-permute-start | bytes 2162696 | tf_op jit(solution)/shard_map/ppermute | solution.py:435
  283.0 38.1 %collective-permute-start.36 = (bf16[512,704]{0,1:T(8,128)(2,1)}, bf16[512,704]{0,1:T(8,128)(2,1)S(1)}, u32[]{:S(2)}, u32[]{:S(2)}) collective-permute-start(bf16[512,704]{0,1:T(8,128)(2,1)} %collective-permute-done.22), channel_id=1, source_target_pairs={{0,8},{8,0},{16,24},{24,16},{1,9},{9,1},{17,25},{25,17},{2,10},{10... | collective-permute-start | bytes 2162696 | tf_op jit(solution)/shard_map/ppermute | solution.py:435
  323.7 40.7 %collective-permute-start.37 = (bf16[256,2048]{1,0:T(8,128)(2,1)}, bf16[256,2048]{1,0:T(8,128)(2,1)}, u32[]{:S(2)}, u32[]{:S(2)}) collective-permute-start(bf16[256,2048]{1,0:T(8,128)(2,1)} %broadcast_select_fusion), channel_id=1, source_target_pairs={{0,1},{1,0},{2,3},{3,2},{4,5},{5,4},{6,7},{7,6},{8,9},{9,8},{10,11... | collective-permute-start | bytes 3145736 | tf_op jit(solution)/shard_map/ppermute | solution.py:435
  396.9 29.3 %collective-permute-start.39 = (bf16[256,2048]{1,0:T(8,128)(2,1)}, bf16[256,2048]{1,0:T(8,128)(2,1)S(1)}, u32[]{:S(2)}, u32[]{:S(2)}) collective-permute-start(bf16[256,2048]{1,0:T(8,128)(2,1)} %get-tuple-element.600), channel_id=1, source_target_pairs={{0,1},{1,0},{2,3},{3,2},{4,5},{5,4},{6,7},{7,6},{8,9},{9,8},{10,11... | collective-permute-start | bytes 3145736 | tf_op jit(solution)/shard_map/ppermute | solution.py:435
  397.7 28.6 %collective-permute-start.40 = (bf16[256,2048]{1,0:T(8,128)(2,1)S(1)}, bf16[256,2048]{1,0:T(8,128)(2,1)S(1)}, u32[]{:S(2)}, u32[]{:S(2)}) collective-permute-start(bf16[256,2048]{1,0:T(8,128)(2,1)S(1)} %add_convert_fusion.20), channel_id=1, source_target_pairs={{0,2},{1,3},{6,4},{7,5},{8,10},{9,11},{14,12},{15,13},{16,18},{17,... | collective-permute-start | bytes 3145736 | tf_op jit(solution)/shard_map/ppermute | solution.py:435
  427.2 34.6 %collective-permute-start.41 = (bf16[256,2048]{1,0:T(8,128)(2,1)}, bf16[256,2048]{1,0:T(8,128)(2,1)}, u32[]{:S(2)}, u32[]{:S(2)}) collective-permute-start(bf16[256,2048]{1,0:T(8,128)(2,1)} %get-tuple-element.619), channel_id=1, source_target_pairs={{0,1},{1,0},{2,3},{3,2},{4,5},{5,4},{6,7},{7,6},{8,9},{9,8},{10,11... | collective-permute-start | bytes 3145736 | tf_op jit(solution)/shard_map/ppermute | solution.py:435
  430.3 31.5 %collective-permute-start.42 = (bf16[256,2048]{1,0:T(8,128)(2,1)}, bf16[256,2048]{1,0:T(8,128)(2,1)}, u32[]{:S(2)}, u32[]{:S(2)}) collective-permute-start(bf16[256,2048]{1,0:T(8,128)(2,1)} %add_convert_fusion.19), channel_id=1, source_target_pairs={{0,2},{1,3},{6,4},{7,5},{8,10},{9,11},{14,12},{15,13},{16,18},{17,... | collective-permute-start | bytes 3145736 | tf_op jit(solution)/shard_map/ppermute | solution.py:435
  434.0 27.8 %collective-permute-start.43 = (bf16[256,2048]{1,0:T(8,128)(2,1)}, bf16[256,2048]{1,0:T(8,128)(2,1)}, u32[]{:S(2)}, u32[]{:S(2)}) collective-permute-start(bf16[256,2048]{1,0:T(8,128)(2,1)} %add_convert_fusion.18), channel_id=1, source_target_pairs={{2,4},{3,5},{4,2},{5,3},{10,12},{11,13},{12,10},{13,11},{18,20},{1... | collective-permute-start | bytes 3145736 | tf_op jit(solution)/shard_map/ppermute | solution.py:435
  527.7 40.0 %collective-permute-start.49 = (bf16[256,2048]{1,0:T(8,128)(2,1)}, bf16[256,2048]{1,0:T(8,128)(2,1)S(1)}, u32[]{:S(2)}, u32[]{:S(2)}) collective-permute-start(bf16[256,2048]{1,0:T(8,128)(2,1)} %get-tuple-element.676), channel_id=1, source_target_pairs={{0,1},{1,0},{2,3},{3,2},{4,5},{5,4},{6,7},{7,6},{8,9},{9,8},{10,11... | collective-permute-start | bytes 3145736 | tf_op jit(solution)/shard_map/ppermute | solution.py:435
  531.0 36.7 %collective-permute-start.50 = (bf16[256,2048]{1,0:T(8,128)(2,1)S(1)}, bf16[256,2048]{1,0:T(8,128)(2,1)}, u32[]{:S(2)}, u32[]{:S(2)}) collective-permute-start(bf16[256,2048]{1,0:T(8,128)(2,1)S(1)} %add_convert_fusion.15), channel_id=1, source_target_pairs={{0,2},{1,3},{6,4},{7,5},{8,10},{9,11},{14,12},{15,13},{16,18},{17,... | collective-permute-start | bytes 3145736 | tf_op jit(solution)/shard_map/ppermute | solution.py:435
  534.6 33.1 %collective-permute-start.51 = (bf16[512,704]{0,1:T(8,128)(2,1)}, bf16[512,704]{0,1:T(8,128)(2,1)S(1)}, u32[]{:S(2)}, u32[]{:S(2)}) collective-permute-start(bf16[512,704]{0,1:T(8,128)(2,1)} %add_convert_fusion.29), channel_id=1, source_target_pairs={{0,16},{8,24},{16,0},{24,8},{1,17},{9,25},{17,1},{25,9},{2,18},{10... | collective-permute-start | bytes 2162696 | tf_op jit(solution)/shard_map/ppermute | solution.py:435
  568.7 30.5 %collective-permute-start.53 = (bf16[256,2048]{1,0:T(8,128)(2,1)}, bf16[256,2048]{1,0:T(8,128)(2,1)}, u32[]{:S(2)}, u32[]{:S(2)}) collective-permute-start(bf16[256,2048]{1,0:T(8,128)(2,1)} %get-tuple-element.693), channel_id=1, source_target_pairs={{0,1},{1,0},{2,3},{3,2},{4,5},{5,4},{6,7},{7,6},{8,9},{9,8},{10,11... | collective-permute-start | bytes 3145736 | tf_op jit(solution)/shard_map/ppermute | solution.py:435
  570.7 28.5 %collective-permute-start.54 = (bf16[256,2048]{1,0:T(8,128)(2,1)S(1)}, bf16[256,2048]{1,0:T(8,128)(2,1)}, u32[]{:S(2)}, u32[]{:S(2)}) collective-permute-start(bf16[256,2048]{1,0:T(8,128)(2,1)S(1)} %add_convert_fusion.13), channel_id=1, source_target_pairs={{0,2},{1,3},{6,4},{7,5},{8,10},{9,11},{14,12},{15,13},{16,18},{17,... | collective-permute-start | bytes 3145736 | tf_op jit(solution)/shard_map/ppermute | solution.py:435
  628.4 31.0 %collective-permute-start.62 = (bf16[256,2048]{1,0:T(8,128)(2,1)}, bf16[256,2048]{1,0:T(8,128)(2,1)}, u32[]{:S(2)}, u32[]{:S(2)}) collective-permute-start(bf16[256,2048]{1,0:T(8,128)(2,1)} %add_convert_fusion.10), channel_id=1, source_target_pairs={{0,2},{1,3},{2,0},{3,1},{4,6},{5,7},{6,4},{7,5},{8,10},{9,11},{10,... | collective-permute-start | bytes 3145736 | tf_op jit(solution)/shard_map/ppermute | solution.py:435
  670.0 32.2 %collective-permute-start.65 = (bf16[64,2112]{1,0:T(8,128)(2,1)S(1)}, bf16[64,2112]{1,0:T(8,128)(2,1)S(1)}, u32[]{:S(2)}, u32[]{:S(2)}) collective-permute-start(bf16[64,2112]{1,0:T(8,128)(2,1)S(1)} %get-tuple-element.760), channel_id=1, source_target_pairs={{0,1},{1,0},{2,3},{3,2},{4,5},{5,4},{6,7},{7,6},{8,9},{9,8},{10,11... | collective-permute-start | bytes 811016 | tf_op jit(solution)/shard_map/ppermute | solution.py:584
  670.4 33.1 %collective-permute-start.66 = (bf16[64,2112]{1,0:T(8,128)(2,1)S(1)}, bf16[64,2112]{1,0:T(8,128)(2,1)S(1)}, u32[]{:S(2)}, u32[]{:S(2)}) collective-permute-start(bf16[64,2112]{1,0:T(8,128)(2,1)S(1)} %get-tuple-element.761), channel_id=1, source_target_pairs={{0,2},{1,3},{2,0},{3,1},{4,6},{5,7},{6,4},{7,5},{8,10},{9,11},{10,... | collective-permute-start | bytes 811016 | tf_op jit(solution)/shard_map/ppermute | solution.py:584
  672.2 33.6 %collective-permute-start.67 = (bf16[64,2112]{1,0:T(8,128)(2,1)S(1)}, bf16[64,2112]{1,0:T(8,128)(2,1)S(1)}, u32[]{:S(2)}, u32[]{:S(2)}) collective-permute-start(bf16[64,2112]{1,0:T(8,128)(2,1)S(1)} %get-tuple-element.762), channel_id=1, source_target_pairs={{0,3},{1,2},{2,1},{3,0},{4,7},{5,6},{6,5},{7,4},{8,11},{9,10},{10,... | collective-permute-start | bytes 811016 | tf_op jit(solution)/shard_map/ppermute | solution.py:584
  673.5 34.4 %collective-permute-start.68 = (bf16[64,2112]{1,0:T(8,128)(2,1)S(1)}, bf16[64,2112]{1,0:T(8,128)(2,1)S(1)}, u32[]{:S(2)}, u32[]{:S(2)}) collective-permute-start(bf16[64,2112]{1,0:T(8,128)(2,1)S(1)} %get-tuple-element.763), channel_id=1, source_target_pairs={{0,4},{1,5},{2,6},{3,7},{4,0},{5,1},{6,2},{7,3},{8,12},{9,13},{10,... | collective-permute-start | bytes 811016 | tf_op jit(solution)/shard_map/ppermute | solution.py:584
  699.3 27.0 %collective-permute-start.69 = (bf16[64,2112]{1,0:T(8,128)(2,1)S(1)}, bf16[64,2112]{1,0:T(8,128)(2,1)S(1)}, u32[]{:S(2)}, u32[]{:S(2)}) collective-permute-start(bf16[64,2112]{1,0:T(8,128)(2,1)S(1)} %get-tuple-element.764), channel_id=1, source_target_pairs={{0,5},{1,4},{2,7},{3,6},{4,1},{5,0},{6,3},{7,2},{8,13},{9,12},{10,... | collective-permute-start | bytes 811016 | tf_op jit(solution)/shard_map/ppermute | solution.py:584
  (143 other events, 2085.7 us)

commit v3 on v2

v3 whole, which is shorter than its diff:
```python
import functools

import jax
import jax.numpy as jnp
from jax import lax
from jax.experimental import pallas as pl
from jax.experimental.pallas import tpu as pltpu
from jax.sharding import PartitionSpec as P

HD = 64
ROT = 16
EPSILON = 1e-05
THETA = 10000.0
NEGATIVE = -1e30
BF = jnp.bfloat16
F32 = jnp.float32
LAST = (((1,), (1,)), ((), ()))
FIRST = (((0,), (0,)), ((), ()))


def dot(left, right):
    return jnp.dot(left, right, preferred_element_type=F32)


def dot_last(left, right):
    return lax.dot_general(left, right, LAST, preferred_element_type=F32)


def dot_first(left, right):
    return lax.dot_general(left, right, FIRST, preferred_element_type=F32)


def rotary_tables(length, width):
    half = ROT // 2
    lane = jnp.arange(width, dtype=jnp.int32) % HD
    frequency = THETA ** (-(2.0 * (lane % half).astype(F32)) / ROT)
    angles = jnp.arange(length, dtype=jnp.int32).astype(F32)[:, None] * frequency[None, :]
    cosine = jnp.where(lane[None, :] < ROT, jnp.cos(angles), 1.0)
    sine = jnp.sin(angles)
    sine = jnp.where(lane[None, :] < half, -sine, jnp.where(lane[None, :] < ROT, sine, 0.0))
    return cosine, sine


def partner(x):
    half = ROT // 2
    lane = lax.broadcasted_iota(jnp.int32, x.shape, 1) % HD
    down = jnp.concatenate([x[:, half:], x[:, :half]], axis=1)
    up = jnp.concatenate([x[:, -half:], x[:, :-half]], axis=1)
    return jnp.where(lane < half, down, up)


def attend_forward(
    length_ref, slot_ref, joined_ref, cos_ref, sin_ref, wide_ref, rot_ref, attn_ref, lse_ref, total
):
    parts, _, rows, triple = joined_ref.shape
    width = triple // 3
    length = parts * rows
    seq = pl.program_id(0)
    head = pl.program_id(1)
    alive_count = length_ref[seq]
    block = min(256, length)
    lane = lax.broadcasted_iota(jnp.int32, (1, width), 1)
    mine = (lane // HD) == head

    @pl.when(head == 0)
    def _():
        for part in range(parts):
            slot = slot_ref[part]
            here = slice(part * rows, (part + 1) * rows)

            def rotated(start):
                x = joined_ref[slot, 0, :, start : start + width]
                return (x * cos_ref[here, :] + partner(x) * sin_ref[here, :]).astype(BF)

            rot_ref[part, 0, :, :width] = rotated(0) * 0.125
            rot_ref[part, 0, :, width : 2 * width] = rotated(width)
            rot_ref[part, 0, :, 2 * width :] = joined_ref[slot, 0, :, 2 * width :].astype(BF)
        total[...] = jnp.zeros_like(total)
        lse_ref[...] = jnp.zeros_like(lse_ref)

    per = block // rows if block >= rows else 1
    block = per * rows
    for step in range(length // block):
        begin, end = step * per, (step + 1) * per
        stop = end * rows

        @pl.when(begin * rows < alive_count)
        def _(begin=begin, end=end, stop=stop):
            q = rot_ref[begin:end, 0, :, :width].reshape(block, width)
            q = jnp.where(mine, q, jnp.zeros_like(q))
            k = rot_ref[:end, 0, :, width : 2 * width].reshape(stop, width)
            v = rot_ref[:end, 0, :, 2 * width :].reshape(stop, width)
            scores = dot_last(q, k)
            q_pos = begin * rows + lax.broadcasted_iota(jnp.int32, (block, 1), 0)
            k_pos = lax.broadcasted_iota(jnp.int32, (block, stop), 1)
            scores = jnp.where(k_pos <= q_pos, scores, NEGATIVE)
            top = jnp.max(scores, axis=1, keepdims=True)
            expo = jnp.exp(scores - top)
            weight = jnp.sum(expo, axis=1, keepdims=True)
            out = dot(expo.astype(BF), v) / weight
            alive = q_pos < alive_count
            here = slice(begin * rows, stop)
            total[here, :] += jnp.where(mine & alive, out, 0.0)
            lse = jnp.where(alive, top + jnp.log(weight), 0.0)
            spot = lax.broadcasted_iota(jnp.int32, (1, lse_ref.shape[3]), 1) == head
            held = lse_ref[begin:end, 0].reshape(block, lse_ref.shape[3])
            lse_ref[begin:end, 0] = jnp.where(spot, lse, held).reshape(per, rows, -1)

    @pl.when(head == pl.num_programs(1) - 1)
    def _():
        for part in range(parts):
            attn_ref[slot_ref[part], 0] = total[part * rows : (part + 1) * rows, :].astype(BF)


def attend_backward(
    length_ref, slot_ref, rot_ref, attn_ref, grad_ref, lse_ref, cos_ref, sin_ref, out_ref, dq, dk, dv
):
    parts, _, rows, triple = rot_ref.shape
    width = triple // 3
    length = parts * rows
    seq = pl.program_id(0)
    head = pl.program_id(1)
    alive_count = length_ref[seq]
    per = max(1, min(256, length) // rows)
    block = per * rows
    lane = lax.broadcasted_iota(jnp.int32, (1, width), 1)
    mine = (lane // HD) == head

    @pl.when(head == 0)
    def _():
        dq[...] = jnp.zeros_like(dq)
        dk[...] = jnp.zeros_like(dk)
        dv[...] = jnp.zeros_like(dv)

    for step in range(length // block):
        begin, end = step * per, (step + 1) * per
        stop = end * rows

        @pl.when(begin * rows < alive_count)
        def _(begin=begin, end=end, stop=stop):
            q_pos = begin * rows + lax.broadcasted_iota(jnp.int32, (block, 1), 0)
            alive = q_pos < alive_count
            q = rot_ref[begin:end, 0, :, :width].reshape(block, width)
            q = jnp.where(mine, q, jnp.zeros_like(q))
            k = rot_ref[:end, 0, :, width : 2 * width].reshape(stop, width)
            v = rot_ref[:end, 0, :, 2 * width :].reshape(stop, width)
            slots = [slot_ref[part] for part in range(begin, end)]
            g = jnp.concatenate([grad_ref[slot, 0] for slot in slots], axis=0)
            g = jnp.where(mine & alive, g, jnp.zeros_like(g))
            o = jnp.concatenate([attn_ref[slot, 0] for slot in slots], axis=0)
            delta = jnp.sum(g.astype(F32) * o.astype(F32), axis=1, keepdims=True)
            held = lse_ref[begin:end, 0].reshape(block, lse_ref.shape[3])
            spot = lax.broadcasted_iota(jnp.int32, (1, lse_ref.shape[3]), 1) == head
            lse = jnp.sum(jnp.where(spot, held, 0.0), axis=1, keepdims=True)
            scores = dot_last(q, k)
            k_pos = lax.broadcasted_iota(jnp.int32, (block, stop), 1)
            probs = jnp.where((k_pos <= q_pos) & alive, jnp.exp(scores - lse), 0.0)
            d_probs = dot_last(g, v)
            d_scores = (probs * (d_probs - delta)).astype(BF)
            here = slice(begin * rows, stop)
            dq[here, :] += jnp.where(mine, dot(d_scores, k), 0.0)
            dk[:stop, :] += dot_first(d_scores, q)
            dv[:stop, :] += dot_first(probs.astype(BF), g)

    @pl.when(head == pl.num_programs(1) - 1)
    def _():
        for part in range(parts):
            slot = slot_ref[part]
            here = slice(part * rows, (part + 1) * rows)

            def unrotated(x):
                return (x * cos_ref[here, :] - partner(x) * sin_ref[here, :]).astype(BF)

            out_ref[slot, 0, :, :width] = unrotated(dq[here, :] * 0.125)
            out_ref[slot, 0, :, width : 2 * width] = unrotated(dk[here, :])
            out_ref[slot, 0, :, 2 * width :] = dv[here, :].astype(BF)


def attention_calls(parts, groups, rows, width, heads, lanes):
    length = parts * rows
    smem = pl.BlockSpec(memory_space=pltpu.SMEM)

    def spec(last):
        return pl.BlockSpec((parts, 1, rows, last), lambda s, h: (0, s, 0, 0))

    table = pl.BlockSpec((length, width), lambda s, h: (0, 0))

    def shape(last, dtype):
        return jax.ShapeDtypeStruct((parts, groups, rows, last), dtype)

    pairs = groups * heads * length * length // 2
    params = pltpu.CompilerParams(vmem_limit_bytes=48 * 1024 * 1024)
    forward = pl.pallas_call(
        attend_forward,
        grid=(groups, heads),
        in_specs=[smem, smem, spec(3 * width), table, table, pl.BlockSpec(memory_space=pl.ANY)],
        out_specs=[spec(3 * width), spec(width), spec(heads)],
        out_shape=[shape(3 * width, BF), shape(lanes, BF), shape(heads, F32)],
        scratch_shapes=[pltpu.VMEM((length, width), F32)],
        input_output_aliases={5: 1},
        compiler_params=params,
        cost_estimate=pl.CostEstimate(
            flops=pairs * 1024, bytes_accessed=16 * length * width, transcendentals=pairs
        ),
        name="attend_forward",
    )
    backward = pl.pallas_call(
        attend_backward,
        grid=(groups, heads),
        in_specs=[smem, smem, spec(3 * width), spec(width), spec(width), spec(heads), table, table],
        out_specs=spec(3 * width),
        out_shape=shape(3 * width, BF),
        scratch_shapes=[pltpu.VMEM((length, width), F32)] * 3,
        compiler_params=params,
        cost_estimate=pl.CostEstimate(
            flops=pairs * 2560, bytes_accessed=16 * length * width, transcendentals=pairs
        ),
        name="attend_backward",
    )
    return forward, backward


class Plan:
    def __init__(self, n, own, width, units):
        self.n, self.own, self.width, self.units = n, own, width, units
        self.body = units // 128 * 128
        self.tail = units - self.body
        self.joined = 3 * width
        self.first = self.joined + 2 * units
        self.used = width + units
        self.second = self.used + own
        spans = [(0, r * n * width, width, width) for r in range(3)]
        for start, span in ((0, self.body), (self.body, self.tail)):
            spans += [(w, start, units, span) for w in (2, 3)]
        self.spans = [*spans, (1, 0, width, width), (4, 0, units, units)]

    def segments(self):
        lane = 0
        for weight, start, stride, span in self.spans:
            yield weight, start, stride, lane, span
            lane += span


def pack_kernel(plan, *refs):
    scale_ref, sources, out_ref = refs[0], refs[1:-1], refs[-1]
    for dest in range(plan.n):
        for weight, start, stride, lane, span in plan.segments():
            begin = start + dest * stride
            out_ref[dest, :, lane : lane + span] = sources[weight][:, begin : begin + span]
        out_ref[dest, :, plan.first + plan.used :] = scale_ref[...]


def unpack_kernel(plan, outs_of, in_ref, *outs):
    own = plan.own
    for out, (source, sources, lane, lanes) in zip(outs, outs_of):
        for index in range(sources):
            block = in_ref[source + index, :, lane : lane + lanes]
            out[index * own : (index + 1) * own, :] = block
    for source in range(plan.n):
        outs[-1][source] = in_ref[source, :, plan.first + plan.used :]


def pack_rows_kernel(own, n_sources, me_ref, *refs):
    sources, outs = refs[:n_sources], refs[n_sources:]
    for step, out in enumerate(outs):
        row = pl.multiple_of((me_ref[0] ^ step) * own, own)
        lane = 0
        for source in sources:
            lanes = source.shape[1]
            out[:, lane : lane + lanes] = source[pl.ds(row, own), :]
            lane += lanes


def unpack_rows_kernel(n, own, layout, me_ref, *refs):
    pieces, outs, held = refs[:n], refs[n:-1], refs[-1]
    for step, piece in enumerate(pieces):
        held[me_ref[0] ^ step] = piece[...]
    for source in range(n):
        for out, start, stride, lane, span in layout:
            begin = start + source * stride
            block = held[source, :, lane : lane + span].astype(F32)
            outs[out][:, begin : begin + span] = block


def in_vmem(kernel, name, out_shape, scratch=(), scalars=0):
    def call(*operands):
        places = [pltpu.SMEM] * scalars + [pltpu.VMEM] * (len(operands) - scalars)
        outs = jax.tree.map(lambda _: pl.BlockSpec(memory_space=pltpu.VMEM), out_shape)
        moved = sum(o.size * o.dtype.itemsize for o in operands)
        return pl.pallas_call(
            kernel,
            in_specs=[pl.BlockSpec(memory_space=place) for place in places],
            out_specs=outs,
            out_shape=out_shape,
            scratch_shapes=list(scratch),
            compiler_params=pltpu.CompilerParams(vmem_limit_bytes=48 * 1024 * 1024),
            cost_estimate=pl.CostEstimate(flops=0, bytes_accessed=3 * moved, transcendentals=0),
            name=name,
        )(*operands)

    return call


def pack_columns(plan, weights, scales):
    shape = jax.ShapeDtypeStruct((plan.n, plan.own, plan.first + plan.second), BF)
    scales = jnp.pad(scales.reshape(2, plan.own), ((0, plan.own - 2), (0, 0)))
    return in_vmem(functools.partial(pack_kernel, plan), "pack_columns", shape)(scales, *weights)


def unpack_columns(plan, packed):
    n, own = plan.n, plan.own
    outs_of = [(half * n // 2, n // 2, 0, plan.first) for half in range(2)]
    outs_of.append((0, n, plan.first, plan.second))
    shapes = [jax.ShapeDtypeStruct((c * own, lanes), BF) for _, c, _, lanes in outs_of]
    shapes.append(jax.ShapeDtypeStruct((n, own, own), BF))
    kernel = functools.partial(unpack_kernel, plan, outs_of)
    *parts, scales = in_vmem(kernel, "unpack_columns", shapes)(packed)
    return parts, scales[:, :2]


def pack_rows(own, n, me, gradients):
    lanes = sum(g.shape[1] for g in gradients)
    shapes = [jax.ShapeDtypeStruct((own, lanes), BF)] * n
    kernel = functools.partial(pack_rows_kernel, own, len(gradients))
    return in_vmem(kernel, "pack_rows", shapes, scalars=1)(me.reshape(1), *gradients)


def unpack_rows(plan, me, pieces):
    layout = list(plan.segments())
    widths = [3 * plan.width, plan.width, plan.units, plan.units, plan.units]
    shapes = [jax.ShapeDtypeStruct((plan.own, plan.n * w), F32) for w in widths]
    kernel = functools.partial(unpack_rows_kernel, plan.n, plan.own, layout)
    held = pltpu.VMEM((plan.n, plan.own, pieces[0].shape[1]), BF)
    return in_vmem(kernel, "unpack_rows", shapes, scratch=[held], scalars=1)(
        me.reshape(1), *pieces
    )


def fetch_pieces(pieces, held, sems):
    rows = pieces[0].shape[0]
    return [
        pltpu.make_async_copy(piece, held.at[pl.ds(i * rows, rows), :], sems.at[i])
        for i, piece in enumerate(pieces)
    ]


def stream_kernel(n, n_pieces, n_extra, n_into, finish, *refs):
    blocks, refs = refs[:n], refs[n:]
    pieces, refs = refs[:n_pieces], refs[n_pieces + n_into :]
    extra, outs, (held, rows_ref, rows_sem, weight_sem) = refs[:n_extra], refs[n_extra:-4], refs[-4:]
    size = blocks[0].shape[0]
    step = pl.program_id(0)
    steps = n // 2
    weight = fetch_pieces(pieces, held, weight_sem)

    def copy(block, buffer, half):
        there = rows_ref.at[buffer, pl.ds(half * size, size), :]
        return pltpu.make_async_copy(block, there, rows_sem.at[buffer, half])

    def fetch(index):
        for place in range(steps):

            @pl.when(index == place)
            def _(place=place):
                for half in range(2):
                    copy(blocks[2 * place + half], place % 2, half).start()

    @pl.when(step == 0)
    def _():
        fetch(0)
        for piece in weight:
            piece.start()

    @pl.when(step + 1 < steps)
    def _():
        fetch(step + 1)

    buffer = lax.rem(step, 2)
    for half in range(2):
        copy(blocks[half], buffer, half).wait()

    @pl.when(step == 0)
    def _():
        for piece in weight:
            piece.wait()

    rows = rows_ref[buffer]
    outs[0][...] = rows
    finish(rows, held, extra, outs[1:])


def stream(name, blocks, pieces, extra, finish, outs, all_blocks, into=()):
    size, features = blocks[0].shape
    n = len(blocks)
    first = (all_blocks - n) // 2 if into else 0
    anywhere = pl.BlockSpec(memory_space=pl.ANY)

    def rows(width):
        return pl.BlockSpec((2 * size, width), lambda i: (first + i, 0))

    outs = [(features, BF), *outs]
    width = pieces[0].shape[1]
    begin = n + len(pieces)
    return pl.pallas_call(
        functools.partial(stream_kernel, n, len(pieces), len(extra), len(into), finish),
        grid=(n // 2,),
        in_specs=[anywhere] * (begin + len(into)) + [rows(e.shape[1]) for e in extra],
        out_specs=[rows(w) for w, _ in outs],
        out_shape=[jax.ShapeDtypeStruct((all_blocks * size, w), dtype) for w, dtype in outs],
        input_output_aliases={begin + i: i for i in range(len(into))},
        scratch_shapes=[
            pltpu.VMEM((features, width), BF),
            pltpu.VMEM((2, 2 * size, features), BF),
            pltpu.SemaphoreType.DMA((2, 2)),
            pltpu.SemaphoreType.DMA((len(pieces),)),
        ],
        compiler_params=pltpu.CompilerParams(vmem_limit_bytes=52 * 1024 * 1024),
        cost_estimate=pl.CostEstimate(
            flops=2 * n * size * features * width,
            bytes_accessed=2 * (n * size + width) * features * 2,
            transcendentals=0,
        ),
        name=name,
    )(*blocks, *pieces, *into, *extra)


def swiglu(plan, both):
    body, tail = plan.body, plan.tail
    hidden, factors = [], []
    for start, span in ((0, body), (2 * body, tail)):
        gate, up = both[:, start : start + span], both[:, start + span : start + 2 * span]
        sigmoid = jax.nn.sigmoid(gate)
        silu = gate * sigmoid
        hidden.append((silu * up).astype(BF))
        factors += [up * sigmoid * (1.0 + gate * (1.0 - sigmoid)), silu]
    return hidden, factors


def project_finish(plan, rows, held, extra, outs):
    joined, factor_ref, wide = outs
    joined[...] = dot(rows, held[:, : plan.joined])
    hidden, factors = swiglu(plan, dot(rows, held[:, plan.joined :]))
    lane = 0
    for factor in factors:
        factor_ref[:, lane : lane + factor.shape[1]] = factor
        lane += factor.shape[1]
    wide[:, : plan.width] = jnp.zeros((rows.shape[0], plan.width), BF)
    wide[:, plan.width : plan.width + plan.body] = hidden[0]
    pad = jnp.zeros((rows.shape[0], plan.second - plan.used), BF)
    wide[:, plan.width + plan.body :] = jnp.concatenate([hidden[1], pad], axis=1)


def return_finish(plan, rows, held, extra, outs):
    (factor_ref,), (d_attn, d_both) = extra, outs
    total = dot(rows, held[...])
    d_attn[...] = total[:, : plan.width].astype(BF)
    begin, body, tail = plan.width, plan.body, plan.tail
    for lane, start, span in (
        (0, begin, body),
        (body, begin, body),
        (2 * body, begin + body, tail),
        (2 * body + tail, begin + body, tail),
    ):
        here = slice(lane, lane + span)
        d_both[:, here] = (total[:, start : start + span] * factor_ref[:, here]).astype(BF)


def spread_kernel(count, n_pieces, places, *refs):
    lefts, refs = refs[: count * places], refs[count * places :]
    pieces, outs, (held, sems) = refs[:n_pieces], refs[n_pieces:-2], refs[-2:]
    weight = fetch_pieces(pieces, held, sems)
    for piece in weight:
        piece.start()
    size = outs[0].shape[0]
    each = n_pieces // 4
    rows = each * pieces[0].shape[0]
    for part in range(4):
        here = slice(part * rows, (part + 1) * rows)
        for piece in weight[part * each : (part + 1) * each]:
            piece.wait()
        for place in range(places):
            total, lane = 0.0, 0
            for left in lefts[place * count : (place + 1) * count]:
                lanes = left.shape[1]
                total += dot_last(left[...], held[here, lane : lane + lanes])
                lane += lanes
            outs[2 * place][:, here] = total[:size].astype(BF)
            outs[2 * place + 1][:, here] = total[size:].astype(BF)


def spread(name, lefts, pieces, places, size):
    anywhere = pl.BlockSpec(memory_space=pl.ANY)
    features = len(pieces) * pieces[0].shape[0]
    width = pieces[0].shape[1]
    tokens = 2 * size * len(places)

    def rows(left, place):
        return pl.BlockSpec((2 * size, left.shape[1]), lambda i: (place, 0))

    blocks = 2 * len(places)
    return pl.pallas_call(
        functools.partial(spread_kernel, len(lefts), len(pieces), len(places)),
        grid=(1,),
        in_specs=[rows(left, place) for place in places for left in lefts]
        + [anywhere] * len(pieces),
        out_specs=[pl.BlockSpec((size, features), lambda i: (0, 0))] * blocks,
        out_shape=[jax.ShapeDtypeStruct((size, features), BF)] * blocks,
        scratch_shapes=[
            pltpu.VMEM((features, width), BF),
            pltpu.SemaphoreType.DMA((len(pieces),)),
        ],
        compiler_params=pltpu.CompilerParams(vmem_limit_bytes=52 * 1024 * 1024),
        cost_estimate=pl.CostEstimate(
            flops=2 * tokens * features * width,
            bytes_accessed=2 * (tokens + features) * width + 2 * tokens * features,
            transcendentals=0,
        ),
        name=name,
    )(*[left for _ in places for left in lefts], *pieces)


class Layer:
    def __init__(self, n_ctx, slots, inputs, norm_gain, cotangent, lengths, units):
        self.groups, self.rows, self.features = inputs.shape
        self.tokens = self.groups * self.rows
        self.n_ctx, self.slots, self.lengths = n_ctx, slots, lengths
        self.own = norm_gain.shape[0]
        self.width = self.features // n_ctx
        self.plan = Plan(n_ctx, self.own, self.width, units)
        self.flat = inputs.reshape(self.tokens, self.features).astype(F32)
        self.cot = cotangent.reshape(self.tokens, self.features)
        self.tables = rotary_tables(n_ctx * self.rows, self.width)
        self.blocks = (n_ctx, self.groups, self.rows)

    def calls(self, lanes):
        heads = self.width // HD
        return attention_calls(self.n_ctx, self.groups, self.rows, self.width, heads, lanes)

    def standardize(self):
        center = self.flat - jnp.mean(self.flat, axis=-1, keepdims=True)
        variance = jnp.mean(center * center, axis=-1, keepdims=True)
        inverse = lax.rsqrt(variance + EPSILON)
        return center * inverse, inverse

    def norm(self, standard, scales):
        gain = scales[:, 0].astype(F32).reshape(1, self.features)
        bias = scales[:, 1].astype(F32).reshape(1, self.features)
        return (standard * gain + bias).astype(BF), gain

    def attend(self, joined, wide):
        lanes = wide.shape[1]
        shape = (*self.blocks, lanes)
        joined = joined.reshape(*self.blocks, 3 * self.width)
        rotated, wide, lse = self.calls(lanes)[0](
            self.lengths, self.slots, joined, *self.tables, wide.reshape(shape)
        )
        return rotated, wide.reshape(-1, lanes), lse

    def attend_back(self, rotated, wide, d_attn, lse):
        lanes = wide.shape[1]
        return self.calls(lanes)[1](
            self.lengths,
            self.slots,
            rotated,
            wide.reshape(*self.blocks, lanes),
            d_attn.reshape(*self.blocks, self.width),
            lse,
            *self.tables,
        ).reshape(-1, 3 * self.width)

    def finish_output(self, branches):
        return (self.flat + branches.astype(F32)).astype(BF)

    def norm_back(self, d_normed, standard, inverse, gain):
        d_normed = d_normed.astype(F32)
        grad = d_normed * gain
        centered = (
            grad
            - jnp.mean(grad, axis=-1, keepdims=True)
            - standard * jnp.mean(grad * standard, axis=-1, keepdims=True)
        )
        sums = [jnp.sum(d_normed * standard, axis=0), jnp.sum(d_normed, axis=0)]
        sums = jnp.concatenate([v.reshape(-1, self.own) for v in sums], axis=1)
        return (self.cot.astype(F32) + inverse * centered).astype(BF), sums


def on_any_mesh(layer, weights, scales):
    plan = layer.plan
    n, own, width = plan.n, plan.own, plan.width
    me = jnp.zeros((), jnp.int32)

    def swap(pieces):
        return lax.all_to_all(pieces, "ctx", split_axis=0, concat_axis=0, tiled=True)

    def gather(v, axis):
        return lax.all_gather(v, axis, axis=0, tiled=True)

    def scatter(v, axis):
        return lax.psum_scatter(v, axis, scatter_dimension=0, tiled=True)

    parts, scales = unpack_columns(plan, swap(pack_columns(plan, weights, scales)))
    w_first = gather(jnp.concatenate(parts[:2], axis=0), "dp")
    w_second = gather(parts[2], "dp")[:, : plan.used]
    standard, inverse = layer.standardize()
    normed, gain = layer.norm(standard, gather(scales, "dp"))
    normed, cot = gather(normed, "ctx"), gather(layer.cot, "ctx")
    total = dot(normed, w_first)
    hidden, factors = swiglu(plan, total[:, plan.joined :])
    empty = jnp.zeros((normed.shape[0], width), BF)
    rotated, attn, lse = layer.attend(total[:, : plan.joined], empty)
    wide = jnp.concatenate([attn, *hidden], axis=1)
    branches = scatter(dot_last(wide, w_second).astype(BF), "ctx")
    total = dot(cot, w_second)
    body = total[:, width : width + plan.body]
    tail = total[:, width + plan.body :]
    d_both = jnp.concatenate([body, body, tail, tail], axis=1) * jnp.concatenate(factors, axis=1)
    d_joined = layer.attend_back(rotated, attn, total[:, :width].astype(BF), lse)
    d_first = jnp.concatenate([d_joined, d_both.astype(BF)], axis=1)
    d_normed = scatter(dot_last(d_first, w_first).astype(BF), "ctx")
    sums = [scatter(dot_first(*v).astype(BF), "dp") for v in ((normed, d_first), (cot, wide))]
    pieces = list(swap(jnp.stack(pack_rows(own, n, me, sums))))
    grads = unpack_rows(plan, me, pieces)
    input_grad, norm_sums = layer.norm_back(d_normed, standard, inverse, gain)
    return layer.finish_output(branches), input_grad, scatter(norm_sums, ("dp", "ctx")), grads


def swaps(bit, n):
    return [(i, i ^ bit) for i in range(n)]


class State:
    def __init__(self, **arrays):
        self.held = arrays

    def __getitem__(self, name):
        return self.held[name]

    def drop(self, *names):
        for name in names:
            del self.held[name]

    def tick(self, before=(), sends=(), work=()):
        for action in before:
            self.held.update(action(self.held))
        view = dict(self.held)
        for name, source, axis, pairs in sends:
            view[name] = lax.ppermute(self.held[source], axis, pairs)
        for action in work:
            view.update(action(view))
        self.held = lax.optimization_barrier(view)


def on_grid(layer, weights, scales):
    plan = layer.plan
    n, own, features = plan.n, plan.own, layer.features
    ctx, dp = lax.axis_index("ctx"), lax.axis_index("dp")
    z = ctx // 2
    inner = (z == 1) | (z == 2)
    quarter = features // 4
    side, pair = ("ctx", swaps(1, n)), ("ctx", swaps(2, n))
    middle = ("ctx", [(2, 4), (3, 5), (4, 2), (5, 3)])
    outward = ("ctx", [(2, 0), (3, 1), (4, 6), (5, 7)])
    inward = ("ctx", [(b, a) for a, b in outward[1]])
    core, across = ("dp", swaps(1, 4)), ("dp", swaps(2, 4))

    def blocks_of(v, first, steps):
        blocks = [
            lax.dynamic_slice_in_dim(v, (first ^ step) * quarter, quarter, 1) for step in steps
        ]
        return jnp.concatenate(blocks, axis=1)

    def reorder(v):
        return blocks_of(v, dp, (0, 2, 1, 3))

    def unorder(v):
        return blocks_of(v, (dp % 2) * 2 + dp // 2, (0, 2, 1, 3))

    def weights_in(s):
        packed = pack_columns(plan, weights, scales)
        packed = lax.all_to_all(packed, "ctx", split_axis=0, concat_axis=0, tiled=True)
        parts, held = unpack_columns(plan, packed)
        return {"a0": parts[0], "b0": parts[1], "w0": parts[2], "scales": held}

    def standardize(s):
        standard, inverse = layer.standardize()
        return {"standard": standard, "inverse": inverse}

    def normalize(s):
        held = s["scales"]
        for bit in (1, 2):
            mine = dp // bit % 2
            got = lax.ppermute(held, "dp", swaps(bit, 4))
            first, second = jnp.where(mine == 0, held, got), jnp.where(mine == 0, got, held)
            held = jnp.concatenate([first, second], axis=0)
        normed, gain = layer.norm(s["standard"], held)
        return {"n0": reorder(normed), "gain": gain}

    def select(name):
        return lambda s: {name: jnp.where(inner, s[name + "i"], s[name + "o"])}

    def plus(name, *parts):
        return lambda s: {name: sum(s[part].astype(F32) for part in parts).astype(BF)}

    def pieces(s, *names):
        return [s[name + i] for i in "0213" for name in names]

    def slots(s, letter):
        return [s.get(letter + i) for i in ("0", "0x", "1", "1x", "2", "2x", "3", "3x")]

    def project(half):
        names = ("n", "joined", "factors", "wide")

        def work(s):
            outs = [(plan.joined, F32), (2 * plan.units, F32), (plan.second, BF)]
            finish = functools.partial(project_finish, plan)
            blocks = slots(s, "n")[half * n // 2 : (half + 1) * n // 2]
            into = [s[name] for name in names] if half else []
            made = stream("project", blocks, pieces(s, "a", "b"), [], finish, outs, n, into)
            return dict(zip(names, made))

        return work

    def attend(s):
        return dict(zip(("rotated", "wide", "lse"), layer.attend(s["joined"], s["wide"])))

    def bring_back(s):
        outs = [(plan.width, BF), (2 * plan.units, BF)]
        finish = functools.partial(return_finish, plan)
        made = stream(
            "bring_back", slots(s, "c"), pieces(s, "w"), [s["factors"]], finish, outs, n
        )
        return dict(zip(("c", "d_attn", "d_both"), made))

    def attend_back(s):
        d_joined = layer.attend_back(s["rotated"], s["wide"], s["d_attn"], s["lse"])
        return {"d_joined": d_joined}

    def scattered(name, letter, lefts, weight, places):
        def work(s):
            size = s["c0"].shape[0]
            made = spread(name, [s[v] for v in lefts], pieces(s, *weight), places, size)
            keys = [f"{letter}{place}{kind}" for place in places for kind in "ka"]
            return dict(zip(keys, made))

        return work

    def output_part(*places):
        return scattered("output_part", "o", ["wide"], "w", places)

    def normed_part(*places):
        return scattered("normed_part", "d", ["d_joined", "d_both"], "ab", places)

    factors = {"J": ("n", "d_joined"), "G": ("n", "d_both"), "W": ("c", "wide")}

    def product(s, name, begin, end):
        left, right = factors[name]
        return dot_first(s[left][:, begin * quarter : end * quarter], s[right])

    def grad_a(name):
        return lambda s: {name + "A": product(s, name, 2, 4).astype(BF)}

    def grad_b(name):
        def work(s):
            total = product(s, name, 1, 2) + s[name + "Ar"][quarter:].astype(F32)
            return {name + "B": total.astype(BF)}

        return work

    def grad_c(name):
        def work(s):
            total = product(s, name, 0, 1) + s[name + "Ar"][:quarter].astype(F32)
            return {name + "C": (total + s[name + "Br"].astype(F32)).astype(BF)}

        return work

    def to(name, source, way):
        return (name, source, *way)

    def send_a(name):
        return to(name + "Ar", name + "A", core)

    def send_b(name):
        return to(name + "Br", name + "B", across)

    def deal(s):
        dealt = pack_rows(own, n, ctx, [s[name + "C"] for name in "JGW"])
        return {f"q{step}": piece for step, piece in enumerate(dealt)}

    def swap(step):
        return to(f"q{step}r", f"q{step}", ("ctx", swaps(step, n)))

    def undeal(s):
        held = [s["q0"]] + [s[f"q{step}r"] for step in range(1, n)]
        grads = unpack_rows(plan, ctx, held)
        return {f"grad{weight}": grad for weight, grad in enumerate(grads)}

    def norm_back(s):
        input_grad, sums = layer.norm_back(unorder(s["d"]), s["standard"], s["inverse"], s["gain"])
        for axis, bit, size in [("dp", b, 4) for b in (2, 1)] + [("ctx", b, n) for b in (4, 2, 1)]:
            mine = lax.axis_index(axis) // bit % 2
            halves = sums.reshape(2, -1, sums.shape[1])
            first, second = halves[0], halves[1]
            give = jnp.where(mine == 0, second, first)
            keep = jnp.where(mine == 0, first, second)
            sums = keep + lax.ppermute(give, axis, swaps(bit, size))
        return {"input_grad": input_grad, "norm_sums": sums}

    def y(name):
        return to(name + "2", name + "0", across)

    def near(name):
        return to(name + "1", name + "0", core)

    def far(name):
        return to(name + "3", name + "2", core)

    st = State(c0=reorder(layer.cot))
    tick = st.tick
    tick((), [to("c0x", "c0", side), to("c1", "c0", pair)], [weights_in, standardize])
    tick(
        [normalize],
        [to("n0x", "n0", side), to("n1", "n0", pair), to("n2i", "n0", middle), y("a"), near("a")],
    )
    tick(
        (),
        [
            to("n1x", "n1", side),
            to("n3i", "n1", middle),
            to("n2o", "n2i", outward),
            y("b"),
            far("a"),
        ],
    )
    tick(
        [select("n2")],
        [
            to("n2x", "n2", side),
            to("n3o", "n3i", outward),
            to("c2i", "c0", middle),
            near("b"),
            far("b"),
        ],
    )
    tick(
        [select("n3")],
        [
            to("n3x", "n3", side),
            to("c3i", "c1", middle),
            to("c2o", "c2i", outward),
            y("w"),
            near("w"),
        ],
        [project(0)],
    )
    tick(
        [select("c2")],
        [to("c2x", "c2", side), to("c3o", "c3i", outward), far("w")],
        [project(1), attend],
    )
    tick(
        [select("c3")],
        [to("c3x", "c3", side), to("c1x", "c0x", pair)],
        [output_part(1, 3), output_part(0, 2)],
    )
    tick((), [to("o3x", "o3a", side), to("o1p", "o1a", pair)], [bring_back, grad_a("W")])
    tick(
        [plus("o3", "o3k", "o3x")],
        [to("o2x", "o2a", side), to("o3i", "o3", inward), send_a("W")],
        [attend_back],
    )
    tick(
        [plus("o2", "o2k", "o2x"), plus("o3", "o3", "o3i"), plus("o0a", "o0a", "o1p")],
        [to("o0x", "o0a", side), to("o2i", "o2", inward), to("o3m", "o3", middle)],
        [normed_part(1, 3), grad_b("W")],
    )
    tick(
        [plus("o2", "o2", "o2i"), plus("o1", "o1k", "o3m")],
        [to("d3x", "d3a", side), to("o2m", "o2", middle), to("o1r", "o1", pair), send_b("W")],
        [normed_part(0, 2), grad_a("G")],
    )
    tick(
        [plus("d3", "d3k", "d3x")],
        [to("d2x", "d2a", side), to("d3i", "d3", inward), send_a("G")],
        [grad_b("G"), grad_a("J"), plus("o", "o0k", "o0x", "o2m", "o1r")],
    )
    tick(
        [plus("d2", "d2k", "d2x"), plus("d3", "d3", "d3i")],
        [
            to("d1x", "d1a", side),
            to("d2i", "d2", inward),
            to("d3m", "d3", middle),
            send_b("G"),
            send_a("J"),
        ],
        [grad_c("W"), grad_b("J")],
    )
    tick(
        [plus("d2", "d2", "d2i")],
        [to("d0x", "d0a", side), to("d2m", "d2", middle), send_b("J")],
        [grad_c("G"), grad_c("J"), deal],
    )
    tick(
        [plus("d1", "d1k", "d1x", "d3m")],
        [to("d1r", "d1", pair), *map(swap, (4, 5, 6, 7))],
    )
    tick([plus("d", "d0k", "d0x", "d2m", "d1r")], map(swap, (1, 2, 3)), [norm_back])
    tick((), (), [undeal])
    grads = [st[f"grad{weight}"] for weight in range(5)]
    return layer.finish_output(unorder(st["o"])), st["input_grad"], st["norm_sums"], grads


def on_device(
    n_ctx,
    n_dp,
    inputs,
    norm_gain,
    norm_bias,
    joined_weight,
    gate_weight,
    up_weight,
    out_weight,
    down_weight,
    cotangent,
    lengths,
):
    grid = (n_ctx, n_dp) == (8, 4)
    if grid:
        ctx = lax.axis_index("ctx")
        z, x = ctx // 2, ctx % 2
        high = z >= 2
        order = [z, z ^ 1, jnp.where(high, 1, 2), jnp.where(high, 0, 3)]
        natural = [2 * o + (x ^ r) for o in order for r in range(2)]
        slots = jnp.zeros((n_ctx,), jnp.int32)
        for slot, part in enumerate(natural):
            slots = jnp.where(jnp.arange(n_ctx) == part, slot, slots)
    else:
        slots = jnp.arange(n_ctx, dtype=jnp.int32)
    units = gate_weight.shape[1] // n_ctx
    layer = Layer(n_ctx, slots, inputs, norm_gain, cotangent, lengths, units)
    weights = (joined_weight, out_weight, gate_weight, up_weight, down_weight)
    scales = jnp.concatenate([norm_gain, norm_bias])
    run = on_grid if grid else on_any_mesh
    output, input_grad, norm_sums, grads = run(layer, weights, scales)
    joined_grad, out_grad, gate_grad, up_grad, down_grad = grads
    return (
        output.reshape(inputs.shape),
        input_grad.reshape(inputs.shape),
        norm_sums[0, : layer.own],
        norm_sums[0, layer.own :],
        joined_grad,
        gate_grad,
        up_grad,
        out_grad,
        down_grad,
    )


def solution(mesh):
    rows = P(("dp", "ctx"), None)
    vector = P(("dp", "ctx"))
    tokens = P("dp", "ctx", None)
    return jax.shard_map(
        functools.partial(on_device, mesh.shape["ctx"], mesh.shape["dp"]),
        mesh=mesh,
        in_specs=(tokens, vector, vector, rows, rows, rows, rows, rows, tokens, P("dp")),
        out_specs=(tokens, tokens, vector, vector, rows, rows, rows, rows, rows),
        check_vma=False,
    )
```

time: 778 us -> 652 us (0.84)
  matrix products: 166 us -> 49.2 us
  Pallas kernels: 55.2 us -> 156 us
  local copies, waits for them, and re-layouts: 102 us -> 18.7 us
  waiting for transfers between devices: 240 us -> 272 us
  starting transfers between devices: 136 us -> 106 us
  other arithmetic: 66.4 us -> 41.5 us
    pallas_call x2 -> x9, Pallas kernels: 45.5 us -> 145 us  [the longest x3 52 us: stream(): pl.pallas_call(functools.partial(stream_kernel, n, len(pieces), len(extra...]
    ppermute x19 -> x2, waiting for transfers between devices: 99.6 us -> 2.78 us  [normalize(): got = lax.ppermute(held, 'dp', swaps(bit, 4))]
    dot_general x25 -> x0, matrix products: 96.4 us -> none  [the longest x5 56.9 us: dot(): return jnp.dot(left, right, preferred_element_type=F32)]
    ppermute x61 -> x58, waiting for transfers between devices: 124 us -> 195 us  [tick(): view[name] = lax.ppermute(self.held[source], axis, pairs)]
    all_to_all x1, waiting for transfers between devices: 0.01 us -> 67.1 us  [weights_in(): lax.all_to_all(packed, 'ctx', split_axis=0, concat_axis=0, tiled=True)]
    ppermute x19 -> x2, starting transfers between devices: 41 us -> 1.59 us  [normalize(): got = lax.ppermute(held, 'dp', swaps(bit, 4))]
    optimization_barrier x21 -> x0, local copies, waits for them, and re-layouts: 39.2 us -> none  [tick(): self.held = lax.optimization_barrier(view)]
    unnamed x195 -> x124, local copies, waits for them, and re-layouts: 47.1 us -> 14.6 us
  transfers between devices with their start and end apart: 86 -> 66, of which waited for: 30 -> 33; matrix products, arithmetic and copies ran while one was open for 36% -> 12% of each run, Pallas kernels for 7% -> 23%
where the time goes in v3:
time: 652 us; the launch traced here: 646 us
  waiting for transfers between devices  272 us (42%)
  Pallas kernels  156 us (24%)
  starting transfers between devices  106 us (16%)
  matrix products  49.2 us (8%)
  other arithmetic  41.5 us (6%)
  local copies, waits for them, and re-layouts  18.7 us (3%)
    ppermute x58, waiting for transfers between devices, tick(): view[name] = lax.ppermute(self.held[source], axis, pairs)  195 us
    ppermute x58, starting transfers between devices, tick(): view[name] = lax.ppermute(self.held[source], axis, pairs)  78.6 us
    all_to_all x1, waiting for transfers between devices, weights_in(): lax.all_to_all(packed, 'ctx', split_axis=0, concat_axis=0, tiled=True)  67.1 us
    pallas_call x3, Pallas kernels, stream(): pl.pallas_call(functools.partial(stream_kernel, n, len(pieces), len(extra...  52 us
    pallas_call x4, Pallas kernels, spread(): pl.pallas_call(functools.partial(spread_kernel, len(lefts), len(pieces),...  50.2 us
    dot_general x9, matrix products, dot_first(): return lax.dot_general(left, right, FIRST, preferred_element_type=F32)  49.2 us
    pallas_call x1, Pallas kernels, attend(): self.calls(lanes)[0]  21.9 us
    pallas_call x1, Pallas kernels, attend_back(): self.calls(lanes)[1]  20.7 us
  transfers between devices with their start and end apart: 66, of which 33 were waited for; matrix products, arithmetic and copies ran while one was open for 12% of the time, Pallas kernels for 23%

profile of v3, /device:TPU:0, one launch (start us, length us, event | category | flops | bytes accessed | tf_op | source)
XLA Modules:
  0.0 646.3 jit_solution(9098664370717445376)
XLA Ops:
  9.2 7.4 %all-to-all-start = ((bf16[8,64,3200]{2,1,0:T(8,128)(2,1)}), bf16[8,64,3200]{2,1,0:T(8,128)(2,1)}, u32[]{:S(2)}, u32[]{:S(2)}) async-start(bf16[8,64,3200]{2,1,0:T(8,128)(2,1)} %pack_columns.1), calls=%async_computation | async-start | bytes 6553600 | tf_op jit(solution)/shard_map/all_to_all | solution.py:680
  23.3 67.1 %all-to-all-done.in_ref = bf16[8,64,3200]{2,1,0:T(8,128)(2,1)} async-done(((bf16[8,64,3200]{2,1,0:T(8,128)(2,1)}), bf16[8,64,3200]{2,1,0:T(8,128)(2,1)}, u32[]{:S(2)}, u32[]{:S(2)}) %all-to-all-start) | async-done | bytes 3276832 | tf_op jit(solution)/shard_map/all_to_all | solution.py:680
  108.1 18.8 %collective-permute-done.6.refs_1_ = bf16[256,2048]{1,0:T(8,128)(2,1)} collective-permute-done((bf16[256,2048]{1,0:T(8,128)(2,1)S(1)}, bf16[256,2048]{1,0:T(8,128)(2,1)}, u32[]{:S(2)}, u32[]{:S(2)}) %collective-permute-start.6) | collective-permute-done | bytes 1048608 | tf_op jit(solution)/shard_map/ppermute | solution.py:647
  132.4 23.3 %collective-permute-done.11.refs_3_ = bf16[256,2048]{1,0:T(8,128)(2,1)} collective-permute-done((bf16[256,2048]{1,0:T(8,128)(2,1)}, bf16[256,2048]{1,0:T(8,128)(2,1)}, u32[]{:S(2)}, u32[]{:S(2)}) %collective-permute-start.11) | collective-permute-done | bytes 1048608 | tf_op jit(solution)/shard_map/ppermute | solution.py:647
  166.3 21.1 %collective-permute-done.17.refs_1_ = bf16[256,2048]{1,0:T(8,128)(2,1)S(1)} collective-permute-done((bf16[256,2048]{1,0:T(8,128)(2,1)S(1)}, bf16[256,2048]{1,0:T(8,128)(2,1)S(1)}, u32[]{:S(2)}, u32[]{:S(2)}) %collective-permute-start.17) | collective-permute-done | bytes 1048608 | tf_op jit(solution)/shard_map/ppermute | solution.py:647
  187.4 8.4 %collective-permute-done.18 = bf16[256,2048]{1,0:T(8,128)(2,1)S(1)} collective-permute-done((bf16[256,2048]{1,0:T(8,128)(2,1)S(1)}, bf16[256,2048]{1,0:T(8,128)(2,1)S(1)}, u32[]{:S(2)}, u32[]{:S(2)}) %collective-permute-start.18) | collective-permute-done | bytes 1048608 | tf_op jit(solution)/shard_map/ppermute | solution.py:647
  206.3 16.9 %project.2 = (bf16[2048,2048]{1,0:T(8,128)(2,1)}, f32[2048,768]{1,0:T(8,128)}, f32[2048,1408]{1,0:T(8,128)}, bf16[2048,1024]{1,0:T(8,128)(2,1)}) custom-call(bf16[256,2048]{1,0:T(8,128)(2,1)S(1)} %copy-done.3, bf16[256,2048]{1,0:T(8,128)(2,1)} %collective-permute-done.6.refs_1_, bf16[256,2048]{1,0:T(8,128)(2,1)} %collective-permute-done.7.refs_2_, ...), custom_call_target="tpu_custom_call" | custom-call | flops 9126805504 | bytes 26214400 | tf_op jit(solution)/shard_map/project/pallas_call | solution.py:404
  229.8 17.0 %project.3 = (bf16[2048,2048]{1,0:T(8,128)(2,1)}, f32[2048,768]{1,0:T(8,128)}, f32[2048,1408]{1,0:T(8,128)}, bf16[2048,1024]{1,0:T(8,128)(2,1)}) custom-call(bf16[256,2048]{1,0:T(8,128)(2,1)S(1)} %broadcast_select_fusion.3.refs_0_, bf16[256,2048]{1,0:T(8,128)(2,1)} %copy-done.28, ...), custom_call_target="tpu_custom_call", output_to_operand_aliasing={{0}: (12, {}), {1}: (13, {}), {2}: (14, {}), {3}: (15, {})} | custom-call | flops 9126805504 | bytes 26214400 | tf_op jit(solution)/shard_map/project/pallas_call | solution.py:404
  246.9 21.9 %attend_forward.1 = (bf16[8,2,128,768]{3,2,1,0:T(8,128)(2,1)}, bf16[8,2,128,1024]{3,2,1,0:T(8,128)(2,1)}, f32[8,2,128,4]{3,2,1,0:T(8,128)S(1)}) custom-call(s32[2]{0:T(128)S(1)} %copy-done.13, s32[8]{0:T(128)S(1)} %compare_select_fusion.8.slot_ref, f32[8,2,128,768]{3,2,1,0:T(8,128)} %bitcast.46, ...), custom_call_target="tpu_custom_call", output_to_operand_aliasing={{1}: (5, {})} | custom-call | flops 4294967296 | bytes 4194304 | tf_op jit(solution)/shard_map/attend_forward/pallas_call | solution.py:554
  270.5 5.9 collective-permute-start.27
  276.4 9.2 %output_part.3 = (bf16[256,2048]{1,0:T(8,128)(2,1)S(1)}, bf16[256,2048]{1,0:T(8,128)(2,1)}, bf16[256,2048]{1,0:T(8,128)(2,1)}, bf16[256,2048]{1,0:T(8,128)(2,1)}) custom-call(bf16[2048,1024]{1,0:T(8,128)(2,1)} %bitcast.49, bf16[2048,1024]{1,0:T(8,128)(2,1)} %bitcast.50, bf16[512,1024]{1,0:T(8,128)(2,1)} %get-tuple-element.568.refs_2_.refs_8_, ...), custom_call_target="tpu_custom_call" | custom-call | flops 4294967296 | bytes 10485760 | tf_op jit(solution)/shard_map/output_part/pallas_call | solution.py:501
  285.6 9.3 %output_part.2 = (bf16[256,2048]{1,0:T(8,128)(2,1)S(1)}, bf16[256,2048]{1,0:T(8,128)(2,1)}, bf16[256,2048]{1,0:T(8,128)(2,1)}, bf16[256,2048]{1,0:T(8,128)(2,1)}) custom-call(bf16[2048,1024]{1,0:T(8,128)(2,1)} %bitcast.51, bf16[2048,1024]{1,0:T(8,128)(2,1)} %bitcast.52, bf16[512,1024]{1,0:T(8,128)(2,1)} %get-tuple-element.568.refs_2_.refs_8_, ...), custom_call_target="tpu_custom_call" | custom-call | flops 4294967296 | bytes 10485760 | tf_op jit(solution)/shard_map/output_part/pallas_call | solution.py:501
  295.6 4.5 collective-permute-done.27.refs_3_
  305.0 18.0 %bring_back.1 = (bf16[2048,2048]{1,0:T(8,128)(2,1)}, bf16[2048,256]{1,0:T(8,128)(2,1)S(1)}, bf16[2048,1408]{1,0:T(8,128)(2,1)}) custom-call(bf16[256,2048]{1,0:T(8,128)(2,1)} %copy-done.36, bf16[256,2048]{1,0:T(8,128)(2,1)} %collective-permute-done.refs_1_, bf16[256,2048]{1,0:T(8,128)(2,1)} %collective-permute-done.1.refs_2_, bf16[256,2048]{1,0:T(8,128)(2,1)} %copy-done.56, ...), custom_call_target="tpu_custom_call" | custom-call | flops 8589934592 | bytes 25165824 | tf_op jit(solution)/shard_map/bring_back/pallas_call | solution.py:404
  323.0 8.3 %fusion.29 = bf16[1024,1024]{1,0:T(8,128)(2,1)} fusion(bf16[2048,1024]{1,0:T(8,128)(2,1)S(1)} %bitcast.53, bf16[2048,2048]{1,0:T(8,128)(2,1)} %get-tuple-element.717), kind=kOutput, calls=%fused_computation.51 | convolution fusion | flops 4296015872 | bytes 10485760 | tf_op jit(solution)/shard_map/dot_general | solution.py:30
  336.0 20.7 %attend_backward.1 = bf16[8,2,128,768]{3,2,1,0:T(8,128)(2,1)} custom-call(s32[2]{0:T(128)S(1)} %copy-done.13, s32[8]{0:T(128)S(1)} %compare_select_fusion.8.slot_ref, bf16[8,2,128,768]{3,2,1,0:T(8,128)(2,1)} %get-tuple-element.611.rot_ref, bf16[8,2,128,1024]{3,2,1,0:T(8,128)(2,1)} %get-tuple-element.524, bf16[8,2,128,256]{3,2,1,0:T(8,128)(2,1)S(1)} %bitcast.43, ...), custom_call_target="tpu_custom_call" | custom-call | flops 10737418240 | bytes 4194304 | tf_op jit(solution)/shard_map/attend_backward/pallas_call | solution.py:561
  369.0 5.2 add_convert_fusion.14
  374.2 15.7 %normed_part.2 = (bf16[256,2048]{1,0:T(8,128)(2,1)S(1)}, bf16[256,2048]{1,0:T(8,128)(2,1)}, bf16[256,2048]{1,0:T(8,128)(2,1)}, bf16[256,2048]{1,0:T(8,128)(2,1)}) custom-call(bf16[2048,768]{1,0:T(8,128)(2,1)} %bitcast.71, bf16[2048,1408]{1,0:T(8,128)(2,1)} %get-tuple-element.735.refs_1_.refs_3_, bf16[2048,768]{1,0:T(8,128)(2,1)} %bitcast.72, ...), custom_call_target="tpu_custom_call" | custom-call | flops 9126805504 | bytes 17563648 | tf_op jit(solution)/shard_map/normed_part/pallas_call | solution.py:501
  400.6 11.5 %fusion.6 = bf16[1024,1408]{1,0:T(8,128)(2,1)} fusion(bf16[2048,1408]{1,0:T(8,128)(2,1)} %get-tuple-element.735.refs_1_.refs_3_, bf16[2048,2048]{1,0:T(8,128)(2,1)} %get-tuple-element.734), kind=kOutput, calls=%fused_computation.6 | convolution fusion | flops 5907021824 | bytes 12845056 | tf_op jit(solution)/shard_map/dot_general | solution.py:30
  412.1 16.0 %normed_part.3 = (bf16[256,2048]{1,0:T(8,128)(2,1)S(1)}, bf16[256,2048]{1,0:T(8,128)(2,1)}, bf16[256,2048]{1,0:T(8,128)(2,1)}, bf16[256,2048]{1,0:T(8,128)(2,1)}) custom-call(bf16[2048,768]{1,0:T(8,128)(2,1)} %bitcast.73, bf16[2048,1408]{1,0:T(8,128)(2,1)} %get-tuple-element.735.refs_1_.refs_3_, bf16[2048,768]{1,0:T(8,128)(2,1)} %bitcast.74, ...), custom_call_target="tpu_custom_call" | custom-call | flops 9126805504 | bytes 17563648 | tf_op jit(solution)/shard_map/normed_part/pallas_call | solution.py:501
  434.4 5.4 fusion.35
  446.6 9.5 %collective-permute-done.43 = bf16[256,2048]{1,0:T(8,128)(2,1)S(1)} collective-permute-done((bf16[256,2048]{1,0:T(8,128)(2,1)S(1)}, bf16[256,2048]{1,0:T(8,128)(2,1)S(1)}, u32[]{:S(2)}, u32[]{:S(2)}) %collective-permute-start.43) | collective-permute-done | bytes 1048608 | tf_op jit(solution)/shard_map/ppermute | solution.py:647
  461.1 4.8 collective-permute-start.47
  473.5 14.8 %collective-permute-done.47 = bf16[256,2048]{1,0:T(8,128)(2,1)S(1)} collective-permute-done((bf16[256,2048]{1,0:T(8,128)(2,1)S(1)}, bf16[256,2048]{1,0:T(8,128)(2,1)S(1)}, u32[]{:S(2)}, u32[]{:S(2)}) %collective-permute-start.47) | collective-permute-done | bytes 1048608 | tf_op jit(solution)/shard_map/ppermute | solution.py:647
  498.2 7.3 %fusion.11.refs_1_ = bf16[512,1408]{1,0:T(8,128)(2,1)} fusion(bf16[2048,1408]{1,0:T(8,128)(2,1)} %get-tuple-element.735.refs_1_.refs_3_, bf16[512,1408]{1,0:T(8,128)(2,1)S(1)} %collective-permute-done.44, bf16[2048,2048]{1,0:T(8,128)(2,1)S(1)} %bitcast.45, bf16[1024,1408]{1,0:T(8,128)(2,1)S(1)} %collective-permute-done.41), kind=kOutput, calls=%fused_computation.14 | convolution fusion | flops 2956394496 | bytes 12189696 | tf_op jit(solution)/shard_map/dot_general | solution.py:30
  505.4 7.7 %collective-permute-done.49 = bf16[512,768]{1,0:T(8,128)(2,1)S(1)} collective-permute-done((bf16[512,768]{1,0:T(8,128)(2,1)S(1)}, bf16[512,768]{1,0:T(8,128)(2,1)S(1)}, u32[]{:S(2)}, u32[]{:S(2)}) %collective-permute-start.49) | collective-permute-done | bytes 786464 | tf_op jit(solution)/shard_map/ppermute | solution.py:647
  534.7 25.1 %collective-permute-done.53.refs_4_ = bf16[64,3200]{1,0:T(8,128)(2,1)S(1)} collective-permute-done((bf16[64,3200]{1,0:T(8,128)(2,1)}, bf16[64,3200]{1,0:T(8,128)(2,1)S(1)}, u32[]{:S(2)}, u32[]{:S(2)}) %collective-permute-start.53) | collective-permute-done | bytes 409632 | tf_op jit(solution)/shard_map/ppermute | solution.py:647
  559.8 8.8 %collective-permute-done.54.refs_5_ = bf16[64,3200]{1,0:T(8,128)(2,1)S(1)} collective-permute-done((bf16[64,3200]{1,0:T(8,128)(2,1)}, bf16[64,3200]{1,0:T(8,128)(2,1)S(1)}, u32[]{:S(2)}, u32[]{:S(2)}) %collective-permute-start.54) | collective-permute-done | bytes 409632 | tf_op jit(solution)/shard_map/ppermute | solution.py:647
  568.6 11.3 %collective-permute-done.55.refs_6_ = bf16[64,3200]{1,0:T(8,128)(2,1)S(1)} collective-permute-done((bf16[64,3200]{1,0:T(8,128)(2,1)}, bf16[64,3200]{1,0:T(8,128)(2,1)S(1)}, u32[]{:S(2)}, u32[]{:S(2)}) %collective-permute-start.55) | collective-permute-done | bytes 409632 | tf_op jit(solution)/shard_map/ppermute | solution.py:647
  579.9 6.4 collective-permute-done.56.refs_7_
  602.0 14.4 %collective-permute-start.59 = (f32[4,128]{1,0:T(4,128)S(1)}, f32[4,128]{1,0:T(4,128)S(1)}, u32[]{:S(2)}, u32[]{:S(2)}) collective-permute-start(f32[4,128]{1,0:T(4,128)S(1)} %slice_select_fusion.1), channel_id=1, source_target_pairs={{0,4},{1,5},{2,6},{3,7},{4,0},{5,1},{6,2},{7,3},{8,12},{9,13},{10,... | collective-permute-start | bytes 6152 | tf_op jit(solution)/shard_map/ppermute | solution.py:805
  634.0 6.8 %collective-permute-done.64.refs_3_ = bf16[64,3200]{1,0:T(8,128)(2,1)S(1)} collective-permute-done((bf16[64,3200]{1,0:T(8,128)(2,1)S(1)}, bf16[64,3200]{1,0:T(8,128)(2,1)S(1)}, u32[]{:S(2)}, u32[]{:S(2)}) %collective-permute-start.64) | collective-permute-done | bytes 409632 | tf_op jit(solution)/shard_map/ppermute | solution.py:647
  (312 shorter events, 195.8 us)
Async XLA Ops:
  9.2 81.1 %all-to-all-start = ((bf16[8,64,3200]{2,1,0:T(8,128)(2,1)}), bf16[8,64,3200]{2,1,0:T(8,128)(2,1)}, u32[]{:S(2)}, u32[]{:S(2)}) async-start(bf16[8,64,3200]{2,1,0:T(8,128)(2,1)} %pack_columns.1), calls=%async_computation | async-start | bytes 6553600 | tf_op jit(solution)/shard_map/all_to_all | solution.py:680
  16.9 76.6 %collective-permute-start = (bf16[256,2048]{1,0:T(8,128)(2,1)S(1)}, bf16[256,2048]{1,0:T(8,128)(2,1)}, u32[]{:S(2)}, u32[]{:S(2)}) collective-permute-start(bf16[256,2048]{1,0:T(8,128)(2,1)S(1)} %pad_maximum_fusion.refs_0_), channel_id=1, source_target_pairs={{0,1},{1,0},{2,3},{3,2},{4,5},{5,4},{6,7},{7,6},{8,9},{9,8},{10,11... | collective-permute-start | bytes 3145736 | tf_op jit(solution)/shard_map/ppermute | solution.py:647
  19.0 75.3 %collective-permute-start.1 = (bf16[256,2048]{1,0:T(8,128)(2,1)S(1)}, bf16[256,2048]{1,0:T(8,128)(2,1)}, u32[]{:S(2)}, u32[]{:S(2)}) collective-permute-start(bf16[256,2048]{1,0:T(8,128)(2,1)S(1)} %pad_maximum_fusion.refs_0_), channel_id=1, source_target_pairs={{0,2},{1,3},{2,0},{3,1},{4,6},{5,7},{6,4},{7,5},{8,10},{9,11},{10,... | collective-permute-start | bytes 3145736 | tf_op jit(solution)/shard_map/ppermute | solution.py:647
  97.0 31.1 %collective-permute-start.2 = (bf16[256,2176]{1,0:T(8,128)(2,1)S(1)}, bf16[256,2176]{1,0:T(8,128)(2,1)}, u32[]{:S(2)}, u32[]{:S(2)}) collective-permute-start(bf16[256,2176]{1,0:T(8,128)(2,1)S(1)} %get-tuple-element.659.refs_4_), channel_id=1, source_target_pairs={{0,8},{8,0},{16,24},{24,16},{1,9},{9,1},{17,25},{25,17},{2,10},{10... | collective-permute-start | bytes 3342344 | tf_op jit(solution)/shard_map/ppermute | solution.py:647
  97.0 31.1 %collective-permute-start.3 = (bf16[256,2176]{1,0:T(8,128)(2,1)S(1)}, bf16[256,2176]{1,0:T(8,128)(2,1)}, u32[]{:S(2)}, u32[]{:S(2)}) collective-permute-start(bf16[256,2176]{1,0:T(8,128)(2,1)S(1)} %get-tuple-element.659.refs_4_), channel_id=1, source_target_pairs={{0,16},{8,24},{16,0},{24,8},{1,17},{9,25},{17,1},{25,9},{2,18},{10... | collective-permute-start | bytes 3342344 | tf_op jit(solution)/shard_map/ppermute | solution.py:647
  128.2 30.8 %collective-permute-start.10 = (bf16[256,2176]{1,0:T(8,128)(2,1)S(1)}, bf16[256,2176]{1,0:T(8,128)(2,1)}, u32[]{:S(2)}, u32[]{:S(2)}) collective-permute-start(bf16[256,2176]{1,0:T(8,128)(2,1)S(1)} %get-tuple-element.663.refs_5_), channel_id=1, source_target_pairs={{0,16},{8,24},{16,0},{24,8},{1,17},{9,25},{17,1},{25,9},{2,18},{10... | collective-permute-start | bytes 3342344 | tf_op jit(solution)/shard_map/ppermute | solution.py:647
  129.7 29.3 %collective-permute-start.9 = (bf16[256,2176]{1,0:T(8,128)(2,1)}, bf16[256,2176]{1,0:T(8,128)(2,1)S(1)}, u32[]{:S(2)}, u32[]{:S(2)}) collective-permute-start(bf16[256,2176]{1,0:T(8,128)(2,1)} %collective-permute-done.3.refs_6_), channel_id=1, source_target_pairs={{0,8},{8,0},{16,24},{24,16},{1,9},{9,1},{17,25},{25,17},{2,10},{10... | collective-permute-start | bytes 3342344 | tf_op jit(solution)/shard_map/ppermute | solution.py:647
  130.3 28.7 %collective-permute-start.12 = (bf16[256,2048]{1,0:T(8,128)(2,1)}, bf16[256,2048]{1,0:T(8,128)(2,1)}, u32[]{:S(2)}, u32[]{:S(2)}) collective-permute-start(bf16[256,2048]{1,0:T(8,128)(2,1)} %collective-permute-done.8), channel_id=1, source_target_pairs={{2,0},{3,1},{4,6},{5,7},{10,8},{11,9},{12,14},{13,15},{18,16},{19,... | collective-permute-start | bytes 3145736 | tf_op jit(solution)/shard_map/ppermute | solution.py:647
  131.6 27.4 %collective-permute-start.13 = (bf16[256,2048]{1,0:T(8,128)(2,1)}, bf16[256,2048]{1,0:T(8,128)(2,1)S(1)}, u32[]{:S(2)}, u32[]{:S(2)}) collective-permute-start(bf16[256,2048]{1,0:T(8,128)(2,1)} %collective-permute-done.7.refs_2_), channel_id=1, source_target_pairs={{2,4},{3,5},{4,2},{5,3},{10,12},{11,13},{12,10},{13,11},{18,20},{1... | collective-permute-start | bytes 3145736 | tf_op jit(solution)/shard_map/ppermute | solution.py:647
  159.0 36.8 %collective-permute-start.14 = (bf16[256,2176]{1,0:T(8,128)(2,1)S(1)}, bf16[256,2176]{1,0:T(8,128)(2,1)S(1)}, u32[]{:S(2)}, u32[]{:S(2)}) collective-permute-start(bf16[256,2176]{1,0:T(8,128)(2,1)S(1)} %get-tuple-element.663.refs_5_), channel_id=1, source_target_pairs={{0,8},{8,0},{16,24},{24,16},{1,9},{9,1},{17,25},{25,17},{2,10},{10... | collective-permute-start | bytes 3342344 | tf_op jit(solution)/shard_map/ppermute | solution.py:647
  160.3 35.5 %collective-permute-start.15 = (bf16[256,2176]{1,0:T(8,128)(2,1)}, bf16[256,2176]{1,0:T(8,128)(2,1)S(1)}, u32[]{:S(2)}, u32[]{:S(2)}) collective-permute-start(bf16[256,2176]{1,0:T(8,128)(2,1)} %collective-permute-done.10.refs_7_), channel_id=1, source_target_pairs={{0,8},{8,0},{16,24},{24,16},{1,9},{9,1},{17,25},{25,17},{2,10},{10... | collective-permute-start | bytes 3342344 | tf_op jit(solution)/shard_map/ppermute | solution.py:647
  165.0 30.8 %collective-permute-start.18 = (bf16[256,2048]{1,0:T(8,128)(2,1)S(1)}, bf16[256,2048]{1,0:T(8,128)(2,1)S(1)}, u32[]{:S(2)}, u32[]{:S(2)}) collective-permute-start(bf16[256,2048]{1,0:T(8,128)(2,1)S(1)} %copy-done.39), channel_id=1, source_target_pairs={{2,0},{3,1},{4,6},{5,7},{10,8},{11,9},{12,14},{13,15},{18,16},{19,... | collective-permute-start | bytes 3145736 | tf_op jit(solution)/shard_map/ppermute | solution.py:647
  195.8 29.4 %collective-permute-start.22 = (bf16[512,1024]{1,0:T(8,128)(2,1)}, bf16[512,1024]{1,0:T(8,128)(2,1)}, u32[]{:S(2)}, u32[]{:S(2)}) collective-permute-start(bf16[512,1024]{1,0:T(8,128)(2,1)} %get-tuple-element.568.refs_2_.refs_8_), channel_id=1, source_target_pairs={{0,8},{8,0},{16,24},{24,16},{1,9},{9,1},{17,25},{25,17},{2,10},{10... | collective-permute-start | bytes 3145736 | tf_op jit(solution)/shard_map/ppermute | solution.py:647
  195.9 29.3 %collective-permute-start.23 = (bf16[512,1024]{1,0:T(8,128)(2,1)}, bf16[512,1024]{1,0:T(8,128)(2,1)}, u32[]{:S(2)}, u32[]{:S(2)}) collective-permute-start(bf16[512,1024]{1,0:T(8,128)(2,1)} %get-tuple-element.568.refs_2_.refs_8_), channel_id=1, source_target_pairs={{0,16},{8,24},{16,0},{24,8},{1,17},{9,25},{17,1},{25,9},{2,18},{10... | collective-permute-start | bytes 3145736 | tf_op jit(solution)/shard_map/ppermute | solution.py:647
  226.6 42.3 %collective-permute-start.24 = (bf16[256,2048]{1,0:T(8,128)(2,1)S(1)}, bf16[256,2048]{1,0:T(8,128)(2,1)S(1)}, u32[]{:S(2)}, u32[]{:S(2)}) collective-permute-start(bf16[256,2048]{1,0:T(8,128)(2,1)S(1)} %broadcast_select_fusion.1.refs_4_), channel_id=1, source_target_pairs={{0,1},{1,0},{2,3},{3,2},{4,5},{5,4},{6,7},{7,6},{8,9},{9,8},{10,11... | collective-permute-start | bytes 3145736 | tf_op jit(solution)/shard_map/ppermute | solution.py:647
  228.2 40.6 %collective-permute-start.25 = (bf16[256,2048]{1,0:T(8,128)(2,1)}, bf16[256,2048]{1,0:T(8,128)(2,1)S(1)}, u32[]{:S(2)}, u32[]{:S(2)}) collective-permute-start(bf16[256,2048]{1,0:T(8,128)(2,1)} %collective-permute-done.20), channel_id=1, source_target_pairs={{2,0},{3,1},{4,6},{5,7},{10,8},{11,9},{12,14},{13,15},{18,16},{19,... | collective-permute-start | bytes 3145736 | tf_op jit(solution)/shard_map/ppermute | solution.py:647
  229.8 39.1 %collective-permute-start.26 = (bf16[512,1024]{1,0:T(8,128)(2,1)}, bf16[512,1024]{1,0:T(8,128)(2,1)S(1)}, u32[]{:S(2)}, u32[]{:S(2)}) collective-permute-start(bf16[512,1024]{1,0:T(8,128)(2,1)} %collective-permute-done.23.refs_3_.refs_9_), channel_id=1, source_target_pairs={{0,8},{8,0},{16,24},{24,16},{1,9},{9,1},{17,25},{25,17},{2,10},{10... | collective-permute-start | bytes 3145736 | tf_op jit(solution)/shard_map/ppermute | solution.py:647
  270.5 29.7 %collective-permute-start.27 = (bf16[256,2048]{1,0:T(8,128)(2,1)}, bf16[256,2048]{1,0:T(8,128)(2,1)S(1)}, u32[]{:S(2)}, u32[]{:S(2)}) collective-permute-start(bf16[256,2048]{1,0:T(8,128)(2,1)} %collective-permute-done.refs_1_), channel_id=1, source_target_pairs={{0,2},{1,3},{2,0},{3,1},{4,6},{5,7},{6,4},{7,5},{8,10},{9,11},{10,... | collective-permute-start | bytes 3145736 | tf_op jit(solution)/shard_map/ppermute | solution.py:647
  301.2 30.2 %collective-permute-start.29 = (bf16[256,2048]{1,0:T(8,128)(2,1)}, bf16[256,2048]{1,0:T(8,128)(2,1)S(1)}, u32[]{:S(2)}, u32[]{:S(2)}) collective-permute-start(bf16[256,2048]{1,0:T(8,128)(2,1)} %get-tuple-element.591), channel_id=1, source_target_pairs={{0,2},{1,3},{2,0},{3,1},{4,6},{5,7},{6,4},{7,5},{8,10},{9,11},{10,... | collective-permute-start | bytes 3145736 | tf_op jit(solution)/shard_map/ppermute | solution.py:647
  303.4 28.0 %collective-permute-start.30 = (bf16[256,2048]{1,0:T(8,128)(2,1)}, bf16[256,2048]{1,0:T(8,128)(2,1)}, u32[]{:S(2)}, u32[]{:S(2)}) collective-permute-start(bf16[256,2048]{1,0:T(8,128)(2,1)} %get-tuple-element.595), channel_id=1, source_target_pairs={{0,1},{1,0},{2,3},{3,2},{4,5},{5,4},{6,7},{7,6},{8,9},{9,8},{10,11... | collective-permute-start | bytes 3145736 | tf_op jit(solution)/shard_map/ppermute | solution.py:647
  331.4 29.1 %collective-permute-start.31 = (bf16[1024,1024]{1,0:T(8,128)(2,1)}, bf16[1024,1024]{1,0:T(8,128)(2,1)S(1)}, u32[]{:S(2)}, u32[]{:S(2)}) collective-permute-start(bf16[1024,1024]{1,0:T(8,128)(2,1)} %fusion.29), channel_id=1, source_target_pairs={{0,8},{8,0},{16,24},{24,16},{1,9},{9,1},{17,25},{25,17},{2,10},{10... | collective-permute-start | bytes 6291464 | tf_op jit(solution)/shard_map/ppermute | solution.py:647
  362.2 27.7 %collective-permute-start.36 = (bf16[256,2048]{1,0:T(8,128)(2,1)S(1)}, bf16[256,2048]{1,0:T(8,128)(2,1)S(1)}, u32[]{:S(2)}, u32[]{:S(2)}) collective-permute-start(bf16[256,2048]{1,0:T(8,128)(2,1)S(1)} %add_convert_fusion.11), channel_id=1, source_target_pairs={{2,4},{3,5},{4,2},{5,3},{10,12},{11,13},{12,10},{13,11},{18,20},{1... | collective-permute-start | bytes 3145736 | tf_op jit(solution)/shard_map/ppermute | solution.py:647
  393.6 34.5 %collective-permute-start.40 = (bf16[256,2048]{1,0:T(8,128)(2,1)}, bf16[256,2048]{1,0:T(8,128)(2,1)}, u32[]{:S(2)}, u32[]{:S(2)}) collective-permute-start(bf16[256,2048]{1,0:T(8,128)(2,1)} %add_convert_fusion.9), channel_id=1, source_target_pairs={{2,4},{3,5},{4,2},{5,3},{10,12},{11,13},{12,10},{13,11},{18,20},{1... | collective-permute-start | bytes 3145736 | tf_op jit(solution)/shard_map/ppermute | solution.py:647
  397.0 31.1 %collective-permute-start.39 = (bf16[256,2048]{1,0:T(8,128)(2,1)}, bf16[256,2048]{1,0:T(8,128)(2,1)}, u32[]{:S(2)}, u32[]{:S(2)}) collective-permute-start(bf16[256,2048]{1,0:T(8,128)(2,1)} %add_convert_fusion.10), channel_id=1, source_target_pairs={{0,2},{1,3},{2,0},{3,1},{4,6},{5,7},{6,4},{7,5},{8,10},{9,11},{10,... | collective-permute-start | bytes 3145736 | tf_op jit(solution)/shard_map/ppermute | solution.py:647
  398.5 29.6 %collective-permute-start.37 = (bf16[512,1024]{1,0:T(8,128)(2,1)}, bf16[512,1024]{1,0:T(8,128)(2,1)}, u32[]{:S(2)}, u32[]{:S(2)}) collective-permute-start(bf16[512,1024]{1,0:T(8,128)(2,1)} %add_convert_fusion.14), channel_id=1, source_target_pairs={{0,16},{8,24},{16,0},{24,8},{1,17},{9,25},{17,1},{25,9},{2,18},{10... | collective-permute-start | bytes 3145736 | tf_op jit(solution)/shard_map/ppermute | solution.py:647
  399.8 28.4 %collective-permute-start.38 = (bf16[256,2048]{1,0:T(8,128)(2,1)}, bf16[256,2048]{1,0:T(8,128)(2,1)}, u32[]{:S(2)}, u32[]{:S(2)}) collective-permute-start(bf16[256,2048]{1,0:T(8,128)(2,1)} %get-tuple-element.675), channel_id=1, source_target_pairs={{0,1},{1,0},{2,3},{3,2},{4,5},{5,4},{6,7},{7,6},{8,9},{9,8},{10,11... | collective-permute-start | bytes 3145736 | tf_op jit(solution)/shard_map/ppermute | solution.py:647
  459.9 34.1 %collective-permute-start.44 = (bf16[512,1408]{1,0:T(8,128)(2,1)S(1)}, bf16[512,1408]{1,0:T(8,128)(2,1)S(1)}, u32[]{:S(2)}, u32[]{:S(2)}) collective-permute-start(bf16[512,1408]{1,0:T(8,128)(2,1)S(1)} %fusion.10), channel_id=1, source_target_pairs={{0,16},{8,24},{16,0},{24,8},{1,17},{9,25},{17,1},{25,9},{2,18},{10... | collective-permute-start | bytes 4325384 | tf_op jit(solution)/shard_map/ppermute | solution.py:647
  523.4 63.0 %collective-permute-start.52 = (bf16[256,2048]{1,0:T(8,128)(2,1)}, bf16[256,2048]{1,0:T(8,128)(2,1)}, u32[]{:S(2)}, u32[]{:S(2)}) collective-permute-start(bf16[256,2048]{1,0:T(8,128)(2,1)} %add_convert_fusion.2), channel_id=1, source_target_pairs={{0,2},{1,3},{2,0},{3,1},{4,6},{5,7},{6,4},{7,5},{8,10},{9,11},{10,... | collective-permute-start | bytes 3145736 | tf_op jit(solution)/shard_map/ppermute | solution.py:647
  527.0 32.8 %collective-permute-start.53 = (bf16[64,3200]{1,0:T(8,128)(2,1)}, bf16[64,3200]{1,0:T(8,128)(2,1)S(1)}, u32[]{:S(2)}, u32[]{:S(2)}) collective-permute-start(bf16[64,3200]{1,0:T(8,128)(2,1)} %get-tuple-element.772), channel_id=1, source_target_pairs={{0,4},{1,5},{2,6},{3,7},{4,0},{5,1},{6,2},{7,3},{8,12},{9,13},{10,... | collective-permute-start | bytes 1228808 | tf_op jit(solution)/shard_map/ppermute | solution.py:647
  527.8 40.7 %collective-permute-start.54 = (bf16[64,3200]{1,0:T(8,128)(2,1)}, bf16[64,3200]{1,0:T(8,128)(2,1)S(1)}, u32[]{:S(2)}, u32[]{:S(2)}) collective-permute-start(bf16[64,3200]{1,0:T(8,128)(2,1)} %get-tuple-element.773), channel_id=1, source_target_pairs={{0,5},{1,4},{2,7},{3,6},{4,1},{5,0},{6,3},{7,2},{8,13},{9,12},{10,... | collective-permute-start | bytes 1228808 | tf_op jit(solution)/shard_map/ppermute | solution.py:647
  530.5 49.4 %collective-permute-start.55 = (bf16[64,3200]{1,0:T(8,128)(2,1)}, bf16[64,3200]{1,0:T(8,128)(2,1)S(1)}, u32[]{:S(2)}, u32[]{:S(2)}) collective-permute-start(bf16[64,3200]{1,0:T(8,128)(2,1)} %get-tuple-element.774), channel_id=1, source_target_pairs={{0,6},{1,7},{2,4},{3,5},{4,2},{5,3},{6,0},{7,1},{8,14},{9,15},{10,... | collective-permute-start | bytes 1228808 | tf_op jit(solution)/shard_map/ppermute | solution.py:647
  532.9 53.5 %collective-permute-start.56 = (bf16[64,3200]{1,0:T(8,128)(2,1)}, bf16[64,3200]{1,0:T(8,128)(2,1)S(1)}, u32[]{:S(2)}, u32[]{:S(2)}) collective-permute-start(bf16[64,3200]{1,0:T(8,128)(2,1)} %get-tuple-element.775), channel_id=1, source_target_pairs={{0,7},{1,6},{2,5},{3,4},{4,3},{5,2},{6,1},{7,0},{8,15},{9,14},{10,... | collective-permute-start | bytes 1228808 | tf_op jit(solution)/shard_map/ppermute | solution.py:647
  (96 other events, 1746.2 us)

commit v4 on v3

--- a/solution.py
+++ b/solution.py
@@ -260,21 +260,17 @@
         outs[-1][source] = in_ref[source, :, plan.first + plan.used :]
 
 
-def pack_rows_kernel(own, n_sources, me_ref, *refs):
-    sources, outs = refs[:n_sources], refs[n_sources:]
-    for step, out in enumerate(outs):
-        row = pl.multiple_of((me_ref[0] ^ step) * own, own)
+def pack_rows_kernel(own, *refs):
+    sources, out = refs[:-1], refs[-1]
+    for dest in range(out.shape[0]):
         lane = 0
         for source in sources:
             lanes = source.shape[1]
-            out[:, lane : lane + lanes] = source[pl.ds(row, own), :]
+            out[dest, :, lane : lane + lanes] = source[dest * own : (dest + 1) * own, :]
             lane += lanes
 
 
-def unpack_rows_kernel(n, own, layout, me_ref, *refs):
-    pieces, outs, held = refs[:n], refs[n:-1], refs[-1]
-    for step, piece in enumerate(pieces):
-        held[me_ref[0] ^ step] = piece[...]
+def unpack_rows_kernel(n, layout, held, *outs):
     for source in range(n):
         for out, start, stride, lane, span in layout:
             begin = start + source * stride
@@ -282,17 +278,15 @@
             outs[out][:, begin : begin + span] = block
 
 
-def in_vmem(kernel, name, out_shape, scratch=(), scalars=0):
+def in_vmem(kernel, name, out_shape):
     def call(*operands):
-        places = [pltpu.SMEM] * scalars + [pltpu.VMEM] * (len(operands) - scalars)
-        outs = jax.tree.map(lambda _: pl.BlockSpec(memory_space=pltpu.VMEM), out_shape)
+        place = pl.BlockSpec(memory_space=pltpu.VMEM)
         moved = sum(o.size * o.dtype.itemsize for o in operands)
         return pl.pallas_call(
             kernel,
-            in_specs=[pl.BlockSpec(memory_space=place) for place in places],
-            out_specs=outs,
+            in_specs=[place] * len(operands),
+            out_specs=jax.tree.map(lambda _: place, out_shape),
             out_shape=out_shape,
-            scratch_shapes=list(scratch),
             compiler_params=pltpu.CompilerParams(vmem_limit_bytes=48 * 1024 * 1024),
             cost_estimate=pl.CostEstimate(flops=0, bytes_accessed=3 * moved, transcendentals=0),
             name=name,
@@ -310,7 +304,7 @@
 def unpack_columns(plan, packed):
     n, own = plan.n, plan.own
     outs_of = [(half * n // 2, n // 2, 0, plan.first) for half in range(2)]
-    outs_of.append((0, n, plan.first, plan.second))
+    outs_of += [(0, n, 0, plan.first), (0, n, plan.first, plan.second)]
     shapes = [jax.ShapeDtypeStruct((c * own, lanes), BF) for _, c, _, lanes in outs_of]
     shapes.append(jax.ShapeDtypeStruct((n, own, own), BF))
     kernel = functools.partial(unpack_kernel, plan, outs_of)
@@ -318,35 +312,31 @@
     return parts, scales[:, :2]
 
 
-def pack_rows(own, n, me, gradients):
+def pack_rows(own, n, gradients):
     lanes = sum(g.shape[1] for g in gradients)
-    shapes = [jax.ShapeDtypeStruct((own, lanes), BF)] * n
-    kernel = functools.partial(pack_rows_kernel, own, len(gradients))
-    return in_vmem(kernel, "pack_rows", shapes, scalars=1)(me.reshape(1), *gradients)
-
-
-def unpack_rows(plan, me, pieces):
-    layout = list(plan.segments())
+    shape = jax.ShapeDtypeStruct((n, own, lanes), BF)
+    return in_vmem(functools.partial(pack_rows_kernel, own), "pack_rows", shape)(*gradients)
+
+
+def unpack_rows(plan, packed):
     widths = [3 * plan.width, plan.width, plan.units, plan.units, plan.units]
     shapes = [jax.ShapeDtypeStruct((plan.own, plan.n * w), F32) for w in widths]
-    kernel = functools.partial(unpack_rows_kernel, plan.n, plan.own, layout)
-    held = pltpu.VMEM((plan.n, plan.own, pieces[0].shape[1]), BF)
-    return in_vmem(kernel, "unpack_rows", shapes, scratch=[held], scalars=1)(
-        me.reshape(1), *pieces
-    )
+    kernel = functools.partial(unpack_rows_kernel, plan.n, list(plan.segments()))
+    return in_vmem(kernel, "unpack_rows", shapes)(packed)
 
 
 def fetch_pieces(pieces, held, sems):
-    rows = pieces[0].shape[0]
-    return [
-        pltpu.make_async_copy(piece, held.at[pl.ds(i * rows, rows), :], sems.at[i])
-        for i, piece in enumerate(pieces)
-    ]
-
-
-def stream_kernel(n, n_pieces, n_extra, n_into, finish, *refs):
+    copies, row = [], 0
+    for i, piece in enumerate(pieces):
+        there = held.at[pl.ds(row, piece.shape[0]), :]
+        copies.append(pltpu.make_async_copy(piece, there, sems.at[i]))
+        row += piece.shape[0]
+    return copies
+
+
+def stream_kernel(n, n_pieces, n_extra, finish, *refs):
     blocks, refs = refs[:n], refs[n:]
-    pieces, refs = refs[:n_pieces], refs[n_pieces + n_into :]
+    pieces, refs = refs[:n_pieces], refs[n_pieces:]
     extra, outs, (held, rows_ref, rows_sem, weight_sem) = refs[:n_extra], refs[n_extra:-4], refs[-4:]
     size = blocks[0].shape[0]
     step = pl.program_id(0)
@@ -384,30 +374,30 @@
         for piece in weight:
             piece.wait()
 
-    rows = rows_ref[buffer]
-    outs[0][...] = rows
-    finish(rows, held, extra, outs[1:])
-
-
-def stream(name, blocks, pieces, extra, finish, outs, all_blocks, into=()):
+    finish(rows_ref[buffer], held, extra, outs)
+
+
+def stream(name, blocks, pieces, extra, finish, outs):
     size, features = blocks[0].shape
     n = len(blocks)
-    first = (all_blocks - n) // 2 if into else 0
     anywhere = pl.BlockSpec(memory_space=pl.ANY)
 
     def rows(width):
-        return pl.BlockSpec((2 * size, width), lambda i: (first + i, 0))
+        return pl.BlockSpec((2 * size, width), lambda i: (i, 0))
+
+    def beside(array):
+        if array.shape[0] == n * size:
+            return rows(array.shape[1])
+        return pl.BlockSpec(array.shape, lambda i: (0, 0))
 
     outs = [(features, BF), *outs]
     width = pieces[0].shape[1]
-    begin = n + len(pieces)
     return pl.pallas_call(
-        functools.partial(stream_kernel, n, len(pieces), len(extra), len(into), finish),
+        functools.partial(stream_kernel, n, len(pieces), len(extra), finish),
         grid=(n // 2,),
-        in_specs=[anywhere] * (begin + len(into)) + [rows(e.shape[1]) for e in extra],
+        in_specs=[anywhere] * (n + len(pieces)) + [beside(e) for e in extra],
         out_specs=[rows(w) for w, _ in outs],
-        out_shape=[jax.ShapeDtypeStruct((all_blocks * size, w), dtype) for w, dtype in outs],
-        input_output_aliases={begin + i: i for i in range(len(into))},
+        out_shape=[jax.ShapeDtypeStruct((n * size, w), dtype) for w, dtype in outs],
         scratch_shapes=[
             pltpu.VMEM((features, width), BF),
             pltpu.VMEM((2, 2 * size, features), BF),
@@ -421,7 +411,7 @@
             transcendentals=0,
         ),
         name=name,
-    )(*blocks, *pieces, *into, *extra)
+    )(*blocks, *pieces, *extra)
 
 
 def swiglu(plan, both):
@@ -437,12 +427,14 @@
 
 
 def project_finish(plan, rows, held, extra, outs):
-    joined, factor_ref, wide = outs
+    (scales,), (normed, joined, factor_ref, wide) = extra, outs
+    rows = (rows.astype(F32) * scales[0:1, :] + scales[1:2, :]).astype(BF)
+    normed[...] = rows
     joined[...] = dot(rows, held[:, : plan.joined])
     hidden, factors = swiglu(plan, dot(rows, held[:, plan.joined :]))
     lane = 0
     for factor in factors:
-        factor_ref[:, lane : lane + factor.shape[1]] = factor
+        factor_ref[:, lane : lane + factor.shape[1]] = factor.astype(factor_ref.dtype)
         lane += factor.shape[1]
     wide[:, : plan.width] = jnp.zeros((rows.shape[0], plan.width), BF)
     wide[:, plan.width : plan.width + plan.body] = hidden[0]
@@ -451,7 +443,8 @@
 
 
 def return_finish(plan, rows, held, extra, outs):
-    (factor_ref,), (d_attn, d_both) = extra, outs
+    (factor_ref,), (cot, d_attn, d_both) = extra, outs
+    cot[...] = rows
     total = dot(rows, held[...])
     d_attn[...] = total[:, : plan.width].astype(BF)
     begin, body, tail = plan.width, plan.body, plan.tail
@@ -472,12 +465,13 @@
     for piece in weight:
         piece.start()
     size = outs[0].shape[0]
-    each = n_pieces // 4
-    rows = each * pieces[0].shape[0]
+    rows = held.shape[0] // 4
+    begins = [sum(p.shape[0] for p in pieces[:i]) for i in range(n_pieces)]
     for part in range(4):
         here = slice(part * rows, (part + 1) * rows)
-        for piece in weight[part * each : (part + 1) * each]:
-            piece.wait()
+        for begin, piece in zip(begins, weight):
+            if begin // rows == part:
+                piece.wait()
         for place in range(places):
             total, lane = 0.0, 0
             for left in lefts[place * count : (place + 1) * count]:
@@ -490,7 +484,7 @@
 
 def spread(name, lefts, pieces, places, size):
     anywhere = pl.BlockSpec(memory_space=pl.ANY)
-    features = len(pieces) * pieces[0].shape[0]
+    features = sum(piece.shape[0] for piece in pieces)
     width = pieces[0].shape[1]
     tokens = 2 * size * len(places)
 
@@ -543,20 +537,22 @@
         return center * inverse, inverse
 
     def norm(self, standard, scales):
-        gain = scales[:, 0].astype(F32).reshape(1, self.features)
-        bias = scales[:, 1].astype(F32).reshape(1, self.features)
+        gain, bias = self.scales(scales)
         return (standard * gain + bias).astype(BF), gain
 
-    def attend(self, joined, wide):
+    def scales(self, scales):
+        return [scales[:, i].astype(F32).reshape(1, self.features) for i in range(2)]
+
+    def attend(self, joined, wide, tables):
         lanes = wide.shape[1]
         shape = (*self.blocks, lanes)
         joined = joined.reshape(*self.blocks, 3 * self.width)
         rotated, wide, lse = self.calls(lanes)[0](
-            self.lengths, self.slots, joined, *self.tables, wide.reshape(shape)
+            self.lengths, self.slots, joined, *tables, wide.reshape(shape)
         )
         return rotated, wide.reshape(-1, lanes), lse
 
-    def attend_back(self, rotated, wide, d_attn, lse):
+    def attend_back(self, rotated, wide, d_attn, lse, tables):
         lanes = wide.shape[1]
         return self.calls(lanes)[1](
             self.lengths,
@@ -565,7 +561,7 @@
             wide.reshape(*self.blocks, lanes),
             d_attn.reshape(*self.blocks, self.width),
             lse,
-            *self.tables,
+            *tables,
         ).reshape(-1, 3 * self.width)
 
     def finish_output(self, branches):
@@ -587,7 +583,6 @@
 def on_any_mesh(layer, weights, scales):
     plan = layer.plan
     n, own, width = plan.n, plan.own, plan.width
-    me = jnp.zeros((), jnp.int32)
 
     def swap(pieces):
         return lax.all_to_all(pieces, "ctx", split_axis=0, concat_axis=0, tiled=True)
@@ -599,27 +594,26 @@
         return lax.psum_scatter(v, axis, scatter_dimension=0, tiled=True)
 
     parts, scales = unpack_columns(plan, swap(pack_columns(plan, weights, scales)))
-    w_first = gather(jnp.concatenate(parts[:2], axis=0), "dp")
-    w_second = gather(parts[2], "dp")[:, : plan.used]
+    w_first, w_second = gather(parts[2], "dp"), gather(parts[3], "dp")[:, : plan.used]
     standard, inverse = layer.standardize()
     normed, gain = layer.norm(standard, gather(scales, "dp"))
     normed, cot = gather(normed, "ctx"), gather(layer.cot, "ctx")
     total = dot(normed, w_first)
     hidden, factors = swiglu(plan, total[:, plan.joined :])
     empty = jnp.zeros((normed.shape[0], width), BF)
-    rotated, attn, lse = layer.attend(total[:, : plan.joined], empty)
+    rotated, attn, lse = layer.attend(total[:, : plan.joined], empty, layer.tables)
     wide = jnp.concatenate([attn, *hidden], axis=1)
     branches = scatter(dot_last(wide, w_second).astype(BF), "ctx")
     total = dot(cot, w_second)
     body = total[:, width : width + plan.body]
     tail = total[:, width + plan.body :]
     d_both = jnp.concatenate([body, body, tail, tail], axis=1) * jnp.concatenate(factors, axis=1)
-    d_joined = layer.attend_back(rotated, attn, total[:, :width].astype(BF), lse)
+    d_attn = total[:, :width].astype(BF)
+    d_joined = layer.attend_back(rotated, attn, d_attn, lse, layer.tables)
     d_first = jnp.concatenate([d_joined, d_both.astype(BF)], axis=1)
     d_normed = scatter(dot_last(d_first, w_first).astype(BF), "ctx")
     sums = [scatter(dot_first(*v).astype(BF), "dp") for v in ((normed, d_first), (cot, wide))]
-    pieces = list(swap(jnp.stack(pack_rows(own, n, me, sums))))
-    grads = unpack_rows(plan, me, pieces)
+    grads = unpack_rows(plan, swap(pack_rows(own, n, sums)))
     input_grad, norm_sums = layer.norm_back(d_normed, standard, inverse, gain)
     return layer.finish_output(branches), input_grad, scatter(norm_sums, ("dp", "ctx")), grads
 
@@ -679,21 +673,17 @@
         packed = pack_columns(plan, weights, scales)
         packed = lax.all_to_all(packed, "ctx", split_axis=0, concat_axis=0, tiled=True)
         parts, held = unpack_columns(plan, packed)
-        return {"a0": parts[0], "b0": parts[1], "w0": parts[2], "scales": held}
-
-    def standardize(s):
-        standard, inverse = layer.standardize()
-        return {"standard": standard, "inverse": inverse}
-
-    def normalize(s):
+        return {"scales": held, **dict(zip(("a0", "b0", "ab0", "w0"), parts))}
+
+    def all_scales(s):
         held = s["scales"]
         for bit in (1, 2):
             mine = dp // bit % 2
             got = lax.ppermute(held, "dp", swaps(bit, 4))
             first, second = jnp.where(mine == 0, held, got), jnp.where(mine == 0, got, held)
             held = jnp.concatenate([first, second], axis=0)
-        normed, gain = layer.norm(s["standard"], held)
-        return {"n0": reorder(normed), "gain": gain}
+        gain, bias = layer.scales(held)
+        return {"gain": gain, "both": reorder(jnp.concatenate([gain, bias], axis=0))}
 
     def select(name):
         return lambda s: {name: jnp.where(inner, s[name + "i"], s[name + "o"])}
@@ -701,44 +691,45 @@
     def plus(name, *parts):
         return lambda s: {name: sum(s[part].astype(F32) for part in parts).astype(BF)}
 
-    def pieces(s, *names):
-        return [s[name + i] for i in "0213" for name in names]
+    def pieces(s, name):
+        names = "a0 b0 a2 b2 ab1 a3 b3" if name == "ab" else "w0 w2 w1 w3"
+        return [s[key] for key in names.split()]
 
     def slots(s, letter):
-        return [s.get(letter + i) for i in ("0", "0x", "1", "1x", "2", "2x", "3", "3x")]
-
-    def project(half):
-        names = ("n", "joined", "factors", "wide")
-
-        def work(s):
-            outs = [(plan.joined, F32), (2 * plan.units, F32), (plan.second, BF)]
-            finish = functools.partial(project_finish, plan)
-            blocks = slots(s, "n")[half * n // 2 : (half + 1) * n // 2]
-            into = [s[name] for name in names] if half else []
-            made = stream("project", blocks, pieces(s, "a", "b"), [], finish, outs, n, into)
-            return dict(zip(names, made))
-
-        return work
+        return [s[letter + i] for i in ("0", "0x", "1", "1x", "2", "2x", "3", "3x")]
+
+    def project(s):
+        outs = [(plan.joined, F32), (2 * plan.units, BF), (plan.second, BF)]
+        finish = functools.partial(project_finish, plan)
+        held = pieces(s, "ab")
+        made = stream("project", slots(s, "n"), held, [s["both"]], finish, outs)
+        return dict(zip(("n", "joined", "factors", "wide"), made))
+
+    def tables(s):
+        return {"tables": layer.tables}
 
     def attend(s):
-        return dict(zip(("rotated", "wide", "lse"), layer.attend(s["joined"], s["wide"])))
+        made = layer.attend(s["joined"], s["wide"], s["tables"])
+        return dict(zip(("rotated", "wide", "lse"), made))
 
     def bring_back(s):
         outs = [(plan.width, BF), (2 * plan.units, BF)]
         finish = functools.partial(return_finish, plan)
         made = stream(
-            "bring_back", slots(s, "c"), pieces(s, "w"), [s["factors"]], finish, outs, n
+            "bring_back", slots(s, "c"), pieces(s, "w"), [s["factors"]], finish, outs
         )
         return dict(zip(("c", "d_attn", "d_both"), made))
 
     def attend_back(s):
-        d_joined = layer.attend_back(s["rotated"], s["wide"], s["d_attn"], s["lse"])
+        d_joined = layer.attend_back(
+            s["rotated"], s["wide"], s["d_attn"], s["lse"], s["tables"]
+        )
         return {"d_joined": d_joined}
 
     def scattered(name, letter, lefts, weight, places):
         def work(s):
             size = s["c0"].shape[0]
-            made = spread(name, [s[v] for v in lefts], pieces(s, *weight), places, size)
+            made = spread(name, [s[v] for v in lefts], pieces(s, weight), places, size)
             keys = [f"{letter}{place}{kind}" for place in places for kind in "ka"]
             return dict(zip(keys, made))
 
@@ -782,20 +773,13 @@
     def send_b(name):
         return to(name + "Br", name + "B", across)
 
-    def deal(s):
-        dealt = pack_rows(own, n, ctx, [s[name + "C"] for name in "JGW"])
-        return {f"q{step}": piece for step, piece in enumerate(dealt)}
-
-    def swap(step):
-        return to(f"q{step}r", f"q{step}", ("ctx", swaps(step, n)))
-
-    def undeal(s):
-        held = [s["q0"]] + [s[f"q{step}r"] for step in range(1, n)]
-        grads = unpack_rows(plan, ctx, held)
-        return {f"grad{weight}": grad for weight, grad in enumerate(grads)}
+    def swap_rows(s):
+        held = pack_rows(own, n, [s[name + "C"] for name in "JGW"])
+        held = lax.all_to_all(held, "ctx", split_axis=0, concat_axis=0, tiled=True)
+        return {f"grad{weight}": grad for weight, grad in enumerate(unpack_rows(plan, held))}
 
     def norm_back(s):
-        input_grad, sums = layer.norm_back(unorder(s["d"]), s["standard"], s["inverse"], s["gain"])
+        input_grad, sums = layer.norm_back(unorder(s["d"]), standard, inverse, s["gain"])
         for axis, bit, size in [("dp", b, 4) for b in (2, 1)] + [("ctx", b, n) for b in (4, 2, 1)]:
             mine = lax.axis_index(axis) // bit % 2
             halves = sums.reshape(2, -1, sums.shape[1])
@@ -814,22 +798,24 @@
     def far(name):
         return to(name + "3", name + "2", core)
 
-    st = State(c0=reorder(layer.cot))
+    standard, inverse = layer.standardize()
+    st = State(c0=reorder(layer.cot), n0=reorder(standard.astype(BF)))
     tick = st.tick
-    tick((), [to("c0x", "c0", side), to("c1", "c0", pair)], [weights_in, standardize])
-    tick(
-        [normalize],
-        [to("n0x", "n0", side), to("n1", "n0", pair), to("n2i", "n0", middle), y("a"), near("a")],
-    )
     tick(
         (),
         [
-            to("n1x", "n1", side),
-            to("n3i", "n1", middle),
-            to("n2o", "n2i", outward),
-            y("b"),
-            far("a"),
+            to("n0x", "n0", side),
+            to("n1", "n0", pair),
+            to("n2i", "n0", middle),
+            to("c0x", "c0", side),
+            to("c1", "c0", pair),
         ],
+        [weights_in],
+    )
+    tick(
+        (),
+        [to("n1x", "n1", side), to("n3i", "n1", middle), to("n2o", "n2i", outward), y("a")],
+        [all_scales, tables],
     )
     tick(
         [select("n2")],
@@ -837,51 +823,54 @@
             to("n2x", "n2", side),
             to("n3o", "n3i", outward),
             to("c2i", "c0", middle),
-            near("b"),
-            far("b"),
+            y("b"),
+            far("a"),
         ],
     )
     tick(
         [select("n3")],
         [
             to("n3x", "n3", side),
+            to("c2o", "c2i", outward),
             to("c3i", "c1", middle),
-            to("c2o", "c2i", outward),
-            y("w"),
-            near("w"),
+            far("b"),
+            near("ab"),
         ],
-        [project(0)],
     )
     tick(
         [select("c2")],
-        [to("c2x", "c2", side), to("c3o", "c3i", outward), far("w")],
-        [project(1), attend],
+        [to("c2x", "c2", side), to("c3o", "c3i", outward), y("w"), near("w")],
+        [project],
     )
     tick(
         [select("c3")],
-        [to("c3x", "c3", side), to("c1x", "c0x", pair)],
-        [output_part(1, 3), output_part(0, 2)],
-    )
-    tick((), [to("o3x", "o3a", side), to("o1p", "o1a", pair)], [bring_back, grad_a("W")])
+        [to("c3x", "c3", side), to("c1x", "c0x", pair), far("w")],
+        [attend, output_part(1, 3)],
+    )
+    tick(
+        (),
+        [to("o3x", "o3a", side), to("o1p", "o1a", pair)],
+        [output_part(0, 2), bring_back, grad_a("G")],
+    )
     tick(
         [plus("o3", "o3k", "o3x")],
-        [to("o2x", "o2a", side), to("o3i", "o3", inward), send_a("W")],
+        [to("o2x", "o2a", side), to("o3i", "o3", inward), send_a("G")],
         [attend_back],
     )
     tick(
         [plus("o2", "o2k", "o2x"), plus("o3", "o3", "o3i"), plus("o0a", "o0a", "o1p")],
         [to("o0x", "o0a", side), to("o2i", "o2", inward), to("o3m", "o3", middle)],
-        [normed_part(1, 3), grad_b("W")],
+        [normed_part(1, 3), grad_b("G")],
     )
     tick(
         [plus("o2", "o2", "o2i"), plus("o1", "o1k", "o3m")],
-        [to("d3x", "d3a", side), to("o2m", "o2", middle), to("o1r", "o1", pair), send_b("W")],
-        [normed_part(0, 2), grad_a("G")],
+        [to("d3x", "d3a", side), to("o2m", "o2", middle), to("o1r", "o1", pair), send_b("G")],
+        [normed_part(0, 2), grad_a("W")],
     )
     tick(
         [plus("d3", "d3k", "d3x")],
-        [to("d2x", "d2a", side), to("d3i", "d3", inward), send_a("G")],
-        [grad_b("G"), grad_a("J"), plus("o", "o0k", "o0x", "o2m", "o1r")],
+        [to("d2x", "d2a", side), to("d3i", "d3", inward), send_a("W")],
+        [grad_b("W"), grad_a("J"), plus("o", "o0k", "o0x", "o2m", "o1r")],
     )
     tick(
         [plus("d2", "d2k", "d2x"), plus("d3", "d3", "d3i")],
@@ -889,22 +878,17 @@
             to("d1x", "d1a", side),
             to("d2i", "d2", inward),
             to("d3m", "d3", middle),
-            send_b("G"),
+            send_b("W"),
             send_a("J"),
         ],
-        [grad_c("W"), grad_b("J")],
-    )
-    tick(
-        [plus("d2", "d2", "d2i")],
-        [to("d0x", "d0a", side), to("d2m", "d2", middle), send_b("J")],
-        [grad_c("G"), grad_c("J"), deal],
-    )
-    tick(
-        [plus("d1", "d1k", "d1x", "d3m")],
-        [to("d1r", "d1", pair), *map(swap, (4, 5, 6, 7))],
-    )
-    tick([plus("d", "d0k", "d0x", "d2m", "d1r")], map(swap, (1, 2, 3)), [norm_back])
-    tick((), (), [undeal])
+        [grad_c("G"), grad_b("J")],
+    )
+    tick(
+        [plus("d2", "d2", "d2i"), plus("d1", "d1k", "d1x", "d3m")],
+        [to("d0x", "d0a", side), to("d2m", "d2", middle), to("d1r", "d1", pair), send_b("J")],
+        [grad_c("W"), grad_c("J")],
+    )
+    tick([plus("d", "d0k", "d0x", "d2m", "d1r")], (), [swap_rows, norm_back])
     grads = [st[f"grad{weight}"] for weight in range(5)]
     return layer.finish_output(unorder(st["o"])), st["input_grad"], st["norm_sums"], grads
 

time: 652 us -> 608 us (0.933)
  starting transfers between devices: 106 us -> 84.5 us
  other arithmetic: 41.5 us -> 30.3 us
  Pallas kernels: 156 us -> 146 us
    ppermute x58 -> x50, waiting for transfers between devices: 195 us -> 125 us  [tick(): view[name] = lax.ppermute(self.held[source], axis, pairs)]
    ppermute x5, waiting for transfers between devices: 7.82 us -> 57.2 us  [norm_back(): sums = keep + lax.ppermute(give, axis, swaps(bit, size))]
    ppermute x2, waiting for transfers between devices: 2.78 us -> 21 us  [all_scales(): got = lax.ppermute(held, 'dp', swaps(bit, 4))]
    ppermute x5, starting transfers between devices: 18.7 us -> 5.95 us  [norm_back(): sums = keep + lax.ppermute(give, axis, swaps(bit, size))]
    ppermute x58 -> x50, starting transfers between devices: 78.6 us -> 66.6 us  [tick(): view[name] = lax.ppermute(self.held[source], axis, pairs)]
    convert_element_type x13, other arithmetic: 17.1 us -> 9.14 us  [plus(): sum((s[part].astype(F32) for part in parts)).astype(BF)]
    pallas_call x3 -> x2, Pallas kernels: 52 us -> 45.1 us  [stream(): pl.pallas_call(functools.partial(stream_kernel, n, len(pieces), len(extra...]
    unnamed x124 -> x106, local copies, waits for them, and re-layouts: 14.6 us -> 13.9 us
  transfers between devices with their start and end apart: 66 -> 59, of which waited for: 33 -> 21; matrix products, arithmetic and copies ran while one was open for 12% -> 14% of each run, Pallas kernels for 23% -> 23%
where the time goes in v4:
time: 608 us; the launch traced here: 600 us
  waiting for transfers between devices  267 us (44%)
  Pallas kernels  146 us (24%)
  starting transfers between devices  84.5 us (14%)
  matrix products  53.1 us (9%)
  other arithmetic  30.3 us (5%)
  local copies, waits for them, and re-layouts  16.5 us (3%)
    ppermute x50, waiting for transfers between devices, tick(): view[name] = lax.ppermute(self.held[source], axis, pairs)  125 us
    ppermute x50, starting transfers between devices, tick(): view[name] = lax.ppermute(self.held[source], axis, pairs)  66.6 us
    all_to_all x1, waiting for transfers between devices, weights_in(): lax.all_to_all(packed, 'ctx', split_axis=0, concat_axis=0, tiled=True)  63.1 us
    ppermute x5, waiting for transfers between devices, norm_back(): sums = keep + lax.ppermute(give, axis, swaps(bit, size))  57.2 us
    dot_general x9, matrix products, dot_first(): return lax.dot_general(left, right, FIRST, preferred_element_type=F32)  53.1 us
    pallas_call x4, Pallas kernels, spread(): pl.pallas_call(functools.partial(spread_kernel, len(lefts), len(pieces),...  49.9 us
    pallas_call x2, Pallas kernels, stream(): pl.pallas_call(functools.partial(stream_kernel, n, len(pieces), len(extra...  45.1 us
    pallas_call x1, Pallas kernels, attend_back(): self.calls(lanes)[1]  21.1 us
  transfers between devices with their start and end apart: 59, of which 21 were waited for; matrix products, arithmetic and copies ran while one was open for 14% of the time, Pallas kernels for 23%

profile of v4, /device:TPU:0, one launch (start us, length us, event | category | flops | bytes accessed | tf_op | source)
XLA Modules:
  0.0 599.7 jit_solution(16956877750079333045)
XLA Ops:
  9.2 7.4 %all-to-all-start = ((bf16[8,64,3200]{2,1,0:T(8,128)(2,1)}), bf16[8,64,3200]{2,1,0:T(8,128)(2,1)}, u32[]{:S(2)}, u32[]{:S(2)}) async-start(bf16[8,64,3200]{2,1,0:T(8,128)(2,1)} %pack_columns.1), calls=%async_computation | async-start | bytes 6553600 | tf_op jit(solution)/shard_map/all_to_all | solution.py:674
  28.5 63.1 %all-to-all-done.in_ref = bf16[8,64,3200]{2,1,0:T(8,128)(2,1)} async-done(((bf16[8,64,3200]{2,1,0:T(8,128)(2,1)}), bf16[8,64,3200]{2,1,0:T(8,128)(2,1)}, u32[]{:S(2)}, u32[]{:S(2)}) %all-to-all-start) | async-done | bytes 3276832 | tf_op jit(solution)/shard_map/all_to_all | solution.py:674
  98.4 18.3 %collective-permute-done.3.refs_2_ = bf16[256,2048]{1,0:T(8,128)(2,1)} collective-permute-done((bf16[256,2048]{1,0:T(8,128)(2,1)S(1)}, bf16[256,2048]{1,0:T(8,128)(2,1)}, u32[]{:S(2)}, u32[]{:S(2)}) %collective-permute-start.3) | collective-permute-done | bytes 1048608 | tf_op jit(solution)/shard_map/ppermute | solution.py:641
  127.3 21.0 %collective-permute-done.7 = bf16[16,2,64]{2,1,0:T(2,128)(2,1)S(1)} collective-permute-done((bf16[16,2,64]{2,1,0:T(2,128)(2,1)S(1)}, bf16[16,2,64]{2,1,0:T(2,128)(2,1)S(1)}, u32[]{:S(2)}, u32[]{:S(2)}) %collective-permute-start.7) | collective-permute-done | bytes 4128 | tf_op jit(solution)/shard_map/ppermute | solution.py:682
  154.6 22.5 %collective-permute-done.14.refs_5_ = bf16[256,2048]{1,0:T(8,128)(2,1)S(1)} collective-permute-done((bf16[256,2048]{1,0:T(8,128)(2,1)S(1)}, bf16[256,2048]{1,0:T(8,128)(2,1)S(1)}, u32[]{:S(2)}, u32[]{:S(2)}) %collective-permute-start.14) | collective-permute-done | bytes 1048608 | tf_op jit(solution)/shard_map/ppermute | solution.py:641
  177.1 6.3 %collective-permute-done.15 = bf16[256,2048]{1,0:T(8,128)(2,1)S(1)} collective-permute-done((bf16[256,2048]{1,0:T(8,128)(2,1)}, bf16[256,2048]{1,0:T(8,128)(2,1)S(1)}, u32[]{:S(2)}, u32[]{:S(2)}) %collective-permute-start.15) | collective-permute-done | bytes 1048608 | tf_op jit(solution)/shard_map/ppermute | solution.py:641
  188.3 22.0 %collective-permute-done.20.refs_7_ = bf16[256,2048]{1,0:T(8,128)(2,1)S(1)} collective-permute-done((bf16[256,2048]{1,0:T(8,128)(2,1)S(1)}, bf16[256,2048]{1,0:T(8,128)(2,1)S(1)}, u32[]{:S(2)}, u32[]{:S(2)}) %collective-permute-start.20) | collective-permute-done | bytes 1048608 | tf_op jit(solution)/shard_map/ppermute | solution.py:641
  210.3 4.6 collective-permute-done.18
  218.4 27.8 %project.1 = (bf16[2048,2048]{1,0:T(8,128)(2,1)}, f32[2048,768]{1,0:T(8,128)}, bf16[2048,1408]{1,0:T(8,128)(2,1)}, bf16[2048,1024]{1,0:T(8,128)(2,1)}) custom-call(bf16[256,2048]{1,0:T(8,128)(2,1)S(1)} %pad_maximum_fusion.1.refs_0_, bf16[256,2048]{1,0:T(8,128)(2,1)} %collective-permute-done.2.refs_1_, bf16[256,2048]{1,0:T(8,128)(2,1)} %collective-permute-done.3.refs_2_, ...), custom_call_target="tpu_custom_call" | custom-call | flops 18253611008 | bytes 34603008 | tf_op jit(solution)/shard_map/project/pallas_call | solution.py:395
  251.1 19.6 %attend_forward.1 = (bf16[8,2,128,768]{3,2,1,0:T(8,128)(2,1)}, bf16[8,2,128,1024]{3,2,1,0:T(8,128)(2,1)}, f32[8,2,128,4]{3,2,1,0:T(8,128)S(1)}) custom-call(s32[2]{0:T(128)S(1)} %copy-done.11, s32[8]{0:T(128)S(1)} %compare_select_fusion.8.slot_ref, f32[8,2,128,768]{3,2,1,0:T(8,128)} %bitcast.69, ...), custom_call_target="tpu_custom_call", output_to_operand_aliasing={{1}: (5, {})} | custom-call | flops 4294967296 | bytes 4194304 | tf_op jit(solution)/shard_map/attend_forward/pallas_call | solution.py:550
  270.7 9.2 %output_part.2 = (bf16[256,2048]{1,0:T(8,128)(2,1)S(1)}, bf16[256,2048]{1,0:T(8,128)(2,1)}, bf16[256,2048]{1,0:T(8,128)(2,1)}, bf16[256,2048]{1,0:T(8,128)(2,1)}) custom-call(bf16[2048,1024]{1,0:T(8,128)(2,1)} %bitcast.71, bf16[2048,1024]{1,0:T(8,128)(2,1)} %bitcast.72, bf16[512,1024]{1,0:T(8,128)(2,1)} %copy-done.9, ...), custom_call_target="tpu_custom_call" | custom-call | flops 4294967296 | bytes 10485760 | tf_op jit(solution)/shard_map/output_part/pallas_call | solution.py:495
  281.0 17.4 %bring_back.1 = (bf16[2048,2048]{1,0:T(8,128)(2,1)}, bf16[2048,256]{1,0:T(8,128)(2,1)S(1)}, bf16[2048,1408]{1,0:T(8,128)(2,1)}) custom-call(bf16[256,2048]{1,0:T(8,128)(2,1)} %copy-done.25, bf16[256,2048]{1,0:T(8,128)(2,1)} %collective-permute-done.refs_1_, bf16[256,2048]{1,0:T(8,128)(2,1)} %collective-permute-done.1.refs_2_, ...), custom_call_target="tpu_custom_call" | custom-call | flops 8589934592 | bytes 25165824 | tf_op jit(solution)/shard_map/bring_back/pallas_call | solution.py:395
  298.4 11.5 %fusion.6 = bf16[1024,1408]{1,0:T(8,128)(2,1)} fusion(bf16[2048,1408]{1,0:T(8,128)(2,1)} %get-tuple-element.592.refs_1_.refs_3_, bf16[2048,2048]{1,0:T(8,128)(2,1)} %get-tuple-element.612), kind=kOutput, calls=%fused_computation.6 | convolution fusion | flops 5907021824 | bytes 12845056 | tf_op jit(solution)/shard_map/dot_general | solution.py:30
  310.0 9.3 %output_part.3 = (bf16[256,2048]{1,0:T(8,128)(2,1)S(1)}, bf16[256,2048]{1,0:T(8,128)(2,1)}, bf16[256,2048]{1,0:T(8,128)(2,1)}, bf16[256,2048]{1,0:T(8,128)(2,1)}) custom-call(bf16[2048,1024]{1,0:T(8,128)(2,1)} %bitcast.73, bf16[2048,1024]{1,0:T(8,128)(2,1)} %bitcast.74, bf16[512,1024]{1,0:T(8,128)(2,1)} %copy-done.9, ...), custom_call_target="tpu_custom_call" | custom-call | flops 4294967296 | bytes 10485760 | tf_op jit(solution)/shard_map/output_part/pallas_call | solution.py:495
  326.2 21.1 %attend_backward.1 = bf16[8,2,128,768]{3,2,1,0:T(8,128)(2,1)} custom-call(s32[2]{0:T(128)S(1)} %copy-done.11, s32[8]{0:T(128)S(1)} %compare_select_fusion.8.slot_ref, bf16[8,2,128,768]{3,2,1,0:T(8,128)(2,1)} %get-tuple-element.498.rot_ref, bf16[8,2,128,1024]{3,2,1,0:T(8,128)(2,1)} %get-tuple-element.440, bf16[8,2,128,256]{3,2,1,0:T(8,128)(2,1)S(1)} %bitcast.49, ...), custom_call_target="tpu_custom_call" | custom-call | flops 10737418240 | bytes 4194304 | tf_op jit(solution)/shard_map/attend_backward/pallas_call | solution.py:557
  355.6 15.7 %normed_part.2 = (bf16[256,2048]{1,0:T(8,128)(2,1)S(1)}, bf16[256,2048]{1,0:T(8,128)(2,1)}, bf16[256,2048]{1,0:T(8,128)(2,1)}, bf16[256,2048]{1,0:T(8,128)(2,1)}) custom-call(bf16[2048,768]{1,0:T(8,128)(2,1)} %bitcast.78, bf16[2048,1408]{1,0:T(8,128)(2,1)} %get-tuple-element.592.refs_1_.refs_3_, bf16[2048,768]{1,0:T(8,128)(2,1)} %bitcast.79, ...), custom_call_target="tpu_custom_call" | custom-call | flops 9126805504 | bytes 17563648 | tf_op jit(solution)/shard_map/normed_part/pallas_call | solution.py:495
  371.4 8.2 %fusion.10 = bf16[512,1408]{1,0:T(8,128)(2,1)} fusion(bf16[2048,1408]{1,0:T(8,128)(2,1)} %get-tuple-element.592.refs_1_.refs_3_, bf16[2048,2048]{1,0:T(8,128)(2,1)} %get-tuple-element.612, bf16[1024,1408]{1,0:T(8,128)(2,1)} %collective-permute-done.30), kind=kOutput, calls=%fused_computation.10 | convolution fusion | flops 2954952704 | bytes 10747904 | tf_op jit(solution)/shard_map/dot_general | solution.py:30
  383.6 3.8 collective-permute-start.36
  387.5 15.7 %normed_part.3 = (bf16[256,2048]{1,0:T(8,128)(2,1)S(1)}, bf16[256,2048]{1,0:T(8,128)(2,1)}, bf16[256,2048]{1,0:T(8,128)(2,1)}, bf16[256,2048]{1,0:T(8,128)(2,1)}) custom-call(bf16[2048,768]{1,0:T(8,128)(2,1)} %bitcast.80, bf16[2048,1408]{1,0:T(8,128)(2,1)} %get-tuple-element.592.refs_1_.refs_3_, bf16[2048,768]{1,0:T(8,128)(2,1)} %bitcast.81, ...), custom_call_target="tpu_custom_call" | custom-call | flops 9126805504 | bytes 17563648 | tf_op jit(solution)/shard_map/normed_part/pallas_call | solution.py:495
  403.2 8.4 %fusion.32 = bf16[1024,1024]{1,0:T(8,128)(2,1)S(1)} fusion(bf16[2048,1024]{1,0:T(8,128)(2,1)} %bitcast.75, bf16[2048,2048]{1,0:T(8,128)(2,1)} %get-tuple-element.616), kind=kOutput, calls=%fused_computation.54 | convolution fusion | flops 4296015872 | bytes 10485760 | tf_op jit(solution)/shard_map/dot_general | solution.py:30
  411.7 6.3 %collective-permute-done.36 = bf16[512,1408]{1,0:T(8,128)(2,1)S(1)} collective-permute-done((bf16[512,1408]{1,0:T(8,128)(2,1)}, bf16[512,1408]{1,0:T(8,128)(2,1)S(1)}, u32[]{:S(2)}, u32[]{:S(2)}) %collective-permute-start.36) | collective-permute-done | bytes 1441824 | tf_op jit(solution)/shard_map/ppermute | solution.py:641
  418.4 4.6 collective-permute-start.42
  424.4 5.7 fusion.36
  432.8 4.5 add_convert_fusion.9
  437.3 8.5 %collective-permute-done.42 = bf16[256,2048]{1,0:T(8,128)(2,1)S(1)} collective-permute-done((bf16[256,2048]{1,0:T(8,128)(2,1)S(1)}, bf16[256,2048]{1,0:T(8,128)(2,1)S(1)}, u32[]{:S(2)}, u32[]{:S(2)}) %collective-permute-start.42) | collective-permute-done | bytes 1048608 | tf_op jit(solution)/shard_map/ppermute | solution.py:641
  455.1 6.7 %fusion.11.refs_1_ = bf16[512,1408]{1,0:T(8,128)(2,1)S(1)} fusion(bf16[2048,1408]{1,0:T(8,128)(2,1)} %get-tuple-element.592.refs_1_.refs_3_, bf16[512,1408]{1,0:T(8,128)(2,1)S(1)} %copy-done.37, bf16[2048,2048]{1,0:T(8,128)(2,1)S(1)} %bitcast.86, bf16[1024,1408]{1,0:T(8,128)(2,1)} %collective-permute-done.30), kind=kOutput, calls=%fused_computation.11 | convolution fusion | flops 2956394496 | bytes 12189696 | tf_op jit(solution)/shard_map/dot_general | solution.py:30
  463.7 10.2 %collective-permute-done.46 = bf16[256,2048]{1,0:T(8,128)(2,1)S(1)} collective-permute-done((bf16[256,2048]{1,0:T(8,128)(2,1)S(1)}, bf16[256,2048]{1,0:T(8,128)(2,1)S(1)}, u32[]{:S(2)}, u32[]{:S(2)}) %collective-permute-start.46) | collective-permute-done | bytes 1048608 | tf_op jit(solution)/shard_map/ppermute | solution.py:641
  485.1 4.1 add_convert_fusion.4.refs_2_
  489.1 8.2 %collective-permute-done.48 = bf16[512,768]{1,0:T(8,128)(2,1)S(1)} collective-permute-done((bf16[512,768]{1,0:T(8,128)(2,1)S(1)}, bf16[512,768]{1,0:T(8,128)(2,1)S(1)}, u32[]{:S(2)}, u32[]{:S(2)}) %collective-permute-start.48) | collective-permute-done | bytes 786464 | tf_op jit(solution)/shard_map/ppermute | solution.py:641
  499.3 4.8 collective-permute-done.50
  509.7 4.0 all-to-all-start.1
  534.7 50.6 %collective-permute-done.54 = f32[4,128]{1,0:T(4,128)S(1)} collective-permute-done((f32[4,128]{1,0:T(4,128)S(1)}, f32[4,128]{1,0:T(4,128)S(1)}, u32[]{:S(2)}, u32[]{:S(2)}) %collective-permute-start.54) | collective-permute-done | bytes 2080 | tf_op jit(solution)/shard_map/ppermute | solution.py:789
  (277 shorter events, 146.2 us)
Async XLA Ops:
  9.2 82.5 %all-to-all-start = ((bf16[8,64,3200]{2,1,0:T(8,128)(2,1)}), bf16[8,64,3200]{2,1,0:T(8,128)(2,1)}, u32[]{:S(2)}, u32[]{:S(2)}) async-start(bf16[8,64,3200]{2,1,0:T(8,128)(2,1)} %pack_columns.1), calls=%async_computation | async-start | bytes 6553600 | tf_op jit(solution)/shard_map/all_to_all | solution.py:674
  19.4 79.0 %collective-permute-start.1 = (bf16[256,2048]{1,0:T(8,128)(2,1)S(1)}, bf16[256,2048]{1,0:T(8,128)(2,1)}, u32[]{:S(2)}, u32[]{:S(2)}) collective-permute-start(bf16[256,2048]{1,0:T(8,128)(2,1)S(1)} %pad_maximum_fusion.refs_0_), channel_id=1, source_target_pairs={{0,2},{1,3},{2,0},{3,1},{4,6},{5,7},{6,4},{7,5},{8,10},{9,11},{10,... | collective-permute-start | bytes 3145736 | tf_op jit(solution)/shard_map/ppermute | solution.py:641
  21.5 77.0 %collective-permute-start = (bf16[256,2048]{1,0:T(8,128)(2,1)S(1)}, bf16[256,2048]{1,0:T(8,128)(2,1)}, u32[]{:S(2)}, u32[]{:S(2)}) collective-permute-start(bf16[256,2048]{1,0:T(8,128)(2,1)S(1)} %pad_maximum_fusion.refs_0_), channel_id=1, source_target_pairs={{0,1},{1,0},{2,3},{3,2},{4,5},{5,4},{6,7},{7,6},{8,9},{9,8},{10,11... | collective-permute-start | bytes 3145736 | tf_op jit(solution)/shard_map/ppermute | solution.py:641
  23.1 75.4 %collective-permute-start.4 = (bf16[256,2048]{1,0:T(8,128)(2,1)S(1)}, bf16[256,2048]{1,0:T(8,128)(2,1)}, u32[]{:S(2)}, u32[]{:S(2)}) collective-permute-start(bf16[256,2048]{1,0:T(8,128)(2,1)S(1)} %pad_maximum_fusion.1.refs_0_), channel_id=1, source_target_pairs={{2,4},{3,5},{4,2},{5,3},{10,12},{11,13},{12,10},{13,11},{18,20},{1... | collective-permute-start | bytes 3145736 | tf_op jit(solution)/shard_map/ppermute | solution.py:641
  24.7 92.0 %collective-permute-start.3 = (bf16[256,2048]{1,0:T(8,128)(2,1)S(1)}, bf16[256,2048]{1,0:T(8,128)(2,1)}, u32[]{:S(2)}, u32[]{:S(2)}) collective-permute-start(bf16[256,2048]{1,0:T(8,128)(2,1)S(1)} %pad_maximum_fusion.1.refs_0_), channel_id=1, source_target_pairs={{0,2},{1,3},{2,0},{3,1},{4,6},{5,7},{6,4},{7,5},{8,10},{9,11},{10,... | collective-permute-start | bytes 3145736 | tf_op jit(solution)/shard_map/ppermute | solution.py:641
  28.0 88.7 %collective-permute-start.2 = (bf16[256,2048]{1,0:T(8,128)(2,1)S(1)}, bf16[256,2048]{1,0:T(8,128)(2,1)}, u32[]{:S(2)}, u32[]{:S(2)}) collective-permute-start(bf16[256,2048]{1,0:T(8,128)(2,1)S(1)} %pad_maximum_fusion.1.refs_0_), channel_id=1, source_target_pairs={{0,1},{1,0},{2,3},{3,2},{4,5},{5,4},{6,7},{7,6},{8,9},{9,8},{10,11... | collective-permute-start | bytes 3145736 | tf_op jit(solution)/shard_map/ppermute | solution.py:641
  116.7 32.1 %collective-permute-start.10 = (bf16[256,2048]{1,0:T(8,128)(2,1)}, bf16[256,2048]{1,0:T(8,128)(2,1)}, u32[]{:S(2)}, u32[]{:S(2)}) collective-permute-start(bf16[256,2048]{1,0:T(8,128)(2,1)} %collective-permute-done.3.refs_2_), channel_id=1, source_target_pairs={{2,4},{3,5},{4,2},{5,3},{10,12},{11,13},{12,10},{13,11},{18,20},{1... | collective-permute-start | bytes 3145736 | tf_op jit(solution)/shard_map/ppermute | solution.py:641
  118.4 30.3 %collective-permute-start.8 = (bf16[256,2048]{1,0:T(8,128)(2,1)}, bf16[256,2048]{1,0:T(8,128)(2,1)}, u32[]{:S(2)}, u32[]{:S(2)}) collective-permute-start(bf16[256,2048]{1,0:T(8,128)(2,1)} %collective-permute-done.3.refs_2_), channel_id=1, source_target_pairs={{0,1},{1,0},{2,3},{3,2},{4,5},{5,4},{6,7},{7,6},{8,9},{9,8},{10,11... | collective-permute-start | bytes 3145736 | tf_op jit(solution)/shard_map/ppermute | solution.py:641
  119.9 28.9 %collective-permute-start.9 = (bf16[256,2048]{1,0:T(8,128)(2,1)}, bf16[256,2048]{1,0:T(8,128)(2,1)}, u32[]{:S(2)}, u32[]{:S(2)}) collective-permute-start(bf16[256,2048]{1,0:T(8,128)(2,1)} %collective-permute-done.4), channel_id=1, source_target_pairs={{2,0},{3,1},{4,6},{5,7},{10,8},{11,9},{12,14},{13,15},{18,16},{19,... | collective-permute-start | bytes 3145736 | tf_op jit(solution)/shard_map/ppermute | solution.py:641
  121.2 27.6 %collective-permute-start.5 = (bf16[256,2176]{1,0:T(8,128)(2,1)}, bf16[256,2176]{1,0:T(8,128)(2,1)}, u32[]{:S(2)}, u32[]{:S(2)}) collective-permute-start(bf16[256,2176]{1,0:T(8,128)(2,1)} %get-tuple-element.543.refs_8_.refs_4_), channel_id=1, source_target_pairs={{0,16},{8,24},{16,0},{24,8},{1,17},{9,25},{17,1},{25,9},{2,18},{10... | collective-permute-start | bytes 3342344 | tf_op jit(solution)/shard_map/ppermute | solution.py:641
  148.8 34.7 %collective-permute-start.11 = (bf16[256,2176]{1,0:T(8,128)(2,1)}, bf16[256,2176]{1,0:T(8,128)(2,1)S(1)}, u32[]{:S(2)}, u32[]{:S(2)}) collective-permute-start(bf16[256,2176]{1,0:T(8,128)(2,1)} %collective-permute-done.5.refs_10_.refs_6_), channel_id=1, source_target_pairs={{0,8},{8,0},{16,24},{24,16},{1,9},{9,1},{17,25},{25,17},{2,10},{10... | collective-permute-start | bytes 3342344 | tf_op jit(solution)/shard_map/ppermute | solution.py:641
  148.9 34.6 %collective-permute-start.12 = (bf16[256,2176]{1,0:T(8,128)(2,1)}, bf16[256,2176]{1,0:T(8,128)(2,1)S(1)}, u32[]{:S(2)}, u32[]{:S(2)}) collective-permute-start(bf16[256,2176]{1,0:T(8,128)(2,1)} %copy-done.8), channel_id=1, source_target_pairs={{0,16},{8,24},{16,0},{24,8},{1,17},{9,25},{17,1},{25,9},{2,18},{10... | collective-permute-start | bytes 3342344 | tf_op jit(solution)/shard_map/ppermute | solution.py:641
  153.3 30.2 %collective-permute-start.15 = (bf16[256,2048]{1,0:T(8,128)(2,1)}, bf16[256,2048]{1,0:T(8,128)(2,1)S(1)}, u32[]{:S(2)}, u32[]{:S(2)}) collective-permute-start(bf16[256,2048]{1,0:T(8,128)(2,1)} %collective-permute-done.10), channel_id=1, source_target_pairs={{2,0},{3,1},{4,6},{5,7},{10,8},{11,9},{12,14},{13,15},{18,16},{19,... | collective-permute-start | bytes 3145736 | tf_op jit(solution)/shard_map/ppermute | solution.py:641
  183.5 31.4 %collective-permute-start.16 = (bf16[512,2176]{1,0:T(8,128)(2,1)S(1)}, bf16[512,2176]{1,0:T(8,128)(2,1)S(1)}, u32[]{:S(2)}, u32[]{:S(2)}) collective-permute-start(bf16[512,2176]{1,0:T(8,128)(2,1)S(1)} %copy-done.7), channel_id=1, source_target_pairs={{0,8},{8,0},{16,24},{24,16},{1,9},{9,1},{17,25},{25,17},{2,10},{10... | collective-permute-start | bytes 6684680 | tf_op jit(solution)/shard_map/ppermute | solution.py:641
  184.5 30.4 %collective-permute-start.17 = (bf16[256,2176]{1,0:T(8,128)(2,1)S(1)}, bf16[256,2176]{1,0:T(8,128)(2,1)S(1)}, u32[]{:S(2)}, u32[]{:S(2)}) collective-permute-start(bf16[256,2176]{1,0:T(8,128)(2,1)S(1)} %collective-permute-done.12.refs_11_.refs_7_), channel_id=1, source_target_pairs={{0,8},{8,0},{16,24},{24,16},{1,9},{9,1},{17,25},{25,17},{2,10},{10... | collective-permute-start | bytes 3342344 | tf_op jit(solution)/shard_map/ppermute | solution.py:641
  187.0 27.9 %collective-permute-start.18 = (bf16[256,2048]{1,0:T(8,128)(2,1)S(1)}, bf16[256,2048]{1,0:T(8,128)(2,1)S(1)}, u32[]{:S(2)}, u32[]{:S(2)}) collective-permute-start(bf16[256,2048]{1,0:T(8,128)(2,1)S(1)} %collective-permute-done.13), channel_id=1, source_target_pairs={{2,0},{3,1},{4,6},{5,7},{10,8},{11,9},{12,14},{13,15},{18,16},{19,... | collective-permute-start | bytes 3145736 | tf_op jit(solution)/shard_map/ppermute | solution.py:641
  214.9 31.3 %collective-permute-start.24 = (bf16[512,1024]{1,0:T(8,128)(2,1)S(1)}, bf16[512,1024]{1,0:T(8,128)(2,1)}, u32[]{:S(2)}, u32[]{:S(2)}) collective-permute-start(bf16[512,1024]{1,0:T(8,128)(2,1)S(1)} %copy-done.10), channel_id=1, source_target_pairs={{0,16},{8,24},{16,0},{24,8},{1,17},{9,25},{17,1},{25,9},{2,18},{10... | collective-permute-start | bytes 3145736 | tf_op jit(solution)/shard_map/ppermute | solution.py:641
  215.5 30.7 %collective-permute-start.23 = (bf16[512,1024]{1,0:T(8,128)(2,1)S(1)}, bf16[512,1024]{1,0:T(8,128)(2,1)S(1)}, u32[]{:S(2)}, u32[]{:S(2)}) collective-permute-start(bf16[512,1024]{1,0:T(8,128)(2,1)S(1)} %copy-done.10), channel_id=1, source_target_pairs={{0,8},{8,0},{16,24},{24,16},{1,9},{9,1},{17,25},{25,17},{2,10},{10... | collective-permute-start | bytes 3145736 | tf_op jit(solution)/shard_map/ppermute | solution.py:641
  215.6 30.5 %collective-permute-start.21 = (bf16[256,2048]{1,0:T(8,128)(2,1)S(1)}, bf16[256,2048]{1,0:T(8,128)(2,1)S(1)}, u32[]{:S(2)}, u32[]{:S(2)}) collective-permute-start(bf16[256,2048]{1,0:T(8,128)(2,1)S(1)} %broadcast_select_fusion.1.refs_4_), channel_id=1, source_target_pairs={{0,1},{1,0},{2,3},{3,2},{4,5},{5,4},{6,7},{7,6},{8,9},{9,8},{10,11... | collective-permute-start | bytes 3145736 | tf_op jit(solution)/shard_map/ppermute | solution.py:641
  216.6 29.6 %collective-permute-start.22 = (bf16[256,2048]{1,0:T(8,128)(2,1)S(1)}, bf16[256,2048]{1,0:T(8,128)(2,1)S(1)}, u32[]{:S(2)}, u32[]{:S(2)}) collective-permute-start(bf16[256,2048]{1,0:T(8,128)(2,1)S(1)} %collective-permute-done.19), channel_id=1, source_target_pairs={{2,0},{3,1},{4,6},{5,7},{10,8},{11,9},{12,14},{13,15},{18,16},{19,... | collective-permute-start | bytes 3145736 | tf_op jit(solution)/shard_map/ppermute | solution.py:641
  247.3 32.7 %collective-permute-start.26 = (bf16[256,2048]{1,0:T(8,128)(2,1)S(1)}, bf16[256,2048]{1,0:T(8,128)(2,1)}, u32[]{:S(2)}, u32[]{:S(2)}) collective-permute-start(bf16[256,2048]{1,0:T(8,128)(2,1)S(1)} %broadcast_select_fusion.refs_6_), channel_id=1, source_target_pairs={{0,1},{1,0},{2,3},{3,2},{4,5},{5,4},{6,7},{7,6},{8,9},{9,8},{10,11... | collective-permute-start | bytes 3145736 | tf_op jit(solution)/shard_map/ppermute | solution.py:641
  248.4 31.6 %collective-permute-start.25 = (bf16[256,2048]{1,0:T(8,128)(2,1)}, bf16[256,2048]{1,0:T(8,128)(2,1)}, u32[]{:S(2)}, u32[]{:S(2)}) collective-permute-start(bf16[256,2048]{1,0:T(8,128)(2,1)} %collective-permute-done.refs_1_), channel_id=1, source_target_pairs={{0,2},{1,3},{2,0},{3,1},{4,6},{5,7},{6,4},{7,5},{8,10},{9,11},{10,... | collective-permute-start | bytes 3145736 | tf_op jit(solution)/shard_map/ppermute | solution.py:641
  279.9 39.4 %collective-permute-start.28 = (bf16[256,2048]{1,0:T(8,128)(2,1)}, bf16[256,2048]{1,0:T(8,128)(2,1)S(1)}, u32[]{:S(2)}, u32[]{:S(2)}) collective-permute-start(bf16[256,2048]{1,0:T(8,128)(2,1)} %get-tuple-element.478), channel_id=1, source_target_pairs={{0,2},{1,3},{2,0},{3,1},{4,6},{5,7},{6,4},{7,5},{8,10},{9,11},{10,... | collective-permute-start | bytes 3145736 | tf_op jit(solution)/shard_map/ppermute | solution.py:641
  280.0 39.3 %collective-permute-start.29 = (bf16[256,2048]{1,0:T(8,128)(2,1)}, bf16[256,2048]{1,0:T(8,128)(2,1)S(1)}, u32[]{:S(2)}, u32[]{:S(2)}) collective-permute-start(bf16[256,2048]{1,0:T(8,128)(2,1)} %get-tuple-element.482), channel_id=1, source_target_pairs={{0,1},{1,0},{2,3},{3,2},{4,5},{5,4},{6,7},{7,6},{8,9},{9,8},{10,11... | collective-permute-start | bytes 3145736 | tf_op jit(solution)/shard_map/ppermute | solution.py:641
  319.3 30.3 %collective-permute-start.30 = (bf16[1024,1408]{1,0:T(8,128)(2,1)}, bf16[1024,1408]{1,0:T(8,128)(2,1)}, u32[]{:S(2)}, u32[]{:S(2)}) collective-permute-start(bf16[1024,1408]{1,0:T(8,128)(2,1)} %fusion.6), channel_id=1, source_target_pairs={{0,8},{8,0},{16,24},{24,16},{1,9},{9,1},{17,25},{25,17},{2,10},{10... | collective-permute-start | bytes 8650760 | tf_op jit(solution)/shard_map/ppermute | solution.py:641
  350.0 29.6 %collective-permute-start.34 = (bf16[256,2048]{1,0:T(8,128)(2,1)S(1)}, bf16[256,2048]{1,0:T(8,128)(2,1)S(1)}, u32[]{:S(2)}, u32[]{:S(2)}) collective-permute-start(bf16[256,2048]{1,0:T(8,128)(2,1)S(1)} %add_convert_fusion.13), channel_id=1, source_target_pairs={{0,2},{1,3},{6,4},{7,5},{8,10},{9,11},{14,12},{15,13},{16,18},{17,... | collective-permute-start | bytes 3145736 | tf_op jit(solution)/shard_map/ppermute | solution.py:641
  380.0 31.7 %collective-permute-start.38 = (bf16[256,2048]{1,0:T(8,128)(2,1)S(1)}, bf16[256,2048]{1,0:T(8,128)(2,1)S(1)}, u32[]{:S(2)}, u32[]{:S(2)}) collective-permute-start(bf16[256,2048]{1,0:T(8,128)(2,1)S(1)} %add_convert_fusion.11), channel_id=1, source_target_pairs={{0,2},{1,3},{2,0},{3,1},{4,6},{5,7},{6,4},{7,5},{8,10},{9,11},{10,... | collective-permute-start | bytes 3145736 | tf_op jit(solution)/shard_map/ppermute | solution.py:641
  382.0 29.6 %collective-permute-start.39 = (bf16[256,2048]{1,0:T(8,128)(2,1)S(1)}, bf16[256,2048]{1,0:T(8,128)(2,1)S(1)}, u32[]{:S(2)}, u32[]{:S(2)}) collective-permute-start(bf16[256,2048]{1,0:T(8,128)(2,1)S(1)} %add_convert_fusion.10), channel_id=1, source_target_pairs={{2,4},{3,5},{4,2},{5,3},{10,12},{11,13},{12,10},{13,11},{18,20},{1... | collective-permute-start | bytes 3145736 | tf_op jit(solution)/shard_map/ppermute | solution.py:641
  383.0 28.7 %collective-permute-start.37 = (bf16[256,2048]{1,0:T(8,128)(2,1)}, bf16[256,2048]{1,0:T(8,128)(2,1)S(1)}, u32[]{:S(2)}, u32[]{:S(2)}) collective-permute-start(bf16[256,2048]{1,0:T(8,128)(2,1)} %get-tuple-element.558), channel_id=1, source_target_pairs={{0,1},{1,0},{2,3},{3,2},{4,5},{5,4},{6,7},{7,6},{8,9},{9,8},{10,11... | collective-permute-start | bytes 3145736 | tf_op jit(solution)/shard_map/ppermute | solution.py:641
  383.6 34.4 %collective-permute-start.36 = (bf16[512,1408]{1,0:T(8,128)(2,1)}, bf16[512,1408]{1,0:T(8,128)(2,1)S(1)}, u32[]{:S(2)}, u32[]{:S(2)}) collective-permute-start(bf16[512,1408]{1,0:T(8,128)(2,1)} %fusion.10), channel_id=1, source_target_pairs={{0,16},{8,24},{16,0},{24,8},{1,17},{9,25},{17,1},{25,9},{2,18},{10... | collective-permute-start | bytes 4325384 | tf_op jit(solution)/shard_map/ppermute | solution.py:641
  509.7 84.4 %all-to-all-start.1 = ((bf16[8,64,3200]{2,1,0:T(8,128)(2,1)}), bf16[8,64,3200]{2,1,0:T(8,128)(2,1)S(1)}, u32[]{:S(2)}, u32[]{:S(2)}) async-start(bf16[8,64,3200]{2,1,0:T(8,128)(2,1)} %pack_rows.1), calls=%async_computation.1 | async-start | bytes 6553600 | tf_op jit(solution)/shard_map/all_to_all | solution.py:778
  531.1 54.2 %collective-permute-start.54 = (f32[4,128]{1,0:T(4,128)S(1)}, f32[4,128]{1,0:T(4,128)S(1)}, u32[]{:S(2)}, u32[]{:S(2)}) collective-permute-start(f32[4,128]{1,0:T(4,128)S(1)} %slice_select_fusion.1), channel_id=1, source_target_pairs={{0,4},{1,5},{2,6},{3,7},{4,0},{5,1},{6,2},{7,3},{8,12},{9,13},{10,... | collective-permute-start | bytes 6152 | tf_op jit(solution)/shard_map/ppermute | solution.py:789
  (80 other events, 1159.4 us)

commit v5 on v4

--- a/solution.py
+++ b/solution.py
@@ -241,23 +241,25 @@
             lane += span
 
 
-def pack_kernel(plan, *refs):
-    scale_ref, sources, out_ref = refs[0], refs[1:-1], refs[-1]
-    for dest in range(plan.n):
-        for weight, start, stride, lane, span in plan.segments():
-            begin = start + dest * stride
-            out_ref[dest, :, lane : lane + span] = sources[weight][:, begin : begin + span]
-        out_ref[dest, :, plan.first + plan.used :] = scale_ref[...]
-
-
-def unpack_kernel(plan, outs_of, in_ref, *outs):
-    own = plan.own
+def pack_kernel(plan, chosen, *refs):
+    scale_ref, sources, out_ref = refs[0], dict(zip(chosen, refs[1:-1])), refs[-1]
+    lane = 0
+    for weight, start, stride, _, span in plan.segments():
+        if weight in chosen:
+            for dest in range(plan.n):
+                begin = start + dest * stride
+                out_ref[dest, :, lane : lane + span] = sources[weight][:, begin : begin + span]
+            lane += span
+    if lane < out_ref.shape[2]:
+        for dest in range(plan.n):
+            out_ref[dest, :, lane:] = scale_ref[...]
+
+
+def unpack_kernel(own, outs_of, in_ref, *outs):
     for out, (source, sources, lane, lanes) in zip(outs, outs_of):
         for index in range(sources):
             block = in_ref[source + index, :, lane : lane + lanes]
             out[index * own : (index + 1) * own, :] = block
-    for source in range(plan.n):
-        outs[-1][source] = in_ref[source, :, plan.first + plan.used :]
 
 
 def pack_rows_kernel(own, *refs):
@@ -296,20 +298,22 @@
 
 
 def pack_columns(plan, weights, scales):
-    shape = jax.ShapeDtypeStruct((plan.n, plan.own, plan.first + plan.second), BF)
     scales = jnp.pad(scales.reshape(2, plan.own), ((0, plan.own - 2), (0, 0)))
-    return in_vmem(functools.partial(pack_kernel, plan), "pack_columns", shape)(scales, *weights)
-
-
-def unpack_columns(plan, packed):
-    n, own = plan.n, plan.own
-    outs_of = [(half * n // 2, n // 2, 0, plan.first) for half in range(2)]
-    outs_of += [(0, n, 0, plan.first), (0, n, plan.first, plan.second)]
+    packed = []
+    for chosen, lanes in (((0, 2, 3), plan.first), ((1, 4), plan.second)):
+        shape = jax.ShapeDtypeStruct((plan.n, plan.own, lanes), BF)
+        kernel = functools.partial(pack_kernel, plan, chosen)
+        packed.append(in_vmem(kernel, "pack_columns", shape)(scales, *[weights[w] for w in chosen]))
+    return packed
+
+
+def unpack_columns(plan, packed, parts):
+    n, own, lanes = packed.shape
+    outs_of = [(half * n // 2, n // 2, 0, lanes) for half in range(2)] if parts else []
+    outs_of.append((0, n, 0, lanes))
     shapes = [jax.ShapeDtypeStruct((c * own, lanes), BF) for _, c, _, lanes in outs_of]
-    shapes.append(jax.ShapeDtypeStruct((n, own, own), BF))
-    kernel = functools.partial(unpack_kernel, plan, outs_of)
-    *parts, scales = in_vmem(kernel, "unpack_columns", shapes)(packed)
-    return parts, scales[:, :2]
+    kernel = functools.partial(unpack_kernel, own, outs_of)
+    return in_vmem(kernel, "unpack_columns", shapes)(packed)
 
 
 def pack_rows(own, n, gradients):
@@ -318,10 +322,16 @@
     return in_vmem(functools.partial(pack_rows_kernel, own), "pack_rows", shape)(*gradients)
 
 
-def unpack_rows(plan, packed):
+def unpack_rows(plan, packed, chosen, begins):
+    layout = []
+    for weight, start, stride, lane, span in plan.segments():
+        if weight in chosen:
+            group = 0 if weight == 0 else 1 if weight in (2, 3) else 2
+            lane += begins[group] - (0, plan.joined, plan.first)[group]
+            layout.append((chosen.index(weight), start, stride, lane, span))
     widths = [3 * plan.width, plan.width, plan.units, plan.units, plan.units]
-    shapes = [jax.ShapeDtypeStruct((plan.own, plan.n * w), F32) for w in widths]
-    kernel = functools.partial(unpack_rows_kernel, plan.n, list(plan.segments()))
+    shapes = [jax.ShapeDtypeStruct((plan.own, plan.n * widths[w]), F32) for w in chosen]
+    kernel = functools.partial(unpack_rows_kernel, plan.n, layout)
     return in_vmem(kernel, "unpack_rows", shapes)(packed)
 
 
@@ -334,9 +344,9 @@
     return copies
 
 
-def stream_kernel(n, n_pieces, n_extra, finish, *refs):
+def stream_kernel(n, n_pieces, n_extra, n_into, finish, *refs):
     blocks, refs = refs[:n], refs[n:]
-    pieces, refs = refs[:n_pieces], refs[n_pieces:]
+    pieces, refs = refs[:n_pieces], refs[n_pieces + n_into :]
     extra, outs, (held, rows_ref, rows_sem, weight_sem) = refs[:n_extra], refs[n_extra:-4], refs[-4:]
     size = blocks[0].shape[0]
     step = pl.program_id(0)
@@ -377,27 +387,26 @@
     finish(rows_ref[buffer], held, extra, outs)
 
 
-def stream(name, blocks, pieces, extra, finish, outs):
-    size, features = blocks[0].shape
+def stream(name, slots, places, pieces, extra, finish, outs, into):
+    size, features = slots[0].shape
+    blocks = [slots[2 * place + half] for place in places for half in range(2)]
     n = len(blocks)
+    first, stride = places[0], places[1] - places[0]
     anywhere = pl.BlockSpec(memory_space=pl.ANY)
 
     def rows(width):
-        return pl.BlockSpec((2 * size, width), lambda i: (i, 0))
-
-    def beside(array):
-        if array.shape[0] == n * size:
-            return rows(array.shape[1])
-        return pl.BlockSpec(array.shape, lambda i: (0, 0))
+        return pl.BlockSpec((2 * size, width), lambda i: (first + stride * i, 0))
 
     outs = [(features, BF), *outs]
     width = pieces[0].shape[1]
+    begin = n + len(pieces)
     return pl.pallas_call(
-        functools.partial(stream_kernel, n, len(pieces), len(extra), finish),
+        functools.partial(stream_kernel, n, len(pieces), len(extra), len(into), finish),
         grid=(n // 2,),
-        in_specs=[anywhere] * (n + len(pieces)) + [beside(e) for e in extra],
+        in_specs=[anywhere] * (begin + len(into)) + [rows(e.shape[1]) for e in extra],
         out_specs=[rows(w) for w, _ in outs],
-        out_shape=[jax.ShapeDtypeStruct((n * size, w), dtype) for w, dtype in outs],
+        out_shape=[jax.ShapeDtypeStruct((len(slots) * size, w), dtype) for w, dtype in outs],
+        input_output_aliases={begin + i: i for i in range(len(into))},
         scratch_shapes=[
             pltpu.VMEM((features, width), BF),
             pltpu.VMEM((2, 2 * size, features), BF),
@@ -411,7 +420,7 @@
             transcendentals=0,
         ),
         name=name,
-    )(*blocks, *pieces, *extra)
+    )(*blocks, *pieces, *into, *extra)
 
 
 def swiglu(plan, both):
@@ -427,8 +436,7 @@
 
 
 def project_finish(plan, rows, held, extra, outs):
-    (scales,), (normed, joined, factor_ref, wide) = extra, outs
-    rows = (rows.astype(F32) * scales[0:1, :] + scales[1:2, :]).astype(BF)
+    normed, joined, factor_ref, wide = outs
     normed[...] = rows
     joined[...] = dot(rows, held[:, : plan.joined])
     hidden, factors = swiglu(plan, dot(rows, held[:, plan.joined :]))
@@ -593,8 +601,10 @@
     def scatter(v, axis):
         return lax.psum_scatter(v, axis, scatter_dimension=0, tiled=True)
 
-    parts, scales = unpack_columns(plan, swap(pack_columns(plan, weights, scales)))
-    w_first, w_second = gather(parts[2], "dp"), gather(parts[3], "dp")[:, : plan.used]
+    first, second = (swap(packed) for packed in pack_columns(plan, weights, scales))
+    w_first = gather(unpack_columns(plan, first, False)[0], "dp")
+    w_second = gather(unpack_columns(plan, second, False)[0], "dp")[:, : plan.used]
+    scales = second[:, :2, plan.used :]
     standard, inverse = layer.standardize()
     normed, gain = layer.norm(standard, gather(scales, "dp"))
     normed, cot = gather(normed, "ctx"), gather(layer.cot, "ctx")
@@ -613,7 +623,8 @@
     d_first = jnp.concatenate([d_joined, d_both.astype(BF)], axis=1)
     d_normed = scatter(dot_last(d_first, w_first).astype(BF), "ctx")
     sums = [scatter(dot_first(*v).astype(BF), "dp") for v in ((normed, d_first), (cot, wide))]
-    grads = unpack_rows(plan, swap(pack_rows(own, n, sums)))
+    begins = (0, plan.joined, plan.first)
+    grads = unpack_rows(plan, swap(pack_rows(own, n, sums)), [0, 1, 2, 3, 4], begins)
     input_grad, norm_sums = layer.norm_back(d_normed, standard, inverse, gain)
     return layer.finish_output(branches), input_grad, scatter(norm_sums, ("dp", "ctx")), grads
 
@@ -641,7 +652,9 @@
             view[name] = lax.ppermute(self.held[source], axis, pairs)
         for action in work:
             view.update(action(view))
-        self.held = lax.optimization_barrier(view)
+        names = list(view)
+        held = lax.optimization_barrier([view[name] for name in names])
+        self.held = dict(zip(names, held))
 
 
 def on_grid(layer, weights, scales):
@@ -669,21 +682,36 @@
     def unorder(v):
         return blocks_of(v, (dp % 2) * 2 + dp // 2, (0, 2, 1, 3))
 
-    def weights_in(s):
-        packed = pack_columns(plan, weights, scales)
+    opened = {}
+
+    def doubled(held, axis, bit, size):
+        mine = lax.axis_index(axis) // bit % 2
+        got = lax.ppermute(held, axis, swaps(bit, size))
+        first, second = jnp.where(mine == 0, held, got), jnp.where(mine == 0, got, held)
+        return jnp.concatenate([first, second], axis=0)
+
+    def begin(s):
+        held = scales.reshape(1, 2, own)
+        for bit in (1, 2, 4):
+            held = doubled(held, "ctx", bit, n)
+        packed, second = pack_columns(plan, weights, scales)
+        packed, held, c0 = lax.optimization_barrier((packed, held, s["c0"]))
         packed = lax.all_to_all(packed, "ctx", split_axis=0, concat_axis=0, tiled=True)
-        parts, held = unpack_columns(plan, packed)
-        return {"scales": held, **dict(zip(("a0", "b0", "ab0", "w0"), parts))}
-
-    def all_scales(s):
-        held = s["scales"]
+        made = {"c0x": lax.ppermute(c0, *side), "c1": lax.ppermute(c0, *pair)}
         for bit in (1, 2):
-            mine = dp // bit % 2
-            got = lax.ppermute(held, "dp", swaps(bit, 4))
-            first, second = jnp.where(mine == 0, held, got), jnp.where(mine == 0, got, held)
-            held = jnp.concatenate([first, second], axis=0)
-        gain, bias = layer.scales(held)
-        return {"gain": gain, "both": reorder(jnp.concatenate([gain, bias], axis=0))}
+            held = doubled(held, "dp", bit, 4)
+        normed, gain = layer.norm(standard, held)
+        n0 = reorder(normed)
+        made |= {"n0": n0, "gain": gain, "n0x": lax.ppermute(n0, *side)}
+        made |= {"n1": lax.ppermute(n0, *pair), "n2i": lax.ppermute(n0, *middle)}
+        parts = unpack_columns(plan, packed, True)
+        return made | {"second": second} | dict(zip(("a0", "b0", "ab0"), parts))
+
+    def second_in(s):
+        opened["second"] = lax.all_to_all(
+            s["second"], "ctx", split_axis=0, concat_axis=0, tiled=True
+        )
+        return {}
 
     def select(name):
         return lambda s: {name: jnp.where(inner, s[name + "i"], s[name + "o"])}
@@ -696,14 +724,27 @@
         return [s[key] for key in names.split()]
 
     def slots(s, letter):
-        return [s[letter + i] for i in ("0", "0x", "1", "1x", "2", "2x", "3", "3x")]
-
-    def project(s):
-        outs = [(plan.joined, F32), (2 * plan.units, BF), (plan.second, BF)]
-        finish = functools.partial(project_finish, plan)
-        held = pieces(s, "ab")
-        made = stream("project", slots(s, "n"), held, [s["both"]], finish, outs)
-        return dict(zip(("n", "joined", "factors", "wide"), made))
+        return [s.get(letter + i) for i in ("0", "0x", "1", "1x", "2", "2x", "3", "3x")]
+
+    def streamed(name, letter, weight, names, finish, widths, extra, places):
+        def work(s):
+            done = [s[key] for key in names] if places[0] else []
+            held = (slots(s, letter), places, pieces(s, weight), [s[key] for key in extra])
+            made = stream(name, *held, functools.partial(finish, plan), widths, done)
+            return dict(zip(names, made))
+
+        return work
+
+    def project(*places):
+        names = ("n", "joined", "factors", "wide")
+        widths = [(plan.joined, F32), (2 * plan.units, BF), (plan.second, BF)]
+        return streamed("project", "n", "ab", names, project_finish, widths, [], places)
+
+    def bring_back(*places):
+        names = ("c", "d_attn", "d_both")
+        widths = [(plan.width, BF), (2 * plan.units, BF)]
+        held = ("factors",)
+        return streamed("bring_back", "c", "w", names, return_finish, widths, held, places)
 
     def tables(s):
         return {"tables": layer.tables}
@@ -711,14 +752,6 @@
     def attend(s):
         made = layer.attend(s["joined"], s["wide"], s["tables"])
         return dict(zip(("rotated", "wide", "lse"), made))
-
-    def bring_back(s):
-        outs = [(plan.width, BF), (2 * plan.units, BF)]
-        finish = functools.partial(return_finish, plan)
-        made = stream(
-            "bring_back", slots(s, "c"), pieces(s, "w"), [s["factors"]], finish, outs
-        )
-        return dict(zip(("c", "d_attn", "d_both"), made))
 
     def attend_back(s):
         d_joined = layer.attend_back(
@@ -767,27 +800,45 @@
     def to(name, source, way):
         return (name, source, *way)
 
+    def cross(name):
+        return lambda s: {name + "Ar": lax.ppermute(s[name + "A"], *core)}
+
     def send_a(name):
         return to(name + "Ar", name + "A", core)
 
     def send_b(name):
         return to(name + "Br", name + "B", across)
 
-    def swap_rows(s):
-        held = pack_rows(own, n, [s[name + "C"] for name in "JGW"])
-        held = lax.all_to_all(held, "ctx", split_axis=0, concat_axis=0, tiled=True)
-        return {f"grad{weight}": grad for weight, grad in enumerate(unpack_rows(plan, held))}
+    def packed_rows(*names):
+        return lambda s: {names: pack_rows(own, n, [s[name + "C"] for name in names])}
+
+    def swap_packed(*names):
+        def work(s):
+            opened[names] = lax.all_to_all(
+                s[names], "ctx", split_axis=0, concat_axis=0, tiled=True
+            )
+            return {}
+
+        return work
 
     def norm_back(s):
         input_grad, sums = layer.norm_back(unorder(s["d"]), standard, inverse, s["gain"])
-        for axis, bit, size in [("dp", b, 4) for b in (2, 1)] + [("ctx", b, n) for b in (4, 2, 1)]:
+
+        def halved(sums, dim, axis, bit, size):
             mine = lax.axis_index(axis) // bit % 2
-            halves = sums.reshape(2, -1, sums.shape[1])
-            first, second = halves[0], halves[1]
+            first, second = jnp.split(sums, 2, axis=dim)
             give = jnp.where(mine == 0, second, first)
-            keep = jnp.where(mine == 0, first, second)
-            sums = keep + lax.ppermute(give, axis, swaps(bit, size))
-        return {"input_grad": input_grad, "norm_sums": sums}
+            return jnp.where(mine == 0, first, second) + lax.ppermute(give, axis, swaps(bit, size))
+
+        sums = sums.reshape(4, n, 2 * own)
+        for bit in (4, 2, 1):
+            sums = halved(sums, 1, "ctx", bit, n)
+        names = ("J", "W")
+        packed, sums = lax.optimization_barrier((s[names], sums))
+        opened[names] = lax.all_to_all(packed, "ctx", split_axis=0, concat_axis=0, tiled=True)
+        for bit in (2, 1):
+            sums = halved(sums, 0, "dp", bit, 4)
+        return {"input_grad": input_grad, "norm_sums": sums[0]}
 
     def y(name):
         return to(name + "2", name + "0", across)
@@ -799,23 +850,19 @@
         return to(name + "3", name + "2", core)
 
     standard, inverse = layer.standardize()
-    st = State(c0=reorder(layer.cot), n0=reorder(standard.astype(BF)))
+    st = State(c0=reorder(layer.cot))
     tick = st.tick
+    tick((), (), [begin])
     tick(
         (),
         [
-            to("n0x", "n0", side),
-            to("n1", "n0", pair),
-            to("n2i", "n0", middle),
-            to("c0x", "c0", side),
-            to("c1", "c0", pair),
+            to("n1x", "n1", side),
+            to("n3i", "n1", middle),
+            to("n2o", "n2i", outward),
+            y("a"),
+            near("ab"),
         ],
-        [weights_in],
-    )
-    tick(
-        (),
-        [to("n1x", "n1", side), to("n3i", "n1", middle), to("n2o", "n2i", outward), y("a")],
-        [all_scales, tables],
+        [second_in, tables],
     )
     tick(
         [select("n2")],
@@ -834,43 +881,50 @@
             to("c2o", "c2i", outward),
             to("c3i", "c1", middle),
             far("b"),
-            near("ab"),
         ],
-    )
-    tick(
-        [select("c2")],
+        [project(0, 1)],
+    )
+    tick(
+        [select("c2"), lambda s: {"w0": unpack_columns(plan, opened["second"], False)[0]}],
         [to("c2x", "c2", side), to("c3o", "c3i", outward), y("w"), near("w")],
-        [project],
+        [project(2, 3)],
     )
     tick(
         [select("c3")],
         [to("c3x", "c3", side), to("c1x", "c0x", pair), far("w")],
-        [attend, output_part(1, 3)],
+        [attend, output_part(0, 1, 2, 3)],
     )
     tick(
         (),
         [to("o3x", "o3a", side), to("o1p", "o1a", pair)],
-        [output_part(0, 2), bring_back, grad_a("G")],
+        [bring_back(0, 1, 2, 3), grad_a("G")],
     )
     tick(
         [plus("o3", "o3k", "o3x")],
         [to("o2x", "o2a", side), to("o3i", "o3", inward), send_a("G")],
-        [attend_back],
+        [attend_back, grad_b("G")],
     )
     tick(
         [plus("o2", "o2k", "o2x"), plus("o3", "o3", "o3i"), plus("o0a", "o0a", "o1p")],
-        [to("o0x", "o0a", side), to("o2i", "o2", inward), to("o3m", "o3", middle)],
-        [normed_part(1, 3), grad_b("G")],
+        [to("o0x", "o0a", side), to("o2i", "o2", inward), to("o3m", "o3", middle), send_b("G")],
+        [normed_part(1, 3)],
     )
     tick(
         [plus("o2", "o2", "o2i"), plus("o1", "o1k", "o3m")],
-        [to("d3x", "d3a", side), to("o2m", "o2", middle), to("o1r", "o1", pair), send_b("G")],
-        [normed_part(0, 2), grad_a("W")],
+        [to("d3x", "d3a", side), to("o2m", "o2", middle), to("o1r", "o1", pair)],
+        [normed_part(0, 2), grad_c("G"), packed_rows("G")],
     )
     tick(
         [plus("d3", "d3k", "d3x")],
-        [to("d2x", "d2a", side), to("d3i", "d3", inward), send_a("W")],
-        [grad_b("W"), grad_a("J"), plus("o", "o0k", "o0x", "o2m", "o1r")],
+        [to("d2x", "d2a", side), to("d3i", "d3", inward)],
+        [
+            swap_packed("G"),
+            grad_a("J"),
+            cross("J"),
+            grad_b("J"),
+            grad_a("W"),
+            plus("o", "o0k", "o0x", "o2m", "o1r"),
+        ],
     )
     tick(
         [plus("d2", "d2k", "d2x"), plus("d3", "d3", "d3i")],
@@ -878,18 +932,21 @@
             to("d1x", "d1a", side),
             to("d2i", "d2", inward),
             to("d3m", "d3", middle),
-            send_b("W"),
-            send_a("J"),
+            send_b("J"),
+            send_a("W"),
         ],
-        [grad_c("G"), grad_b("J")],
+        [grad_b("W"), grad_c("J")],
     )
     tick(
         [plus("d2", "d2", "d2i"), plus("d1", "d1k", "d1x", "d3m")],
-        [to("d0x", "d0a", side), to("d2m", "d2", middle), to("d1r", "d1", pair), send_b("J")],
-        [grad_c("W"), grad_c("J")],
-    )
-    tick([plus("d", "d0k", "d0x", "d2m", "d1r")], (), [swap_rows, norm_back])
-    grads = [st[f"grad{weight}"] for weight in range(5)]
+        [to("d0x", "d0a", side), to("d2m", "d2", middle), to("d1r", "d1", pair), send_b("W")],
+        [grad_c("W"), packed_rows("J", "W")],
+    )
+    tick([plus("d", "d0k", "d0x", "d2m", "d1r")], (), [norm_back])
+    gate_grad, up_grad = unpack_rows(plan, opened["G",], [2, 3], (0, 0, 0))
+    begins = (0, 0, plan.joined)
+    joined_grad, out_grad, down_grad = unpack_rows(plan, opened["J", "W"], [0, 1, 4], begins)
+    grads = [joined_grad, out_grad, gate_grad, up_grad, down_grad]
     return layer.finish_output(unorder(st["o"])), st["input_grad"], st["norm_sums"], grads
 
 

time: 608 us -> 592 us (0.974)
  waiting for transfers between devices: 267 us -> 239 us
  local copies, waits for them, and re-layouts: 16.5 us -> 6.44 us
  Pallas kernels: 146 us -> 156 us
  starting transfers between devices: 84.5 us -> 92.7 us
  other arithmetic: 30.3 us -> 36.4 us
    ppermute x7 -> x16, waiting for transfers between devices: 78.2 us -> 53.7 us  [the longest x5 26.2 us: halved(): lax.ppermute(give, axis, swaps(bit, size))]
    ppermute x50 -> x44, waiting for transfers between devices: 125 us -> 106 us  [tick(): view[name] = lax.ppermute(self.held[source], axis, pairs)]
    all_to_all x2 -> x4, waiting for transfers between devices: 63.1 us -> 79.8 us  [the longest x1 39.5 us: begin(): lax.all_to_all(packed, 'ctx', split_axis=0, concat_axis=0, tiled=True)]
    ppermute x50 -> x44, starting transfers between devices: 66.6 us -> 53.8 us  [tick(): view[name] = lax.ppermute(self.held[source], axis, pairs)]
    ppermute x7 -> x16, starting transfers between devices: 6.52 us -> 18.9 us  [the longest x5 8.89 us: doubled(): got = lax.ppermute(held, axis, swaps(bit, size))]
    unnamed x106 -> x96, local copies, waits for them, and re-layouts: 13.9 us -> 1.66 us
    all_to_all x2 -> x4, starting transfers between devices: 11.4 us -> 20 us  [the longest x1 7.44 us: second_in(): lax.all_to_all(s['second'], 'ctx', split_axis=0, concat_axis=0, tiled=True)]
    pallas_call x2 -> x3, Pallas kernels: 45.1 us -> 50.6 us  [stream(): pl.pallas_call(functools.partial(stream_kernel, n, len(pieces), len(extra...]
  transfers between devices with their start and end apart: 59 -> 64, of which waited for: 21 -> 29; matrix products, arithmetic and copies ran while one was open for 14% -> 16% of each run, Pallas kernels for 23% -> 26%
where the time goes in v5:
time: 592 us; the launch traced here: 586 us
  waiting for transfers between devices  239 us (40%)
  Pallas kernels  156 us (26%)
  starting transfers between devices  92.7 us (16%)
  matrix products  53.2 us (9%)
  other arithmetic  36.4 us (6%)
  local copies, waits for them, and re-layouts  6.44 us (1%)
    ppermute x44, waiting for transfers between devices, tick(): view[name] = lax.ppermute(self.held[source], axis, pairs)  106 us
    ppermute x44, starting transfers between devices, tick(): view[name] = lax.ppermute(self.held[source], axis, pairs)  53.8 us
    dot_general x9, matrix products, dot_first(): return lax.dot_general(left, right, FIRST, preferred_element_type=F32)  53.2 us
    pallas_call x3, Pallas kernels, stream(): pl.pallas_call(functools.partial(stream_kernel, n, len(pieces), len(extra...  50.6 us
    pallas_call x3, Pallas kernels, spread(): pl.pallas_call(functools.partial(spread_kernel, len(lefts), len(pieces),...  45.9 us
    all_to_all x1, waiting for transfers between devices, begin(): lax.all_to_all(packed, 'ctx', split_axis=0, concat_axis=0, tiled=True)  39.5 us
    all_to_all x1, waiting for transfers between devices, norm_back(): lax.all_to_all(packed, 'ctx', split_axis=0, concat_axis=0, tiled=True)  26.7 us
    ppermute x5, waiting for transfers between devices, halved(): lax.ppermute(give, axis, swaps(bit, size))  26.2 us
  transfers between devices with their start and end apart: 64, of which 29 were waited for; matrix products, arithmetic and copies ran while one was open for 16% of the time, Pallas kernels for 26%

profile of v5, /device:TPU:0, one launch (start us, length us, event | category | flops | bytes accessed | tf_op | source)
XLA Modules:
  0.0 586.1 jit_solution(3360049829922454329)
XLA Ops:
  15.3 5.4 all-to-all-start
  33.8 39.5 %all-to-all-done.in_ref = bf16[8,64,2176]{2,1,0:T(8,128)(2,1)} async-done(((bf16[8,64,2176]{2,1,0:T(8,128)(2,1)}), bf16[8,64,2176]{2,1,0:T(8,128)(2,1)}, u32[]{:S(2)}, u32[]{:S(2)}) %all-to-all-start) | async-done | bytes 2228256 | tf_op jit(solution)/shard_map/all_to_all | solution.py:699
  76.8 6.1 %collective-permute-done.4.refs_2_ = bf16[256,2048]{1,0:T(8,128)(2,1)} collective-permute-done((bf16[256,2048]{1,0:T(8,128)(2,1)}, bf16[256,2048]{1,0:T(8,128)(2,1)}, u32[]{:S(2)}, u32[]{:S(2)}) %collective-permute-start.4) | collective-permute-done | bytes 1048608 | tf_op jit(solution)/shard_map/ppermute | solution.py:700
  82.9 6.6 %collective-permute-done.7.refs_1_ = bf16[256,2048]{1,0:T(8,128)(2,1)} collective-permute-done((bf16[256,2048]{1,0:T(8,128)(2,1)S(1)}, bf16[256,2048]{1,0:T(8,128)(2,1)}, u32[]{:S(2)}, u32[]{:S(2)}) %collective-permute-start.7) | collective-permute-done | bytes 1048608 | tf_op jit(solution)/shard_map/ppermute | solution.py:705
  89.5 12.0 %collective-permute-done.8.refs_2_ = bf16[256,2048]{1,0:T(8,128)(2,1)} collective-permute-done((bf16[256,2048]{1,0:T(8,128)(2,1)S(1)}, bf16[256,2048]{1,0:T(8,128)(2,1)}, u32[]{:S(2)}, u32[]{:S(2)}) %collective-permute-start.8) | collective-permute-done | bytes 1048608 | tf_op jit(solution)/shard_map/ppermute | solution.py:706
  107.4 5.6 fusion.48
  113.0 15.6 %collective-permute-done.10.refs_3_ = bf16[256,2048]{1,0:T(8,128)(2,1)} collective-permute-done((bf16[256,2048]{1,0:T(8,128)(2,1)}, bf16[256,2048]{1,0:T(8,128)(2,1)}, u32[]{:S(2)}, u32[]{:S(2)}) %collective-permute-start.10) | collective-permute-done | bytes 1048608 | tf_op jit(solution)/shard_map/ppermute | solution.py:652
  128.6 5.1 collective-permute-done.12
  139.7 7.4 %all-to-all-start.1 = ((bf16[8,64,1024]{2,1,0:T(8,128)(2,1)}), bf16[8,64,1024]{2,1,0:T(8,128)(2,1)S(1)}, u32[]{:S(2)}, u32[]{:S(2)}) async-start(bf16[8,64,1024]{2,1,0:T(8,128)(2,1)} %pack_columns.3), calls=%async_computation.1 | async-start | bytes 2097152 | tf_op jit(solution)/shard_map/all_to_all | solution.py:711
  147.2 15.9 %collective-permute-done.15.refs_1_ = bf16[256,2048]{1,0:T(8,128)(2,1)} collective-permute-done((bf16[256,2048]{1,0:T(8,128)(2,1)S(1)}, bf16[256,2048]{1,0:T(8,128)(2,1)}, u32[]{:S(2)}, u32[]{:S(2)}) %collective-permute-start.15) | collective-permute-done | bytes 1048608 | tf_op jit(solution)/shard_map/ppermute | solution.py:652
  163.0 7.5 %collective-permute-done.16 = bf16[256,2048]{1,0:T(8,128)(2,1)} collective-permute-done((bf16[256,2048]{1,0:T(8,128)(2,1)}, bf16[256,2048]{1,0:T(8,128)(2,1)}, u32[]{:S(2)}, u32[]{:S(2)}) %collective-permute-start.16) | collective-permute-done | bytes 1048608 | tf_op jit(solution)/shard_map/ppermute | solution.py:652
  177.3 13.6 %all-to-all-done.1.in_ref = bf16[8,64,1024]{2,1,0:T(8,128)(2,1)S(1)} async-done(((bf16[8,64,1024]{2,1,0:T(8,128)(2,1)}), bf16[8,64,1024]{2,1,0:T(8,128)(2,1)S(1)}, u32[]{:S(2)}, u32[]{:S(2)}) %all-to-all-start.1) | async-done | bytes 1048608 | tf_op jit(solution)/shard_map/all_to_all | solution.py:711
  192.1 16.7 %project.2 = (bf16[2048,2048]{1,0:T(8,128)(2,1)}, f32[2048,768]{1,0:T(8,128)}, bf16[2048,1408]{1,0:T(8,128)(2,1)}, bf16[2048,1024]{1,0:T(8,128)(2,1)}) custom-call(bf16[256,2048]{1,0:T(8,128)(2,1)S(1)} %copy-done.4, bf16[256,2048]{1,0:T(8,128)(2,1)} %collective-permute-done.7.refs_1_, bf16[256,2048]{1,0:T(8,128)(2,1)} %collective-permute-done.8.refs_2_, ...), custom_call_target="tpu_custom_call" | custom-call | flops 9126805504 | bytes 26214400 | tf_op jit(solution)/shard_map/project/pallas_call | solution.py:403
  216.6 16.6 %project.3 = (bf16[2048,2048]{1,0:T(8,128)(2,1)}, f32[2048,768]{1,0:T(8,128)}, bf16[2048,1408]{1,0:T(8,128)(2,1)}, bf16[2048,1024]{1,0:T(8,128)(2,1)}) custom-call(bf16[256,2048]{1,0:T(8,128)(2,1)S(1)} %broadcast_select_fusion.3.refs_0_, ...), custom_call_target="tpu_custom_call", output_to_operand_aliasing={{0}: (11, {}), {1}: (12, {}), {2}: (13, {}), {3}: (14, {})} | custom-call | flops 9126805504 | bytes 26214400 | tf_op jit(solution)/shard_map/project/pallas_call | solution.py:403
  233.3 6.6 %collective-permute-done.24.refs_5_ = bf16[256,2048]{1,0:T(8,128)(2,1)S(1)} collective-permute-done((bf16[256,2048]{1,0:T(8,128)(2,1)S(1)}, bf16[256,2048]{1,0:T(8,128)(2,1)S(1)}, u32[]{:S(2)}, u32[]{:S(2)}) %collective-permute-start.24) | collective-permute-done | bytes 1048608 | tf_op jit(solution)/shard_map/ppermute | solution.py:652
  245.3 22.6 %attend_forward.1 = (bf16[8,2,128,768]{3,2,1,0:T(8,128)(2,1)}, bf16[8,2,128,1024]{3,2,1,0:T(8,128)(2,1)}, f32[8,2,128,4]{3,2,1,0:T(8,128)S(1)}) custom-call(s32[2]{0:T(128)S(1)} %copy-done.11, s32[8]{0:T(128)S(1)} %compare_select_fusion.8.slot_ref, f32[8,2,128,768]{3,2,1,0:T(8,128)} %bitcast.53, ...), custom_call_target="tpu_custom_call", output_to_operand_aliasing={{1}: (5, {})} | custom-call | flops 4294967296 | bytes 4194304 | tf_op jit(solution)/shard_map/attend_forward/pallas_call | solution.py:558
  268.8 14.4 %output_part.1 = (bf16[256,2048]{1,0:T(8,128)(2,1)S(1)}, bf16[256,2048]{1,0:T(8,128)(2,1)}, bf16[256,2048]{1,0:T(8,128)(2,1)}, bf16[256,2048]{1,0:T(8,128)(2,1)}...) custom-call(bf16[2048,1024]{1,0:T(8,128)(2,1)} %bitcast.55, ...), custom_call_target="tpu_custom_call" | custom-call | flops 8589934592 | bytes 16777216 | tf_op jit(solution)/shard_map/output_part/pallas_call | solution.py:503
  285.7 17.4 %bring_back.1 = (bf16[2048,2048]{1,0:T(8,128)(2,1)}, bf16[2048,256]{1,0:T(8,128)(2,1)S(1)}, bf16[2048,1408]{1,0:T(8,128)(2,1)}) custom-call(bf16[256,2048]{1,0:T(8,128)(2,1)} %pad_maximum_fusion.refs_0_, bf16[256,2048]{1,0:T(8,128)(2,1)} %collective-permute-done.3.refs_1_, bf16[256,2048]{1,0:T(8,128)(2,1)} %collective-permute-done.4.refs_2_, ...), custom_call_target="tpu_custom_call" | custom-call | flops 8589934592 | bytes 25165824 | tf_op jit(solution)/shard_map/bring_back/pallas_call | solution.py:403
  303.2 11.7 %fusion.6 = bf16[1024,1408]{1,0:T(8,128)(2,1)} fusion(bf16[2048,1408]{1,0:T(8,128)(2,1)} %get-tuple-element.545.refs_1_.refs_3_, bf16[2048,2048]{1,0:T(8,128)(2,1)} %get-tuple-element.580), kind=kOutput, calls=%fused_computation.6 | convolution fusion | flops 5907021824 | bytes 12845056 | tf_op jit(solution)/shard_map/dot_general | solution.py:30
  319.1 23.6 %attend_backward.1 = bf16[8,2,128,768]{3,2,1,0:T(8,128)(2,1)} custom-call(s32[2]{0:T(128)S(1)} %copy-done.11, s32[8]{0:T(128)S(1)} %compare_select_fusion.8.slot_ref, bf16[8,2,128,768]{3,2,1,0:T(8,128)(2,1)} %get-tuple-element.491.rot_ref, bf16[8,2,128,1024]{3,2,1,0:T(8,128)(2,1)} %get-tuple-element.424, bf16[8,2,128,256]{3,2,1,0:T(8,128)(2,1)S(1)} %bitcast.52, ...), custom_call_target="tpu_custom_call" | custom-call | flops 10737418240 | bytes 4194304 | tf_op jit(solution)/shard_map/attend_backward/pallas_call | solution.py:565
  342.8 7.2 %fusion.10 = bf16[512,1408]{1,0:T(8,128)(2,1)S(1)} fusion(bf16[2048,1408]{1,0:T(8,128)(2,1)} %get-tuple-element.545.refs_1_.refs_3_, bf16[2048,2048]{1,0:T(8,128)(2,1)} %get-tuple-element.580, bf16[1024,1408]{1,0:T(8,128)(2,1)} %collective-permute-done.35), kind=kOutput, calls=%fused_computation.10 | convolution fusion | flops 2954952704 | bytes 10747904 | tf_op jit(solution)/shard_map/dot_general | solution.py:30
  355.0 15.7 %normed_part.2 = (bf16[256,2048]{1,0:T(8,128)(2,1)S(1)}, bf16[256,2048]{1,0:T(8,128)(2,1)}, bf16[256,2048]{1,0:T(8,128)(2,1)}, bf16[256,2048]{1,0:T(8,128)(2,1)}) custom-call(bf16[2048,768]{1,0:T(8,128)(2,1)} %bitcast.82, bf16[2048,1408]{1,0:T(8,128)(2,1)} %get-tuple-element.545.refs_1_.refs_3_, bf16[2048,768]{1,0:T(8,128)(2,1)} %bitcast.83, ...), custom_call_target="tpu_custom_call" | custom-call | flops 9126805504 | bytes 17563648 | tf_op jit(solution)/shard_map/normed_part/pallas_call | solution.py:503
  375.8 11.2 %collective-permute-done.39 = bf16[512,1408]{1,0:T(8,128)(2,1)S(1)} collective-permute-done((bf16[512,1408]{1,0:T(8,128)(2,1)S(1)}, bf16[512,1408]{1,0:T(8,128)(2,1)S(1)}, u32[]{:S(2)}, u32[]{:S(2)}) %collective-permute-start.39) | collective-permute-done | bytes 1441824 | tf_op jit(solution)/shard_map/ppermute | solution.py:652
  391.1 7.2 %fusion.11.refs_0_ = bf16[512,1408]{1,0:T(8,128)(2,1)S(1)} fusion(bf16[2048,1408]{1,0:T(8,128)(2,1)} %get-tuple-element.545.refs_1_.refs_3_, bf16[512,1408]{1,0:T(8,128)(2,1)S(1)} %copy-done.37, bf16[2048,2048]{1,0:T(8,128)(2,1)} %get-tuple-element.580, bf16[1024,1408]{1,0:T(8,128)(2,1)} %collective-permute-done.35), kind=kOutput, calls=%fused_computation.11 | convolution fusion | flops 2956394496 | bytes 12189696 | tf_op jit(solution)/shard_map/dot_general | solution.py:30
  399.6 15.8 %normed_part.3 = (bf16[256,2048]{1,0:T(8,128)(2,1)S(1)}, bf16[256,2048]{1,0:T(8,128)(2,1)}, bf16[256,2048]{1,0:T(8,128)(2,1)}, bf16[256,2048]{1,0:T(8,128)(2,1)}) custom-call(bf16[2048,768]{1,0:T(8,128)(2,1)} %bitcast.84, bf16[2048,1408]{1,0:T(8,128)(2,1)} %get-tuple-element.545.refs_1_.refs_3_, bf16[2048,768]{1,0:T(8,128)(2,1)} %bitcast.85, ...), custom_call_target="tpu_custom_call" | custom-call | flops 9126805504 | bytes 17563648 | tf_op jit(solution)/shard_map/normed_part/pallas_call | solution.py:503
  420.4 5.7 fusion.35
  448.7 12.8 %collective-permute-done.49 = bf16[512,768]{1,0:T(8,128)(2,1)S(1)} collective-permute-done((bf16[512,768]{1,0:T(8,128)(2,1)S(1)}, bf16[512,768]{1,0:T(8,128)(2,1)S(1)}, u32[]{:S(2)}, u32[]{:S(2)}) %collective-permute-start.49) | collective-permute-done | bytes 786464 | tf_op jit(solution)/shard_map/ppermute | solution.py:652
  476.8 5.5 collective-permute-start.53
  485.9 9.2 %collective-permute-done.54 = bf16[512,1024]{1,0:T(8,128)(2,1)} collective-permute-done((bf16[512,1024]{1,0:T(8,128)(2,1)}, bf16[512,1024]{1,0:T(8,128)(2,1)}, u32[]{:S(2)}, u32[]{:S(2)}) %collective-permute-start.54) | collective-permute-done | bytes 1048608 | tf_op jit(solution)/shard_map/ppermute | solution.py:652
  495.1 5.8 add_convert_fusion.2.refs_1_
  516.7 17.5 %collective-permute-done.55 = f32[4,4,128]{2,1,0:T(4,128)S(1)} collective-permute-done((f32[4,4,128]{2,1,0:T(4,128)S(1)}, f32[4,4,128]{2,1,0:T(4,128)S(1)}, u32[]{:S(2)}, u32[]{:S(2)}) %collective-permute-start.55) | collective-permute-done | bytes 8224 | tf_op jit(solution)/shard_map/ppermute | solution.py:831
  557.0 26.7 %all-to-all-done.2.held = bf16[8,64,1792]{2,1,0:T(8,128)(2,1)S(1)} async-done(((bf16[8,64,1792]{2,1,0:T(8,128)(2,1)}), bf16[8,64,1792]{2,1,0:T(8,128)(2,1)S(1)}, u32[]{:S(2)}, u32[]{:S(2)}) %all-to-all-start.2) | async-done | bytes 1835040 | tf_op jit(solution)/shard_map/all_to_all | solution.py:838
  (288 shorter events, 173.6 us)
Async XLA Ops:
  15.3 58.0 %all-to-all-start = ((bf16[8,64,2176]{2,1,0:T(8,128)(2,1)}), bf16[8,64,2176]{2,1,0:T(8,128)(2,1)}, u32[]{:S(2)}, u32[]{:S(2)}) async-start(bf16[8,64,2176]{2,1,0:T(8,128)(2,1)} %pack_columns.2), calls=%async_computation | async-start | bytes 4456448 | tf_op jit(solution)/shard_map/all_to_all | solution.py:699
  24.4 52.4 %collective-permute-start.3 = (bf16[256,2048]{1,0:T(8,128)(2,1)}, bf16[256,2048]{1,0:T(8,128)(2,1)}, u32[]{:S(2)}, u32[]{:S(2)}) collective-permute-start(bf16[256,2048]{1,0:T(8,128)(2,1)} %pad_maximum_fusion.refs_0_), channel_id=1, source_target_pairs={{0,1},{1,0},{2,3},{3,2},{4,5},{5,4},{6,7},{7,6},{8,9},{9,8},{10,11... | collective-permute-start | bytes 3145736 | tf_op jit(solution)/shard_map/ppermute | solution.py:700
  26.4 56.5 %collective-permute-start.4 = (bf16[256,2048]{1,0:T(8,128)(2,1)}, bf16[256,2048]{1,0:T(8,128)(2,1)}, u32[]{:S(2)}, u32[]{:S(2)}) collective-permute-start(bf16[256,2048]{1,0:T(8,128)(2,1)} %pad_maximum_fusion.refs_0_), channel_id=1, source_target_pairs={{0,2},{1,3},{2,0},{3,1},{4,6},{5,7},{6,4},{7,5},{8,10},{9,11},{10,... | collective-permute-start | bytes 3145736 | tf_op jit(solution)/shard_map/ppermute | solution.py:700
  30.1 59.4 %collective-permute-start.7 = (bf16[256,2048]{1,0:T(8,128)(2,1)S(1)}, bf16[256,2048]{1,0:T(8,128)(2,1)}, u32[]{:S(2)}, u32[]{:S(2)}) collective-permute-start(bf16[256,2048]{1,0:T(8,128)(2,1)S(1)} %pad_maximum_fusion.1.refs_0_), channel_id=1, source_target_pairs={{0,1},{1,0},{2,3},{3,2},{4,5},{5,4},{6,7},{7,6},{8,9},{9,8},{10,11... | collective-permute-start | bytes 3145736 | tf_op jit(solution)/shard_map/ppermute | solution.py:705
  30.7 70.7 %collective-permute-start.8 = (bf16[256,2048]{1,0:T(8,128)(2,1)S(1)}, bf16[256,2048]{1,0:T(8,128)(2,1)}, u32[]{:S(2)}, u32[]{:S(2)}) collective-permute-start(bf16[256,2048]{1,0:T(8,128)(2,1)S(1)} %pad_maximum_fusion.1.refs_0_), channel_id=1, source_target_pairs={{0,2},{1,3},{2,0},{3,1},{4,6},{5,7},{6,4},{7,5},{8,10},{9,11},{10,... | collective-permute-start | bytes 3145736 | tf_op jit(solution)/shard_map/ppermute | solution.py:706
  31.7 69.8 %collective-permute-start.9 = (bf16[256,2048]{1,0:T(8,128)(2,1)S(1)}, bf16[256,2048]{1,0:T(8,128)(2,1)S(1)}, u32[]{:S(2)}, u32[]{:S(2)}) collective-permute-start(bf16[256,2048]{1,0:T(8,128)(2,1)S(1)} %pad_maximum_fusion.1.refs_0_), channel_id=1, source_target_pairs={{2,4},{3,5},{4,2},{5,3},{10,12},{11,13},{12,10},{13,11},{18,20},{1... | collective-permute-start | bytes 3145736 | tf_op jit(solution)/shard_map/ppermute | solution.py:706
  101.5 32.2 %collective-permute-start.14 = (bf16[512,2176]{1,0:T(8,128)(2,1)}, bf16[512,2176]{1,0:T(8,128)(2,1)}, u32[]{:S(2)}, u32[]{:S(2)}) collective-permute-start(bf16[512,2176]{1,0:T(8,128)(2,1)} %get-tuple-element.335), channel_id=1, source_target_pairs={{0,8},{8,0},{16,24},{24,16},{1,9},{9,1},{17,25},{25,17},{2,10},{10... | collective-permute-start | bytes 6684680 | tf_op jit(solution)/shard_map/ppermute | solution.py:652
  101.5 32.2 %collective-permute-start.13 = (bf16[256,2176]{1,0:T(8,128)(2,1)S(1)}, bf16[256,2176]{1,0:T(8,128)(2,1)}, u32[]{:S(2)}, u32[]{:S(2)}) collective-permute-start(bf16[256,2176]{1,0:T(8,128)(2,1)S(1)} %get-tuple-element.533.refs_4_), channel_id=1, source_target_pairs={{0,16},{8,24},{16,0},{24,8},{1,17},{9,25},{17,1},{25,9},{2,18},{10... | collective-permute-start | bytes 3342344 | tf_op jit(solution)/shard_map/ppermute | solution.py:652
  133.7 36.9 %collective-permute-start.18 = (bf16[256,2176]{1,0:T(8,128)(2,1)}, bf16[256,2176]{1,0:T(8,128)(2,1)}, u32[]{:S(2)}, u32[]{:S(2)}) collective-permute-start(bf16[256,2176]{1,0:T(8,128)(2,1)} %get-tuple-element.534.refs_5_), channel_id=1, source_target_pairs={{0,16},{8,24},{16,0},{24,8},{1,17},{9,25},{17,1},{25,9},{2,18},{10... | collective-permute-start | bytes 3342344 | tf_op jit(solution)/shard_map/ppermute | solution.py:652
  134.7 35.9 %collective-permute-start.19 = (bf16[256,2176]{1,0:T(8,128)(2,1)}, bf16[256,2176]{1,0:T(8,128)(2,1)}, u32[]{:S(2)}, u32[]{:S(2)}) collective-permute-start(bf16[256,2176]{1,0:T(8,128)(2,1)} %collective-permute-done.13.refs_6_), channel_id=1, source_target_pairs={{0,8},{8,0},{16,24},{24,16},{1,9},{9,1},{17,25},{25,17},{2,10},{10... | collective-permute-start | bytes 3342344 | tf_op jit(solution)/shard_map/ppermute | solution.py:652
  136.8 33.8 %collective-permute-start.16 = (bf16[256,2048]{1,0:T(8,128)(2,1)}, bf16[256,2048]{1,0:T(8,128)(2,1)}, u32[]{:S(2)}, u32[]{:S(2)}) collective-permute-start(bf16[256,2048]{1,0:T(8,128)(2,1)} %collective-permute-done.11), channel_id=1, source_target_pairs={{2,0},{3,1},{4,6},{5,7},{10,8},{11,9},{12,14},{13,15},{18,16},{19,... | collective-permute-start | bytes 3145736 | tf_op jit(solution)/shard_map/ppermute | solution.py:652
  138.0 32.5 %collective-permute-start.17 = (bf16[256,2048]{1,0:T(8,128)(2,1)}, bf16[256,2048]{1,0:T(8,128)(2,1)}, u32[]{:S(2)}, u32[]{:S(2)}) collective-permute-start(bf16[256,2048]{1,0:T(8,128)(2,1)} %pad_maximum_fusion.refs_0_), channel_id=1, source_target_pairs={{2,4},{3,5},{4,2},{5,3},{10,12},{11,13},{12,10},{13,11},{18,20},{1... | collective-permute-start | bytes 3145736 | tf_op jit(solution)/shard_map/ppermute | solution.py:652
  139.7 51.1 %all-to-all-start.1 = ((bf16[8,64,1024]{2,1,0:T(8,128)(2,1)}), bf16[8,64,1024]{2,1,0:T(8,128)(2,1)S(1)}, u32[]{:S(2)}, u32[]{:S(2)}) async-start(bf16[8,64,1024]{2,1,0:T(8,128)(2,1)} %pack_columns.3), calls=%async_computation.1 | async-start | bytes 2097152 | tf_op jit(solution)/shard_map/all_to_all | solution.py:711
  173.0 35.8 %collective-permute-start.20 = (bf16[256,2048]{1,0:T(8,128)(2,1)}, bf16[256,2048]{1,0:T(8,128)(2,1)}, u32[]{:S(2)}, u32[]{:S(2)}) collective-permute-start(bf16[256,2048]{1,0:T(8,128)(2,1)} %broadcast_select_fusion.2.refs_2_), channel_id=1, source_target_pairs={{0,1},{1,0},{2,3},{3,2},{4,5},{5,4},{6,7},{7,6},{8,9},{9,8},{10,11... | collective-permute-start | bytes 3145736 | tf_op jit(solution)/shard_map/ppermute | solution.py:652
  174.3 39.0 %collective-permute-start.21 = (bf16[256,2048]{1,0:T(8,128)(2,1)}, bf16[256,2048]{1,0:T(8,128)(2,1)}, u32[]{:S(2)}, u32[]{:S(2)}) collective-permute-start(bf16[256,2048]{1,0:T(8,128)(2,1)} %collective-permute-done.17), channel_id=1, source_target_pairs={{2,0},{3,1},{4,6},{5,7},{10,8},{11,9},{12,14},{13,15},{18,16},{19,... | collective-permute-start | bytes 3145736 | tf_op jit(solution)/shard_map/ppermute | solution.py:652
  175.6 37.7 %collective-permute-start.22 = (bf16[256,2048]{1,0:T(8,128)(2,1)}, bf16[256,2048]{1,0:T(8,128)(2,1)}, u32[]{:S(2)}, u32[]{:S(2)}) collective-permute-start(bf16[256,2048]{1,0:T(8,128)(2,1)} %collective-permute-done.4.refs_2_), channel_id=1, source_target_pairs={{2,4},{3,5},{4,2},{5,3},{10,12},{11,13},{12,10},{13,11},{18,20},{1... | collective-permute-start | bytes 3145736 | tf_op jit(solution)/shard_map/ppermute | solution.py:652
  190.9 42.3 %collective-permute-start.26 = (bf16[512,1024]{1,0:T(8,128)(2,1)S(1)}, bf16[512,1024]{1,0:T(8,128)(2,1)}, u32[]{:S(2)}, u32[]{:S(2)}) collective-permute-start(bf16[512,1024]{1,0:T(8,128)(2,1)S(1)} %unpack_columns.3.refs_4_.refs_8_), channel_id=1, source_target_pairs={{0,16},{8,24},{16,0},{24,8},{1,17},{9,25},{17,1},{25,9},{2,18},{10... | collective-permute-start | bytes 3145736 | tf_op jit(solution)/shard_map/ppermute | solution.py:652
  192.1 41.2 %collective-permute-start.27 = (bf16[512,1024]{1,0:T(8,128)(2,1)S(1)}, bf16[512,1024]{1,0:T(8,128)(2,1)S(1)}, u32[]{:S(2)}, u32[]{:S(2)}) collective-permute-start(bf16[512,1024]{1,0:T(8,128)(2,1)S(1)} %unpack_columns.3.refs_4_.refs_8_), channel_id=1, source_target_pairs={{0,8},{8,0},{16,24},{24,16},{1,9},{9,1},{17,25},{25,17},{2,10},{10... | collective-permute-start | bytes 3145736 | tf_op jit(solution)/shard_map/ppermute | solution.py:652
  243.5 39.8 %collective-permute-start.28 = (bf16[256,2048]{1,0:T(8,128)(2,1)S(1)}, bf16[256,2048]{1,0:T(8,128)(2,1)S(1)}, u32[]{:S(2)}, u32[]{:S(2)}) collective-permute-start(bf16[256,2048]{1,0:T(8,128)(2,1)S(1)} %broadcast_select_fusion.refs_6_), channel_id=1, source_target_pairs={{0,1},{1,0},{2,3},{3,2},{4,5},{5,4},{6,7},{7,6},{8,9},{9,8},{10,11... | collective-permute-start | bytes 3145736 | tf_op jit(solution)/shard_map/ppermute | solution.py:652
  245.3 38.1 %collective-permute-start.29 = (bf16[256,2048]{1,0:T(8,128)(2,1)}, bf16[256,2048]{1,0:T(8,128)(2,1)S(1)}, u32[]{:S(2)}, u32[]{:S(2)}) collective-permute-start(bf16[256,2048]{1,0:T(8,128)(2,1)} %collective-permute-done.3.refs_1_), channel_id=1, source_target_pairs={{0,2},{1,3},{2,0},{3,1},{4,6},{5,7},{6,4},{7,5},{8,10},{9,11},{10,... | collective-permute-start | bytes 3145736 | tf_op jit(solution)/shard_map/ppermute | solution.py:652
  283.3 31.5 %collective-permute-start.31 = (bf16[256,2048]{1,0:T(8,128)(2,1)}, bf16[256,2048]{1,0:T(8,128)(2,1)S(1)}, u32[]{:S(2)}, u32[]{:S(2)}) collective-permute-start(bf16[256,2048]{1,0:T(8,128)(2,1)} %get-tuple-element.475), channel_id=1, source_target_pairs={{0,1},{1,0},{2,3},{3,2},{4,5},{5,4},{6,7},{7,6},{8,9},{9,8},{10,11... | collective-permute-start | bytes 3145736 | tf_op jit(solution)/shard_map/ppermute | solution.py:652
  283.7 31.2 %collective-permute-start.32 = (bf16[256,2048]{1,0:T(8,128)(2,1)}, bf16[256,2048]{1,0:T(8,128)(2,1)S(1)}, u32[]{:S(2)}, u32[]{:S(2)}) collective-permute-start(bf16[256,2048]{1,0:T(8,128)(2,1)} %get-tuple-element.471), channel_id=1, source_target_pairs={{0,2},{1,3},{2,0},{3,1},{4,6},{5,7},{6,4},{7,5},{8,10},{9,11},{10,... | collective-permute-start | bytes 3145736 | tf_op jit(solution)/shard_map/ppermute | solution.py:652
  314.9 27.9 %collective-permute-start.35 = (bf16[1024,1408]{1,0:T(8,128)(2,1)}, bf16[1024,1408]{1,0:T(8,128)(2,1)}, u32[]{:S(2)}, u32[]{:S(2)}) collective-permute-start(bf16[1024,1408]{1,0:T(8,128)(2,1)} %fusion.6), channel_id=1, source_target_pairs={{0,8},{8,0},{16,24},{24,16},{1,9},{9,1},{17,25},{25,17},{2,10},{10... | collective-permute-start | bytes 8650760 | tf_op jit(solution)/shard_map/ppermute | solution.py:652
  315.0 35.1 %collective-permute-start.33 = (bf16[256,2048]{1,0:T(8,128)(2,1)S(1)}, bf16[256,2048]{1,0:T(8,128)(2,1)S(1)}, u32[]{:S(2)}, u32[]{:S(2)}) collective-permute-start(bf16[256,2048]{1,0:T(8,128)(2,1)S(1)} %copy-done.42), channel_id=1, source_target_pairs={{0,1},{1,0},{2,3},{3,2},{4,5},{5,4},{6,7},{7,6},{8,9},{9,8},{10,11... | collective-permute-start | bytes 3145736 | tf_op jit(solution)/shard_map/ppermute | solution.py:652
  317.1 32.9 %collective-permute-start.34 = (bf16[256,2048]{1,0:T(8,128)(2,1)S(1)}, bf16[256,2048]{1,0:T(8,128)(2,1)S(1)}, u32[]{:S(2)}, u32[]{:S(2)}) collective-permute-start(bf16[256,2048]{1,0:T(8,128)(2,1)S(1)} %add_convert_fusion.15), channel_id=1, source_target_pairs={{0,2},{1,3},{6,4},{7,5},{8,10},{9,11},{14,12},{15,13},{16,18},{17,... | collective-permute-start | bytes 3145736 | tf_op jit(solution)/shard_map/ppermute | solution.py:652
  353.8 33.2 %collective-permute-start.39 = (bf16[512,1408]{1,0:T(8,128)(2,1)S(1)}, bf16[512,1408]{1,0:T(8,128)(2,1)S(1)}, u32[]{:S(2)}, u32[]{:S(2)}) collective-permute-start(bf16[512,1408]{1,0:T(8,128)(2,1)S(1)} %fusion.10), channel_id=1, source_target_pairs={{0,16},{8,24},{16,0},{24,8},{1,17},{9,25},{17,1},{25,9},{2,18},{10... | collective-permute-start | bytes 4325384 | tf_op jit(solution)/shard_map/ppermute | solution.py:652
  387.0 28.4 %collective-permute-start.40 = (bf16[256,2048]{1,0:T(8,128)(2,1)}, bf16[256,2048]{1,0:T(8,128)(2,1)S(1)}, u32[]{:S(2)}, u32[]{:S(2)}) collective-permute-start(bf16[256,2048]{1,0:T(8,128)(2,1)} %get-tuple-element.556), channel_id=1, source_target_pairs={{0,1},{1,0},{2,3},{3,2},{4,5},{5,4},{6,7},{7,6},{8,9},{9,8},{10,11... | collective-permute-start | bytes 3145736 | tf_op jit(solution)/shard_map/ppermute | solution.py:652
  469.7 32.6 %collective-permute-start.51 = (bf16[256,2048]{1,0:T(8,128)(2,1)}, bf16[256,2048]{1,0:T(8,128)(2,1)}, u32[]{:S(2)}, u32[]{:S(2)}) collective-permute-start(bf16[256,2048]{1,0:T(8,128)(2,1)} %get-tuple-element.601), channel_id=1, source_target_pairs={{0,1},{1,0},{2,3},{3,2},{4,5},{5,4},{6,7},{7,6},{8,9},{9,8},{10,11... | collective-permute-start | bytes 3145736 | tf_op jit(solution)/shard_map/ppermute | solution.py:652
  473.7 28.6 %collective-permute-start.52 = (bf16[256,2048]{1,0:T(8,128)(2,1)}, bf16[256,2048]{1,0:T(8,128)(2,1)}, u32[]{:S(2)}, u32[]{:S(2)}) collective-permute-start(bf16[256,2048]{1,0:T(8,128)(2,1)} %add_convert_fusion.4), channel_id=1, source_target_pairs={{2,4},{3,5},{4,2},{5,3},{10,12},{11,13},{12,10},{13,11},{18,20},{1... | collective-permute-start | bytes 3145736 | tf_op jit(solution)/shard_map/ppermute | solution.py:652
  476.8 29.9 %collective-permute-start.53 = (bf16[256,2048]{1,0:T(8,128)(2,1)}, bf16[256,2048]{1,0:T(8,128)(2,1)}, u32[]{:S(2)}, u32[]{:S(2)}) collective-permute-start(bf16[256,2048]{1,0:T(8,128)(2,1)} %add_convert_fusion.3), channel_id=1, source_target_pairs={{0,2},{1,3},{2,0},{3,1},{4,6},{5,7},{6,4},{7,5},{8,10},{9,11},{10,... | collective-permute-start | bytes 3145736 | tf_op jit(solution)/shard_map/ppermute | solution.py:652
  482.3 59.4 %all-to-all-start.3 = ((bf16[8,64,1408]{2,1,0:T(8,128)(2,1)}), bf16[8,64,1408]{2,1,0:T(8,128)(2,1)S(1)}, u32[]{:S(2)}, u32[]{:S(2)}) async-start(bf16[8,64,1408]{2,1,0:T(8,128)(2,1)} %pack_rows.2), calls=%async_computation.3 | async-start | bytes 2883584 | tf_op jit(solution)/shard_map/all_to_all | solution.py:817
  541.7 42.0 %all-to-all-start.2 = ((bf16[8,64,1792]{2,1,0:T(8,128)(2,1)}), bf16[8,64,1792]{2,1,0:T(8,128)(2,1)S(1)}, u32[]{:S(2)}, u32[]{:S(2)}) async-start(bf16[8,64,1792]{2,1,0:T(8,128)(2,1)} %pack_rows.3), calls=%async_computation.2 | async-start | bytes 3670016 | tf_op jit(solution)/shard_map/all_to_all | solution.py:838
  (80 other events, 1629.9 us)

commit v6 on v5

--- a/solution.py
+++ b/solution.py
@@ -9,6 +9,7 @@
 
 HD = 64
 ROT = 16
+ATTEND_ROWS = 512
 EPSILON = 1e-05
 THETA = 10000.0
 NEGATIVE = -1e30
@@ -50,66 +51,60 @@
 
 
 def attend_forward(
-    length_ref, slot_ref, joined_ref, cos_ref, sin_ref, wide_ref, rot_ref, attn_ref, lse_ref, total
+    length_ref, slot_ref, joined_ref, cos_ref, sin_ref, wide_ref, rot_ref, attn_ref, lse_ref
 ):
     parts, _, rows, triple = joined_ref.shape
     width = triple // 3
     length = parts * rows
-    seq = pl.program_id(0)
-    head = pl.program_id(1)
-    alive_count = length_ref[seq]
-    block = min(256, length)
-    lane = lax.broadcasted_iota(jnp.int32, (1, width), 1)
-    mine = (lane // HD) == head
-
-    @pl.when(head == 0)
-    def _():
-        for part in range(parts):
-            slot = slot_ref[part]
-            here = slice(part * rows, (part + 1) * rows)
-
-            def rotated(start):
-                x = joined_ref[slot, 0, :, start : start + width]
-                return (x * cos_ref[here, :] + partner(x) * sin_ref[here, :]).astype(BF)
-
-            rot_ref[part, 0, :, :width] = rotated(0) * 0.125
-            rot_ref[part, 0, :, width : 2 * width] = rotated(width)
-            rot_ref[part, 0, :, 2 * width :] = joined_ref[slot, 0, :, 2 * width :].astype(BF)
-        total[...] = jnp.zeros_like(total)
-        lse_ref[...] = jnp.zeros_like(lse_ref)
-
-    per = block // rows if block >= rows else 1
+    alive_count = length_ref[pl.program_id(0)]
+    per = max(1, min(ATTEND_ROWS, length) // rows)
     block = per * rows
+    for part in range(parts):
+        slot = slot_ref[part]
+        here = slice(part * rows, (part + 1) * rows)
+
+        def rotated(start):
+            x = joined_ref[slot, 0, :, start : start + width]
+            return (x * cos_ref[here, :] + partner(x) * sin_ref[here, :]).astype(BF)
+
+        rot_ref[part, 0, :, :width] = rotated(0) * 0.125
+        rot_ref[part, 0, :, width : 2 * width] = rotated(width)
+        rot_ref[part, 0, :, 2 * width :] = joined_ref[slot, 0, :, 2 * width :].astype(BF)
+    lse_ref[...] = jnp.zeros_like(lse_ref)
+    heads = width // HD
     for step in range(length // block):
         begin, end = step * per, (step + 1) * per
         stop = end * rows
+        slots = [slot_ref[part] for part in range(begin, end)]
+
+        @pl.when(begin * rows >= alive_count)
+        def _(slots=slots):
+            for slot in slots:
+                attn_ref[slot, 0] = jnp.zeros((rows, width), BF)
 
         @pl.when(begin * rows < alive_count)
-        def _(begin=begin, end=end, stop=stop):
-            q = rot_ref[begin:end, 0, :, :width].reshape(block, width)
-            q = jnp.where(mine, q, jnp.zeros_like(q))
-            k = rot_ref[:end, 0, :, width : 2 * width].reshape(stop, width)
-            v = rot_ref[:end, 0, :, 2 * width :].reshape(stop, width)
-            scores = dot_last(q, k)
+        def _(begin=begin, end=end, stop=stop, slots=slots):
             q_pos = begin * rows + lax.broadcasted_iota(jnp.int32, (block, 1), 0)
             k_pos = lax.broadcasted_iota(jnp.int32, (block, stop), 1)
-            scores = jnp.where(k_pos <= q_pos, scores, NEGATIVE)
-            top = jnp.max(scores, axis=1, keepdims=True)
-            expo = jnp.exp(scores - top)
-            weight = jnp.sum(expo, axis=1, keepdims=True)
-            out = dot(expo.astype(BF), v) / weight
+            allowed = k_pos <= q_pos
             alive = q_pos < alive_count
-            here = slice(begin * rows, stop)
-            total[here, :] += jnp.where(mine & alive, out, 0.0)
-            lse = jnp.where(alive, top + jnp.log(weight), 0.0)
-            spot = lax.broadcasted_iota(jnp.int32, (1, lse_ref.shape[3]), 1) == head
-            held = lse_ref[begin:end, 0].reshape(block, lse_ref.shape[3])
-            lse_ref[begin:end, 0] = jnp.where(spot, lse, held).reshape(per, rows, -1)
-
-    @pl.when(head == pl.num_programs(1) - 1)
-    def _():
-        for part in range(parts):
-            attn_ref[slot_ref[part], 0] = total[part * rows : (part + 1) * rows, :].astype(BF)
+            for head in range(heads):
+                lane = head * HD
+                q = rot_ref[begin:end, 0, :, lane : lane + HD].reshape(block, HD)
+                lane += width
+                k = rot_ref[:end, 0, :, lane : lane + HD].reshape(stop, HD)
+                lane += width
+                v = rot_ref[:end, 0, :, lane : lane + HD].reshape(stop, HD)
+                scores = jnp.where(allowed, dot_last(q, k), NEGATIVE)
+                top = jnp.max(scores, axis=1, keepdims=True)
+                expo = jnp.exp(scores - top)
+                weight = jnp.sum(expo, axis=1, keepdims=True)
+                out = jnp.where(alive, dot(expo.astype(BF), v) / weight, 0.0).astype(BF)
+                for index, slot in enumerate(slots):
+                    there = slice(index * rows, (index + 1) * rows)
+                    attn_ref[slot, 0, :, head * HD : (head + 1) * HD] = out[there, :]
+                lse = jnp.where(alive, top + jnp.log(weight), 0.0)
+                lse_ref[begin:end, 0, :, head : head + 1] = lse.reshape(per, rows, 1)
 
 
 def attend_backward(
@@ -121,7 +116,7 @@
     seq = pl.program_id(0)
     head = pl.program_id(1)
     alive_count = length_ref[seq]
-    per = max(1, min(256, length) // rows)
+    per = max(1, min(ATTEND_ROWS, length) // rows)
     block = per * rows
     lane = lax.broadcasted_iota(jnp.int32, (1, width), 1)
     mine = (lane // HD) == head
@@ -181,9 +176,9 @@
     smem = pl.BlockSpec(memory_space=pltpu.SMEM)
 
     def spec(last):
-        return pl.BlockSpec((parts, 1, rows, last), lambda s, h: (0, s, 0, 0))
-
-    table = pl.BlockSpec((length, width), lambda s, h: (0, 0))
+        return pl.BlockSpec((parts, 1, rows, last), lambda s, *_: (0, s, 0, 0))
+
+    table = pl.BlockSpec((length, width), lambda *_: (0, 0))
 
     def shape(last, dtype):
         return jax.ShapeDtypeStruct((parts, groups, rows, last), dtype)
@@ -192,11 +187,10 @@
     params = pltpu.CompilerParams(vmem_limit_bytes=48 * 1024 * 1024)
     forward = pl.pallas_call(
         attend_forward,
-        grid=(groups, heads),
+        grid=(groups,),
         in_specs=[smem, smem, spec(3 * width), table, table, pl.BlockSpec(memory_space=pl.ANY)],
         out_specs=[spec(3 * width), spec(width), spec(heads)],
         out_shape=[shape(3 * width, BF), shape(lanes, BF), shape(heads, F32)],
-        scratch_shapes=[pltpu.VMEM((length, width), F32)],
         input_output_aliases={5: 1},
         compiler_params=params,
         cost_estimate=pl.CostEstimate(

time: 592 us -> 585 us (0.988)
  Pallas kernels: 156 us -> 146 us
    pallas_call x1, Pallas kernels: 22.6 us -> 14.9 us  [attend(): self.calls(lanes)[0]]
  transfers between devices with their start and end apart: 64 -> 64, of which waited for: 29 -> 29; matrix products, arithmetic and copies ran while one was open for 16% -> 16% of each run, Pallas kernels for 26% -> 25%
where the time goes in v6:
time: 585 us; the launch traced here: 576 us
  waiting for transfers between devices  238 us (41%)
  Pallas kernels  146 us (25%)
  starting transfers between devices  94.3 us (16%)
  matrix products  53.2 us (9%)
  other arithmetic  36.4 us (6%)
  local copies, waits for them, and re-layouts  6.44 us (1%)
    ppermute x44, waiting for transfers between devices, tick(): view[name] = lax.ppermute(self.held[source], axis, pairs)  105 us
    ppermute x44, starting transfers between devices, tick(): view[name] = lax.ppermute(self.held[source], axis, pairs)  55 us
    dot_general x9, matrix products, dot_first(): return lax.dot_general(left, right, FIRST, preferred_element_type=F32)  53.2 us
    pallas_call x3, Pallas kernels, stream(): pl.pallas_call(functools.partial(stream_kernel, n, len(pieces), len(extra...  50.6 us
    pallas_call x3, Pallas kernels, spread(): pl.pallas_call(functools.partial(spread_kernel, len(lefts), len(pieces),...  45.9 us
    all_to_all x1, waiting for transfers between devices, begin(): lax.all_to_all(packed, 'ctx', split_axis=0, concat_axis=0, tiled=True)  39.5 us
    all_to_all x1, waiting for transfers between devices, norm_back(): lax.all_to_all(packed, 'ctx', split_axis=0, concat_axis=0, tiled=True)  26.7 us
    ppermute x5, waiting for transfers between devices, halved(): lax.ppermute(give, axis, swaps(bit, size))  25.6 us
  transfers between devices with their start and end apart: 64, of which 29 were waited for; matrix products, arithmetic and copies ran while one was open for 16% of the time, Pallas kernels for 25%

profile of v6, /device:TPU:0, one launch (start us, length us, event | category | flops | bytes accessed | tf_op | source)
XLA Modules:
  0.0 576.2 jit_solution(15955003568704555841)
XLA Ops:
  15.3 5.4 all-to-all-start
  33.8 39.5 %all-to-all-done.in_ref = bf16[8,64,2176]{2,1,0:T(8,128)(2,1)} async-done(((bf16[8,64,2176]{2,1,0:T(8,128)(2,1)}), bf16[8,64,2176]{2,1,0:T(8,128)(2,1)}, u32[]{:S(2)}, u32[]{:S(2)}) %all-to-all-start) | async-done | bytes 2228256 | tf_op jit(solution)/shard_map/all_to_all | solution.py:693
  76.8 6.1 %collective-permute-done.4.refs_2_ = bf16[256,2048]{1,0:T(8,128)(2,1)} collective-permute-done((bf16[256,2048]{1,0:T(8,128)(2,1)}, bf16[256,2048]{1,0:T(8,128)(2,1)}, u32[]{:S(2)}, u32[]{:S(2)}) %collective-permute-start.4) | collective-permute-done | bytes 1048608 | tf_op jit(solution)/shard_map/ppermute | solution.py:694
  82.9 6.6 %collective-permute-done.7.refs_1_ = bf16[256,2048]{1,0:T(8,128)(2,1)} collective-permute-done((bf16[256,2048]{1,0:T(8,128)(2,1)S(1)}, bf16[256,2048]{1,0:T(8,128)(2,1)}, u32[]{:S(2)}, u32[]{:S(2)}) %collective-permute-start.7) | collective-permute-done | bytes 1048608 | tf_op jit(solution)/shard_map/ppermute | solution.py:699
  89.5 12.0 %collective-permute-done.8.refs_2_ = bf16[256,2048]{1,0:T(8,128)(2,1)} collective-permute-done((bf16[256,2048]{1,0:T(8,128)(2,1)S(1)}, bf16[256,2048]{1,0:T(8,128)(2,1)}, u32[]{:S(2)}, u32[]{:S(2)}) %collective-permute-start.8) | collective-permute-done | bytes 1048608 | tf_op jit(solution)/shard_map/ppermute | solution.py:700
  107.4 5.6 fusion.48
  113.0 15.6 %collective-permute-done.10.refs_3_ = bf16[256,2048]{1,0:T(8,128)(2,1)} collective-permute-done((bf16[256,2048]{1,0:T(8,128)(2,1)}, bf16[256,2048]{1,0:T(8,128)(2,1)}, u32[]{:S(2)}, u32[]{:S(2)}) %collective-permute-start.10) | collective-permute-done | bytes 1048608 | tf_op jit(solution)/shard_map/ppermute | solution.py:646
  128.6 5.1 collective-permute-done.12
  139.7 7.4 %all-to-all-start.1 = ((bf16[8,64,1024]{2,1,0:T(8,128)(2,1)}), bf16[8,64,1024]{2,1,0:T(8,128)(2,1)S(1)}, u32[]{:S(2)}, u32[]{:S(2)}) async-start(bf16[8,64,1024]{2,1,0:T(8,128)(2,1)} %pack_columns.3), calls=%async_computation.1 | async-start | bytes 2097152 | tf_op jit(solution)/shard_map/all_to_all | solution.py:705
  147.2 15.9 %collective-permute-done.15.refs_1_ = bf16[256,2048]{1,0:T(8,128)(2,1)} collective-permute-done((bf16[256,2048]{1,0:T(8,128)(2,1)S(1)}, bf16[256,2048]{1,0:T(8,128)(2,1)}, u32[]{:S(2)}, u32[]{:S(2)}) %collective-permute-start.15) | collective-permute-done | bytes 1048608 | tf_op jit(solution)/shard_map/ppermute | solution.py:646
  163.0 7.5 %collective-permute-done.16 = bf16[256,2048]{1,0:T(8,128)(2,1)} collective-permute-done((bf16[256,2048]{1,0:T(8,128)(2,1)}, bf16[256,2048]{1,0:T(8,128)(2,1)}, u32[]{:S(2)}, u32[]{:S(2)}) %collective-permute-start.16) | collective-permute-done | bytes 1048608 | tf_op jit(solution)/shard_map/ppermute | solution.py:646
  177.3 13.6 %all-to-all-done.1.in_ref = bf16[8,64,1024]{2,1,0:T(8,128)(2,1)S(1)} async-done(((bf16[8,64,1024]{2,1,0:T(8,128)(2,1)}), bf16[8,64,1024]{2,1,0:T(8,128)(2,1)S(1)}, u32[]{:S(2)}, u32[]{:S(2)}) %all-to-all-start.1) | async-done | bytes 1048608 | tf_op jit(solution)/shard_map/all_to_all | solution.py:705
  192.1 16.7 %project.2 = (bf16[2048,2048]{1,0:T(8,128)(2,1)}, f32[2048,768]{1,0:T(8,128)}, bf16[2048,1408]{1,0:T(8,128)(2,1)}, bf16[2048,1024]{1,0:T(8,128)(2,1)}) custom-call(bf16[256,2048]{1,0:T(8,128)(2,1)S(1)} %copy-done.4, bf16[256,2048]{1,0:T(8,128)(2,1)} %collective-permute-done.7.refs_1_, bf16[256,2048]{1,0:T(8,128)(2,1)} %collective-permute-done.8.refs_2_, ...), custom_call_target="tpu_custom_call" | custom-call | flops 9126805504 | bytes 26214400 | tf_op jit(solution)/shard_map/project/pallas_call | solution.py:397
  216.6 16.6 %project.3 = (bf16[2048,2048]{1,0:T(8,128)(2,1)}, f32[2048,768]{1,0:T(8,128)}, bf16[2048,1408]{1,0:T(8,128)(2,1)}, bf16[2048,1024]{1,0:T(8,128)(2,1)}) custom-call(bf16[256,2048]{1,0:T(8,128)(2,1)S(1)} %broadcast_select_fusion.3.refs_0_, ...), custom_call_target="tpu_custom_call", output_to_operand_aliasing={{0}: (11, {}), {1}: (12, {}), {2}: (13, {}), {3}: (14, {})} | custom-call | flops 9126805504 | bytes 26214400 | tf_op jit(solution)/shard_map/project/pallas_call | solution.py:397
  233.3 6.6 %collective-permute-done.24.refs_5_ = bf16[256,2048]{1,0:T(8,128)(2,1)S(1)} collective-permute-done((bf16[256,2048]{1,0:T(8,128)(2,1)S(1)}, bf16[256,2048]{1,0:T(8,128)(2,1)S(1)}, u32[]{:S(2)}, u32[]{:S(2)}) %collective-permute-start.24) | collective-permute-done | bytes 1048608 | tf_op jit(solution)/shard_map/ppermute | solution.py:646
  245.3 14.9 %attend_forward.1 = (bf16[8,2,128,768]{3,2,1,0:T(8,128)(2,1)}, bf16[8,2,128,1024]{3,2,1,0:T(8,128)(2,1)}, f32[8,2,128,4]{3,2,1,0:T(8,128)S(1)}) custom-call(s32[2]{0:T(128)S(1)} %copy-done.11, s32[8]{0:T(128)S(1)} %compare_select_fusion.8.slot_ref, f32[8,2,128,768]{3,2,1,0:T(8,128)} %bitcast.53, ...), custom_call_target="tpu_custom_call", output_to_operand_aliasing={{1}: (5, {})} | custom-call | flops 4294967296 | bytes 4194304 | tf_op jit(solution)/shard_map/attend_forward/pallas_call | solution.py:552
  261.2 14.4 %output_part.1 = (bf16[256,2048]{1,0:T(8,128)(2,1)S(1)}, bf16[256,2048]{1,0:T(8,128)(2,1)}, bf16[256,2048]{1,0:T(8,128)(2,1)}, bf16[256,2048]{1,0:T(8,128)(2,1)}...) custom-call(bf16[2048,1024]{1,0:T(8,128)(2,1)} %bitcast.55, ...), custom_call_target="tpu_custom_call" | custom-call | flops 8589934592 | bytes 16777216 | tf_op jit(solution)/shard_map/output_part/pallas_call | solution.py:497
  278.0 17.4 %bring_back.1 = (bf16[2048,2048]{1,0:T(8,128)(2,1)}, bf16[2048,256]{1,0:T(8,128)(2,1)S(1)}, bf16[2048,1408]{1,0:T(8,128)(2,1)}) custom-call(bf16[256,2048]{1,0:T(8,128)(2,1)} %pad_maximum_fusion.refs_0_, bf16[256,2048]{1,0:T(8,128)(2,1)} %collective-permute-done.3.refs_1_, bf16[256,2048]{1,0:T(8,128)(2,1)} %collective-permute-done.4.refs_2_, ...), custom_call_target="tpu_custom_call" | custom-call | flops 8589934592 | bytes 25165824 | tf_op jit(solution)/shard_map/bring_back/pallas_call | solution.py:397
  295.5 11.7 %fusion.6 = bf16[1024,1408]{1,0:T(8,128)(2,1)} fusion(bf16[2048,1408]{1,0:T(8,128)(2,1)} %get-tuple-element.545.refs_1_.refs_3_, bf16[2048,2048]{1,0:T(8,128)(2,1)} %get-tuple-element.580), kind=kOutput, calls=%fused_computation.6 | convolution fusion | flops 5907021824 | bytes 12845056 | tf_op jit(solution)/shard_map/dot_general | solution.py:31
  311.5 21.4 %attend_backward.1 = bf16[8,2,128,768]{3,2,1,0:T(8,128)(2,1)} custom-call(s32[2]{0:T(128)S(1)} %copy-done.11, s32[8]{0:T(128)S(1)} %compare_select_fusion.8.slot_ref, bf16[8,2,128,768]{3,2,1,0:T(8,128)(2,1)} %get-tuple-element.491.rot_ref, bf16[8,2,128,1024]{3,2,1,0:T(8,128)(2,1)} %get-tuple-element.424, bf16[8,2,128,256]{3,2,1,0:T(8,128)(2,1)S(1)} %bitcast.52, ...), custom_call_target="tpu_custom_call" | custom-call | flops 10737418240 | bytes 4194304 | tf_op jit(solution)/shard_map/attend_backward/pallas_call | solution.py:559
  332.9 7.2 %fusion.10 = bf16[512,1408]{1,0:T(8,128)(2,1)S(1)} fusion(bf16[2048,1408]{1,0:T(8,128)(2,1)} %get-tuple-element.545.refs_1_.refs_3_, bf16[2048,2048]{1,0:T(8,128)(2,1)} %get-tuple-element.580, bf16[1024,1408]{1,0:T(8,128)(2,1)} %collective-permute-done.35), kind=kOutput, calls=%fused_computation.10 | convolution fusion | flops 2954952704 | bytes 10747904 | tf_op jit(solution)/shard_map/dot_general | solution.py:31
  346.3 15.7 %normed_part.2 = (bf16[256,2048]{1,0:T(8,128)(2,1)S(1)}, bf16[256,2048]{1,0:T(8,128)(2,1)}, bf16[256,2048]{1,0:T(8,128)(2,1)}, bf16[256,2048]{1,0:T(8,128)(2,1)}) custom-call(bf16[2048,768]{1,0:T(8,128)(2,1)} %bitcast.82, bf16[2048,1408]{1,0:T(8,128)(2,1)} %get-tuple-element.545.refs_1_.refs_3_, bf16[2048,768]{1,0:T(8,128)(2,1)} %bitcast.83, ...), custom_call_target="tpu_custom_call" | custom-call | flops 9126805504 | bytes 17563648 | tf_op jit(solution)/shard_map/normed_part/pallas_call | solution.py:497
  365.9 11.2 %collective-permute-done.39 = bf16[512,1408]{1,0:T(8,128)(2,1)S(1)} collective-permute-done((bf16[512,1408]{1,0:T(8,128)(2,1)S(1)}, bf16[512,1408]{1,0:T(8,128)(2,1)S(1)}, u32[]{:S(2)}, u32[]{:S(2)}) %collective-permute-start.39) | collective-permute-done | bytes 1441824 | tf_op jit(solution)/shard_map/ppermute | solution.py:646
  381.3 7.2 %fusion.11.refs_0_ = bf16[512,1408]{1,0:T(8,128)(2,1)S(1)} fusion(bf16[2048,1408]{1,0:T(8,128)(2,1)} %get-tuple-element.545.refs_1_.refs_3_, bf16[512,1408]{1,0:T(8,128)(2,1)S(1)} %copy-done.37, bf16[2048,2048]{1,0:T(8,128)(2,1)} %get-tuple-element.580, bf16[1024,1408]{1,0:T(8,128)(2,1)} %collective-permute-done.35), kind=kOutput, calls=%fused_computation.11 | convolution fusion | flops 2956394496 | bytes 12189696 | tf_op jit(solution)/shard_map/dot_general | solution.py:31
  389.7 15.8 %normed_part.3 = (bf16[256,2048]{1,0:T(8,128)(2,1)S(1)}, bf16[256,2048]{1,0:T(8,128)(2,1)}, bf16[256,2048]{1,0:T(8,128)(2,1)}, bf16[256,2048]{1,0:T(8,128)(2,1)}) custom-call(bf16[2048,768]{1,0:T(8,128)(2,1)} %bitcast.84, bf16[2048,1408]{1,0:T(8,128)(2,1)} %get-tuple-element.545.refs_1_.refs_3_, bf16[2048,768]{1,0:T(8,128)(2,1)} %bitcast.85, ...), custom_call_target="tpu_custom_call" | custom-call | flops 9126805504 | bytes 17563648 | tf_op jit(solution)/shard_map/normed_part/pallas_call | solution.py:497
  410.5 5.7 fusion.35
  439.3 12.3 %collective-permute-done.49 = bf16[512,768]{1,0:T(8,128)(2,1)S(1)} collective-permute-done((bf16[512,768]{1,0:T(8,128)(2,1)S(1)}, bf16[512,768]{1,0:T(8,128)(2,1)S(1)}, u32[]{:S(2)}, u32[]{:S(2)}) %collective-permute-start.49) | collective-permute-done | bytes 786464 | tf_op jit(solution)/shard_map/ppermute | solution.py:646
  467.0 5.5 collective-permute-start.53
  476.1 9.7 %collective-permute-done.54 = bf16[512,1024]{1,0:T(8,128)(2,1)} collective-permute-done((bf16[512,1024]{1,0:T(8,128)(2,1)}, bf16[512,1024]{1,0:T(8,128)(2,1)}, u32[]{:S(2)}, u32[]{:S(2)}) %collective-permute-start.54) | collective-permute-done | bytes 1048608 | tf_op jit(solution)/shard_map/ppermute | solution.py:646
  485.7 5.8 %add_convert_fusion.2.refs_1_ = bf16[512,1024]{1,0:T(8,128)(2,1)S(1)} fusion(bf16[512,1024]{1,0:T(8,128)(2,1)} %collective-permute-done.54, bf16[2048,1024]{1,0:T(8,128)(2,1)} %bitcast.59, bf16[2048,2048]{1,0:T(8,128)(2,1)} %get-tuple-element.598, bf16[1024,1024]{1,0:T(8,128)(2,1)} %copy-done.35), kind=kOutput, calls=%fused_computation.29 | convolution fusion | flops 2150105088 | bytes 9437184 | tf_op jit(solution)/shard_map/dot_general | solution.py:31
  506.8 17.5 %collective-permute-done.55 = f32[4,4,128]{2,1,0:T(4,128)S(1)} collective-permute-done((f32[4,4,128]{2,1,0:T(4,128)S(1)}, f32[4,4,128]{2,1,0:T(4,128)S(1)}, u32[]{:S(2)}, u32[]{:S(2)}) %collective-permute-start.55) | collective-permute-done | bytes 8224 | tf_op jit(solution)/shard_map/ppermute | solution.py:825
  547.1 26.7 %all-to-all-done.2.held = bf16[8,64,1792]{2,1,0:T(8,128)(2,1)S(1)} async-done(((bf16[8,64,1792]{2,1,0:T(8,128)(2,1)}), bf16[8,64,1792]{2,1,0:T(8,128)(2,1)S(1)}, u32[]{:S(2)}, u32[]{:S(2)}) %all-to-all-start.2) | async-done | bytes 1835040 | tf_op jit(solution)/shard_map/all_to_all | solution.py:832
  (288 shorter events, 173.6 us)
Async XLA Ops:
  15.3 58.0 %all-to-all-start = ((bf16[8,64,2176]{2,1,0:T(8,128)(2,1)}), bf16[8,64,2176]{2,1,0:T(8,128)(2,1)}, u32[]{:S(2)}, u32[]{:S(2)}) async-start(bf16[8,64,2176]{2,1,0:T(8,128)(2,1)} %pack_columns.2), calls=%async_computation | async-start | bytes 4456448 | tf_op jit(solution)/shard_map/all_to_all | solution.py:693
  24.4 52.4 %collective-permute-start.3 = (bf16[256,2048]{1,0:T(8,128)(2,1)}, bf16[256,2048]{1,0:T(8,128)(2,1)}, u32[]{:S(2)}, u32[]{:S(2)}) collective-permute-start(bf16[256,2048]{1,0:T(8,128)(2,1)} %pad_maximum_fusion.refs_0_), channel_id=1, source_target_pairs={{0,1},{1,0},{2,3},{3,2},{4,5},{5,4},{6,7},{7,6},{8,9},{9,8},{10,11... | collective-permute-start | bytes 3145736 | tf_op jit(solution)/shard_map/ppermute | solution.py:694
  26.4 56.5 %collective-permute-start.4 = (bf16[256,2048]{1,0:T(8,128)(2,1)}, bf16[256,2048]{1,0:T(8,128)(2,1)}, u32[]{:S(2)}, u32[]{:S(2)}) collective-permute-start(bf16[256,2048]{1,0:T(8,128)(2,1)} %pad_maximum_fusion.refs_0_), channel_id=1, source_target_pairs={{0,2},{1,3},{2,0},{3,1},{4,6},{5,7},{6,4},{7,5},{8,10},{9,11},{10,... | collective-permute-start | bytes 3145736 | tf_op jit(solution)/shard_map/ppermute | solution.py:694
  30.1 59.4 %collective-permute-start.7 = (bf16[256,2048]{1,0:T(8,128)(2,1)S(1)}, bf16[256,2048]{1,0:T(8,128)(2,1)}, u32[]{:S(2)}, u32[]{:S(2)}) collective-permute-start(bf16[256,2048]{1,0:T(8,128)(2,1)S(1)} %pad_maximum_fusion.1.refs_0_), channel_id=1, source_target_pairs={{0,1},{1,0},{2,3},{3,2},{4,5},{5,4},{6,7},{7,6},{8,9},{9,8},{10,11... | collective-permute-start | bytes 3145736 | tf_op jit(solution)/shard_map/ppermute | solution.py:699
  30.7 70.7 %collective-permute-start.8 = (bf16[256,2048]{1,0:T(8,128)(2,1)S(1)}, bf16[256,2048]{1,0:T(8,128)(2,1)}, u32[]{:S(2)}, u32[]{:S(2)}) collective-permute-start(bf16[256,2048]{1,0:T(8,128)(2,1)S(1)} %pad_maximum_fusion.1.refs_0_), channel_id=1, source_target_pairs={{0,2},{1,3},{2,0},{3,1},{4,6},{5,7},{6,4},{7,5},{8,10},{9,11},{10,... | collective-permute-start | bytes 3145736 | tf_op jit(solution)/shard_map/ppermute | solution.py:700
  31.7 69.8 %collective-permute-start.9 = (bf16[256,2048]{1,0:T(8,128)(2,1)S(1)}, bf16[256,2048]{1,0:T(8,128)(2,1)S(1)}, u32[]{:S(2)}, u32[]{:S(2)}) collective-permute-start(bf16[256,2048]{1,0:T(8,128)(2,1)S(1)} %pad_maximum_fusion.1.refs_0_), channel_id=1, source_target_pairs={{2,4},{3,5},{4,2},{5,3},{10,12},{11,13},{12,10},{13,11},{18,20},{1... | collective-permute-start | bytes 3145736 | tf_op jit(solution)/shard_map/ppermute | solution.py:700
  101.5 32.2 %collective-permute-start.14 = (bf16[512,2176]{1,0:T(8,128)(2,1)}, bf16[512,2176]{1,0:T(8,128)(2,1)}, u32[]{:S(2)}, u32[]{:S(2)}) collective-permute-start(bf16[512,2176]{1,0:T(8,128)(2,1)} %get-tuple-element.335), channel_id=1, source_target_pairs={{0,8},{8,0},{16,24},{24,16},{1,9},{9,1},{17,25},{25,17},{2,10},{10... | collective-permute-start | bytes 6684680 | tf_op jit(solution)/shard_map/ppermute | solution.py:646
  101.5 32.2 %collective-permute-start.13 = (bf16[256,2176]{1,0:T(8,128)(2,1)S(1)}, bf16[256,2176]{1,0:T(8,128)(2,1)}, u32[]{:S(2)}, u32[]{:S(2)}) collective-permute-start(bf16[256,2176]{1,0:T(8,128)(2,1)S(1)} %get-tuple-element.533.refs_4_), channel_id=1, source_target_pairs={{0,16},{8,24},{16,0},{24,8},{1,17},{9,25},{17,1},{25,9},{2,18},{10... | collective-permute-start | bytes 3342344 | tf_op jit(solution)/shard_map/ppermute | solution.py:646
  106.1 27.6 %collective-permute-start.12 = (bf16[256,2048]{1,0:T(8,128)(2,1)S(1)}, bf16[256,2048]{1,0:T(8,128)(2,1)S(1)}, u32[]{:S(2)}, u32[]{:S(2)}) collective-permute-start(bf16[256,2048]{1,0:T(8,128)(2,1)S(1)} %collective-permute-done.9), channel_id=1, source_target_pairs={{2,0},{3,1},{4,6},{5,7},{10,8},{11,9},{12,14},{13,15},{18,16},{19,... | collective-permute-start | bytes 3145736 | tf_op jit(solution)/shard_map/ppermute | solution.py:646
  133.7 36.9 %collective-permute-start.18 = (bf16[256,2176]{1,0:T(8,128)(2,1)}, bf16[256,2176]{1,0:T(8,128)(2,1)}, u32[]{:S(2)}, u32[]{:S(2)}) collective-permute-start(bf16[256,2176]{1,0:T(8,128)(2,1)} %get-tuple-element.534.refs_5_), channel_id=1, source_target_pairs={{0,16},{8,24},{16,0},{24,8},{1,17},{9,25},{17,1},{25,9},{2,18},{10... | collective-permute-start | bytes 3342344 | tf_op jit(solution)/shard_map/ppermute | solution.py:646
  134.7 35.9 %collective-permute-start.19 = (bf16[256,2176]{1,0:T(8,128)(2,1)}, bf16[256,2176]{1,0:T(8,128)(2,1)}, u32[]{:S(2)}, u32[]{:S(2)}) collective-permute-start(bf16[256,2176]{1,0:T(8,128)(2,1)} %collective-permute-done.13.refs_6_), channel_id=1, source_target_pairs={{0,8},{8,0},{16,24},{24,16},{1,9},{9,1},{17,25},{25,17},{2,10},{10... | collective-permute-start | bytes 3342344 | tf_op jit(solution)/shard_map/ppermute | solution.py:646
  136.8 33.8 %collective-permute-start.16 = (bf16[256,2048]{1,0:T(8,128)(2,1)}, bf16[256,2048]{1,0:T(8,128)(2,1)}, u32[]{:S(2)}, u32[]{:S(2)}) collective-permute-start(bf16[256,2048]{1,0:T(8,128)(2,1)} %collective-permute-done.11), channel_id=1, source_target_pairs={{2,0},{3,1},{4,6},{5,7},{10,8},{11,9},{12,14},{13,15},{18,16},{19,... | collective-permute-start | bytes 3145736 | tf_op jit(solution)/shard_map/ppermute | solution.py:646
  138.0 32.5 %collective-permute-start.17 = (bf16[256,2048]{1,0:T(8,128)(2,1)}, bf16[256,2048]{1,0:T(8,128)(2,1)}, u32[]{:S(2)}, u32[]{:S(2)}) collective-permute-start(bf16[256,2048]{1,0:T(8,128)(2,1)} %pad_maximum_fusion.refs_0_), channel_id=1, source_target_pairs={{2,4},{3,5},{4,2},{5,3},{10,12},{11,13},{12,10},{13,11},{18,20},{1... | collective-permute-start | bytes 3145736 | tf_op jit(solution)/shard_map/ppermute | solution.py:646
  139.7 51.1 %all-to-all-start.1 = ((bf16[8,64,1024]{2,1,0:T(8,128)(2,1)}), bf16[8,64,1024]{2,1,0:T(8,128)(2,1)S(1)}, u32[]{:S(2)}, u32[]{:S(2)}) async-start(bf16[8,64,1024]{2,1,0:T(8,128)(2,1)} %pack_columns.3), calls=%async_computation.1 | async-start | bytes 2097152 | tf_op jit(solution)/shard_map/all_to_all | solution.py:705
  173.0 35.8 %collective-permute-start.20 = (bf16[256,2048]{1,0:T(8,128)(2,1)}, bf16[256,2048]{1,0:T(8,128)(2,1)}, u32[]{:S(2)}, u32[]{:S(2)}) collective-permute-start(bf16[256,2048]{1,0:T(8,128)(2,1)} %broadcast_select_fusion.2.refs_2_), channel_id=1, source_target_pairs={{0,1},{1,0},{2,3},{3,2},{4,5},{5,4},{6,7},{7,6},{8,9},{9,8},{10,11... | collective-permute-start | bytes 3145736 | tf_op jit(solution)/shard_map/ppermute | solution.py:646
  174.3 39.0 %collective-permute-start.21 = (bf16[256,2048]{1,0:T(8,128)(2,1)}, bf16[256,2048]{1,0:T(8,128)(2,1)}, u32[]{:S(2)}, u32[]{:S(2)}) collective-permute-start(bf16[256,2048]{1,0:T(8,128)(2,1)} %collective-permute-done.17), channel_id=1, source_target_pairs={{2,0},{3,1},{4,6},{5,7},{10,8},{11,9},{12,14},{13,15},{18,16},{19,... | collective-permute-start | bytes 3145736 | tf_op jit(solution)/shard_map/ppermute | solution.py:646
  175.6 37.7 %collective-permute-start.22 = (bf16[256,2048]{1,0:T(8,128)(2,1)}, bf16[256,2048]{1,0:T(8,128)(2,1)}, u32[]{:S(2)}, u32[]{:S(2)}) collective-permute-start(bf16[256,2048]{1,0:T(8,128)(2,1)} %collective-permute-done.4.refs_2_), channel_id=1, source_target_pairs={{2,4},{3,5},{4,2},{5,3},{10,12},{11,13},{12,10},{13,11},{18,20},{1... | collective-permute-start | bytes 3145736 | tf_op jit(solution)/shard_map/ppermute | solution.py:646
  190.9 42.3 %collective-permute-start.26 = (bf16[512,1024]{1,0:T(8,128)(2,1)S(1)}, bf16[512,1024]{1,0:T(8,128)(2,1)}, u32[]{:S(2)}, u32[]{:S(2)}) collective-permute-start(bf16[512,1024]{1,0:T(8,128)(2,1)S(1)} %unpack_columns.3.refs_4_.refs_8_), channel_id=1, source_target_pairs={{0,16},{8,24},{16,0},{24,8},{1,17},{9,25},{17,1},{25,9},{2,18},{10... | collective-permute-start | bytes 3145736 | tf_op jit(solution)/shard_map/ppermute | solution.py:646
  192.1 41.2 %collective-permute-start.27 = (bf16[512,1024]{1,0:T(8,128)(2,1)S(1)}, bf16[512,1024]{1,0:T(8,128)(2,1)S(1)}, u32[]{:S(2)}, u32[]{:S(2)}) collective-permute-start(bf16[512,1024]{1,0:T(8,128)(2,1)S(1)} %unpack_columns.3.refs_4_.refs_8_), channel_id=1, source_target_pairs={{0,8},{8,0},{16,24},{24,16},{1,9},{9,1},{17,25},{25,17},{2,10},{10... | collective-permute-start | bytes 3145736 | tf_op jit(solution)/shard_map/ppermute | solution.py:646
  243.5 32.2 %collective-permute-start.28 = (bf16[256,2048]{1,0:T(8,128)(2,1)S(1)}, bf16[256,2048]{1,0:T(8,128)(2,1)S(1)}, u32[]{:S(2)}, u32[]{:S(2)}) collective-permute-start(bf16[256,2048]{1,0:T(8,128)(2,1)S(1)} %broadcast_select_fusion.refs_6_), channel_id=1, source_target_pairs={{0,1},{1,0},{2,3},{3,2},{4,5},{5,4},{6,7},{7,6},{8,9},{9,8},{10,11... | collective-permute-start | bytes 3145736 | tf_op jit(solution)/shard_map/ppermute | solution.py:646
  245.3 30.4 %collective-permute-start.29 = (bf16[256,2048]{1,0:T(8,128)(2,1)}, bf16[256,2048]{1,0:T(8,128)(2,1)S(1)}, u32[]{:S(2)}, u32[]{:S(2)}) collective-permute-start(bf16[256,2048]{1,0:T(8,128)(2,1)} %collective-permute-done.3.refs_1_), channel_id=1, source_target_pairs={{0,2},{1,3},{2,0},{3,1},{4,6},{5,7},{6,4},{7,5},{8,10},{9,11},{10,... | collective-permute-start | bytes 3145736 | tf_op jit(solution)/shard_map/ppermute | solution.py:646
  275.7 31.5 %collective-permute-start.31 = (bf16[256,2048]{1,0:T(8,128)(2,1)}, bf16[256,2048]{1,0:T(8,128)(2,1)S(1)}, u32[]{:S(2)}, u32[]{:S(2)}) collective-permute-start(bf16[256,2048]{1,0:T(8,128)(2,1)} %get-tuple-element.475), channel_id=1, source_target_pairs={{0,1},{1,0},{2,3},{3,2},{4,5},{5,4},{6,7},{7,6},{8,9},{9,8},{10,11... | collective-permute-start | bytes 3145736 | tf_op jit(solution)/shard_map/ppermute | solution.py:646
  276.0 31.2 %collective-permute-start.32 = (bf16[256,2048]{1,0:T(8,128)(2,1)}, bf16[256,2048]{1,0:T(8,128)(2,1)S(1)}, u32[]{:S(2)}, u32[]{:S(2)}) collective-permute-start(bf16[256,2048]{1,0:T(8,128)(2,1)} %get-tuple-element.471), channel_id=1, source_target_pairs={{0,2},{1,3},{2,0},{3,1},{4,6},{5,7},{6,4},{7,5},{8,10},{9,11},{10,... | collective-permute-start | bytes 3145736 | tf_op jit(solution)/shard_map/ppermute | solution.py:646
  307.3 32.9 %collective-permute-start.33 = (bf16[256,2048]{1,0:T(8,128)(2,1)S(1)}, bf16[256,2048]{1,0:T(8,128)(2,1)S(1)}, u32[]{:S(2)}, u32[]{:S(2)}) collective-permute-start(bf16[256,2048]{1,0:T(8,128)(2,1)S(1)} %copy-done.42), channel_id=1, source_target_pairs={{0,1},{1,0},{2,3},{3,2},{4,5},{5,4},{6,7},{7,6},{8,9},{9,8},{10,11... | collective-permute-start | bytes 3145736 | tf_op jit(solution)/shard_map/ppermute | solution.py:646
  309.5 30.7 %collective-permute-start.34 = (bf16[256,2048]{1,0:T(8,128)(2,1)S(1)}, bf16[256,2048]{1,0:T(8,128)(2,1)S(1)}, u32[]{:S(2)}, u32[]{:S(2)}) collective-permute-start(bf16[256,2048]{1,0:T(8,128)(2,1)S(1)} %add_convert_fusion.15), channel_id=1, source_target_pairs={{0,2},{1,3},{6,4},{7,5},{8,10},{9,11},{14,12},{15,13},{16,18},{17,... | collective-permute-start | bytes 3145736 | tf_op jit(solution)/shard_map/ppermute | solution.py:646
  344.0 33.2 %collective-permute-start.39 = (bf16[512,1408]{1,0:T(8,128)(2,1)S(1)}, bf16[512,1408]{1,0:T(8,128)(2,1)S(1)}, u32[]{:S(2)}, u32[]{:S(2)}) collective-permute-start(bf16[512,1408]{1,0:T(8,128)(2,1)S(1)} %fusion.10), channel_id=1, source_target_pairs={{0,16},{8,24},{16,0},{24,8},{1,17},{9,25},{17,1},{25,9},{2,18},{10... | collective-permute-start | bytes 4325384 | tf_op jit(solution)/shard_map/ppermute | solution.py:646
  377.1 28.4 %collective-permute-start.40 = (bf16[256,2048]{1,0:T(8,128)(2,1)}, bf16[256,2048]{1,0:T(8,128)(2,1)S(1)}, u32[]{:S(2)}, u32[]{:S(2)}) collective-permute-start(bf16[256,2048]{1,0:T(8,128)(2,1)} %get-tuple-element.556), channel_id=1, source_target_pairs={{0,1},{1,0},{2,3},{3,2},{4,5},{5,4},{6,7},{7,6},{8,9},{9,8},{10,11... | collective-permute-start | bytes 3145736 | tf_op jit(solution)/shard_map/ppermute | solution.py:646
  460.4 32.6 %collective-permute-start.51 = (bf16[256,2048]{1,0:T(8,128)(2,1)}, bf16[256,2048]{1,0:T(8,128)(2,1)}, u32[]{:S(2)}, u32[]{:S(2)}) collective-permute-start(bf16[256,2048]{1,0:T(8,128)(2,1)} %get-tuple-element.601), channel_id=1, source_target_pairs={{0,1},{1,0},{2,3},{3,2},{4,5},{5,4},{6,7},{7,6},{8,9},{9,8},{10,11... | collective-permute-start | bytes 3145736 | tf_op jit(solution)/shard_map/ppermute | solution.py:646
  463.8 29.1 %collective-permute-start.52 = (bf16[256,2048]{1,0:T(8,128)(2,1)}, bf16[256,2048]{1,0:T(8,128)(2,1)}, u32[]{:S(2)}, u32[]{:S(2)}) collective-permute-start(bf16[256,2048]{1,0:T(8,128)(2,1)} %add_convert_fusion.4), channel_id=1, source_target_pairs={{2,4},{3,5},{4,2},{5,3},{10,12},{11,13},{12,10},{13,11},{18,20},{1... | collective-permute-start | bytes 3145736 | tf_op jit(solution)/shard_map/ppermute | solution.py:646
  467.0 29.9 %collective-permute-start.53 = (bf16[256,2048]{1,0:T(8,128)(2,1)}, bf16[256,2048]{1,0:T(8,128)(2,1)}, u32[]{:S(2)}, u32[]{:S(2)}) collective-permute-start(bf16[256,2048]{1,0:T(8,128)(2,1)} %add_convert_fusion.3), channel_id=1, source_target_pairs={{0,2},{1,3},{2,0},{3,1},{4,6},{5,7},{6,4},{7,5},{8,10},{9,11},{10,... | collective-permute-start | bytes 3145736 | tf_op jit(solution)/shard_map/ppermute | solution.py:646
  472.5 59.3 %all-to-all-start.3 = ((bf16[8,64,1408]{2,1,0:T(8,128)(2,1)}), bf16[8,64,1408]{2,1,0:T(8,128)(2,1)S(1)}, u32[]{:S(2)}, u32[]{:S(2)}) async-start(bf16[8,64,1408]{2,1,0:T(8,128)(2,1)} %pack_rows.2), calls=%async_computation.3 | async-start | bytes 2883584 | tf_op jit(solution)/shard_map/all_to_all | solution.py:811
  531.8 42.0 %all-to-all-start.2 = ((bf16[8,64,1792]{2,1,0:T(8,128)(2,1)}), bf16[8,64,1792]{2,1,0:T(8,128)(2,1)S(1)}, u32[]{:S(2)}, u32[]{:S(2)}) async-start(bf16[8,64,1792]{2,1,0:T(8,128)(2,1)} %pack_rows.3), calls=%async_computation.2 | async-start | bytes 3670016 | tf_op jit(solution)/shard_map/all_to_all | solution.py:832
  (80 other events, 1600.9 us)

commit v7 on v6

--- a/solution.py
+++ b/solution.py
@@ -824,15 +824,16 @@
             give = jnp.where(mine == 0, second, first)
             return jnp.where(mine == 0, first, second) + lax.ppermute(give, axis, swaps(bit, size))
 
-        sums = sums.reshape(4, n, 2 * own)
-        for bit in (4, 2, 1):
-            sums = halved(sums, 1, "ctx", bit, n)
+        sums = sums.reshape(4, 2, 2, 2, 2 * own)
+        for dim, bit in ((3, 1), (2, 2), (1, 4)):
+            sums = halved(sums, dim, "ctx", bit, n)
         names = ("J", "W")
         packed, sums = lax.optimization_barrier((s[names], sums))
         opened[names] = lax.all_to_all(packed, "ctx", split_axis=0, concat_axis=0, tiled=True)
+        sums = sums.reshape(4, 2 * own)
         for bit in (2, 1):
             sums = halved(sums, 0, "dp", bit, 4)
-        return {"input_grad": input_grad, "norm_sums": sums[0]}
+        return {"input_grad": input_grad, "norm_sums": sums}
 
     def y(name):
         return to(name + "2", name + "0", across)

time: 585 us -> 580 us (level)
  waiting for transfers between devices: 238 us -> 229 us
    ppermute x5, waiting for transfers between devices: 25.6 us -> 14.4 us  [halved(): lax.ppermute(give, axis, swaps(bit, size))]
where the time goes in v7:
time: 580 us; the launch traced here: 571 us
  waiting for transfers between devices  229 us (39%)
  Pallas kernels  146 us (25%)
  starting transfers between devices  97.9 us (17%)
  matrix products  53.2 us (9%)
  other arithmetic  36.5 us (6%)
  local copies, waits for them, and re-layouts  6.46 us (1%)
    ppermute x44, waiting for transfers between devices, tick(): view[name] = lax.ppermute(self.held[source], axis, pairs)  105 us
    ppermute x44, starting transfers between devices, tick(): view[name] = lax.ppermute(self.held[source], axis, pairs)  55 us
    dot_general x9, matrix products, dot_first(): return lax.dot_general(left, right, FIRST, preferred_element_type=F32)  53.2 us
    pallas_call x3, Pallas kernels, stream(): pl.pallas_call(functools.partial(stream_kernel, n, len(pieces), len(extra...  50.7 us
    pallas_call x3, Pallas kernels, spread(): pl.pallas_call(functools.partial(spread_kernel, len(lefts), len(pieces),...  45.9 us
    all_to_all x1, waiting for transfers between devices, begin(): lax.all_to_all(packed, 'ctx', split_axis=0, concat_axis=0, tiled=True)  39.5 us
    all_to_all x1, waiting for transfers between devices, norm_back(): lax.all_to_all(packed, 'ctx', split_axis=0, concat_axis=0, tiled=True)  28.8 us
    pallas_call x1, Pallas kernels, attend_back(): self.calls(lanes)[1]  21.4 us
  transfers between devices with their start and end apart: 64, of which 29 were waited for; matrix products, arithmetic and copies ran while one was open for 16% of the time, Pallas kernels for 25%

profile of v7, /device:TPU:0, one launch (start us, length us, event | category | flops | bytes accessed | tf_op | source)
XLA Modules:
  0.0 570.8 jit_solution(14781127347305718805)
XLA Ops:
  15.3 5.3 all-to-all-start
  33.8 39.5 %all-to-all-done.in_ref = bf16[8,64,2176]{2,1,0:T(8,128)(2,1)} async-done(((bf16[8,64,2176]{2,1,0:T(8,128)(2,1)}), bf16[8,64,2176]{2,1,0:T(8,128)(2,1)}, u32[]{:S(2)}, u32[]{:S(2)}) %all-to-all-start) | async-done | bytes 2228256 | tf_op jit(solution)/shard_map/all_to_all | solution.py:693
  76.8 6.1 %collective-permute-done.4.refs_2_ = bf16[256,2048]{1,0:T(8,128)(2,1)} collective-permute-done((bf16[256,2048]{1,0:T(8,128)(2,1)}, bf16[256,2048]{1,0:T(8,128)(2,1)}, u32[]{:S(2)}, u32[]{:S(2)}) %collective-permute-start.4) | collective-permute-done | bytes 1048608 | tf_op jit(solution)/shard_map/ppermute | solution.py:694
  82.9 6.6 %collective-permute-done.7.refs_1_ = bf16[256,2048]{1,0:T(8,128)(2,1)} collective-permute-done((bf16[256,2048]{1,0:T(8,128)(2,1)S(1)}, bf16[256,2048]{1,0:T(8,128)(2,1)}, u32[]{:S(2)}, u32[]{:S(2)}) %collective-permute-start.7) | collective-permute-done | bytes 1048608 | tf_op jit(solution)/shard_map/ppermute | solution.py:699
  89.5 12.0 %collective-permute-done.8.refs_2_ = bf16[256,2048]{1,0:T(8,128)(2,1)} collective-permute-done((bf16[256,2048]{1,0:T(8,128)(2,1)S(1)}, bf16[256,2048]{1,0:T(8,128)(2,1)}, u32[]{:S(2)}, u32[]{:S(2)}) %collective-permute-start.8) | collective-permute-done | bytes 1048608 | tf_op jit(solution)/shard_map/ppermute | solution.py:700
  107.4 5.6 fusion.48
  113.0 15.6 %collective-permute-done.10.refs_3_ = bf16[256,2048]{1,0:T(8,128)(2,1)} collective-permute-done((bf16[256,2048]{1,0:T(8,128)(2,1)}, bf16[256,2048]{1,0:T(8,128)(2,1)}, u32[]{:S(2)}, u32[]{:S(2)}) %collective-permute-start.10) | collective-permute-done | bytes 1048608 | tf_op jit(solution)/shard_map/ppermute | solution.py:646
  128.6 5.1 collective-permute-done.12
  139.7 7.5 %all-to-all-start.1 = ((bf16[8,64,1024]{2,1,0:T(8,128)(2,1)}), bf16[8,64,1024]{2,1,0:T(8,128)(2,1)S(1)}, u32[]{:S(2)}, u32[]{:S(2)}) async-start(bf16[8,64,1024]{2,1,0:T(8,128)(2,1)} %pack_columns.3), calls=%async_computation.1 | async-start | bytes 2097152 | tf_op jit(solution)/shard_map/all_to_all | solution.py:705
  147.2 15.9 %collective-permute-done.15.refs_1_ = bf16[256,2048]{1,0:T(8,128)(2,1)} collective-permute-done((bf16[256,2048]{1,0:T(8,128)(2,1)S(1)}, bf16[256,2048]{1,0:T(8,128)(2,1)}, u32[]{:S(2)}, u32[]{:S(2)}) %collective-permute-start.15) | collective-permute-done | bytes 1048608 | tf_op jit(solution)/shard_map/ppermute | solution.py:646
  163.1 7.5 %collective-permute-done.16 = bf16[256,2048]{1,0:T(8,128)(2,1)} collective-permute-done((bf16[256,2048]{1,0:T(8,128)(2,1)}, bf16[256,2048]{1,0:T(8,128)(2,1)}, u32[]{:S(2)}, u32[]{:S(2)}) %collective-permute-start.16) | collective-permute-done | bytes 1048608 | tf_op jit(solution)/shard_map/ppermute | solution.py:646
  177.3 13.6 %all-to-all-done.1.in_ref = bf16[8,64,1024]{2,1,0:T(8,128)(2,1)S(1)} async-done(((bf16[8,64,1024]{2,1,0:T(8,128)(2,1)}), bf16[8,64,1024]{2,1,0:T(8,128)(2,1)S(1)}, u32[]{:S(2)}, u32[]{:S(2)}) %all-to-all-start.1) | async-done | bytes 1048608 | tf_op jit(solution)/shard_map/all_to_all | solution.py:705
  192.2 16.7 %project.2 = (bf16[2048,2048]{1,0:T(8,128)(2,1)}, f32[2048,768]{1,0:T(8,128)}, bf16[2048,1408]{1,0:T(8,128)(2,1)}, bf16[2048,1024]{1,0:T(8,128)(2,1)}) custom-call(bf16[256,2048]{1,0:T(8,128)(2,1)S(1)} %copy-done.4, bf16[256,2048]{1,0:T(8,128)(2,1)} %collective-permute-done.7.refs_1_, bf16[256,2048]{1,0:T(8,128)(2,1)} %collective-permute-done.8.refs_2_, ...), custom_call_target="tpu_custom_call" | custom-call | flops 9126805504 | bytes 26214400 | tf_op jit(solution)/shard_map/project/pallas_call | solution.py:397
  216.7 16.5 %project.3 = (bf16[2048,2048]{1,0:T(8,128)(2,1)}, f32[2048,768]{1,0:T(8,128)}, bf16[2048,1408]{1,0:T(8,128)(2,1)}, bf16[2048,1024]{1,0:T(8,128)(2,1)}) custom-call(bf16[256,2048]{1,0:T(8,128)(2,1)S(1)} %broadcast_select_fusion.3.refs_0_, ...), custom_call_target="tpu_custom_call", output_to_operand_aliasing={{0}: (11, {}), {1}: (12, {}), {2}: (13, {}), {3}: (14, {})} | custom-call | flops 9126805504 | bytes 26214400 | tf_op jit(solution)/shard_map/project/pallas_call | solution.py:397
  233.3 6.6 %collective-permute-done.24.refs_5_ = bf16[256,2048]{1,0:T(8,128)(2,1)S(1)} collective-permute-done((bf16[256,2048]{1,0:T(8,128)(2,1)S(1)}, bf16[256,2048]{1,0:T(8,128)(2,1)S(1)}, u32[]{:S(2)}, u32[]{:S(2)}) %collective-permute-start.24) | collective-permute-done | bytes 1048608 | tf_op jit(solution)/shard_map/ppermute | solution.py:646
  245.3 14.9 %attend_forward.1 = (bf16[8,2,128,768]{3,2,1,0:T(8,128)(2,1)}, bf16[8,2,128,1024]{3,2,1,0:T(8,128)(2,1)}, f32[8,2,128,4]{3,2,1,0:T(8,128)S(1)}) custom-call(s32[2]{0:T(128)S(1)} %copy-done.11, s32[8]{0:T(128)S(1)} %compare_select_fusion.8.slot_ref, f32[8,2,128,768]{3,2,1,0:T(8,128)} %bitcast.57, ...), custom_call_target="tpu_custom_call", output_to_operand_aliasing={{1}: (5, {})} | custom-call | flops 4294967296 | bytes 4194304 | tf_op jit(solution)/shard_map/attend_forward/pallas_call | solution.py:552
  261.3 14.4 %output_part.1 = (bf16[256,2048]{1,0:T(8,128)(2,1)S(1)}, bf16[256,2048]{1,0:T(8,128)(2,1)}, bf16[256,2048]{1,0:T(8,128)(2,1)}, bf16[256,2048]{1,0:T(8,128)(2,1)}...) custom-call(bf16[2048,1024]{1,0:T(8,128)(2,1)} %bitcast.59, ...), custom_call_target="tpu_custom_call" | custom-call | flops 8589934592 | bytes 16777216 | tf_op jit(solution)/shard_map/output_part/pallas_call | solution.py:497
  278.1 17.4 %bring_back.1 = (bf16[2048,2048]{1,0:T(8,128)(2,1)}, bf16[2048,256]{1,0:T(8,128)(2,1)S(1)}, bf16[2048,1408]{1,0:T(8,128)(2,1)}) custom-call(bf16[256,2048]{1,0:T(8,128)(2,1)} %pad_maximum_fusion.refs_0_, bf16[256,2048]{1,0:T(8,128)(2,1)} %collective-permute-done.3.refs_1_, bf16[256,2048]{1,0:T(8,128)(2,1)} %collective-permute-done.4.refs_2_, ...), custom_call_target="tpu_custom_call" | custom-call | flops 8589934592 | bytes 25165824 | tf_op jit(solution)/shard_map/bring_back/pallas_call | solution.py:397
  295.6 11.7 %fusion.6 = bf16[1024,1408]{1,0:T(8,128)(2,1)} fusion(bf16[2048,1408]{1,0:T(8,128)(2,1)} %get-tuple-element.545.refs_1_.refs_3_, bf16[2048,2048]{1,0:T(8,128)(2,1)} %get-tuple-element.580), kind=kOutput, calls=%fused_computation.6 | convolution fusion | flops 5907021824 | bytes 12845056 | tf_op jit(solution)/shard_map/dot_general | solution.py:31
  311.6 21.4 %attend_backward.1 = bf16[8,2,128,768]{3,2,1,0:T(8,128)(2,1)} custom-call(s32[2]{0:T(128)S(1)} %copy-done.11, s32[8]{0:T(128)S(1)} %compare_select_fusion.8.slot_ref, bf16[8,2,128,768]{3,2,1,0:T(8,128)(2,1)} %get-tuple-element.491.rot_ref, bf16[8,2,128,1024]{3,2,1,0:T(8,128)(2,1)} %get-tuple-element.424, bf16[8,2,128,256]{3,2,1,0:T(8,128)(2,1)S(1)} %bitcast.56, ...), custom_call_target="tpu_custom_call" | custom-call | flops 10737418240 | bytes 4194304 | tf_op jit(solution)/shard_map/attend_backward/pallas_call | solution.py:559
  333.0 7.2 %fusion.10 = bf16[512,1408]{1,0:T(8,128)(2,1)S(1)} fusion(bf16[2048,1408]{1,0:T(8,128)(2,1)} %get-tuple-element.545.refs_1_.refs_3_, bf16[2048,2048]{1,0:T(8,128)(2,1)} %get-tuple-element.580, bf16[1024,1408]{1,0:T(8,128)(2,1)} %collective-permute-done.35), kind=kOutput, calls=%fused_computation.10 | convolution fusion | flops 2954952704 | bytes 10747904 | tf_op jit(solution)/shard_map/dot_general | solution.py:31
  346.4 15.7 %normed_part.2 = (bf16[256,2048]{1,0:T(8,128)(2,1)S(1)}, bf16[256,2048]{1,0:T(8,128)(2,1)}, bf16[256,2048]{1,0:T(8,128)(2,1)}, bf16[256,2048]{1,0:T(8,128)(2,1)}) custom-call(bf16[2048,768]{1,0:T(8,128)(2,1)} %bitcast.91, bf16[2048,1408]{1,0:T(8,128)(2,1)} %get-tuple-element.545.refs_1_.refs_3_, bf16[2048,768]{1,0:T(8,128)(2,1)} %bitcast.92, ...), custom_call_target="tpu_custom_call" | custom-call | flops 9126805504 | bytes 17563648 | tf_op jit(solution)/shard_map/normed_part/pallas_call | solution.py:497
  366.0 11.2 %collective-permute-done.39 = bf16[512,1408]{1,0:T(8,128)(2,1)S(1)} collective-permute-done((bf16[512,1408]{1,0:T(8,128)(2,1)S(1)}, bf16[512,1408]{1,0:T(8,128)(2,1)S(1)}, u32[]{:S(2)}, u32[]{:S(2)}) %collective-permute-start.39) | collective-permute-done | bytes 1441824 | tf_op jit(solution)/shard_map/ppermute | solution.py:646
  381.4 7.2 %fusion.11.refs_0_ = bf16[512,1408]{1,0:T(8,128)(2,1)S(1)} fusion(bf16[2048,1408]{1,0:T(8,128)(2,1)} %get-tuple-element.545.refs_1_.refs_3_, bf16[512,1408]{1,0:T(8,128)(2,1)S(1)} %copy-done.37, bf16[2048,2048]{1,0:T(8,128)(2,1)} %get-tuple-element.580, bf16[1024,1408]{1,0:T(8,128)(2,1)} %collective-permute-done.35), kind=kOutput, calls=%fused_computation.11 | convolution fusion | flops 2956394496 | bytes 12189696 | tf_op jit(solution)/shard_map/dot_general | solution.py:31
  389.8 15.8 %normed_part.3 = (bf16[256,2048]{1,0:T(8,128)(2,1)S(1)}, bf16[256,2048]{1,0:T(8,128)(2,1)}, bf16[256,2048]{1,0:T(8,128)(2,1)}, bf16[256,2048]{1,0:T(8,128)(2,1)}) custom-call(bf16[2048,768]{1,0:T(8,128)(2,1)} %bitcast.93, bf16[2048,1408]{1,0:T(8,128)(2,1)} %get-tuple-element.545.refs_1_.refs_3_, bf16[2048,768]{1,0:T(8,128)(2,1)} %bitcast.94, ...), custom_call_target="tpu_custom_call" | custom-call | flops 9126805504 | bytes 17563648 | tf_op jit(solution)/shard_map/normed_part/pallas_call | solution.py:497
  410.6 5.7 %fusion.35 = bf16[1024,768]{1,0:T(8,128)(2,1)S(1)} fusion(bf16[2048,768]{1,0:T(8,128)(2,1)S(1)} %bitcast.95, bf16[2048,2048]{1,0:T(8,128)(2,1)} %get-tuple-element.580), kind=kOutput, calls=%fused_computation.58 | convolution fusion | flops 3222011904 | bytes 8912896 | tf_op jit(solution)/shard_map/dot_general | solution.py:31
  439.4 12.3 %collective-permute-done.49 = bf16[512,768]{1,0:T(8,128)(2,1)S(1)} collective-permute-done((bf16[512,768]{1,0:T(8,128)(2,1)S(1)}, bf16[512,768]{1,0:T(8,128)(2,1)S(1)}, u32[]{:S(2)}, u32[]{:S(2)}) %collective-permute-start.49) | collective-permute-done | bytes 786464 | tf_op jit(solution)/shard_map/ppermute | solution.py:646
  467.1 5.5 collective-permute-start.53
  476.2 9.7 %collective-permute-done.54 = bf16[512,1024]{1,0:T(8,128)(2,1)} collective-permute-done((bf16[512,1024]{1,0:T(8,128)(2,1)}, bf16[512,1024]{1,0:T(8,128)(2,1)}, u32[]{:S(2)}, u32[]{:S(2)}) %collective-permute-start.54) | collective-permute-done | bytes 1048608 | tf_op jit(solution)/shard_map/ppermute | solution.py:646
  485.8 5.8 %add_convert_fusion.2.refs_1_ = bf16[512,1024]{1,0:T(8,128)(2,1)S(1)} fusion(bf16[512,1024]{1,0:T(8,128)(2,1)} %collective-permute-done.54, bf16[2048,1024]{1,0:T(8,128)(2,1)} %bitcast.63, bf16[2048,2048]{1,0:T(8,128)(2,1)} %get-tuple-element.598, bf16[1024,1024]{1,0:T(8,128)(2,1)} %copy-done.35), kind=kOutput, calls=%fused_computation.29 | convolution fusion | flops 2150105088 | bytes 9437184 | tf_op jit(solution)/shard_map/dot_general | solution.py:31
  510.5 6.5 %collective-permute-done.56 = f32[4,2,1,1,128]{4,3,2,1,0:T(1,128)S(1)} collective-permute-done((f32[4,2,1,1,128]{4,3,2,1,0:T(1,128)S(1)}, f32[4,2,1,1,128]{4,3,2,1,0:T(1,128)S(1)}, u32[]{:S(2)}, u32[]{:S(2)}) %collective-permute-start.56) | collective-permute-done | bytes 4128 | tf_op jit(solution)/shard_map/ppermute | solution.py:825
  539.6 28.8 %all-to-all-done.2.held = bf16[8,64,1792]{2,1,0:T(8,128)(2,1)S(1)} async-done(((bf16[8,64,1792]{2,1,0:T(8,128)(2,1)}), bf16[8,64,1792]{2,1,0:T(8,128)(2,1)S(1)}, u32[]{:S(2)}, u32[]{:S(2)}) %all-to-all-start.2) | async-done | bytes 1835040 | tf_op jit(solution)/shard_map/all_to_all | solution.py:832
  (289 shorter events, 176.9 us)
Async XLA Ops:
  15.3 58.0 %all-to-all-start = ((bf16[8,64,2176]{2,1,0:T(8,128)(2,1)}), bf16[8,64,2176]{2,1,0:T(8,128)(2,1)}, u32[]{:S(2)}, u32[]{:S(2)}) async-start(bf16[8,64,2176]{2,1,0:T(8,128)(2,1)} %pack_columns.2), calls=%async_computation | async-start | bytes 4456448 | tf_op jit(solution)/shard_map/all_to_all | solution.py:693
  24.4 52.4 %collective-permute-start.3 = (bf16[256,2048]{1,0:T(8,128)(2,1)}, bf16[256,2048]{1,0:T(8,128)(2,1)}, u32[]{:S(2)}, u32[]{:S(2)}) collective-permute-start(bf16[256,2048]{1,0:T(8,128)(2,1)} %pad_maximum_fusion.refs_0_), channel_id=1, source_target_pairs={{0,1},{1,0},{2,3},{3,2},{4,5},{5,4},{6,7},{7,6},{8,9},{9,8},{10,11... | collective-permute-start | bytes 3145736 | tf_op jit(solution)/shard_map/ppermute | solution.py:694
  26.4 56.5 %collective-permute-start.4 = (bf16[256,2048]{1,0:T(8,128)(2,1)}, bf16[256,2048]{1,0:T(8,128)(2,1)}, u32[]{:S(2)}, u32[]{:S(2)}) collective-permute-start(bf16[256,2048]{1,0:T(8,128)(2,1)} %pad_maximum_fusion.refs_0_), channel_id=1, source_target_pairs={{0,2},{1,3},{2,0},{3,1},{4,6},{5,7},{6,4},{7,5},{8,10},{9,11},{10,... | collective-permute-start | bytes 3145736 | tf_op jit(solution)/shard_map/ppermute | solution.py:694
  30.1 59.4 %collective-permute-start.7 = (bf16[256,2048]{1,0:T(8,128)(2,1)S(1)}, bf16[256,2048]{1,0:T(8,128)(2,1)}, u32[]{:S(2)}, u32[]{:S(2)}) collective-permute-start(bf16[256,2048]{1,0:T(8,128)(2,1)S(1)} %pad_maximum_fusion.1.refs_0_), channel_id=1, source_target_pairs={{0,1},{1,0},{2,3},{3,2},{4,5},{5,4},{6,7},{7,6},{8,9},{9,8},{10,11... | collective-permute-start | bytes 3145736 | tf_op jit(solution)/shard_map/ppermute | solution.py:699
  30.7 70.8 %collective-permute-start.8 = (bf16[256,2048]{1,0:T(8,128)(2,1)S(1)}, bf16[256,2048]{1,0:T(8,128)(2,1)}, u32[]{:S(2)}, u32[]{:S(2)}) collective-permute-start(bf16[256,2048]{1,0:T(8,128)(2,1)S(1)} %pad_maximum_fusion.1.refs_0_), channel_id=1, source_target_pairs={{0,2},{1,3},{2,0},{3,1},{4,6},{5,7},{6,4},{7,5},{8,10},{9,11},{10,... | collective-permute-start | bytes 3145736 | tf_op jit(solution)/shard_map/ppermute | solution.py:700
  31.7 69.8 %collective-permute-start.9 = (bf16[256,2048]{1,0:T(8,128)(2,1)S(1)}, bf16[256,2048]{1,0:T(8,128)(2,1)S(1)}, u32[]{:S(2)}, u32[]{:S(2)}) collective-permute-start(bf16[256,2048]{1,0:T(8,128)(2,1)S(1)} %pad_maximum_fusion.1.refs_0_), channel_id=1, source_target_pairs={{2,4},{3,5},{4,2},{5,3},{10,12},{11,13},{12,10},{13,11},{18,20},{1... | collective-permute-start | bytes 3145736 | tf_op jit(solution)/shard_map/ppermute | solution.py:700
  101.5 32.2 %collective-permute-start.14 = (bf16[512,2176]{1,0:T(8,128)(2,1)}, bf16[512,2176]{1,0:T(8,128)(2,1)}, u32[]{:S(2)}, u32[]{:S(2)}) collective-permute-start(bf16[512,2176]{1,0:T(8,128)(2,1)} %get-tuple-element.335), channel_id=1, source_target_pairs={{0,8},{8,0},{16,24},{24,16},{1,9},{9,1},{17,25},{25,17},{2,10},{10... | collective-permute-start | bytes 6684680 | tf_op jit(solution)/shard_map/ppermute | solution.py:646
  101.5 32.2 %collective-permute-start.13 = (bf16[256,2176]{1,0:T(8,128)(2,1)S(1)}, bf16[256,2176]{1,0:T(8,128)(2,1)}, u32[]{:S(2)}, u32[]{:S(2)}) collective-permute-start(bf16[256,2176]{1,0:T(8,128)(2,1)S(1)} %get-tuple-element.533.refs_4_), channel_id=1, source_target_pairs={{0,16},{8,24},{16,0},{24,8},{1,17},{9,25},{17,1},{25,9},{2,18},{10... | collective-permute-start | bytes 3342344 | tf_op jit(solution)/shard_map/ppermute | solution.py:646
  106.1 27.6 %collective-permute-start.12 = (bf16[256,2048]{1,0:T(8,128)(2,1)S(1)}, bf16[256,2048]{1,0:T(8,128)(2,1)S(1)}, u32[]{:S(2)}, u32[]{:S(2)}) collective-permute-start(bf16[256,2048]{1,0:T(8,128)(2,1)S(1)} %collective-permute-done.9), channel_id=1, source_target_pairs={{2,0},{3,1},{4,6},{5,7},{10,8},{11,9},{12,14},{13,15},{18,16},{19,... | collective-permute-start | bytes 3145736 | tf_op jit(solution)/shard_map/ppermute | solution.py:646
  133.7 36.9 %collective-permute-start.18 = (bf16[256,2176]{1,0:T(8,128)(2,1)}, bf16[256,2176]{1,0:T(8,128)(2,1)}, u32[]{:S(2)}, u32[]{:S(2)}) collective-permute-start(bf16[256,2176]{1,0:T(8,128)(2,1)} %get-tuple-element.534.refs_5_), channel_id=1, source_target_pairs={{0,16},{8,24},{16,0},{24,8},{1,17},{9,25},{17,1},{25,9},{2,18},{10... | collective-permute-start | bytes 3342344 | tf_op jit(solution)/shard_map/ppermute | solution.py:646
  134.7 35.9 %collective-permute-start.19 = (bf16[256,2176]{1,0:T(8,128)(2,1)}, bf16[256,2176]{1,0:T(8,128)(2,1)}, u32[]{:S(2)}, u32[]{:S(2)}) collective-permute-start(bf16[256,2176]{1,0:T(8,128)(2,1)} %collective-permute-done.13.refs_6_), channel_id=1, source_target_pairs={{0,8},{8,0},{16,24},{24,16},{1,9},{9,1},{17,25},{25,17},{2,10},{10... | collective-permute-start | bytes 3342344 | tf_op jit(solution)/shard_map/ppermute | solution.py:646
  136.8 33.8 %collective-permute-start.16 = (bf16[256,2048]{1,0:T(8,128)(2,1)}, bf16[256,2048]{1,0:T(8,128)(2,1)}, u32[]{:S(2)}, u32[]{:S(2)}) collective-permute-start(bf16[256,2048]{1,0:T(8,128)(2,1)} %collective-permute-done.11), channel_id=1, source_target_pairs={{2,0},{3,1},{4,6},{5,7},{10,8},{11,9},{12,14},{13,15},{18,16},{19,... | collective-permute-start | bytes 3145736 | tf_op jit(solution)/shard_map/ppermute | solution.py:646
  138.1 32.5 %collective-permute-start.17 = (bf16[256,2048]{1,0:T(8,128)(2,1)}, bf16[256,2048]{1,0:T(8,128)(2,1)}, u32[]{:S(2)}, u32[]{:S(2)}) collective-permute-start(bf16[256,2048]{1,0:T(8,128)(2,1)} %pad_maximum_fusion.refs_0_), channel_id=1, source_target_pairs={{2,4},{3,5},{4,2},{5,3},{10,12},{11,13},{12,10},{13,11},{18,20},{1... | collective-permute-start | bytes 3145736 | tf_op jit(solution)/shard_map/ppermute | solution.py:646
  139.7 51.1 %all-to-all-start.1 = ((bf16[8,64,1024]{2,1,0:T(8,128)(2,1)}), bf16[8,64,1024]{2,1,0:T(8,128)(2,1)S(1)}, u32[]{:S(2)}, u32[]{:S(2)}) async-start(bf16[8,64,1024]{2,1,0:T(8,128)(2,1)} %pack_columns.3), calls=%async_computation.1 | async-start | bytes 2097152 | tf_op jit(solution)/shard_map/all_to_all | solution.py:705
  173.0 35.9 %collective-permute-start.20 = (bf16[256,2048]{1,0:T(8,128)(2,1)}, bf16[256,2048]{1,0:T(8,128)(2,1)}, u32[]{:S(2)}, u32[]{:S(2)}) collective-permute-start(bf16[256,2048]{1,0:T(8,128)(2,1)} %broadcast_select_fusion.2.refs_2_), channel_id=1, source_target_pairs={{0,1},{1,0},{2,3},{3,2},{4,5},{5,4},{6,7},{7,6},{8,9},{9,8},{10,11... | collective-permute-start | bytes 3145736 | tf_op jit(solution)/shard_map/ppermute | solution.py:646
  174.4 39.0 %collective-permute-start.21 = (bf16[256,2048]{1,0:T(8,128)(2,1)}, bf16[256,2048]{1,0:T(8,128)(2,1)}, u32[]{:S(2)}, u32[]{:S(2)}) collective-permute-start(bf16[256,2048]{1,0:T(8,128)(2,1)} %collective-permute-done.17), channel_id=1, source_target_pairs={{2,0},{3,1},{4,6},{5,7},{10,8},{11,9},{12,14},{13,15},{18,16},{19,... | collective-permute-start | bytes 3145736 | tf_op jit(solution)/shard_map/ppermute | solution.py:646
  175.6 37.7 %collective-permute-start.22 = (bf16[256,2048]{1,0:T(8,128)(2,1)}, bf16[256,2048]{1,0:T(8,128)(2,1)}, u32[]{:S(2)}, u32[]{:S(2)}) collective-permute-start(bf16[256,2048]{1,0:T(8,128)(2,1)} %collective-permute-done.4.refs_2_), channel_id=1, source_target_pairs={{2,4},{3,5},{4,2},{5,3},{10,12},{11,13},{12,10},{13,11},{18,20},{1... | collective-permute-start | bytes 3145736 | tf_op jit(solution)/shard_map/ppermute | solution.py:646
  191.0 42.3 %collective-permute-start.26 = (bf16[512,1024]{1,0:T(8,128)(2,1)S(1)}, bf16[512,1024]{1,0:T(8,128)(2,1)}, u32[]{:S(2)}, u32[]{:S(2)}) collective-permute-start(bf16[512,1024]{1,0:T(8,128)(2,1)S(1)} %unpack_columns.3.refs_4_.refs_8_), channel_id=1, source_target_pairs={{0,16},{8,24},{16,0},{24,8},{1,17},{9,25},{17,1},{25,9},{2,18},{10... | collective-permute-start | bytes 3145736 | tf_op jit(solution)/shard_map/ppermute | solution.py:646
  192.2 41.1 %collective-permute-start.27 = (bf16[512,1024]{1,0:T(8,128)(2,1)S(1)}, bf16[512,1024]{1,0:T(8,128)(2,1)S(1)}, u32[]{:S(2)}, u32[]{:S(2)}) collective-permute-start(bf16[512,1024]{1,0:T(8,128)(2,1)S(1)} %unpack_columns.3.refs_4_.refs_8_), channel_id=1, source_target_pairs={{0,8},{8,0},{16,24},{24,16},{1,9},{9,1},{17,25},{25,17},{2,10},{10... | collective-permute-start | bytes 3145736 | tf_op jit(solution)/shard_map/ppermute | solution.py:646
  243.5 32.2 %collective-permute-start.28 = (bf16[256,2048]{1,0:T(8,128)(2,1)S(1)}, bf16[256,2048]{1,0:T(8,128)(2,1)S(1)}, u32[]{:S(2)}, u32[]{:S(2)}) collective-permute-start(bf16[256,2048]{1,0:T(8,128)(2,1)S(1)} %broadcast_select_fusion.refs_6_), channel_id=1, source_target_pairs={{0,1},{1,0},{2,3},{3,2},{4,5},{5,4},{6,7},{7,6},{8,9},{9,8},{10,11... | collective-permute-start | bytes 3145736 | tf_op jit(solution)/shard_map/ppermute | solution.py:646
  245.3 30.4 %collective-permute-start.29 = (bf16[256,2048]{1,0:T(8,128)(2,1)}, bf16[256,2048]{1,0:T(8,128)(2,1)S(1)}, u32[]{:S(2)}, u32[]{:S(2)}) collective-permute-start(bf16[256,2048]{1,0:T(8,128)(2,1)} %collective-permute-done.3.refs_1_), channel_id=1, source_target_pairs={{0,2},{1,3},{2,0},{3,1},{4,6},{5,7},{6,4},{7,5},{8,10},{9,11},{10,... | collective-permute-start | bytes 3145736 | tf_op jit(solution)/shard_map/ppermute | solution.py:646
  275.8 31.5 %collective-permute-start.31 = (bf16[256,2048]{1,0:T(8,128)(2,1)}, bf16[256,2048]{1,0:T(8,128)(2,1)S(1)}, u32[]{:S(2)}, u32[]{:S(2)}) collective-permute-start(bf16[256,2048]{1,0:T(8,128)(2,1)} %get-tuple-element.475), channel_id=1, source_target_pairs={{0,1},{1,0},{2,3},{3,2},{4,5},{5,4},{6,7},{7,6},{8,9},{9,8},{10,11... | collective-permute-start | bytes 3145736 | tf_op jit(solution)/shard_map/ppermute | solution.py:646
  276.1 31.2 %collective-permute-start.32 = (bf16[256,2048]{1,0:T(8,128)(2,1)}, bf16[256,2048]{1,0:T(8,128)(2,1)S(1)}, u32[]{:S(2)}, u32[]{:S(2)}) collective-permute-start(bf16[256,2048]{1,0:T(8,128)(2,1)} %get-tuple-element.471), channel_id=1, source_target_pairs={{0,2},{1,3},{2,0},{3,1},{4,6},{5,7},{6,4},{7,5},{8,10},{9,11},{10,... | collective-permute-start | bytes 3145736 | tf_op jit(solution)/shard_map/ppermute | solution.py:646
  307.4 32.9 %collective-permute-start.33 = (bf16[256,2048]{1,0:T(8,128)(2,1)S(1)}, bf16[256,2048]{1,0:T(8,128)(2,1)S(1)}, u32[]{:S(2)}, u32[]{:S(2)}) collective-permute-start(bf16[256,2048]{1,0:T(8,128)(2,1)S(1)} %copy-done.42), channel_id=1, source_target_pairs={{0,1},{1,0},{2,3},{3,2},{4,5},{5,4},{6,7},{7,6},{8,9},{9,8},{10,11... | collective-permute-start | bytes 3145736 | tf_op jit(solution)/shard_map/ppermute | solution.py:646
  309.6 30.7 %collective-permute-start.34 = (bf16[256,2048]{1,0:T(8,128)(2,1)S(1)}, bf16[256,2048]{1,0:T(8,128)(2,1)S(1)}, u32[]{:S(2)}, u32[]{:S(2)}) collective-permute-start(bf16[256,2048]{1,0:T(8,128)(2,1)S(1)} %add_convert_fusion.15), channel_id=1, source_target_pairs={{0,2},{1,3},{6,4},{7,5},{8,10},{9,11},{14,12},{15,13},{16,18},{17,... | collective-permute-start | bytes 3145736 | tf_op jit(solution)/shard_map/ppermute | solution.py:646
  344.1 33.2 %collective-permute-start.39 = (bf16[512,1408]{1,0:T(8,128)(2,1)S(1)}, bf16[512,1408]{1,0:T(8,128)(2,1)S(1)}, u32[]{:S(2)}, u32[]{:S(2)}) collective-permute-start(bf16[512,1408]{1,0:T(8,128)(2,1)S(1)} %fusion.10), channel_id=1, source_target_pairs={{0,16},{8,24},{16,0},{24,8},{1,17},{9,25},{17,1},{25,9},{2,18},{10... | collective-permute-start | bytes 4325384 | tf_op jit(solution)/shard_map/ppermute | solution.py:646
  377.2 28.4 %collective-permute-start.40 = (bf16[256,2048]{1,0:T(8,128)(2,1)}, bf16[256,2048]{1,0:T(8,128)(2,1)S(1)}, u32[]{:S(2)}, u32[]{:S(2)}) collective-permute-start(bf16[256,2048]{1,0:T(8,128)(2,1)} %get-tuple-element.556), channel_id=1, source_target_pairs={{0,1},{1,0},{2,3},{3,2},{4,5},{5,4},{6,7},{7,6},{8,9},{9,8},{10,11... | collective-permute-start | bytes 3145736 | tf_op jit(solution)/shard_map/ppermute | solution.py:646
  460.5 32.5 %collective-permute-start.51 = (bf16[256,2048]{1,0:T(8,128)(2,1)}, bf16[256,2048]{1,0:T(8,128)(2,1)}, u32[]{:S(2)}, u32[]{:S(2)}) collective-permute-start(bf16[256,2048]{1,0:T(8,128)(2,1)} %get-tuple-element.601), channel_id=1, source_target_pairs={{0,1},{1,0},{2,3},{3,2},{4,5},{5,4},{6,7},{7,6},{8,9},{9,8},{10,11... | collective-permute-start | bytes 3145736 | tf_op jit(solution)/shard_map/ppermute | solution.py:646
  463.9 29.1 %collective-permute-start.52 = (bf16[256,2048]{1,0:T(8,128)(2,1)}, bf16[256,2048]{1,0:T(8,128)(2,1)}, u32[]{:S(2)}, u32[]{:S(2)}) collective-permute-start(bf16[256,2048]{1,0:T(8,128)(2,1)} %add_convert_fusion.4), channel_id=1, source_target_pairs={{2,4},{3,5},{4,2},{5,3},{10,12},{11,13},{12,10},{13,11},{18,20},{1... | collective-permute-start | bytes 3145736 | tf_op jit(solution)/shard_map/ppermute | solution.py:646
  467.1 29.9 %collective-permute-start.53 = (bf16[256,2048]{1,0:T(8,128)(2,1)}, bf16[256,2048]{1,0:T(8,128)(2,1)}, u32[]{:S(2)}, u32[]{:S(2)}) collective-permute-start(bf16[256,2048]{1,0:T(8,128)(2,1)} %add_convert_fusion.3), channel_id=1, source_target_pairs={{0,2},{1,3},{2,0},{3,1},{4,6},{5,7},{6,4},{7,5},{8,10},{9,11},{10,... | collective-permute-start | bytes 3145736 | tf_op jit(solution)/shard_map/ppermute | solution.py:646
  472.6 51.7 %all-to-all-start.3 = ((bf16[8,64,1408]{2,1,0:T(8,128)(2,1)}), bf16[8,64,1408]{2,1,0:T(8,128)(2,1)S(1)}, u32[]{:S(2)}, u32[]{:S(2)}) async-start(bf16[8,64,1408]{2,1,0:T(8,128)(2,1)} %pack_rows.2), calls=%async_computation.3 | async-start | bytes 2883584 | tf_op jit(solution)/shard_map/all_to_all | solution.py:811
  524.3 44.1 %all-to-all-start.2 = ((bf16[8,64,1792]{2,1,0:T(8,128)(2,1)}), bf16[8,64,1792]{2,1,0:T(8,128)(2,1)S(1)}, u32[]{:S(2)}, u32[]{:S(2)}) async-start(bf16[8,64,1792]{2,1,0:T(8,128)(2,1)} %pack_rows.3), calls=%async_computation.2 | async-start | bytes 3670016 | tf_op jit(solution)/shard_map/all_to_all | solution.py:832
  (80 other events, 1570.7 us)

commit v8 on v7

--- a/solution.py
+++ b/solution.py
@@ -385,7 +385,7 @@
     size, features = slots[0].shape
     blocks = [slots[2 * place + half] for place in places for half in range(2)]
     n = len(blocks)
-    first, stride = places[0], places[1] - places[0]
+    first, stride = places[0], places[-1] - places[-2] if len(places) > 1 else 1
     anywhere = pl.BlockSpec(memory_space=pl.ANY)
 
     def rows(width):
@@ -877,17 +877,17 @@
             to("c3i", "c1", middle),
             far("b"),
         ],
-        [project(0, 1)],
+        [project(0, 1, 2)],
     )
     tick(
         [select("c2"), lambda s: {"w0": unpack_columns(plan, opened["second"], False)[0]}],
         [to("c2x", "c2", side), to("c3o", "c3i", outward), y("w"), near("w")],
-        [project(2, 3)],
+        [project(3), attend],
     )
     tick(
         [select("c3")],
         [to("c3x", "c3", side), to("c1x", "c0x", pair), far("w")],
-        [attend, output_part(0, 1, 2, 3)],
+        [output_part(0, 1, 2, 3)],
     )
     tick(
         (),

time: 580 us -> 575 us (level)
  waiting for transfers between devices: 229 us -> 219 us
    all_to_all x1, waiting for transfers between devices: 13.6 us -> 0.01 us  [second_in(): lax.all_to_all(s['second'], 'ctx', split_axis=0, concat_axis=0, tiled=True)]
where the time goes in v8:
time: 575 us; the launch traced here: 567 us
  waiting for transfers between devices  219 us (38%)
  Pallas kernels  146 us (25%)
  starting transfers between devices  101 us (18%)
  matrix products  55 us (10%)
  other arithmetic  33.1 us (6%)
  local copies, waits for them, and re-layouts  10.2 us (2%)
    ppermute x44, waiting for transfers between devices, tick(): view[name] = lax.ppermute(self.held[source], axis, pairs)  109 us
    ppermute x44, starting transfers between devices, tick(): view[name] = lax.ppermute(self.held[source], axis, pairs)  58 us
    dot_general x9, matrix products, dot_first(): return lax.dot_general(left, right, FIRST, preferred_element_type=F32)  55 us
    pallas_call x3, Pallas kernels, stream(): pl.pallas_call(functools.partial(stream_kernel, n, len(pieces), len(extra...  50.6 us
    pallas_call x3, Pallas kernels, spread(): pl.pallas_call(functools.partial(spread_kernel, len(lefts), len(pieces),...  46.1 us
    all_to_all x1, waiting for transfers between devices, begin(): lax.all_to_all(packed, 'ctx', split_axis=0, concat_axis=0, tiled=True)  38.7 us
    all_to_all x1, waiting for transfers between devices, norm_back(): lax.all_to_all(packed, 'ctx', split_axis=0, concat_axis=0, tiled=True)  28.9 us
    pallas_call x1, Pallas kernels, attend_back(): self.calls(lanes)[1]  21.4 us
  transfers between devices with their start and end apart: 64, of which 29 were waited for; matrix products, arithmetic and copies ran while one was open for 16% of the time, Pallas kernels for 25%

profile of v8, /device:TPU:0, one launch (start us, length us, event | category | flops | bytes accessed | tf_op | source)
XLA Modules:
  0.0 566.5 jit_solution(5414635368818545903)
XLA Ops:
  15.3 5.4 all-to-all-start
  34.6 38.7 %all-to-all-done.in_ref = bf16[8,64,2176]{2,1,0:T(8,128)(2,1)} async-done(((bf16[8,64,2176]{2,1,0:T(8,128)(2,1)}), bf16[8,64,2176]{2,1,0:T(8,128)(2,1)}, u32[]{:S(2)}, u32[]{:S(2)}) %all-to-all-start) | async-done | bytes 2228256 | tf_op jit(solution)/shard_map/all_to_all | solution.py:693
  76.6 6.3 %collective-permute-done.4.refs_2_ = bf16[256,2048]{1,0:T(8,128)(2,1)} collective-permute-done((bf16[256,2048]{1,0:T(8,128)(2,1)}, bf16[256,2048]{1,0:T(8,128)(2,1)}, u32[]{:S(2)}, u32[]{:S(2)}) %collective-permute-start.4) | collective-permute-done | bytes 1048608 | tf_op jit(solution)/shard_map/ppermute | solution.py:694
  82.9 6.5 %collective-permute-done.7.refs_1_ = bf16[256,2048]{1,0:T(8,128)(2,1)} collective-permute-done((bf16[256,2048]{1,0:T(8,128)(2,1)S(1)}, bf16[256,2048]{1,0:T(8,128)(2,1)}, u32[]{:S(2)}, u32[]{:S(2)}) %collective-permute-start.7) | collective-permute-done | bytes 1048608 | tf_op jit(solution)/shard_map/ppermute | solution.py:699
  89.4 12.0 %collective-permute-done.8.refs_2_ = bf16[256,2048]{1,0:T(8,128)(2,1)} collective-permute-done((bf16[256,2048]{1,0:T(8,128)(2,1)S(1)}, bf16[256,2048]{1,0:T(8,128)(2,1)}, u32[]{:S(2)}, u32[]{:S(2)}) %collective-permute-start.8) | collective-permute-done | bytes 1048608 | tf_op jit(solution)/shard_map/ppermute | solution.py:700
  107.3 5.7 %fusion.48 = (f32[1024,256]{1,0:T(8,128)}, f32[1024,256]{1,0:T(8,128)}) fusion(f32[256]{0:T(256)S(1)} %fusion.60, f32[1024]{0:T(1024)S(1)} %iota_convert_fusion, pred[256]{0:T(512)(128)(4,1)S(1)} %get-tuple-element.670, pred[256]{0:T(512)(128)(4,1)S(1)} %get-tuple-element.671), kind=kLoop, calls=%fused_computation.65 | loop fusion | flops 1310720 | bytes 2102784 | tf_op jit(solution)/shard_map/jit(_where)/select_n | solution.py:41
  113.0 5.9 %all-to-all-start.1 = ((bf16[8,64,1024]{2,1,0:T(8,128)(2,1)}), bf16[8,64,1024]{2,1,0:T(8,128)(2,1)S(1)}, u32[]{:S(2)}, u32[]{:S(2)}) async-start(bf16[8,64,1024]{2,1,0:T(8,128)(2,1)} %pack_columns.3), calls=%async_computation.1 | async-start | bytes 2097152 | tf_op jit(solution)/shard_map/all_to_all | solution.py:705
  118.9 12.1 %collective-permute-done.10.refs_3_ = bf16[256,2048]{1,0:T(8,128)(2,1)} collective-permute-done((bf16[256,2048]{1,0:T(8,128)(2,1)}, bf16[256,2048]{1,0:T(8,128)(2,1)}, u32[]{:S(2)}, u32[]{:S(2)}) %collective-permute-start.10) | collective-permute-done | bytes 1048608 | tf_op jit(solution)/shard_map/ppermute | solution.py:646
  131.0 9.6 %collective-permute-done.12 = bf16[256,2048]{1,0:T(8,128)(2,1)} collective-permute-done((bf16[256,2048]{1,0:T(8,128)(2,1)}, bf16[256,2048]{1,0:T(8,128)(2,1)}, u32[]{:S(2)}, u32[]{:S(2)}) %collective-permute-start.12) | collective-permute-done | bytes 1048608 | tf_op jit(solution)/shard_map/ppermute | solution.py:646
  145.3 25.2 %collective-permute-done.15.refs_5_ = bf16[256,2048]{1,0:T(8,128)(2,1)S(1)} collective-permute-done((bf16[256,2048]{1,0:T(8,128)(2,1)S(1)}, bf16[256,2048]{1,0:T(8,128)(2,1)S(1)}, u32[]{:S(2)}, u32[]{:S(2)}) %collective-permute-start.15) | collective-permute-done | bytes 1048608 | tf_op jit(solution)/shard_map/ppermute | solution.py:646
  170.5 6.7 %collective-permute-done.16 = bf16[256,2048]{1,0:T(8,128)(2,1)S(1)} collective-permute-done((bf16[256,2048]{1,0:T(8,128)(2,1)}, bf16[256,2048]{1,0:T(8,128)(2,1)S(1)}, u32[]{:S(2)}, u32[]{:S(2)}) %collective-permute-start.16) | collective-permute-done | bytes 1048608 | tf_op jit(solution)/shard_map/ppermute | solution.py:646
  184.5 22.1 %project.2 = (bf16[2048,2048]{1,0:T(8,128)(2,1)}, f32[2048,768]{1,0:T(8,128)}, bf16[2048,1408]{1,0:T(8,128)(2,1)}, bf16[2048,1024]{1,0:T(8,128)(2,1)}) custom-call(bf16[256,2048]{1,0:T(8,128)(2,1)S(1)} %copy-done.5, bf16[256,2048]{1,0:T(8,128)(2,1)} %collective-permute-done.7.refs_1_, bf16[256,2048]{1,0:T(8,128)(2,1)} %collective-permute-done.8.refs_2_, ...), custom_call_target="tpu_custom_call" | custom-call | flops 13690208256 | bytes 30408704 | tf_op jit(solution)/shard_map/project/pallas_call | solution.py:397
  212.2 11.1 %project.3 = (bf16[2048,2048]{1,0:T(8,128)(2,1)}, f32[2048,768]{1,0:T(8,128)}, bf16[2048,1408]{1,0:T(8,128)(2,1)}, bf16[2048,1024]{1,0:T(8,128)(2,1)}) custom-call(bf16[256,2048]{1,0:T(8,128)(2,1)S(1)} %broadcast_select_fusion.2.refs_0_, bf16[256,2048]{1,0:T(8,128)(2,1)} %copy-done.25, ...), custom_call_target="tpu_custom_call", output_to_operand_aliasing={{0}: (9, {}), {1}: (10, {}), {2}: (11, {}), {3}: (12, {})} | custom-call | flops 4563402752 | bytes 22020096 | tf_op jit(solution)/shard_map/project/pallas_call | solution.py:397
  223.3 14.9 %attend_forward.1 = (bf16[8,2,128,768]{3,2,1,0:T(8,128)(2,1)}, bf16[8,2,128,1024]{3,2,1,0:T(8,128)(2,1)}, f32[8,2,128,4]{3,2,1,0:T(8,128)S(1)}) custom-call(s32[2]{0:T(128)S(1)} %copy-done.12, s32[8]{0:T(128)S(1)} %compare_select_fusion.8.slot_ref, f32[8,2,128,768]{3,2,1,0:T(8,128)} %bitcast.57, ...), custom_call_target="tpu_custom_call", output_to_operand_aliasing={{1}: (5, {})} | custom-call | flops 4294967296 | bytes 4194304 | tf_op jit(solution)/shard_map/attend_forward/pallas_call | solution.py:552
  240.2 5.0 collective-permute-start.29
  246.2 14.4 %output_part.1 = (bf16[256,2048]{1,0:T(8,128)(2,1)S(1)}, bf16[256,2048]{1,0:T(8,128)(2,1)}, bf16[256,2048]{1,0:T(8,128)(2,1)}, bf16[256,2048]{1,0:T(8,128)(2,1)}...) custom-call(bf16[2048,1024]{1,0:T(8,128)(2,1)} %bitcast.59, ...), custom_call_target="tpu_custom_call" | custom-call | flops 8589934592 | bytes 16777216 | tf_op jit(solution)/shard_map/output_part/pallas_call | solution.py:497
  272.4 17.4 %bring_back.1 = (bf16[2048,2048]{1,0:T(8,128)(2,1)}, bf16[2048,256]{1,0:T(8,128)(2,1)S(1)}, bf16[2048,1408]{1,0:T(8,128)(2,1)}) custom-call(bf16[256,2048]{1,0:T(8,128)(2,1)} %pad_maximum_fusion.refs_0_, bf16[256,2048]{1,0:T(8,128)(2,1)} %collective-permute-done.3.refs_1_, bf16[256,2048]{1,0:T(8,128)(2,1)} %collective-permute-done.4.refs_2_, ...), custom_call_target="tpu_custom_call" | custom-call | flops 8589934592 | bytes 25165824 | tf_op jit(solution)/shard_map/bring_back/pallas_call | solution.py:397
  289.8 11.7 %fusion.6 = bf16[1024,1408]{1,0:T(8,128)(2,1)} fusion(bf16[2048,1408]{1,0:T(8,128)(2,1)} %get-tuple-element.543.refs_1_.refs_3_, bf16[2048,2048]{1,0:T(8,128)(2,1)} %get-tuple-element.578), kind=kOutput, calls=%fused_computation.6 | convolution fusion | flops 5907021824 | bytes 12845056 | tf_op jit(solution)/shard_map/dot_general | solution.py:31
  305.0 21.4 %attend_backward.1 = bf16[8,2,128,768]{3,2,1,0:T(8,128)(2,1)} custom-call(s32[2]{0:T(128)S(1)} %copy-done.12, s32[8]{0:T(128)S(1)} %compare_select_fusion.8.slot_ref, bf16[8,2,128,768]{3,2,1,0:T(8,128)(2,1)} %get-tuple-element.489.rot_ref, bf16[8,2,128,1024]{3,2,1,0:T(8,128)(2,1)} %get-tuple-element.403, bf16[8,2,128,256]{3,2,1,0:T(8,128)(2,1)S(1)} %bitcast.56, ...), custom_call_target="tpu_custom_call" | custom-call | flops 10737418240 | bytes 4194304 | tf_op jit(solution)/shard_map/attend_backward/pallas_call | solution.py:559
  326.4 8.9 %fusion.10 = bf16[512,1408]{1,0:T(8,128)(2,1)} fusion(bf16[2048,1408]{1,0:T(8,128)(2,1)} %get-tuple-element.543.refs_1_.refs_3_, bf16[2048,2048]{1,0:T(8,128)(2,1)} %get-tuple-element.578, bf16[1024,1408]{1,0:T(8,128)(2,1)S(1)} %collective-permute-done.35), kind=kOutput, calls=%fused_computation.10 | convolution fusion | flops 2954952704 | bytes 10747904 | tf_op jit(solution)/shard_map/dot_general | solution.py:31
  341.5 15.8 %normed_part.2 = (bf16[256,2048]{1,0:T(8,128)(2,1)S(1)}, bf16[256,2048]{1,0:T(8,128)(2,1)}, bf16[256,2048]{1,0:T(8,128)(2,1)}, bf16[256,2048]{1,0:T(8,128)(2,1)}) custom-call(bf16[2048,768]{1,0:T(8,128)(2,1)} %bitcast.91, bf16[2048,1408]{1,0:T(8,128)(2,1)} %get-tuple-element.543.refs_1_.refs_3_, bf16[2048,768]{1,0:T(8,128)(2,1)} %bitcast.92, ...), custom_call_target="tpu_custom_call" | custom-call | flops 9126805504 | bytes 17563648 | tf_op jit(solution)/shard_map/normed_part/pallas_call | solution.py:497
  361.3 11.4 %collective-permute-done.39 = bf16[512,1408]{1,0:T(8,128)(2,1)S(1)} collective-permute-done((bf16[512,1408]{1,0:T(8,128)(2,1)}, bf16[512,1408]{1,0:T(8,128)(2,1)S(1)}, u32[]{:S(2)}, u32[]{:S(2)}) %collective-permute-start.39) | collective-permute-done | bytes 1441824 | tf_op jit(solution)/shard_map/ppermute | solution.py:646
  378.1 6.9 %fusion.11.refs_0_ = bf16[512,1408]{1,0:T(8,128)(2,1)S(1)} fusion(bf16[2048,1408]{1,0:T(8,128)(2,1)} %get-tuple-element.543.refs_1_.refs_3_, bf16[512,1408]{1,0:T(8,128)(2,1)S(1)} %collective-permute-done.39, bf16[2048,2048]{1,0:T(8,128)(2,1)} %get-tuple-element.578, bf16[1024,1408]{1,0:T(8,128)(2,1)S(1)} %copy-done.44), kind=kOutput, calls=%fused_computation.11 | convolution fusion | flops 2956394496 | bytes 12189696 | tf_op jit(solution)/shard_map/dot_general | solution.py:31
  386.2 15.9 %normed_part.3 = (bf16[256,2048]{1,0:T(8,128)(2,1)S(1)}, bf16[256,2048]{1,0:T(8,128)(2,1)}, bf16[256,2048]{1,0:T(8,128)(2,1)}, bf16[256,2048]{1,0:T(8,128)(2,1)}) custom-call(bf16[2048,768]{1,0:T(8,128)(2,1)} %bitcast.93, bf16[2048,1408]{1,0:T(8,128)(2,1)} %get-tuple-element.543.refs_1_.refs_3_, bf16[2048,768]{1,0:T(8,128)(2,1)} %bitcast.94, ...), custom_call_target="tpu_custom_call" | custom-call | flops 9126805504 | bytes 17563648 | tf_op jit(solution)/shard_map/normed_part/pallas_call | solution.py:497
  406.2 6.3 %fusion.35 = bf16[1024,768]{1,0:T(8,128)(2,1)S(1)} fusion(bf16[2048,768]{1,0:T(8,128)(2,1)S(1)} %bitcast.95, bf16[2048,2048]{1,0:T(8,128)(2,1)} %get-tuple-element.578), kind=kOutput, calls=%fused_computation.58 | convolution fusion | flops 3222011904 | bytes 8912896 | tf_op jit(solution)/shard_map/dot_general | solution.py:31
  412.6 4.8 fusion.32
  435.3 12.4 %collective-permute-done.49 = bf16[512,768]{1,0:T(8,128)(2,1)S(1)} collective-permute-done((bf16[512,768]{1,0:T(8,128)(2,1)S(1)}, bf16[512,768]{1,0:T(8,128)(2,1)S(1)}, u32[]{:S(2)}, u32[]{:S(2)}) %collective-permute-start.49) | collective-permute-done | bytes 786464 | tf_op jit(solution)/shard_map/ppermute | solution.py:646
  462.6 5.3 collective-permute-start.53
  472.0 9.3 %collective-permute-done.54 = bf16[512,1024]{1,0:T(8,128)(2,1)} collective-permute-done((bf16[512,1024]{1,0:T(8,128)(2,1)}, bf16[512,1024]{1,0:T(8,128)(2,1)}, u32[]{:S(2)}, u32[]{:S(2)}) %collective-permute-start.54) | collective-permute-done | bytes 1048608 | tf_op jit(solution)/shard_map/ppermute | solution.py:646
  481.2 5.8 %add_convert_fusion.2.refs_1_ = bf16[512,1024]{1,0:T(8,128)(2,1)S(1)} fusion(bf16[512,1024]{1,0:T(8,128)(2,1)} %collective-permute-done.54, bf16[2048,1024]{1,0:T(8,128)(2,1)} %bitcast.63, bf16[2048,2048]{1,0:T(8,128)(2,1)} %get-tuple-element.596, bf16[1024,1024]{1,0:T(8,128)(2,1)} %copy-done.45), kind=kOutput, calls=%fused_computation.29 | convolution fusion | flops 2150105088 | bytes 9437184 | tf_op jit(solution)/shard_map/dot_general | solution.py:31
  505.9 6.4 %collective-permute-done.56 = f32[4,2,1,1,128]{4,3,2,1,0:T(1,128)S(1)} collective-permute-done((f32[4,2,1,1,128]{4,3,2,1,0:T(1,128)S(1)}, f32[4,2,1,1,128]{4,3,2,1,0:T(1,128)S(1)}, u32[]{:S(2)}, u32[]{:S(2)}) %collective-permute-start.56) | collective-permute-done | bytes 4128 | tf_op jit(solution)/shard_map/ppermute | solution.py:825
  535.2 28.9 %all-to-all-done.2.held = bf16[8,64,1792]{2,1,0:T(8,128)(2,1)S(1)} async-done(((bf16[8,64,1792]{2,1,0:T(8,128)(2,1)}), bf16[8,64,1792]{2,1,0:T(8,128)(2,1)S(1)}, u32[]{:S(2)}, u32[]{:S(2)}) %all-to-all-start.2) | async-done | bytes 1835040 | tf_op jit(solution)/shard_map/all_to_all | solution.py:832
  (301 shorter events, 174.1 us)
Async XLA Ops:
  15.3 58.0 %all-to-all-start = ((bf16[8,64,2176]{2,1,0:T(8,128)(2,1)}), bf16[8,64,2176]{2,1,0:T(8,128)(2,1)}, u32[]{:S(2)}, u32[]{:S(2)}) async-start(bf16[8,64,2176]{2,1,0:T(8,128)(2,1)} %pack_columns.2), calls=%async_computation | async-start | bytes 4456448 | tf_op jit(solution)/shard_map/all_to_all | solution.py:693
  24.4 52.2 %collective-permute-start.3 = (bf16[256,2048]{1,0:T(8,128)(2,1)}, bf16[256,2048]{1,0:T(8,128)(2,1)}, u32[]{:S(2)}, u32[]{:S(2)}) collective-permute-start(bf16[256,2048]{1,0:T(8,128)(2,1)} %pad_maximum_fusion.refs_0_), channel_id=1, source_target_pairs={{0,1},{1,0},{2,3},{3,2},{4,5},{5,4},{6,7},{7,6},{8,9},{9,8},{10,11... | collective-permute-start | bytes 3145736 | tf_op jit(solution)/shard_map/ppermute | solution.py:694
  26.4 56.5 %collective-permute-start.4 = (bf16[256,2048]{1,0:T(8,128)(2,1)}, bf16[256,2048]{1,0:T(8,128)(2,1)}, u32[]{:S(2)}, u32[]{:S(2)}) collective-permute-start(bf16[256,2048]{1,0:T(8,128)(2,1)} %pad_maximum_fusion.refs_0_), channel_id=1, source_target_pairs={{0,2},{1,3},{2,0},{3,1},{4,6},{5,7},{6,4},{7,5},{8,10},{9,11},{10,... | collective-permute-start | bytes 3145736 | tf_op jit(solution)/shard_map/ppermute | solution.py:694
  30.1 59.3 %collective-permute-start.7 = (bf16[256,2048]{1,0:T(8,128)(2,1)S(1)}, bf16[256,2048]{1,0:T(8,128)(2,1)}, u32[]{:S(2)}, u32[]{:S(2)}) collective-permute-start(bf16[256,2048]{1,0:T(8,128)(2,1)S(1)} %pad_maximum_fusion.1.refs_0_), channel_id=1, source_target_pairs={{0,1},{1,0},{2,3},{3,2},{4,5},{5,4},{6,7},{7,6},{8,9},{9,8},{10,11... | collective-permute-start | bytes 3145736 | tf_op jit(solution)/shard_map/ppermute | solution.py:699
  30.7 70.7 %collective-permute-start.8 = (bf16[256,2048]{1,0:T(8,128)(2,1)S(1)}, bf16[256,2048]{1,0:T(8,128)(2,1)}, u32[]{:S(2)}, u32[]{:S(2)}) collective-permute-start(bf16[256,2048]{1,0:T(8,128)(2,1)S(1)} %pad_maximum_fusion.1.refs_0_), channel_id=1, source_target_pairs={{0,2},{1,3},{2,0},{3,1},{4,6},{5,7},{6,4},{7,5},{8,10},{9,11},{10,... | collective-permute-start | bytes 3145736 | tf_op jit(solution)/shard_map/ppermute | solution.py:700
  31.7 69.7 %collective-permute-start.9 = (bf16[256,2048]{1,0:T(8,128)(2,1)S(1)}, bf16[256,2048]{1,0:T(8,128)(2,1)}, u32[]{:S(2)}, u32[]{:S(2)}) collective-permute-start(bf16[256,2048]{1,0:T(8,128)(2,1)S(1)} %pad_maximum_fusion.1.refs_0_), channel_id=1, source_target_pairs={{2,4},{3,5},{4,2},{5,3},{10,12},{11,13},{12,10},{13,11},{18,20},{1... | collective-permute-start | bytes 3145736 | tf_op jit(solution)/shard_map/ppermute | solution.py:700
  101.4 39.2 %collective-permute-start.14 = (bf16[512,2176]{1,0:T(8,128)(2,1)}, bf16[512,2176]{1,0:T(8,128)(2,1)}, u32[]{:S(2)}, u32[]{:S(2)}) collective-permute-start(bf16[512,2176]{1,0:T(8,128)(2,1)} %get-tuple-element.334), channel_id=1, source_target_pairs={{0,8},{8,0},{16,24},{24,16},{1,9},{9,1},{17,25},{25,17},{2,10},{10... | collective-permute-start | bytes 6684680 | tf_op jit(solution)/shard_map/ppermute | solution.py:646
  101.4 39.2 %collective-permute-start.13 = (bf16[256,2176]{1,0:T(8,128)(2,1)S(1)}, bf16[256,2176]{1,0:T(8,128)(2,1)}, u32[]{:S(2)}, u32[]{:S(2)}) collective-permute-start(bf16[256,2176]{1,0:T(8,128)(2,1)S(1)} %get-tuple-element.531.refs_6_.refs_2_.refs_4_), channel_id=1, source_target_pairs={{0,16},{8,24},{16,0},{24,8},{1,17},{9,25},{17,1},{25,9},{2,18},{10... | collective-permute-start | bytes 3342344 | tf_op jit(solution)/shard_map/ppermute | solution.py:646
  102.9 28.1 %collective-permute-start.10 = (bf16[256,2048]{1,0:T(8,128)(2,1)}, bf16[256,2048]{1,0:T(8,128)(2,1)}, u32[]{:S(2)}, u32[]{:S(2)}) collective-permute-start(bf16[256,2048]{1,0:T(8,128)(2,1)} %collective-permute-done.8.refs_2_), channel_id=1, source_target_pairs={{0,1},{1,0},{2,3},{3,2},{4,5},{5,4},{6,7},{7,6},{8,9},{9,8},{10,11... | collective-permute-start | bytes 3145736 | tf_op jit(solution)/shard_map/ppermute | solution.py:646
  106.0 34.6 %collective-permute-start.12 = (bf16[256,2048]{1,0:T(8,128)(2,1)}, bf16[256,2048]{1,0:T(8,128)(2,1)}, u32[]{:S(2)}, u32[]{:S(2)}) collective-permute-start(bf16[256,2048]{1,0:T(8,128)(2,1)} %collective-permute-done.9), channel_id=1, source_target_pairs={{2,0},{3,1},{4,6},{5,7},{10,8},{11,9},{12,14},{13,15},{18,16},{19,... | collective-permute-start | bytes 3145736 | tf_op jit(solution)/shard_map/ppermute | solution.py:646
  113.0 66.6 %all-to-all-start.1 = ((bf16[8,64,1024]{2,1,0:T(8,128)(2,1)}), bf16[8,64,1024]{2,1,0:T(8,128)(2,1)S(1)}, u32[]{:S(2)}, u32[]{:S(2)}) async-start(bf16[8,64,1024]{2,1,0:T(8,128)(2,1)} %pack_columns.3), calls=%async_computation.1 | async-start | bytes 2097152 | tf_op jit(solution)/shard_map/all_to_all | solution.py:705
  140.6 36.6 %collective-permute-start.18 = (bf16[256,2176]{1,0:T(8,128)(2,1)S(1)}, bf16[256,2176]{1,0:T(8,128)(2,1)}, u32[]{:S(2)}, u32[]{:S(2)}) collective-permute-start(bf16[256,2176]{1,0:T(8,128)(2,1)S(1)} %get-tuple-element.532.refs_7_.refs_3_.refs_5_), channel_id=1, source_target_pairs={{0,16},{8,24},{16,0},{24,8},{1,17},{9,25},{17,1},{25,9},{2,18},{10... | collective-permute-start | bytes 3342344 | tf_op jit(solution)/shard_map/ppermute | solution.py:646
  141.2 36.1 %collective-permute-start.19 = (bf16[256,2176]{1,0:T(8,128)(2,1)}, bf16[256,2176]{1,0:T(8,128)(2,1)S(1)}, u32[]{:S(2)}, u32[]{:S(2)}) collective-permute-start(bf16[256,2176]{1,0:T(8,128)(2,1)} %collective-permute-done.13.refs_8_.refs_4_.refs_6_), channel_id=1, source_target_pairs={{0,8},{8,0},{16,24},{24,16},{1,9},{9,1},{17,25},{25,17},{2,10},{10... | collective-permute-start | bytes 3342344 | tf_op jit(solution)/shard_map/ppermute | solution.py:646
  143.3 33.9 %collective-permute-start.16 = (bf16[256,2048]{1,0:T(8,128)(2,1)}, bf16[256,2048]{1,0:T(8,128)(2,1)S(1)}, u32[]{:S(2)}, u32[]{:S(2)}) collective-permute-start(bf16[256,2048]{1,0:T(8,128)(2,1)} %collective-permute-done.11), channel_id=1, source_target_pairs={{2,0},{3,1},{4,6},{5,7},{10,8},{11,9},{12,14},{13,15},{18,16},{19,... | collective-permute-start | bytes 3145736 | tf_op jit(solution)/shard_map/ppermute | solution.py:646
  144.6 32.7 %collective-permute-start.17 = (bf16[256,2048]{1,0:T(8,128)(2,1)}, bf16[256,2048]{1,0:T(8,128)(2,1)S(1)}, u32[]{:S(2)}, u32[]{:S(2)}) collective-permute-start(bf16[256,2048]{1,0:T(8,128)(2,1)} %pad_maximum_fusion.refs_0_), channel_id=1, source_target_pairs={{2,4},{3,5},{4,2},{5,3},{10,12},{11,13},{12,10},{13,11},{18,20},{1... | collective-permute-start | bytes 3145736 | tf_op jit(solution)/shard_map/ppermute | solution.py:646
  179.7 58.5 %collective-permute-start.26 = (bf16[512,1024]{1,0:T(8,128)(2,1)S(1)}, bf16[512,1024]{1,0:T(8,128)(2,1)}, u32[]{:S(2)}, u32[]{:S(2)}) collective-permute-start(bf16[512,1024]{1,0:T(8,128)(2,1)S(1)} %unpack_columns.3.refs_4_.refs_8_), channel_id=1, source_target_pairs={{0,16},{8,24},{16,0},{24,8},{1,17},{9,25},{17,1},{25,9},{2,18},{10... | collective-permute-start | bytes 3145736 | tf_op jit(solution)/shard_map/ppermute | solution.py:646
  180.3 57.9 %collective-permute-start.27 = (bf16[512,1024]{1,0:T(8,128)(2,1)S(1)}, bf16[512,1024]{1,0:T(8,128)(2,1)}, u32[]{:S(2)}, u32[]{:S(2)}) collective-permute-start(bf16[512,1024]{1,0:T(8,128)(2,1)S(1)} %unpack_columns.3.refs_4_.refs_8_), channel_id=1, source_target_pairs={{0,8},{8,0},{16,24},{24,16},{1,9},{9,1},{17,25},{25,17},{2,10},{10... | collective-permute-start | bytes 3145736 | tf_op jit(solution)/shard_map/ppermute | solution.py:646
  208.7 29.6 %collective-permute-start.24 = (bf16[256,2048]{1,0:T(8,128)(2,1)S(1)}, bf16[256,2048]{1,0:T(8,128)(2,1)}, u32[]{:S(2)}, u32[]{:S(2)}) collective-permute-start(bf16[256,2048]{1,0:T(8,128)(2,1)S(1)} %broadcast_select_fusion.1.refs_4_), channel_id=1, source_target_pairs={{0,1},{1,0},{2,3},{3,2},{4,5},{5,4},{6,7},{7,6},{8,9},{9,8},{10,11... | collective-permute-start | bytes 3145736 | tf_op jit(solution)/shard_map/ppermute | solution.py:646
  240.2 28.8 %collective-permute-start.29 = (bf16[256,2048]{1,0:T(8,128)(2,1)}, bf16[256,2048]{1,0:T(8,128)(2,1)S(1)}, u32[]{:S(2)}, u32[]{:S(2)}) collective-permute-start(bf16[256,2048]{1,0:T(8,128)(2,1)} %collective-permute-done.3.refs_1_), channel_id=1, source_target_pairs={{0,2},{1,3},{2,0},{3,1},{4,6},{5,7},{6,4},{7,5},{8,10},{9,11},{10,... | collective-permute-start | bytes 3145736 | tf_op jit(solution)/shard_map/ppermute | solution.py:646
  269.0 32.5 %collective-permute-start.31 = (bf16[256,2048]{1,0:T(8,128)(2,1)}, bf16[256,2048]{1,0:T(8,128)(2,1)S(1)}, u32[]{:S(2)}, u32[]{:S(2)}) collective-permute-start(bf16[256,2048]{1,0:T(8,128)(2,1)} %get-tuple-element.473), channel_id=1, source_target_pairs={{0,1},{1,0},{2,3},{3,2},{4,5},{5,4},{6,7},{7,6},{8,9},{9,8},{10,11... | collective-permute-start | bytes 3145736 | tf_op jit(solution)/shard_map/ppermute | solution.py:646
  270.6 30.9 %collective-permute-start.32 = (bf16[256,2048]{1,0:T(8,128)(2,1)}, bf16[256,2048]{1,0:T(8,128)(2,1)S(1)}, u32[]{:S(2)}, u32[]{:S(2)}) collective-permute-start(bf16[256,2048]{1,0:T(8,128)(2,1)} %get-tuple-element.469), channel_id=1, source_target_pairs={{0,2},{1,3},{2,0},{3,1},{4,6},{5,7},{6,4},{7,5},{8,10},{9,11},{10,... | collective-permute-start | bytes 3145736 | tf_op jit(solution)/shard_map/ppermute | solution.py:646
  301.6 33.8 %collective-permute-start.33 = (bf16[256,2048]{1,0:T(8,128)(2,1)}, bf16[256,2048]{1,0:T(8,128)(2,1)S(1)}, u32[]{:S(2)}, u32[]{:S(2)}) collective-permute-start(bf16[256,2048]{1,0:T(8,128)(2,1)} %get-tuple-element.495), channel_id=1, source_target_pairs={{0,1},{1,0},{2,3},{3,2},{4,5},{5,4},{6,7},{7,6},{8,9},{9,8},{10,11... | collective-permute-start | bytes 3145736 | tf_op jit(solution)/shard_map/ppermute | solution.py:646
  302.4 33.0 %collective-permute-start.34 = (bf16[256,2048]{1,0:T(8,128)(2,1)S(1)}, bf16[256,2048]{1,0:T(8,128)(2,1)S(1)}, u32[]{:S(2)}, u32[]{:S(2)}) collective-permute-start(bf16[256,2048]{1,0:T(8,128)(2,1)S(1)} %add_convert_fusion.15), channel_id=1, source_target_pairs={{0,2},{1,3},{6,4},{7,5},{8,10},{9,11},{14,12},{15,13},{16,18},{17,... | collective-permute-start | bytes 3145736 | tf_op jit(solution)/shard_map/ppermute | solution.py:646
  339.3 33.4 %collective-permute-start.39 = (bf16[512,1408]{1,0:T(8,128)(2,1)}, bf16[512,1408]{1,0:T(8,128)(2,1)S(1)}, u32[]{:S(2)}, u32[]{:S(2)}) collective-permute-start(bf16[512,1408]{1,0:T(8,128)(2,1)} %fusion.10), channel_id=1, source_target_pairs={{0,16},{8,24},{16,0},{24,8},{1,17},{9,25},{17,1},{25,9},{2,18},{10... | collective-permute-start | bytes 4325384 | tf_op jit(solution)/shard_map/ppermute | solution.py:646
  372.7 29.4 %collective-permute-start.40 = (bf16[256,2048]{1,0:T(8,128)(2,1)}, bf16[256,2048]{1,0:T(8,128)(2,1)S(1)}, u32[]{:S(2)}, u32[]{:S(2)}) collective-permute-start(bf16[256,2048]{1,0:T(8,128)(2,1)} %get-tuple-element.554), channel_id=1, source_target_pairs={{0,1},{1,0},{2,3},{3,2},{4,5},{5,4},{6,7},{7,6},{8,9},{9,8},{10,11... | collective-permute-start | bytes 3145736 | tf_op jit(solution)/shard_map/ppermute | solution.py:646
  374.1 28.0 %collective-permute-start.41 = (bf16[256,2048]{1,0:T(8,128)(2,1)S(1)}, bf16[256,2048]{1,0:T(8,128)(2,1)S(1)}, u32[]{:S(2)}, u32[]{:S(2)}) collective-permute-start(bf16[256,2048]{1,0:T(8,128)(2,1)S(1)} %add_convert_fusion.11), channel_id=1, source_target_pairs={{2,4},{3,5},{4,2},{5,3},{10,12},{11,13},{12,10},{13,11},{18,20},{1... | collective-permute-start | bytes 3145736 | tf_op jit(solution)/shard_map/ppermute | solution.py:646
  426.7 28.0 %collective-permute-start.46 = (bf16[256,2048]{1,0:T(8,128)(2,1)S(1)}, bf16[256,2048]{1,0:T(8,128)(2,1)S(1)}, u32[]{:S(2)}, u32[]{:S(2)}) collective-permute-start(bf16[256,2048]{1,0:T(8,128)(2,1)S(1)} %copy-done.46), channel_id=1, source_target_pairs={{0,1},{1,0},{2,3},{3,2},{4,5},{5,4},{6,7},{7,6},{8,9},{9,8},{10,11... | collective-permute-start | bytes 3145736 | tf_op jit(solution)/shard_map/ppermute | solution.py:646
  456.3 32.1 %collective-permute-start.51 = (bf16[256,2048]{1,0:T(8,128)(2,1)}, bf16[256,2048]{1,0:T(8,128)(2,1)}, u32[]{:S(2)}, u32[]{:S(2)}) collective-permute-start(bf16[256,2048]{1,0:T(8,128)(2,1)} %get-tuple-element.599), channel_id=1, source_target_pairs={{0,1},{1,0},{2,3},{3,2},{4,5},{5,4},{6,7},{7,6},{8,9},{9,8},{10,11... | collective-permute-start | bytes 3145736 | tf_op jit(solution)/shard_map/ppermute | solution.py:646
  459.4 29.0 %collective-permute-start.52 = (bf16[256,2048]{1,0:T(8,128)(2,1)}, bf16[256,2048]{1,0:T(8,128)(2,1)}, u32[]{:S(2)}, u32[]{:S(2)}) collective-permute-start(bf16[256,2048]{1,0:T(8,128)(2,1)} %add_convert_fusion.4), channel_id=1, source_target_pairs={{2,4},{3,5},{4,2},{5,3},{10,12},{11,13},{12,10},{13,11},{18,20},{1... | collective-permute-start | bytes 3145736 | tf_op jit(solution)/shard_map/ppermute | solution.py:646
  462.6 29.7 %collective-permute-start.53 = (bf16[256,2048]{1,0:T(8,128)(2,1)}, bf16[256,2048]{1,0:T(8,128)(2,1)}, u32[]{:S(2)}, u32[]{:S(2)}) collective-permute-start(bf16[256,2048]{1,0:T(8,128)(2,1)} %add_convert_fusion.3), channel_id=1, source_target_pairs={{0,2},{1,3},{2,0},{3,1},{4,6},{5,7},{6,4},{7,5},{8,10},{9,11},{10,... | collective-permute-start | bytes 3145736 | tf_op jit(solution)/shard_map/ppermute | solution.py:646
  467.8 51.9 %all-to-all-start.3 = ((bf16[8,64,1408]{2,1,0:T(8,128)(2,1)}), bf16[8,64,1408]{2,1,0:T(8,128)(2,1)S(1)}, u32[]{:S(2)}, u32[]{:S(2)}) async-start(bf16[8,64,1408]{2,1,0:T(8,128)(2,1)} %pack_rows.2), calls=%async_computation.3 | async-start | bytes 2883584 | tf_op jit(solution)/shard_map/all_to_all | solution.py:811
  519.7 44.4 %all-to-all-start.2 = ((bf16[8,64,1792]{2,1,0:T(8,128)(2,1)}), bf16[8,64,1792]{2,1,0:T(8,128)(2,1)S(1)}, u32[]{:S(2)}, u32[]{:S(2)}) async-start(bf16[8,64,1792]{2,1,0:T(8,128)(2,1)} %pack_rows.3), calls=%async_computation.2 | async-start | bytes 3670016 | tf_op jit(solution)/shard_map/all_to_all | solution.py:832
  (86 other events, 1591.2 us)

commit v9 on v8

--- a/solution.py
+++ b/solution.py
@@ -256,14 +256,16 @@
             out[index * own : (index + 1) * own, :] = block
 
 
-def pack_rows_kernel(own, *refs):
+def pack_rows_kernel(own, counts, *refs):
     sources, out = refs[:-1], refs[-1]
-    for dest in range(out.shape[0]):
-        lane = 0
-        for source in sources:
-            lanes = source.shape[1]
-            out[dest, :, lane : lane + lanes] = source[dest * own : (dest + 1) * own, :]
-            lane += lanes
+    lane = 0
+    for count in counts:
+        chunks, sources = sources[:count], sources[count:]
+        lanes = chunks[0].shape[1]
+        for dest in range(out.shape[0]):
+            chunk, row = divmod(dest * own, chunks[0].shape[0])
+            out[dest, :, lane : lane + lanes] = chunks[chunk][row : row + own, :]
+        lane += lanes
 
 
 def unpack_rows_kernel(n, layout, held, *outs):
@@ -311,9 +313,10 @@
 
 
 def pack_rows(own, n, gradients):
-    lanes = sum(g.shape[1] for g in gradients)
+    lanes = sum(chunks[0].shape[1] for chunks in gradients)
     shape = jax.ShapeDtypeStruct((n, own, lanes), BF)
-    return in_vmem(functools.partial(pack_rows_kernel, own), "pack_rows", shape)(*gradients)
+    kernel = functools.partial(pack_rows_kernel, own, [len(chunks) for chunks in gradients])
+    return in_vmem(kernel, "pack_rows", shape)(*[c for chunks in gradients for c in chunks])
 
 
 def unpack_rows(plan, packed, chosen, begins):
@@ -618,7 +621,7 @@
     d_normed = scatter(dot_last(d_first, w_first).astype(BF), "ctx")
     sums = [scatter(dot_first(*v).astype(BF), "dp") for v in ((normed, d_first), (cot, wide))]
     begins = (0, plan.joined, plan.first)
-    grads = unpack_rows(plan, swap(pack_rows(own, n, sums)), [0, 1, 2, 3, 4], begins)
+    grads = unpack_rows(plan, swap(pack_rows(own, n, [[v] for v in sums])), [0, 1, 2, 3, 4], begins)
     input_grad, norm_sums = layer.norm_back(d_normed, standard, inverse, gain)
     return layer.finish_output(branches), input_grad, scatter(norm_sums, ("dp", "ctx")), grads
 
@@ -772,7 +775,8 @@
 
     def product(s, name, begin, end):
         left, right = factors[name]
-        return dot_first(s[left][:, begin * quarter : end * quarter], s[right])
+        rows = slice(int(begin * quarter), int(end * quarter))
+        return dot_first(s[left][:, rows], s[right])
 
     def grad_a(name):
         return lambda s: {name + "A": product(s, name, 2, 4).astype(BF)}
@@ -791,6 +795,22 @@
 
         return work
 
+    def half_b(step):
+        def work(s):
+            rows = slice((2 + step) * quarter // 2, (3 + step) * quarter // 2)
+            total = product(s, "G", 1 + step / 2, 1.5 + step / 2) + s["GAr"][rows].astype(F32)
+            return {f"GB{step + 1}": total.astype(BF)}
+
+        return work
+
+    def half_c(step):
+        def work(s):
+            rows = slice(step * quarter // 2, (step + 1) * quarter // 2)
+            total = product(s, "G", step / 2, (step + 1) / 2) + s["GAr"][rows].astype(F32)
+            return {f"GC{step + 1}": (total + s[f"GB{step + 1}r"].astype(F32)).astype(BF)}
+
+        return work
+
     def to(name, source, way):
         return (name, source, *way)
 
@@ -804,7 +824,11 @@
         return to(name + "Br", name + "B", across)
 
     def packed_rows(*names):
-        return lambda s: {names: pack_rows(own, n, [s[name + "C"] for name in names])}
+        def work(s):
+            chunks = [[s[name + "C"]] if name != "G" else [s["GC1"], s["GC2"]] for name in names]
+            return {names: pack_rows(own, n, chunks)}
+
+        return work
 
     def swap_packed(*names):
         def work(s):
@@ -887,27 +911,27 @@
     tick(
         [select("c3")],
         [to("c3x", "c3", side), to("c1x", "c0x", pair), far("w")],
-        [output_part(0, 1, 2, 3)],
+        [output_part(0, 1, 2, 3), bring_back(0, 2)],
     )
     tick(
         (),
         [to("o3x", "o3a", side), to("o1p", "o1a", pair)],
-        [bring_back(0, 1, 2, 3), grad_a("G")],
+        [bring_back(1, 3), grad_a("G")],
     )
     tick(
         [plus("o3", "o3k", "o3x")],
         [to("o2x", "o2a", side), to("o3i", "o3", inward), send_a("G")],
-        [attend_back, grad_b("G")],
+        [attend_back, half_b(0), half_b(1)],
     )
     tick(
         [plus("o2", "o2k", "o2x"), plus("o3", "o3", "o3i"), plus("o0a", "o0a", "o1p")],
-        [to("o0x", "o0a", side), to("o2i", "o2", inward), to("o3m", "o3", middle), send_b("G")],
+        [to("o0x", "o0a", side), to("o2i", "o2", inward), to("o3m", "o3", middle), to("GB1r", "GB1", across)],
         [normed_part(1, 3)],
     )
     tick(
         [plus("o2", "o2", "o2i"), plus("o1", "o1k", "o3m")],
-        [to("d3x", "d3a", side), to("o2m", "o2", middle), to("o1r", "o1", pair)],
-        [normed_part(0, 2), grad_c("G"), packed_rows("G")],
+        [to("d3x", "d3a", side), to("o2m", "o2", middle), to("o1r", "o1", pair), to("GB2r", "GB2", across)],
+        [normed_part(0, 2), half_c(0), half_c(1), packed_rows("G")],
     )
     tick(
         [plus("d3", "d3k", "d3x")],

time: 575 us -> 572 us (level)
  waiting for transfers between devices: 219 us -> 199 us
  other arithmetic: 33.1 us -> 39.1 us
    ppermute x44 -> x45, waiting for transfers between devices: 109 us -> 90.6 us  [tick(): view[name] = lax.ppermute(self.held[source], axis, pairs)]
    convert_element_type x13, other arithmetic: 10.5 us -> 16.4 us  [plus(): sum((s[part].astype(F32) for part in parts)).astype(BF)]
    pallas_call x3 -> x4, Pallas kernels: 50.6 us -> 56 us  [stream(): pl.pallas_call(functools.partial(stream_kernel, n, len(pieces), len(extra...]
    ppermute x44 -> x45, starting transfers between devices: 58 us -> 61.9 us  [tick(): view[name] = lax.ppermute(self.held[source], axis, pairs)]
    dot_general x9 -> x11, matrix products: 55 us -> 54.5 us  [dot_first(): return lax.dot_general(left, right, FIRST, preferred_element_type=F32)]
  transfers between devices with their start and end apart: 64 -> 65, of which waited for: 29 -> 29; matrix products, arithmetic and copies ran while one was open for 16% -> 17% of each run, Pallas kernels for 25% -> 26%
where the time goes in v9:
time: 572 us; the launch traced here: 563 us
  waiting for transfers between devices  199 us (35%)
  Pallas kernels  151 us (26%)
  starting transfers between devices  105 us (18%)
  matrix products  54.5 us (10%)
  other arithmetic  39.1 us (7%)
  local copies, waits for them, and re-layouts  12.3 us (2%)
    ppermute x45, waiting for transfers between devices, tick(): view[name] = lax.ppermute(self.held[source], axis, pairs)  90.6 us
    ppermute x45, starting transfers between devices, tick(): view[name] = lax.ppermute(self.held[source], axis, pairs)  61.9 us
    pallas_call x4, Pallas kernels, stream(): pl.pallas_call(functools.partial(stream_kernel, n, len(pieces), len(extra...  56 us
    dot_general x11, matrix products, dot_first(): return lax.dot_general(left, right, FIRST, preferred_element_type=F32)  54.5 us
    pallas_call x3, Pallas kernels, spread(): pl.pallas_call(functools.partial(spread_kernel, len(lefts), len(pieces),...  45.8 us
    all_to_all x1, waiting for transfers between devices, begin(): lax.all_to_all(packed, 'ctx', split_axis=0, concat_axis=0, tiled=True)  38.1 us
    all_to_all x1, waiting for transfers between devices, norm_back(): lax.all_to_all(packed, 'ctx', split_axis=0, concat_axis=0, tiled=True)  28.7 us
    pallas_call x1, Pallas kernels, attend_back(): self.calls(lanes)[1]  21.4 us
  transfers between devices with their start and end apart: 65, of which 29 were waited for; matrix products, arithmetic and copies ran while one was open for 17% of the time, Pallas kernels for 26%

profile of v9, /device:TPU:0, one launch (start us, length us, event | category | flops | bytes accessed | tf_op | source)
XLA Modules:
  0.0 563.0 jit_solution(16545196920617654473)
XLA Ops:
  15.3 5.4 all-to-all-start
  35.2 38.1 %all-to-all-done.in_ref = bf16[8,64,2176]{2,1,0:T(8,128)(2,1)} async-done(((bf16[8,64,2176]{2,1,0:T(8,128)(2,1)}), bf16[8,64,2176]{2,1,0:T(8,128)(2,1)}, u32[]{:S(2)}, u32[]{:S(2)}) %all-to-all-start) | async-done | bytes 2228256 | tf_op jit(solution)/shard_map/all_to_all | solution.py:696
  76.6 6.3 %collective-permute-done.4.refs_0_ = bf16[256,2048]{1,0:T(8,128)(2,1)} collective-permute-done((bf16[256,2048]{1,0:T(8,128)(2,1)}, bf16[256,2048]{1,0:T(8,128)(2,1)}, u32[]{:S(2)}, u32[]{:S(2)}) %collective-permute-start.4) | collective-permute-done | bytes 1048608 | tf_op jit(solution)/shard_map/ppermute | solution.py:697
  82.9 6.6 %collective-permute-done.7.refs_1_ = bf16[256,2048]{1,0:T(8,128)(2,1)} collective-permute-done((bf16[256,2048]{1,0:T(8,128)(2,1)S(1)}, bf16[256,2048]{1,0:T(8,128)(2,1)}, u32[]{:S(2)}, u32[]{:S(2)}) %collective-permute-start.7) | collective-permute-done | bytes 1048608 | tf_op jit(solution)/shard_map/ppermute | solution.py:702
  89.5 12.0 %collective-permute-done.8.refs_2_ = bf16[256,2048]{1,0:T(8,128)(2,1)} collective-permute-done((bf16[256,2048]{1,0:T(8,128)(2,1)S(1)}, bf16[256,2048]{1,0:T(8,128)(2,1)}, u32[]{:S(2)}, u32[]{:S(2)}) %collective-permute-start.8) | collective-permute-done | bytes 1048608 | tf_op jit(solution)/shard_map/ppermute | solution.py:703
  107.4 5.7 %fusion.49 = (f32[1024,256]{1,0:T(8,128)}, f32[1024,256]{1,0:T(8,128)}) fusion(f32[256]{0:T(256)S(1)} %fusion.65, f32[1024]{0:T(1024)S(1)} %iota_convert_fusion, pred[256]{0:T(512)(128)(4,1)S(1)} %get-tuple-element.678, pred[256]{0:T(512)(128)(4,1)S(1)} %get-tuple-element.679), kind=kLoop, calls=%fused_computation.68 | loop fusion | flops 1310720 | bytes 2102784 | tf_op jit(solution)/shard_map/jit(_where)/select_n | solution.py:41
  113.1 5.8 %all-to-all-start.1 = ((bf16[8,64,1024]{2,1,0:T(8,128)(2,1)}), bf16[8,64,1024]{2,1,0:T(8,128)(2,1)S(1)}, u32[]{:S(2)}, u32[]{:S(2)}) async-start(bf16[8,64,1024]{2,1,0:T(8,128)(2,1)} %pack_columns.3), calls=%async_computation.1 | async-start | bytes 2097152 | tf_op jit(solution)/shard_map/all_to_all | solution.py:708
  118.9 12.2 %collective-permute-done.10.refs_3_ = bf16[256,2048]{1,0:T(8,128)(2,1)} collective-permute-done((bf16[256,2048]{1,0:T(8,128)(2,1)}, bf16[256,2048]{1,0:T(8,128)(2,1)}, u32[]{:S(2)}, u32[]{:S(2)}) %collective-permute-start.10) | collective-permute-done | bytes 1048608 | tf_op jit(solution)/shard_map/ppermute | solution.py:649
  131.1 9.6 %collective-permute-done.12 = bf16[256,2048]{1,0:T(8,128)(2,1)} collective-permute-done((bf16[256,2048]{1,0:T(8,128)(2,1)}, bf16[256,2048]{1,0:T(8,128)(2,1)}, u32[]{:S(2)}, u32[]{:S(2)}) %collective-permute-start.12) | collective-permute-done | bytes 1048608 | tf_op jit(solution)/shard_map/ppermute | solution.py:649
  145.4 25.2 %collective-permute-done.15.refs_5_ = bf16[256,2048]{1,0:T(8,128)(2,1)S(1)} collective-permute-done((bf16[256,2048]{1,0:T(8,128)(2,1)S(1)}, bf16[256,2048]{1,0:T(8,128)(2,1)S(1)}, u32[]{:S(2)}, u32[]{:S(2)}) %collective-permute-start.15) | collective-permute-done | bytes 1048608 | tf_op jit(solution)/shard_map/ppermute | solution.py:649
  170.6 6.7 %collective-permute-done.16 = bf16[256,2048]{1,0:T(8,128)(2,1)S(1)} collective-permute-done((bf16[256,2048]{1,0:T(8,128)(2,1)}, bf16[256,2048]{1,0:T(8,128)(2,1)S(1)}, u32[]{:S(2)}, u32[]{:S(2)}) %collective-permute-start.16) | collective-permute-done | bytes 1048608 | tf_op jit(solution)/shard_map/ppermute | solution.py:649
  184.6 22.1 %project.2 = (bf16[2048,2048]{1,0:T(8,128)(2,1)}, f32[2048,768]{1,0:T(8,128)}, bf16[2048,1408]{1,0:T(8,128)(2,1)}, bf16[2048,1024]{1,0:T(8,128)(2,1)}) custom-call(bf16[256,2048]{1,0:T(8,128)(2,1)S(1)} %copy-done.6, bf16[256,2048]{1,0:T(8,128)(2,1)} %collective-permute-done.7.refs_1_, bf16[256,2048]{1,0:T(8,128)(2,1)} %collective-permute-done.8.refs_2_, ...), custom_call_target="tpu_custom_call" | custom-call | flops 13690208256 | bytes 30408704 | tf_op jit(solution)/shard_map/project/pallas_call | solution.py:400
  212.7 11.1 %project.3 = (bf16[2048,2048]{1,0:T(8,128)(2,1)}, f32[2048,768]{1,0:T(8,128)}, bf16[2048,1408]{1,0:T(8,128)(2,1)}, bf16[2048,1024]{1,0:T(8,128)(2,1)}) custom-call(bf16[256,2048]{1,0:T(8,128)(2,1)S(1)} %broadcast_select_fusion.2.refs_0_, bf16[256,2048]{1,0:T(8,128)(2,1)} %copy-done.27, ...), custom_call_target="tpu_custom_call", output_to_operand_aliasing={{0}: (9, {}), {1}: (10, {}), {2}: (11, {}), {3}: (12, {})} | custom-call | flops 4563402752 | bytes 22020096 | tf_op jit(solution)/shard_map/project/pallas_call | solution.py:400
  223.8 14.8 %attend_forward.1 = (bf16[8,2,128,768]{3,2,1,0:T(8,128)(2,1)}, bf16[8,2,128,1024]{3,2,1,0:T(8,128)(2,1)}, f32[8,2,128,4]{3,2,1,0:T(8,128)S(1)}) custom-call(s32[2]{0:T(128)S(1)} %copy-done.12, s32[8]{0:T(128)S(1)} %compare_select_fusion.8.slot_ref, f32[8,2,128,768]{3,2,1,0:T(8,128)} %bitcast.65, ...), custom_call_target="tpu_custom_call", output_to_operand_aliasing={{1}: (5, {})} | custom-call | flops 4294967296 | bytes 4194304 | tf_op jit(solution)/shard_map/attend_forward/pallas_call | solution.py:555
  240.7 4.9 collective-permute-start.29
  246.5 11.5 %bring_back.2 = (bf16[2048,2048]{1,0:T(8,128)(2,1)}, bf16[2048,256]{1,0:T(8,128)(2,1)S(1)}, bf16[2048,1408]{1,0:T(8,128)(2,1)}) custom-call(bf16[256,2048]{1,0:T(8,128)(2,1)} %pad_maximum_fusion.refs_0_, bf16[256,2048]{1,0:T(8,128)(2,1)} %collective-permute-done.3.refs_1_, bf16[256,2048]{1,0:T(8,128)(2,1)} %copy-done.37, ...), custom_call_target="tpu_custom_call" | custom-call | flops 4294967296 | bytes 16777216 | tf_op jit(solution)/shard_map/bring_back/pallas_call | solution.py:400
  258.0 14.4 %output_part.1 = (bf16[256,2048]{1,0:T(8,128)(2,1)S(1)}, bf16[256,2048]{1,0:T(8,128)(2,1)}, bf16[256,2048]{1,0:T(8,128)(2,1)}, bf16[256,2048]{1,0:T(8,128)(2,1)}...) custom-call(bf16[2048,1024]{1,0:T(8,128)(2,1)} %bitcast.67, ...), custom_call_target="tpu_custom_call" | custom-call | flops 8589934592 | bytes 16777216 | tf_op jit(solution)/shard_map/output_part/pallas_call | solution.py:500
  274.2 11.3 %bring_back.3 = (bf16[2048,2048]{1,0:T(8,128)(2,1)}, bf16[2048,256]{1,0:T(8,128)(2,1)S(1)}, bf16[2048,1408]{1,0:T(8,128)(2,1)}) custom-call(bf16[256,2048]{1,0:T(8,128)(2,1)} %collective-permute-done.4.refs_0_, bf16[256,2048]{1,0:T(8,128)(2,1)} %copy-done.36, ...), custom_call_target="tpu_custom_call", output_to_operand_aliasing={{0}: (8, {}), {1}: (9, {}), {2}: (10, {})} | custom-call | flops 4294967296 | bytes 16777216 | tf_op jit(solution)/shard_map/bring_back/pallas_call | solution.py:400
  285.5 11.7 %fusion.6 = bf16[1024,1408]{1,0:T(8,128)(2,1)} fusion(bf16[2048,1408]{1,0:T(8,128)(2,1)} %get-tuple-element.550.refs_1_.refs_3_, bf16[2048,2048]{1,0:T(8,128)(2,1)} %get-tuple-element.586), kind=kOutput, calls=%fused_computation.6 | convolution fusion | flops 5907021824 | bytes 12845056 | tf_op jit(solution)/shard_map/dot_general | solution.py:31
  305.2 21.4 %attend_backward.1 = bf16[8,2,128,768]{3,2,1,0:T(8,128)(2,1)} custom-call(s32[2]{0:T(128)S(1)} %copy-done.12, s32[8]{0:T(128)S(1)} %compare_select_fusion.8.slot_ref, bf16[8,2,128,768]{3,2,1,0:T(8,128)(2,1)} %get-tuple-element.495.rot_ref, bf16[8,2,128,1024]{3,2,1,0:T(8,128)(2,1)} %get-tuple-element.407, bf16[8,2,128,256]{3,2,1,0:T(8,128)(2,1)S(1)} %bitcast.58, ...), custom_call_target="tpu_custom_call" | custom-call | flops 10737418240 | bytes 4194304 | tf_op jit(solution)/shard_map/attend_backward/pallas_call | solution.py:562
  326.7 4.7 fusion.11
  343.2 15.6 %normed_part.2 = (bf16[256,2048]{1,0:T(8,128)(2,1)S(1)}, bf16[256,2048]{1,0:T(8,128)(2,1)}, bf16[256,2048]{1,0:T(8,128)(2,1)}, bf16[256,2048]{1,0:T(8,128)(2,1)}) custom-call(bf16[2048,768]{1,0:T(8,128)(2,1)} %bitcast.99, bf16[2048,1408]{1,0:T(8,128)(2,1)} %get-tuple-element.550.refs_1_.refs_3_, bf16[2048,768]{1,0:T(8,128)(2,1)} %bitcast.100, ...), custom_call_target="tpu_custom_call" | custom-call | flops 9126805504 | bytes 17563648 | tf_op jit(solution)/shard_map/normed_part/pallas_call | solution.py:500
  366.1 7.4 %collective-permute-start.42 = (bf16[256,2048]{1,0:T(8,128)(2,1)}, bf16[256,2048]{1,0:T(8,128)(2,1)S(1)}, u32[]{:S(2)}, u32[]{:S(2)}) collective-permute-start(bf16[256,2048]{1,0:T(8,128)(2,1)} %add_convert_fusion.10), channel_id=1, source_target_pairs={{0,2},{1,3},{2,0},{3,1},{4,6},{5,7},{6,4},{7,5},{8,10},{9,11},{10,... | collective-permute-start | bytes 3145736 | tf_op jit(solution)/shard_map/ppermute | solution.py:649
  374.2 15.7 %normed_part.3 = (bf16[256,2048]{1,0:T(8,128)(2,1)S(1)}, bf16[256,2048]{1,0:T(8,128)(2,1)}, bf16[256,2048]{1,0:T(8,128)(2,1)}, bf16[256,2048]{1,0:T(8,128)(2,1)}) custom-call(bf16[2048,768]{1,0:T(8,128)(2,1)} %bitcast.101, bf16[2048,1408]{1,0:T(8,128)(2,1)} %get-tuple-element.550.refs_1_.refs_3_, bf16[2048,768]{1,0:T(8,128)(2,1)} %bitcast.102, ...), custom_call_target="tpu_custom_call" | custom-call | flops 9126805504 | bytes 17563648 | tf_op jit(solution)/shard_map/normed_part/pallas_call | solution.py:500
  403.7 5.7 %fusion.36 = bf16[1024,768]{1,0:T(8,128)(2,1)S(1)} fusion(bf16[2048,768]{1,0:T(8,128)(2,1)S(1)} %bitcast.103, bf16[2048,2048]{1,0:T(8,128)(2,1)} %get-tuple-element.586), kind=kOutput, calls=%fused_computation.61 | convolution fusion | flops 3222011904 | bytes 8912896 | tf_op jit(solution)/shard_map/dot_general | solution.py:31
  409.6 4.8 fusion.33
  431.6 12.4 %collective-permute-done.50 = bf16[512,768]{1,0:T(8,128)(2,1)S(1)} collective-permute-done((bf16[512,768]{1,0:T(8,128)(2,1)S(1)}, bf16[512,768]{1,0:T(8,128)(2,1)S(1)}, u32[]{:S(2)}, u32[]{:S(2)}) %collective-permute-start.50) | collective-permute-done | bytes 786464 | tf_op jit(solution)/shard_map/ppermute | solution.py:649
  459.4 4.8 collective-permute-start.54
  468.4 9.7 %collective-permute-done.55 = bf16[512,1024]{1,0:T(8,128)(2,1)} collective-permute-done((bf16[512,1024]{1,0:T(8,128)(2,1)}, bf16[512,1024]{1,0:T(8,128)(2,1)}, u32[]{:S(2)}, u32[]{:S(2)}) %collective-permute-start.55) | collective-permute-done | bytes 1048608 | tf_op jit(solution)/shard_map/ppermute | solution.py:649
  478.1 5.8 %add_convert_fusion.2.refs_1_ = bf16[512,1024]{1,0:T(8,128)(2,1)S(1)} fusion(bf16[512,1024]{1,0:T(8,128)(2,1)} %collective-permute-done.55, bf16[2048,1024]{1,0:T(8,128)(2,1)} %bitcast.71, bf16[2048,2048]{1,0:T(8,128)(2,1)} %get-tuple-element.604, bf16[1024,1024]{1,0:T(8,128)(2,1)} %copy-done.50), kind=kOutput, calls=%fused_computation.34 | convolution fusion | flops 2150105088 | bytes 9437184 | tf_op jit(solution)/shard_map/dot_general | solution.py:31
  502.7 5.9 %collective-permute-done.57 = f32[4,2,1,1,128]{4,3,2,1,0:T(1,128)S(1)} collective-permute-done((f32[4,2,1,1,128]{4,3,2,1,0:T(1,128)S(1)}, f32[4,2,1,1,128]{4,3,2,1,0:T(1,128)S(1)}, u32[]{:S(2)}, u32[]{:S(2)}) %collective-permute-start.57) | collective-permute-done | bytes 4128 | tf_op jit(solution)/shard_map/ppermute | solution.py:849
  531.9 28.7 %all-to-all-done.2.held = bf16[8,64,1792]{2,1,0:T(8,128)(2,1)S(1)} async-done(((bf16[8,64,1792]{2,1,0:T(8,128)(2,1)}), bf16[8,64,1792]{2,1,0:T(8,128)(2,1)S(1)}, u32[]{:S(2)}, u32[]{:S(2)}) %all-to-all-start.2) | async-done | bytes 1835040 | tf_op jit(solution)/shard_map/all_to_all | solution.py:856
  (320 shorter events, 182.6 us)
Async XLA Ops:
  15.3 58.0 %all-to-all-start = ((bf16[8,64,2176]{2,1,0:T(8,128)(2,1)}), bf16[8,64,2176]{2,1,0:T(8,128)(2,1)}, u32[]{:S(2)}, u32[]{:S(2)}) async-start(bf16[8,64,2176]{2,1,0:T(8,128)(2,1)} %pack_columns.2), calls=%async_computation | async-start | bytes 4456448 | tf_op jit(solution)/shard_map/all_to_all | solution.py:696
  24.4 52.2 %collective-permute-start.3 = (bf16[256,2048]{1,0:T(8,128)(2,1)}, bf16[256,2048]{1,0:T(8,128)(2,1)}, u32[]{:S(2)}, u32[]{:S(2)}) collective-permute-start(bf16[256,2048]{1,0:T(8,128)(2,1)} %pad_maximum_fusion.refs_0_), channel_id=1, source_target_pairs={{0,1},{1,0},{2,3},{3,2},{4,5},{5,4},{6,7},{7,6},{8,9},{9,8},{10,11... | collective-permute-start | bytes 3145736 | tf_op jit(solution)/shard_map/ppermute | solution.py:697
  26.4 56.5 %collective-permute-start.4 = (bf16[256,2048]{1,0:T(8,128)(2,1)}, bf16[256,2048]{1,0:T(8,128)(2,1)}, u32[]{:S(2)}, u32[]{:S(2)}) collective-permute-start(bf16[256,2048]{1,0:T(8,128)(2,1)} %pad_maximum_fusion.refs_0_), channel_id=1, source_target_pairs={{0,2},{1,3},{2,0},{3,1},{4,6},{5,7},{6,4},{7,5},{8,10},{9,11},{10,... | collective-permute-start | bytes 3145736 | tf_op jit(solution)/shard_map/ppermute | solution.py:697
  30.1 59.4 %collective-permute-start.7 = (bf16[256,2048]{1,0:T(8,128)(2,1)S(1)}, bf16[256,2048]{1,0:T(8,128)(2,1)}, u32[]{:S(2)}, u32[]{:S(2)}) collective-permute-start(bf16[256,2048]{1,0:T(8,128)(2,1)S(1)} %pad_maximum_fusion.1.refs_0_), channel_id=1, source_target_pairs={{0,1},{1,0},{2,3},{3,2},{4,5},{5,4},{6,7},{7,6},{8,9},{9,8},{10,11... | collective-permute-start | bytes 3145736 | tf_op jit(solution)/shard_map/ppermute | solution.py:702
  30.7 70.8 %collective-permute-start.8 = (bf16[256,2048]{1,0:T(8,128)(2,1)S(1)}, bf16[256,2048]{1,0:T(8,128)(2,1)}, u32[]{:S(2)}, u32[]{:S(2)}) collective-permute-start(bf16[256,2048]{1,0:T(8,128)(2,1)S(1)} %pad_maximum_fusion.1.refs_0_), channel_id=1, source_target_pairs={{0,2},{1,3},{2,0},{3,1},{4,6},{5,7},{6,4},{7,5},{8,10},{9,11},{10,... | collective-permute-start | bytes 3145736 | tf_op jit(solution)/shard_map/ppermute | solution.py:703
  31.7 69.8 %collective-permute-start.9 = (bf16[256,2048]{1,0:T(8,128)(2,1)S(1)}, bf16[256,2048]{1,0:T(8,128)(2,1)}, u32[]{:S(2)}, u32[]{:S(2)}) collective-permute-start(bf16[256,2048]{1,0:T(8,128)(2,1)S(1)} %pad_maximum_fusion.1.refs_0_), channel_id=1, source_target_pairs={{2,4},{3,5},{4,2},{5,3},{10,12},{11,13},{12,10},{13,11},{18,20},{1... | collective-permute-start | bytes 3145736 | tf_op jit(solution)/shard_map/ppermute | solution.py:703
  101.5 39.2 %collective-permute-start.14 = (bf16[512,2176]{1,0:T(8,128)(2,1)}, bf16[512,2176]{1,0:T(8,128)(2,1)}, u32[]{:S(2)}, u32[]{:S(2)}) collective-permute-start(bf16[512,2176]{1,0:T(8,128)(2,1)} %get-tuple-element.338), channel_id=1, source_target_pairs={{0,8},{8,0},{16,24},{24,16},{1,9},{9,1},{17,25},{25,17},{2,10},{10... | collective-permute-start | bytes 6684680 | tf_op jit(solution)/shard_map/ppermute | solution.py:649
  101.5 39.2 %collective-permute-start.13 = (bf16[256,2176]{1,0:T(8,128)(2,1)S(1)}, bf16[256,2176]{1,0:T(8,128)(2,1)}, u32[]{:S(2)}, u32[]{:S(2)}) collective-permute-start(bf16[256,2176]{1,0:T(8,128)(2,1)S(1)} %get-tuple-element.538.refs_6_.refs_2_.refs_4_), channel_id=1, source_target_pairs={{0,16},{8,24},{16,0},{24,8},{1,17},{9,25},{17,1},{25,9},{2,18},{10... | collective-permute-start | bytes 3342344 | tf_op jit(solution)/shard_map/ppermute | solution.py:649
  103.0 28.1 %collective-permute-start.10 = (bf16[256,2048]{1,0:T(8,128)(2,1)}, bf16[256,2048]{1,0:T(8,128)(2,1)}, u32[]{:S(2)}, u32[]{:S(2)}) collective-permute-start(bf16[256,2048]{1,0:T(8,128)(2,1)} %collective-permute-done.8.refs_2_), channel_id=1, source_target_pairs={{0,1},{1,0},{2,3},{3,2},{4,5},{5,4},{6,7},{7,6},{8,9},{9,8},{10,11... | collective-permute-start | bytes 3145736 | tf_op jit(solution)/shard_map/ppermute | solution.py:649
  106.1 34.6 %collective-permute-start.12 = (bf16[256,2048]{1,0:T(8,128)(2,1)}, bf16[256,2048]{1,0:T(8,128)(2,1)}, u32[]{:S(2)}, u32[]{:S(2)}) collective-permute-start(bf16[256,2048]{1,0:T(8,128)(2,1)} %collective-permute-done.9), channel_id=1, source_target_pairs={{2,0},{3,1},{4,6},{5,7},{10,8},{11,9},{12,14},{13,15},{18,16},{19,... | collective-permute-start | bytes 3145736 | tf_op jit(solution)/shard_map/ppermute | solution.py:649
  113.1 66.6 %all-to-all-start.1 = ((bf16[8,64,1024]{2,1,0:T(8,128)(2,1)}), bf16[8,64,1024]{2,1,0:T(8,128)(2,1)S(1)}, u32[]{:S(2)}, u32[]{:S(2)}) async-start(bf16[8,64,1024]{2,1,0:T(8,128)(2,1)} %pack_columns.3), calls=%async_computation.1 | async-start | bytes 2097152 | tf_op jit(solution)/shard_map/all_to_all | solution.py:708
  140.7 36.6 %collective-permute-start.18 = (bf16[256,2176]{1,0:T(8,128)(2,1)S(1)}, bf16[256,2176]{1,0:T(8,128)(2,1)}, u32[]{:S(2)}, u32[]{:S(2)}) collective-permute-start(bf16[256,2176]{1,0:T(8,128)(2,1)S(1)} %get-tuple-element.539.refs_7_.refs_3_.refs_5_), channel_id=1, source_target_pairs={{0,16},{8,24},{16,0},{24,8},{1,17},{9,25},{17,1},{25,9},{2,18},{10... | collective-permute-start | bytes 3342344 | tf_op jit(solution)/shard_map/ppermute | solution.py:649
  141.3 36.1 %collective-permute-start.19 = (bf16[256,2176]{1,0:T(8,128)(2,1)}, bf16[256,2176]{1,0:T(8,128)(2,1)S(1)}, u32[]{:S(2)}, u32[]{:S(2)}) collective-permute-start(bf16[256,2176]{1,0:T(8,128)(2,1)} %collective-permute-done.13.refs_8_.refs_4_.refs_6_), channel_id=1, source_target_pairs={{0,8},{8,0},{16,24},{24,16},{1,9},{9,1},{17,25},{25,17},{2,10},{10... | collective-permute-start | bytes 3342344 | tf_op jit(solution)/shard_map/ppermute | solution.py:649
  142.6 28.0 %collective-permute-start.15 = (bf16[256,2048]{1,0:T(8,128)(2,1)S(1)}, bf16[256,2048]{1,0:T(8,128)(2,1)S(1)}, u32[]{:S(2)}, u32[]{:S(2)}) collective-permute-start(bf16[256,2048]{1,0:T(8,128)(2,1)S(1)} %broadcast_select_fusion.3.refs_4_), channel_id=1, source_target_pairs={{0,1},{1,0},{2,3},{3,2},{4,5},{5,4},{6,7},{7,6},{8,9},{9,8},{10,11... | collective-permute-start | bytes 3145736 | tf_op jit(solution)/shard_map/ppermute | solution.py:649
  143.4 33.9 %collective-permute-start.16 = (bf16[256,2048]{1,0:T(8,128)(2,1)}, bf16[256,2048]{1,0:T(8,128)(2,1)S(1)}, u32[]{:S(2)}, u32[]{:S(2)}) collective-permute-start(bf16[256,2048]{1,0:T(8,128)(2,1)} %collective-permute-done.11), channel_id=1, source_target_pairs={{2,0},{3,1},{4,6},{5,7},{10,8},{11,9},{12,14},{13,15},{18,16},{19,... | collective-permute-start | bytes 3145736 | tf_op jit(solution)/shard_map/ppermute | solution.py:649
  144.6 32.7 %collective-permute-start.17 = (bf16[256,2048]{1,0:T(8,128)(2,1)}, bf16[256,2048]{1,0:T(8,128)(2,1)S(1)}, u32[]{:S(2)}, u32[]{:S(2)}) collective-permute-start(bf16[256,2048]{1,0:T(8,128)(2,1)} %pad_maximum_fusion.refs_0_), channel_id=1, source_target_pairs={{2,4},{3,5},{4,2},{5,3},{10,12},{11,13},{12,10},{13,11},{18,20},{1... | collective-permute-start | bytes 3145736 | tf_op jit(solution)/shard_map/ppermute | solution.py:649
  179.8 58.7 %collective-permute-start.26 = (bf16[512,1024]{1,0:T(8,128)(2,1)S(1)}, bf16[512,1024]{1,0:T(8,128)(2,1)}, u32[]{:S(2)}, u32[]{:S(2)}) collective-permute-start(bf16[512,1024]{1,0:T(8,128)(2,1)S(1)} %unpack_columns.3.refs_4_), channel_id=1, source_target_pairs={{0,16},{8,24},{16,0},{24,8},{1,17},{9,25},{17,1},{25,9},{2,18},{10... | collective-permute-start | bytes 3145736 | tf_op jit(solution)/shard_map/ppermute | solution.py:649
  180.4 58.1 %collective-permute-start.27 = (bf16[512,1024]{1,0:T(8,128)(2,1)S(1)}, bf16[512,1024]{1,0:T(8,128)(2,1)}, u32[]{:S(2)}, u32[]{:S(2)}) collective-permute-start(bf16[512,1024]{1,0:T(8,128)(2,1)S(1)} %unpack_columns.3.refs_4_), channel_id=1, source_target_pairs={{0,8},{8,0},{16,24},{24,16},{1,9},{9,1},{17,25},{25,17},{2,10},{10... | collective-permute-start | bytes 3145736 | tf_op jit(solution)/shard_map/ppermute | solution.py:649
  209.1 29.4 %collective-permute-start.24 = (bf16[256,2048]{1,0:T(8,128)(2,1)S(1)}, bf16[256,2048]{1,0:T(8,128)(2,1)}, u32[]{:S(2)}, u32[]{:S(2)}) collective-permute-start(bf16[256,2048]{1,0:T(8,128)(2,1)S(1)} %broadcast_select_fusion.1.refs_2_), channel_id=1, source_target_pairs={{0,1},{1,0},{2,3},{3,2},{4,5},{5,4},{6,7},{7,6},{8,9},{9,8},{10,11... | collective-permute-start | bytes 3145736 | tf_op jit(solution)/shard_map/ppermute | solution.py:649
  210.8 27.9 %collective-permute-start.25 = (bf16[256,2048]{1,0:T(8,128)(2,1)}, bf16[256,2048]{1,0:T(8,128)(2,1)}, u32[]{:S(2)}, u32[]{:S(2)}) collective-permute-start(bf16[256,2048]{1,0:T(8,128)(2,1)} %collective-permute-done.22), channel_id=1, source_target_pairs={{2,0},{3,1},{4,6},{5,7},{10,8},{11,9},{12,14},{13,15},{18,16},{19,... | collective-permute-start | bytes 3145736 | tf_op jit(solution)/shard_map/ppermute | solution.py:649
  240.1 32.3 %collective-permute-start.28 = (bf16[256,2048]{1,0:T(8,128)(2,1)S(1)}, bf16[256,2048]{1,0:T(8,128)(2,1)S(1)}, u32[]{:S(2)}, u32[]{:S(2)}) collective-permute-start(bf16[256,2048]{1,0:T(8,128)(2,1)S(1)} %broadcast_select_fusion.refs_2_), channel_id=1, source_target_pairs={{0,1},{1,0},{2,3},{3,2},{4,5},{5,4},{6,7},{7,6},{8,9},{9,8},{10,11... | collective-permute-start | bytes 3145736 | tf_op jit(solution)/shard_map/ppermute | solution.py:649
  240.7 31.8 %collective-permute-start.29 = (bf16[256,2048]{1,0:T(8,128)(2,1)}, bf16[256,2048]{1,0:T(8,128)(2,1)S(1)}, u32[]{:S(2)}, u32[]{:S(2)}) collective-permute-start(bf16[256,2048]{1,0:T(8,128)(2,1)} %collective-permute-done.3.refs_1_), channel_id=1, source_target_pairs={{0,2},{1,3},{2,0},{3,1},{4,6},{5,7},{6,4},{7,5},{8,10},{9,11},{10,... | collective-permute-start | bytes 3145736 | tf_op jit(solution)/shard_map/ppermute | solution.py:649
  300.0 35.5 %collective-permute-start.33 = (bf16[256,2048]{1,0:T(8,128)(2,1)}, bf16[256,2048]{1,0:T(8,128)(2,1)}, u32[]{:S(2)}, u32[]{:S(2)}) collective-permute-start(bf16[256,2048]{1,0:T(8,128)(2,1)} %get-tuple-element.501), channel_id=1, source_target_pairs={{0,1},{1,0},{2,3},{3,2},{4,5},{5,4},{6,7},{7,6},{8,9},{9,8},{10,11... | collective-permute-start | bytes 3145736 | tf_op jit(solution)/shard_map/ppermute | solution.py:649
  300.8 34.7 %collective-permute-start.34 = (bf16[256,2048]{1,0:T(8,128)(2,1)S(1)}, bf16[256,2048]{1,0:T(8,128)(2,1)}, u32[]{:S(2)}, u32[]{:S(2)}) collective-permute-start(bf16[256,2048]{1,0:T(8,128)(2,1)S(1)} %add_convert_fusion.15), channel_id=1, source_target_pairs={{0,2},{1,3},{6,4},{7,5},{8,10},{9,11},{14,12},{15,13},{16,18},{17,... | collective-permute-start | bytes 3145736 | tf_op jit(solution)/shard_map/ppermute | solution.py:649
  361.5 36.7 %collective-permute-start.40 = (bf16[256,2048]{1,0:T(8,128)(2,1)}, bf16[256,2048]{1,0:T(8,128)(2,1)}, u32[]{:S(2)}, u32[]{:S(2)}) collective-permute-start(bf16[256,2048]{1,0:T(8,128)(2,1)} %get-tuple-element.562), channel_id=1, source_target_pairs={{0,1},{1,0},{2,3},{3,2},{4,5},{5,4},{6,7},{7,6},{8,9},{9,8},{10,11... | collective-permute-start | bytes 3145736 | tf_op jit(solution)/shard_map/ppermute | solution.py:649
  363.9 34.4 %collective-permute-start.41 = (bf16[256,2048]{1,0:T(8,128)(2,1)}, bf16[256,2048]{1,0:T(8,128)(2,1)S(1)}, u32[]{:S(2)}, u32[]{:S(2)}) collective-permute-start(bf16[256,2048]{1,0:T(8,128)(2,1)} %add_convert_fusion.11), channel_id=1, source_target_pairs={{2,4},{3,5},{4,2},{5,3},{10,12},{11,13},{12,10},{13,11},{18,20},{1... | collective-permute-start | bytes 3145736 | tf_op jit(solution)/shard_map/ppermute | solution.py:649
  366.1 32.1 %collective-permute-start.42 = (bf16[256,2048]{1,0:T(8,128)(2,1)}, bf16[256,2048]{1,0:T(8,128)(2,1)S(1)}, u32[]{:S(2)}, u32[]{:S(2)}) collective-permute-start(bf16[256,2048]{1,0:T(8,128)(2,1)} %add_convert_fusion.10), channel_id=1, source_target_pairs={{0,2},{1,3},{2,0},{3,1},{4,6},{5,7},{6,4},{7,5},{8,10},{9,11},{10,... | collective-permute-start | bytes 3145736 | tf_op jit(solution)/shard_map/ppermute | solution.py:649
  452.7 32.6 %collective-permute-start.52 = (bf16[256,2048]{1,0:T(8,128)(2,1)}, bf16[256,2048]{1,0:T(8,128)(2,1)}, u32[]{:S(2)}, u32[]{:S(2)}) collective-permute-start(bf16[256,2048]{1,0:T(8,128)(2,1)} %get-tuple-element.607), channel_id=1, source_target_pairs={{0,1},{1,0},{2,3},{3,2},{4,5},{5,4},{6,7},{7,6},{8,9},{9,8},{10,11... | collective-permute-start | bytes 3145736 | tf_op jit(solution)/shard_map/ppermute | solution.py:649
  456.2 29.0 %collective-permute-start.53 = (bf16[256,2048]{1,0:T(8,128)(2,1)}, bf16[256,2048]{1,0:T(8,128)(2,1)}, u32[]{:S(2)}, u32[]{:S(2)}) collective-permute-start(bf16[256,2048]{1,0:T(8,128)(2,1)} %add_convert_fusion.4), channel_id=1, source_target_pairs={{2,4},{3,5},{4,2},{5,3},{10,12},{11,13},{12,10},{13,11},{18,20},{1... | collective-permute-start | bytes 3145736 | tf_op jit(solution)/shard_map/ppermute | solution.py:649
  459.4 29.1 %collective-permute-start.54 = (bf16[256,2048]{1,0:T(8,128)(2,1)}, bf16[256,2048]{1,0:T(8,128)(2,1)}, u32[]{:S(2)}, u32[]{:S(2)}) collective-permute-start(bf16[256,2048]{1,0:T(8,128)(2,1)} %add_convert_fusion.3), channel_id=1, source_target_pairs={{0,2},{1,3},{2,0},{3,1},{4,6},{5,7},{6,4},{7,5},{8,10},{9,11},{10,... | collective-permute-start | bytes 3145736 | tf_op jit(solution)/shard_map/ppermute | solution.py:649
  464.2 52.4 %all-to-all-start.3 = ((bf16[8,64,1408]{2,1,0:T(8,128)(2,1)}), bf16[8,64,1408]{2,1,0:T(8,128)(2,1)S(1)}, u32[]{:S(2)}, u32[]{:S(2)}) async-start(bf16[8,64,1408]{2,1,0:T(8,128)(2,1)} %pack_rows.2), calls=%async_computation.3 | async-start | bytes 2883584 | tf_op jit(solution)/shard_map/all_to_all | solution.py:835
  516.6 44.1 %all-to-all-start.2 = ((bf16[8,64,1792]{2,1,0:T(8,128)(2,1)}), bf16[8,64,1792]{2,1,0:T(8,128)(2,1)S(1)}, u32[]{:S(2)}, u32[]{:S(2)}) async-start(bf16[8,64,1792]{2,1,0:T(8,128)(2,1)} %pack_rows.3), calls=%async_computation.2 | async-start | bytes 3670016 | tf_op jit(solution)/shard_map/all_to_all | solution.py:856
  (93 other events, 1195.7 us)

commit v10 on v9

--- a/solution.py
+++ b/solution.py
@@ -921,12 +921,12 @@
     tick(
         [plus("o3", "o3k", "o3x")],
         [to("o2x", "o2a", side), to("o3i", "o3", inward), send_a("G")],
-        [attend_back, half_b(0), half_b(1)],
+        [attend_back, half_b(0)],
     )
     tick(
         [plus("o2", "o2k", "o2x"), plus("o3", "o3", "o3i"), plus("o0a", "o0a", "o1p")],
         [to("o0x", "o0a", side), to("o2i", "o2", inward), to("o3m", "o3", middle), to("GB1r", "GB1", across)],
-        [normed_part(1, 3)],
+        [normed_part(1, 3), half_b(1)],
     )
     tick(
         [plus("o2", "o2", "o2i"), plus("o1", "o1k", "o3m")],

time: 572 us -> 571 us (level)
  transfers between devices with their start and end apart: 65 -> 65, of which waited for: 29 -> 26; matrix products, arithmetic and copies ran while one was open for 17% -> 18% of each run, Pallas kernels for 26% -> 26%
where the time goes in v10:
time: 571 us; the launch traced here: 562 us
  waiting for transfers between devices  195 us (34%)
  Pallas kernels  151 us (26%)
  starting transfers between devices  104 us (18%)
  matrix products  54.3 us (10%)
  other arithmetic  42.3 us (7%)
  local copies, waits for them, and re-layouts  12.2 us (2%)
    ppermute x45, waiting for transfers between devices, tick(): view[name] = lax.ppermute(self.held[source], axis, pairs)  87.2 us
    ppermute x45, starting transfers between devices, tick(): view[name] = lax.ppermute(self.held[source], axis, pairs)  60.2 us
    pallas_call x4, Pallas kernels, stream(): pl.pallas_call(functools.partial(stream_kernel, n, len(pieces), len(extra...  56 us
    dot_general x11, matrix products, dot_first(): return lax.dot_general(left, right, FIRST, preferred_element_type=F32)  54.3 us
    pallas_call x3, Pallas kernels, spread(): pl.pallas_call(functools.partial(spread_kernel, len(lefts), len(pieces),...  45.8 us
    all_to_all x1, waiting for transfers between devices, begin(): lax.all_to_all(packed, 'ctx', split_axis=0, concat_axis=0, tiled=True)  38.1 us
    all_to_all x1, waiting for transfers between devices, norm_back(): lax.all_to_all(packed, 'ctx', split_axis=0, concat_axis=0, tiled=True)  28.8 us
    pallas_call x1, Pallas kernels, attend_back(): self.calls(lanes)[1]  21.4 us
  transfers between devices with their start and end apart: 65, of which 26 were waited for; matrix products, arithmetic and copies ran while one was open for 18% of the time, Pallas kernels for 26%

profile of v10, /device:TPU:0, one launch (start us, length us, event | category | flops | bytes accessed | tf_op | source)
XLA Modules:
  0.0 561.6 jit_solution(10939039215738800428)
XLA Ops:
  15.3 5.4 all-to-all-start
  35.2 38.1 %all-to-all-done.in_ref = bf16[8,64,2176]{2,1,0:T(8,128)(2,1)} async-done(((bf16[8,64,2176]{2,1,0:T(8,128)(2,1)}), bf16[8,64,2176]{2,1,0:T(8,128)(2,1)}, u32[]{:S(2)}, u32[]{:S(2)}) %all-to-all-start) | async-done | bytes 2228256 | tf_op jit(solution)/shard_map/all_to_all | solution.py:696
  76.6 6.3 %collective-permute-done.4.refs_0_ = bf16[256,2048]{1,0:T(8,128)(2,1)} collective-permute-done((bf16[256,2048]{1,0:T(8,128)(2,1)}, bf16[256,2048]{1,0:T(8,128)(2,1)}, u32[]{:S(2)}, u32[]{:S(2)}) %collective-permute-start.4) | collective-permute-done | bytes 1048608 | tf_op jit(solution)/shard_map/ppermute | solution.py:697
  82.9 6.6 %collective-permute-done.7.refs_1_ = bf16[256,2048]{1,0:T(8,128)(2,1)} collective-permute-done((bf16[256,2048]{1,0:T(8,128)(2,1)S(1)}, bf16[256,2048]{1,0:T(8,128)(2,1)}, u32[]{:S(2)}, u32[]{:S(2)}) %collective-permute-start.7) | collective-permute-done | bytes 1048608 | tf_op jit(solution)/shard_map/ppermute | solution.py:702
  89.5 12.0 %collective-permute-done.8.refs_2_ = bf16[256,2048]{1,0:T(8,128)(2,1)} collective-permute-done((bf16[256,2048]{1,0:T(8,128)(2,1)S(1)}, bf16[256,2048]{1,0:T(8,128)(2,1)}, u32[]{:S(2)}, u32[]{:S(2)}) %collective-permute-start.8) | collective-permute-done | bytes 1048608 | tf_op jit(solution)/shard_map/ppermute | solution.py:703
  107.4 5.7 %fusion.49 = (f32[1024,256]{1,0:T(8,128)}, f32[1024,256]{1,0:T(8,128)}) fusion(f32[256]{0:T(256)S(1)} %fusion.65, f32[1024]{0:T(1024)S(1)} %iota_convert_fusion, pred[256]{0:T(512)(128)(4,1)S(1)} %get-tuple-element.676, pred[256]{0:T(512)(128)(4,1)S(1)} %get-tuple-element.677), kind=kLoop, calls=%fused_computation.68 | loop fusion | flops 1310720 | bytes 2102784 | tf_op jit(solution)/shard_map/jit(_where)/select_n | solution.py:41
  113.1 5.8 %all-to-all-start.1 = ((bf16[8,64,1024]{2,1,0:T(8,128)(2,1)}), bf16[8,64,1024]{2,1,0:T(8,128)(2,1)S(1)}, u32[]{:S(2)}, u32[]{:S(2)}) async-start(bf16[8,64,1024]{2,1,0:T(8,128)(2,1)} %pack_columns.3), calls=%async_computation.1 | async-start | bytes 2097152 | tf_op jit(solution)/shard_map/all_to_all | solution.py:708
  118.9 12.2 %collective-permute-done.10.refs_3_ = bf16[256,2048]{1,0:T(8,128)(2,1)} collective-permute-done((bf16[256,2048]{1,0:T(8,128)(2,1)}, bf16[256,2048]{1,0:T(8,128)(2,1)}, u32[]{:S(2)}, u32[]{:S(2)}) %collective-permute-start.10) | collective-permute-done | bytes 1048608 | tf_op jit(solution)/shard_map/ppermute | solution.py:649
  131.1 9.6 %collective-permute-done.12 = bf16[256,2048]{1,0:T(8,128)(2,1)} collective-permute-done((bf16[256,2048]{1,0:T(8,128)(2,1)}, bf16[256,2048]{1,0:T(8,128)(2,1)}, u32[]{:S(2)}, u32[]{:S(2)}) %collective-permute-start.12) | collective-permute-done | bytes 1048608 | tf_op jit(solution)/shard_map/ppermute | solution.py:649
  145.4 25.2 %collective-permute-done.15.refs_5_ = bf16[256,2048]{1,0:T(8,128)(2,1)S(1)} collective-permute-done((bf16[256,2048]{1,0:T(8,128)(2,1)S(1)}, bf16[256,2048]{1,0:T(8,128)(2,1)S(1)}, u32[]{:S(2)}, u32[]{:S(2)}) %collective-permute-start.15) | collective-permute-done | bytes 1048608 | tf_op jit(solution)/shard_map/ppermute | solution.py:649
  170.6 6.7 %collective-permute-done.16 = bf16[256,2048]{1,0:T(8,128)(2,1)S(1)} collective-permute-done((bf16[256,2048]{1,0:T(8,128)(2,1)}, bf16[256,2048]{1,0:T(8,128)(2,1)S(1)}, u32[]{:S(2)}, u32[]{:S(2)}) %collective-permute-start.16) | collective-permute-done | bytes 1048608 | tf_op jit(solution)/shard_map/ppermute | solution.py:649
  184.6 22.1 %project.2 = (bf16[2048,2048]{1,0:T(8,128)(2,1)}, f32[2048,768]{1,0:T(8,128)}, bf16[2048,1408]{1,0:T(8,128)(2,1)}, bf16[2048,1024]{1,0:T(8,128)(2,1)}) custom-call(bf16[256,2048]{1,0:T(8,128)(2,1)S(1)} %copy-done.6, bf16[256,2048]{1,0:T(8,128)(2,1)} %collective-permute-done.7.refs_1_, bf16[256,2048]{1,0:T(8,128)(2,1)} %collective-permute-done.8.refs_2_, ...), custom_call_target="tpu_custom_call" | custom-call | flops 13690208256 | bytes 30408704 | tf_op jit(solution)/shard_map/project/pallas_call | solution.py:400
  212.7 11.1 %project.3 = (bf16[2048,2048]{1,0:T(8,128)(2,1)}, f32[2048,768]{1,0:T(8,128)}, bf16[2048,1408]{1,0:T(8,128)(2,1)}, bf16[2048,1024]{1,0:T(8,128)(2,1)}) custom-call(bf16[256,2048]{1,0:T(8,128)(2,1)S(1)} %broadcast_select_fusion.2.refs_0_, bf16[256,2048]{1,0:T(8,128)(2,1)} %copy-done.29, ...), custom_call_target="tpu_custom_call", output_to_operand_aliasing={{0}: (9, {}), {1}: (10, {}), {2}: (11, {}), {3}: (12, {})} | custom-call | flops 4563402752 | bytes 22020096 | tf_op jit(solution)/shard_map/project/pallas_call | solution.py:400
  223.8 14.8 %attend_forward.1 = (bf16[8,2,128,768]{3,2,1,0:T(8,128)(2,1)}, bf16[8,2,128,1024]{3,2,1,0:T(8,128)(2,1)}, f32[8,2,128,4]{3,2,1,0:T(8,128)S(1)}) custom-call(s32[2]{0:T(128)S(1)} %copy-done.12, s32[8]{0:T(128)S(1)} %compare_select_fusion.8.slot_ref, f32[8,2,128,768]{3,2,1,0:T(8,128)} %bitcast.65, ...), custom_call_target="tpu_custom_call", output_to_operand_aliasing={{1}: (5, {})} | custom-call | flops 4294967296 | bytes 4194304 | tf_op jit(solution)/shard_map/attend_forward/pallas_call | solution.py:555
  240.7 4.8 collective-permute-start.29
  246.5 11.5 %bring_back.2 = (bf16[2048,2048]{1,0:T(8,128)(2,1)}, bf16[2048,256]{1,0:T(8,128)(2,1)S(1)}, bf16[2048,1408]{1,0:T(8,128)(2,1)}) custom-call(bf16[256,2048]{1,0:T(8,128)(2,1)} %pad_maximum_fusion.refs_0_, bf16[256,2048]{1,0:T(8,128)(2,1)} %collective-permute-done.3.refs_1_, bf16[256,2048]{1,0:T(8,128)(2,1)} %copy-done.40, ...), custom_call_target="tpu_custom_call" | custom-call | flops 4294967296 | bytes 16777216 | tf_op jit(solution)/shard_map/bring_back/pallas_call | solution.py:400
  258.0 14.4 %output_part.1 = (bf16[256,2048]{1,0:T(8,128)(2,1)S(1)}, bf16[256,2048]{1,0:T(8,128)(2,1)}, bf16[256,2048]{1,0:T(8,128)(2,1)}, bf16[256,2048]{1,0:T(8,128)(2,1)}...) custom-call(bf16[2048,1024]{1,0:T(8,128)(2,1)} %bitcast.67, ...), custom_call_target="tpu_custom_call" | custom-call | flops 8589934592 | bytes 16777216 | tf_op jit(solution)/shard_map/output_part/pallas_call | solution.py:500
  274.1 11.3 %bring_back.3 = (bf16[2048,2048]{1,0:T(8,128)(2,1)}, bf16[2048,256]{1,0:T(8,128)(2,1)S(1)}, bf16[2048,1408]{1,0:T(8,128)(2,1)}) custom-call(bf16[256,2048]{1,0:T(8,128)(2,1)} %collective-permute-done.4.refs_0_, bf16[256,2048]{1,0:T(8,128)(2,1)} %copy-done.38, ...), custom_call_target="tpu_custom_call", output_to_operand_aliasing={{0}: (8, {}), {1}: (9, {}), {2}: (10, {})} | custom-call | flops 4294967296 | bytes 16777216 | tf_op jit(solution)/shard_map/bring_back/pallas_call | solution.py:400
  285.5 11.7 %fusion.6 = bf16[1024,1408]{1,0:T(8,128)(2,1)} fusion(bf16[2048,1408]{1,0:T(8,128)(2,1)} %get-tuple-element.548.refs_1_.refs_3_, bf16[2048,2048]{1,0:T(8,128)(2,1)} %get-tuple-element.584), kind=kOutput, calls=%fused_computation.6 | convolution fusion | flops 5907021824 | bytes 12845056 | tf_op jit(solution)/shard_map/dot_general | solution.py:31
  305.2 21.4 %attend_backward.1 = bf16[8,2,128,768]{3,2,1,0:T(8,128)(2,1)} custom-call(s32[2]{0:T(128)S(1)} %copy-done.12, s32[8]{0:T(128)S(1)} %compare_select_fusion.8.slot_ref, bf16[8,2,128,768]{3,2,1,0:T(8,128)(2,1)} %get-tuple-element.494.rot_ref, bf16[8,2,128,1024]{3,2,1,0:T(8,128)(2,1)} %get-tuple-element.406, bf16[8,2,128,256]{3,2,1,0:T(8,128)(2,1)S(1)} %bitcast.58, ...), custom_call_target="tpu_custom_call" | custom-call | flops 10737418240 | bytes 4194304 | tf_op jit(solution)/shard_map/attend_backward/pallas_call | solution.py:562
  326.7 4.9 fusion.11
  345.1 15.7 %normed_part.2 = (bf16[256,2048]{1,0:T(8,128)(2,1)S(1)}, bf16[256,2048]{1,0:T(8,128)(2,1)}, bf16[256,2048]{1,0:T(8,128)(2,1)}, bf16[256,2048]{1,0:T(8,128)(2,1)}) custom-call(bf16[2048,768]{1,0:T(8,128)(2,1)} %bitcast.99, bf16[2048,1408]{1,0:T(8,128)(2,1)} %get-tuple-element.548.refs_1_.refs_3_, bf16[2048,768]{1,0:T(8,128)(2,1)} %bitcast.100, ...), custom_call_target="tpu_custom_call" | custom-call | flops 9126805504 | bytes 17563648 | tf_op jit(solution)/shard_map/normed_part/pallas_call | solution.py:500
  367.3 5.8 %collective-permute-start.42 = (bf16[256,2048]{1,0:T(8,128)(2,1)}, bf16[256,2048]{1,0:T(8,128)(2,1)S(1)}, u32[]{:S(2)}, u32[]{:S(2)}) collective-permute-start(bf16[256,2048]{1,0:T(8,128)(2,1)} %add_convert_fusion.10), channel_id=1, source_target_pairs={{0,2},{1,3},{2,0},{3,1},{4,6},{5,7},{6,4},{7,5},{8,10},{9,11},{10,... | collective-permute-start | bytes 3145736 | tf_op jit(solution)/shard_map/ppermute | solution.py:649
  373.7 15.7 %normed_part.3 = (bf16[256,2048]{1,0:T(8,128)(2,1)S(1)}, bf16[256,2048]{1,0:T(8,128)(2,1)}, bf16[256,2048]{1,0:T(8,128)(2,1)}, bf16[256,2048]{1,0:T(8,128)(2,1)}) custom-call(bf16[2048,768]{1,0:T(8,128)(2,1)} %bitcast.101, bf16[2048,1408]{1,0:T(8,128)(2,1)} %get-tuple-element.548.refs_1_.refs_3_, bf16[2048,768]{1,0:T(8,128)(2,1)} %bitcast.102, ...), custom_call_target="tpu_custom_call" | custom-call | flops 9126805504 | bytes 17563648 | tf_op jit(solution)/shard_map/normed_part/pallas_call | solution.py:500
  402.7 5.7 %fusion.36 = bf16[1024,768]{1,0:T(8,128)(2,1)S(1)} fusion(bf16[2048,768]{1,0:T(8,128)(2,1)S(1)} %bitcast.103, bf16[2048,2048]{1,0:T(8,128)(2,1)} %get-tuple-element.584), kind=kOutput, calls=%fused_computation.61 | convolution fusion | flops 3222011904 | bytes 8912896 | tf_op jit(solution)/shard_map/dot_general | solution.py:31
  408.6 4.8 fusion.33
  430.8 12.2 %collective-permute-done.50 = bf16[512,768]{1,0:T(8,128)(2,1)S(1)} collective-permute-done((bf16[512,768]{1,0:T(8,128)(2,1)S(1)}, bf16[512,768]{1,0:T(8,128)(2,1)S(1)}, u32[]{:S(2)}, u32[]{:S(2)}) %collective-permute-start.50) | collective-permute-done | bytes 786464 | tf_op jit(solution)/shard_map/ppermute | solution.py:649
  458.0 4.7 collective-permute-start.54
  467.3 9.6 %collective-permute-done.55 = bf16[512,1024]{1,0:T(8,128)(2,1)} collective-permute-done((bf16[512,1024]{1,0:T(8,128)(2,1)}, bf16[512,1024]{1,0:T(8,128)(2,1)}, u32[]{:S(2)}, u32[]{:S(2)}) %collective-permute-start.55) | collective-permute-done | bytes 1048608 | tf_op jit(solution)/shard_map/ppermute | solution.py:649
  476.8 5.8 %add_convert_fusion.2.refs_1_ = bf16[512,1024]{1,0:T(8,128)(2,1)S(1)} fusion(bf16[512,1024]{1,0:T(8,128)(2,1)} %collective-permute-done.55, bf16[2048,1024]{1,0:T(8,128)(2,1)} %bitcast.71, bf16[2048,2048]{1,0:T(8,128)(2,1)} %get-tuple-element.602, bf16[1024,1024]{1,0:T(8,128)(2,1)} %copy-done.52), kind=kOutput, calls=%fused_computation.34 | convolution fusion | flops 2150105088 | bytes 9437184 | tf_op jit(solution)/shard_map/dot_general | solution.py:31
  501.2 5.9 %collective-permute-done.57 = f32[4,2,1,1,128]{4,3,2,1,0:T(1,128)S(1)} collective-permute-done((f32[4,2,1,1,128]{4,3,2,1,0:T(1,128)S(1)}, f32[4,2,1,1,128]{4,3,2,1,0:T(1,128)S(1)}, u32[]{:S(2)}, u32[]{:S(2)}) %collective-permute-start.57) | collective-permute-done | bytes 4128 | tf_op jit(solution)/shard_map/ppermute | solution.py:849
  530.4 28.8 %all-to-all-done.2.held = bf16[8,64,1792]{2,1,0:T(8,128)(2,1)S(1)} async-done(((bf16[8,64,1792]{2,1,0:T(8,128)(2,1)}), bf16[8,64,1792]{2,1,0:T(8,128)(2,1)S(1)}, u32[]{:S(2)}, u32[]{:S(2)}) %all-to-all-start.2) | async-done | bytes 1835040 | tf_op jit(solution)/shard_map/all_to_all | solution.py:856
  (324 shorter events, 182.9 us)
Async XLA Ops:
  15.3 58.0 %all-to-all-start = ((bf16[8,64,2176]{2,1,0:T(8,128)(2,1)}), bf16[8,64,2176]{2,1,0:T(8,128)(2,1)}, u32[]{:S(2)}, u32[]{:S(2)}) async-start(bf16[8,64,2176]{2,1,0:T(8,128)(2,1)} %pack_columns.2), calls=%async_computation | async-start | bytes 4456448 | tf_op jit(solution)/shard_map/all_to_all | solution.py:696
  24.4 52.2 %collective-permute-start.3 = (bf16[256,2048]{1,0:T(8,128)(2,1)}, bf16[256,2048]{1,0:T(8,128)(2,1)}, u32[]{:S(2)}, u32[]{:S(2)}) collective-permute-start(bf16[256,2048]{1,0:T(8,128)(2,1)} %pad_maximum_fusion.refs_0_), channel_id=1, source_target_pairs={{0,1},{1,0},{2,3},{3,2},{4,5},{5,4},{6,7},{7,6},{8,9},{9,8},{10,11... | collective-permute-start | bytes 3145736 | tf_op jit(solution)/shard_map/ppermute | solution.py:697
  26.4 56.5 %collective-permute-start.4 = (bf16[256,2048]{1,0:T(8,128)(2,1)}, bf16[256,2048]{1,0:T(8,128)(2,1)}, u32[]{:S(2)}, u32[]{:S(2)}) collective-permute-start(bf16[256,2048]{1,0:T(8,128)(2,1)} %pad_maximum_fusion.refs_0_), channel_id=1, source_target_pairs={{0,2},{1,3},{2,0},{3,1},{4,6},{5,7},{6,4},{7,5},{8,10},{9,11},{10,... | collective-permute-start | bytes 3145736 | tf_op jit(solution)/shard_map/ppermute | solution.py:697
  30.1 59.4 %collective-permute-start.7 = (bf16[256,2048]{1,0:T(8,128)(2,1)S(1)}, bf16[256,2048]{1,0:T(8,128)(2,1)}, u32[]{:S(2)}, u32[]{:S(2)}) collective-permute-start(bf16[256,2048]{1,0:T(8,128)(2,1)S(1)} %pad_maximum_fusion.1.refs_0_), channel_id=1, source_target_pairs={{0,1},{1,0},{2,3},{3,2},{4,5},{5,4},{6,7},{7,6},{8,9},{9,8},{10,11... | collective-permute-start | bytes 3145736 | tf_op jit(solution)/shard_map/ppermute | solution.py:702
  30.7 70.8 %collective-permute-start.8 = (bf16[256,2048]{1,0:T(8,128)(2,1)S(1)}, bf16[256,2048]{1,0:T(8,128)(2,1)}, u32[]{:S(2)}, u32[]{:S(2)}) collective-permute-start(bf16[256,2048]{1,0:T(8,128)(2,1)S(1)} %pad_maximum_fusion.1.refs_0_), channel_id=1, source_target_pairs={{0,2},{1,3},{2,0},{3,1},{4,6},{5,7},{6,4},{7,5},{8,10},{9,11},{10,... | collective-permute-start | bytes 3145736 | tf_op jit(solution)/shard_map/ppermute | solution.py:703
  31.7 69.8 %collective-permute-start.9 = (bf16[256,2048]{1,0:T(8,128)(2,1)S(1)}, bf16[256,2048]{1,0:T(8,128)(2,1)}, u32[]{:S(2)}, u32[]{:S(2)}) collective-permute-start(bf16[256,2048]{1,0:T(8,128)(2,1)S(1)} %pad_maximum_fusion.1.refs_0_), channel_id=1, source_target_pairs={{2,4},{3,5},{4,2},{5,3},{10,12},{11,13},{12,10},{13,11},{18,20},{1... | collective-permute-start | bytes 3145736 | tf_op jit(solution)/shard_map/ppermute | solution.py:703
  101.5 39.2 %collective-permute-start.14 = (bf16[512,2176]{1,0:T(8,128)(2,1)}, bf16[512,2176]{1,0:T(8,128)(2,1)}, u32[]{:S(2)}, u32[]{:S(2)}) collective-permute-start(bf16[512,2176]{1,0:T(8,128)(2,1)} %get-tuple-element.337), channel_id=1, source_target_pairs={{0,8},{8,0},{16,24},{24,16},{1,9},{9,1},{17,25},{25,17},{2,10},{10... | collective-permute-start | bytes 6684680 | tf_op jit(solution)/shard_map/ppermute | solution.py:649
  101.5 39.2 %collective-permute-start.13 = (bf16[256,2176]{1,0:T(8,128)(2,1)S(1)}, bf16[256,2176]{1,0:T(8,128)(2,1)}, u32[]{:S(2)}, u32[]{:S(2)}) collective-permute-start(bf16[256,2176]{1,0:T(8,128)(2,1)S(1)} %get-tuple-element.536.refs_6_.refs_2_.refs_4_), channel_id=1, source_target_pairs={{0,16},{8,24},{16,0},{24,8},{1,17},{9,25},{17,1},{25,9},{2,18},{10... | collective-permute-start | bytes 3342344 | tf_op jit(solution)/shard_map/ppermute | solution.py:649
  103.0 28.1 %collective-permute-start.10 = (bf16[256,2048]{1,0:T(8,128)(2,1)}, bf16[256,2048]{1,0:T(8,128)(2,1)}, u32[]{:S(2)}, u32[]{:S(2)}) collective-permute-start(bf16[256,2048]{1,0:T(8,128)(2,1)} %collective-permute-done.8.refs_2_), channel_id=1, source_target_pairs={{0,1},{1,0},{2,3},{3,2},{4,5},{5,4},{6,7},{7,6},{8,9},{9,8},{10,11... | collective-permute-start | bytes 3145736 | tf_op jit(solution)/shard_map/ppermute | solution.py:649
  106.1 34.6 %collective-permute-start.12 = (bf16[256,2048]{1,0:T(8,128)(2,1)}, bf16[256,2048]{1,0:T(8,128)(2,1)}, u32[]{:S(2)}, u32[]{:S(2)}) collective-permute-start(bf16[256,2048]{1,0:T(8,128)(2,1)} %collective-permute-done.9), channel_id=1, source_target_pairs={{2,0},{3,1},{4,6},{5,7},{10,8},{11,9},{12,14},{13,15},{18,16},{19,... | collective-permute-start | bytes 3145736 | tf_op jit(solution)/shard_map/ppermute | solution.py:649
  113.1 66.6 %all-to-all-start.1 = ((bf16[8,64,1024]{2,1,0:T(8,128)(2,1)}), bf16[8,64,1024]{2,1,0:T(8,128)(2,1)S(1)}, u32[]{:S(2)}, u32[]{:S(2)}) async-start(bf16[8,64,1024]{2,1,0:T(8,128)(2,1)} %pack_columns.3), calls=%async_computation.1 | async-start | bytes 2097152 | tf_op jit(solution)/shard_map/all_to_all | solution.py:708
  140.7 36.6 %collective-permute-start.18 = (bf16[256,2176]{1,0:T(8,128)(2,1)S(1)}, bf16[256,2176]{1,0:T(8,128)(2,1)}, u32[]{:S(2)}, u32[]{:S(2)}) collective-permute-start(bf16[256,2176]{1,0:T(8,128)(2,1)S(1)} %get-tuple-element.537.refs_7_.refs_3_.refs_5_), channel_id=1, source_target_pairs={{0,16},{8,24},{16,0},{24,8},{1,17},{9,25},{17,1},{25,9},{2,18},{10... | collective-permute-start | bytes 3342344 | tf_op jit(solution)/shard_map/ppermute | solution.py:649
  141.3 36.1 %collective-permute-start.19 = (bf16[256,2176]{1,0:T(8,128)(2,1)}, bf16[256,2176]{1,0:T(8,128)(2,1)S(1)}, u32[]{:S(2)}, u32[]{:S(2)}) collective-permute-start(bf16[256,2176]{1,0:T(8,128)(2,1)} %collective-permute-done.13.refs_8_.refs_4_.refs_6_), channel_id=1, source_target_pairs={{0,8},{8,0},{16,24},{24,16},{1,9},{9,1},{17,25},{25,17},{2,10},{10... | collective-permute-start | bytes 3342344 | tf_op jit(solution)/shard_map/ppermute | solution.py:649
  142.6 28.0 %collective-permute-start.15 = (bf16[256,2048]{1,0:T(8,128)(2,1)S(1)}, bf16[256,2048]{1,0:T(8,128)(2,1)S(1)}, u32[]{:S(2)}, u32[]{:S(2)}) collective-permute-start(bf16[256,2048]{1,0:T(8,128)(2,1)S(1)} %broadcast_select_fusion.3.refs_4_), channel_id=1, source_target_pairs={{0,1},{1,0},{2,3},{3,2},{4,5},{5,4},{6,7},{7,6},{8,9},{9,8},{10,11... | collective-permute-start | bytes 3145736 | tf_op jit(solution)/shard_map/ppermute | solution.py:649
  143.4 33.9 %collective-permute-start.16 = (bf16[256,2048]{1,0:T(8,128)(2,1)}, bf16[256,2048]{1,0:T(8,128)(2,1)S(1)}, u32[]{:S(2)}, u32[]{:S(2)}) collective-permute-start(bf16[256,2048]{1,0:T(8,128)(2,1)} %collective-permute-done.11), channel_id=1, source_target_pairs={{2,0},{3,1},{4,6},{5,7},{10,8},{11,9},{12,14},{13,15},{18,16},{19,... | collective-permute-start | bytes 3145736 | tf_op jit(solution)/shard_map/ppermute | solution.py:649
  144.7 32.7 %collective-permute-start.17 = (bf16[256,2048]{1,0:T(8,128)(2,1)}, bf16[256,2048]{1,0:T(8,128)(2,1)S(1)}, u32[]{:S(2)}, u32[]{:S(2)}) collective-permute-start(bf16[256,2048]{1,0:T(8,128)(2,1)} %pad_maximum_fusion.refs_0_), channel_id=1, source_target_pairs={{2,4},{3,5},{4,2},{5,3},{10,12},{11,13},{12,10},{13,11},{18,20},{1... | collective-permute-start | bytes 3145736 | tf_op jit(solution)/shard_map/ppermute | solution.py:649
  179.8 58.7 %collective-permute-start.26 = (bf16[512,1024]{1,0:T(8,128)(2,1)S(1)}, bf16[512,1024]{1,0:T(8,128)(2,1)}, u32[]{:S(2)}, u32[]{:S(2)}) collective-permute-start(bf16[512,1024]{1,0:T(8,128)(2,1)S(1)} %unpack_columns.3.refs_4_), channel_id=1, source_target_pairs={{0,16},{8,24},{16,0},{24,8},{1,17},{9,25},{17,1},{25,9},{2,18},{10... | collective-permute-start | bytes 3145736 | tf_op jit(solution)/shard_map/ppermute | solution.py:649
  180.4 58.1 %collective-permute-start.27 = (bf16[512,1024]{1,0:T(8,128)(2,1)S(1)}, bf16[512,1024]{1,0:T(8,128)(2,1)}, u32[]{:S(2)}, u32[]{:S(2)}) collective-permute-start(bf16[512,1024]{1,0:T(8,128)(2,1)S(1)} %unpack_columns.3.refs_4_), channel_id=1, source_target_pairs={{0,8},{8,0},{16,24},{24,16},{1,9},{9,1},{17,25},{25,17},{2,10},{10... | collective-permute-start | bytes 3145736 | tf_op jit(solution)/shard_map/ppermute | solution.py:649
  209.1 29.4 %collective-permute-start.24 = (bf16[256,2048]{1,0:T(8,128)(2,1)S(1)}, bf16[256,2048]{1,0:T(8,128)(2,1)}, u32[]{:S(2)}, u32[]{:S(2)}) collective-permute-start(bf16[256,2048]{1,0:T(8,128)(2,1)S(1)} %broadcast_select_fusion.1.refs_2_), channel_id=1, source_target_pairs={{0,1},{1,0},{2,3},{3,2},{4,5},{5,4},{6,7},{7,6},{8,9},{9,8},{10,11... | collective-permute-start | bytes 3145736 | tf_op jit(solution)/shard_map/ppermute | solution.py:649
  210.8 27.9 %collective-permute-start.25 = (bf16[256,2048]{1,0:T(8,128)(2,1)}, bf16[256,2048]{1,0:T(8,128)(2,1)}, u32[]{:S(2)}, u32[]{:S(2)}) collective-permute-start(bf16[256,2048]{1,0:T(8,128)(2,1)} %collective-permute-done.22), channel_id=1, source_target_pairs={{2,0},{3,1},{4,6},{5,7},{10,8},{11,9},{12,14},{13,15},{18,16},{19,... | collective-permute-start | bytes 3145736 | tf_op jit(solution)/shard_map/ppermute | solution.py:649
  240.1 32.3 %collective-permute-start.28 = (bf16[256,2048]{1,0:T(8,128)(2,1)S(1)}, bf16[256,2048]{1,0:T(8,128)(2,1)S(1)}, u32[]{:S(2)}, u32[]{:S(2)}) collective-permute-start(bf16[256,2048]{1,0:T(8,128)(2,1)S(1)} %broadcast_select_fusion.refs_2_), channel_id=1, source_target_pairs={{0,1},{1,0},{2,3},{3,2},{4,5},{5,4},{6,7},{7,6},{8,9},{9,8},{10,11... | collective-permute-start | bytes 3145736 | tf_op jit(solution)/shard_map/ppermute | solution.py:649
  240.7 31.8 %collective-permute-start.29 = (bf16[256,2048]{1,0:T(8,128)(2,1)}, bf16[256,2048]{1,0:T(8,128)(2,1)S(1)}, u32[]{:S(2)}, u32[]{:S(2)}) collective-permute-start(bf16[256,2048]{1,0:T(8,128)(2,1)} %collective-permute-done.3.refs_1_), channel_id=1, source_target_pairs={{0,2},{1,3},{2,0},{3,1},{4,6},{5,7},{6,4},{7,5},{8,10},{9,11},{10,... | collective-permute-start | bytes 3145736 | tf_op jit(solution)/shard_map/ppermute | solution.py:649
  300.0 31.6 %collective-permute-start.33 = (bf16[256,2048]{1,0:T(8,128)(2,1)}, bf16[256,2048]{1,0:T(8,128)(2,1)}, u32[]{:S(2)}, u32[]{:S(2)}) collective-permute-start(bf16[256,2048]{1,0:T(8,128)(2,1)} %get-tuple-element.500), channel_id=1, source_target_pairs={{0,1},{1,0},{2,3},{3,2},{4,5},{5,4},{6,7},{7,6},{8,9},{9,8},{10,11... | collective-permute-start | bytes 3145736 | tf_op jit(solution)/shard_map/ppermute | solution.py:649
  300.8 30.8 %collective-permute-start.34 = (bf16[256,2048]{1,0:T(8,128)(2,1)S(1)}, bf16[256,2048]{1,0:T(8,128)(2,1)}, u32[]{:S(2)}, u32[]{:S(2)}) collective-permute-start(bf16[256,2048]{1,0:T(8,128)(2,1)S(1)} %add_convert_fusion.15), channel_id=1, source_target_pairs={{0,2},{1,3},{6,4},{7,5},{8,10},{9,11},{14,12},{15,13},{16,18},{17,... | collective-permute-start | bytes 3145736 | tf_op jit(solution)/shard_map/ppermute | solution.py:649
  360.8 36.7 %collective-permute-start.40 = (bf16[256,2048]{1,0:T(8,128)(2,1)}, bf16[256,2048]{1,0:T(8,128)(2,1)}, u32[]{:S(2)}, u32[]{:S(2)}) collective-permute-start(bf16[256,2048]{1,0:T(8,128)(2,1)} %get-tuple-element.559), channel_id=1, source_target_pairs={{0,1},{1,0},{2,3},{3,2},{4,5},{5,4},{6,7},{7,6},{8,9},{9,8},{10,11... | collective-permute-start | bytes 3145736 | tf_op jit(solution)/shard_map/ppermute | solution.py:649
  363.6 33.9 %collective-permute-start.41 = (bf16[256,2048]{1,0:T(8,128)(2,1)}, bf16[256,2048]{1,0:T(8,128)(2,1)S(1)}, u32[]{:S(2)}, u32[]{:S(2)}) collective-permute-start(bf16[256,2048]{1,0:T(8,128)(2,1)} %add_convert_fusion.11), channel_id=1, source_target_pairs={{2,4},{3,5},{4,2},{5,3},{10,12},{11,13},{12,10},{13,11},{18,20},{1... | collective-permute-start | bytes 3145736 | tf_op jit(solution)/shard_map/ppermute | solution.py:649
  367.3 30.3 %collective-permute-start.42 = (bf16[256,2048]{1,0:T(8,128)(2,1)}, bf16[256,2048]{1,0:T(8,128)(2,1)S(1)}, u32[]{:S(2)}, u32[]{:S(2)}) collective-permute-start(bf16[256,2048]{1,0:T(8,128)(2,1)} %add_convert_fusion.10), channel_id=1, source_target_pairs={{0,2},{1,3},{2,0},{3,1},{4,6},{5,7},{6,4},{7,5},{8,10},{9,11},{10,... | collective-permute-start | bytes 3145736 | tf_op jit(solution)/shard_map/ppermute | solution.py:649
  451.9 32.1 %collective-permute-start.52 = (bf16[256,2048]{1,0:T(8,128)(2,1)}, bf16[256,2048]{1,0:T(8,128)(2,1)}, u32[]{:S(2)}, u32[]{:S(2)}) collective-permute-start(bf16[256,2048]{1,0:T(8,128)(2,1)} %get-tuple-element.605), channel_id=1, source_target_pairs={{0,1},{1,0},{2,3},{3,2},{4,5},{5,4},{6,7},{7,6},{8,9},{9,8},{10,11... | collective-permute-start | bytes 3145736 | tf_op jit(solution)/shard_map/ppermute | solution.py:649
  454.8 29.3 %collective-permute-start.53 = (bf16[256,2048]{1,0:T(8,128)(2,1)}, bf16[256,2048]{1,0:T(8,128)(2,1)}, u32[]{:S(2)}, u32[]{:S(2)}) collective-permute-start(bf16[256,2048]{1,0:T(8,128)(2,1)} %add_convert_fusion.4), channel_id=1, source_target_pairs={{2,4},{3,5},{4,2},{5,3},{10,12},{11,13},{12,10},{13,11},{18,20},{1... | collective-permute-start | bytes 3145736 | tf_op jit(solution)/shard_map/ppermute | solution.py:649
  458.0 29.1 %collective-permute-start.54 = (bf16[256,2048]{1,0:T(8,128)(2,1)}, bf16[256,2048]{1,0:T(8,128)(2,1)}, u32[]{:S(2)}, u32[]{:S(2)}) collective-permute-start(bf16[256,2048]{1,0:T(8,128)(2,1)} %add_convert_fusion.3), channel_id=1, source_target_pairs={{0,2},{1,3},{2,0},{3,1},{4,6},{5,7},{6,4},{7,5},{8,10},{9,11},{10,... | collective-permute-start | bytes 3145736 | tf_op jit(solution)/shard_map/ppermute | solution.py:649
  462.7 52.4 %all-to-all-start.3 = ((bf16[8,64,1408]{2,1,0:T(8,128)(2,1)}), bf16[8,64,1408]{2,1,0:T(8,128)(2,1)S(1)}, u32[]{:S(2)}, u32[]{:S(2)}) async-start(bf16[8,64,1408]{2,1,0:T(8,128)(2,1)} %pack_rows.2), calls=%async_computation.3 | async-start | bytes 2883584 | tf_op jit(solution)/shard_map/all_to_all | solution.py:835
  515.1 44.1 %all-to-all-start.2 = ((bf16[8,64,1792]{2,1,0:T(8,128)(2,1)}), bf16[8,64,1792]{2,1,0:T(8,128)(2,1)S(1)}, u32[]{:S(2)}, u32[]{:S(2)}) async-start(bf16[8,64,1792]{2,1,0:T(8,128)(2,1)} %pack_rows.3), calls=%async_computation.2 | async-start | bytes 3670016 | tf_op jit(solution)/shard_map/all_to_all | solution.py:856
  (95 other events, 1221.5 us)
